TPU v7x, 32 devices: a whole 2x2x4 slice. The times are simulated.
32 devices in a mesh: clu: 8 (over z, x), frq: 4 (over y, core).
Axes of the slice: x: 2, y: 2, z: 4, core: 2. Of those that a mesh axis runs over, the one named last changes fastest.
Arguments:
- incident: float32 [4, 2, 16384, 128], P('frq', None, 'clu'), may hold values from -6 to 6
- initial: float32 [4, 2, 16384, 128], P('frq', None, 'clu'), may hold values from -3 to 3
- near_blocks: bfloat16 [128, 8, 4, 2, 128, 128], P('clu', None, 'frq'), may hold values from -0.125 to 0.125
- near_pattern: int32 [128, 8], P('clu'), may hold values from 0 to 47
- crack_blocks: bfloat16 [256, 4, 2, 128, 128], P('clu', 'frq'), may hold values from -0.25 to 0.25
- crack_cluster: int32 [256, 1], P('clu'), may hold values from 0 to 7; in each aligned block of 32 rows (0 to 31, 32 to 63, ...) at most 8 rows name the same one
- crack_source: int32 [256], P('clu'), may hold values from 0 to 3
- crack_target: int32 [256], P('clu'), may hold values from 0 to 15
- pulse_spectrum: float32 [4, 2], P('frq'), may hold values from -4 to 4
Outputs:
- scattered: float32 [4, 2, 16384, 128], P('frq', None, 'clu')
- time_trace: float32 [4, 16384, 128], P('frq', 'clu')
Inputs may be any that keep to these rules, and one draw needn't show every extreme that they name: `crack_cluster`: in the rows of one cluster no source cluster is named more than 8 times, a bound that some block reaches.
All inputs are finite; a program needn't handle non-finite values.
Results may differ from a plain program's by a relative error of at most 0.0014.
Values may be sent and summed in bfloat16 or wider, within the bound.
No kernel may reach another device: no remote copies, remote signals or barrier semaphores. Data moves between devices by JAX's collectives and lax.ppermute only.
A program may use at most 128 MiB of HBM per device.

v0:
```python
import jax
import jax.numpy as jnp
from jax import lax
from jax.sharding import PartitionSpec as P

FR_DEV = 1


epsilon = 1e-06


def with_halo(block, sides, width):
    for axis, dim in sides:
        count = lax.axis_size(axis)
        forward = [(i, i + 1) for i in range(count - 1)]
        forward.append((count - 1, 0))
        backward = [(target, source) for source, target in forward]
        low = lax.ppermute(
            lax.slice_in_dim(block, block.shape[dim] - width, None, axis=dim), axis, forward
        )
        high = lax.ppermute(lax.slice_in_dim(block, 0, width, axis=dim), axis, backward)
        block = jnp.concatenate([low, block, high], axis=dim)
    return block


def complex_times(factor, vector):
    real_part = factor[0][:, None, :] * vector[:, 0] - factor[1][:, None, :] * vector[:, 1]
    imag_part = factor[0][:, None, :] * vector[:, 1] + factor[1][:, None, :] * vector[:, 0]
    return jnp.stack([real_part, imag_part], axis=1)


def inner_local(former, latter):
    real_part = jnp.sum(former[:, 0] * latter[:, 0] + former[:, 1] * latter[:, 1], axis=1)
    imag_part = jnp.sum(former[:, 0] * latter[:, 1] - former[:, 1] * latter[:, 0], axis=1)
    return (real_part, imag_part)


def square_local(vector):
    return jnp.sum(vector[:, 0] * vector[:, 0] + vector[:, 1] * vector[:, 1], axis=1)


def least_squares(beta_norm, first_h, sub_one, second_h, third_h, sub_two):
    r_one = jnp.sqrt(first_h[0] ** 2 + first_h[1] ** 2 + sub_one**2)
    q_real = first_h[0] / r_one
    q_imag = first_h[1] / r_one
    q_low = sub_one / r_one
    mix_real = q_real * second_h[0] + q_imag * second_h[1] + q_low * third_h[0]
    mix_imag = q_real * second_h[1] - q_imag * second_h[0] + q_low * third_h[1]
    top_real = second_h[0] - (mix_real * q_real - mix_imag * q_imag)
    top_imag = second_h[1] - (mix_real * q_imag + mix_imag * q_real)
    mid_real = third_h[0] - mix_real * q_low
    mid_imag = third_h[1] - mix_imag * q_low
    r_two_sq = top_real**2 + top_imag**2 + mid_real**2 + mid_imag**2 + sub_two**2
    later_real = beta_norm * top_real / r_two_sq
    later_imag = -beta_norm * top_imag / r_two_sq
    early_real = (beta_norm * q_real - (mix_real * later_real - mix_imag * later_imag)) / r_one
    early_imag = (-beta_norm * q_imag - (mix_real * later_imag + mix_imag * later_real)) / r_one
    return ((early_real, early_imag), (later_real, later_imag))


def project(vectors, latter):
    terms = []
    for former in vectors:
        real_part, imag_part = inner_local(former, latter)
        terms.append(real_part)
        terms.append(imag_part)
    summed = lax.psum(tuple(terms), "clu")
    return [(summed[2 * place], summed[2 * place + 1]) for place in range(len(vectors))]


def lengths(vector):
    return lax.psum(square_local(vector), "clu")


def arnoldi_column(vectors, image):
    heights = project(vectors, image)
    for height, former in zip(heights, vectors):
        image = image - complex_times(height, former)
    squared = lengths(image)
    return (heights, image, jnp.sqrt(squared + epsilon))


def local(
    incident,
    initial,
    near_blocks,
    near_pattern,
    crack_blocks,
    crack_cluster,
    crack_source,
    crack_target,
    pulse_spectrum,
):
    freq_dev = incident.shape[0]
    panels = incident.shape[2]
    directions = incident.shape[3]
    nblocks = near_blocks.shape[0]
    near_span = near_blocks.shape[1]
    block_width = near_blocks.shape[4]
    edges = crack_blocks.shape[0]
    clusters = lax.axis_size("clu")
    capacity = max(2, (2 * edges + clusters - 1) // clusters)
    near_flat = near_pattern.reshape(-1)
    source_cluster = crack_cluster[:, 0]
    target_hot = (crack_target[None, :] == jnp.arange(nblocks, dtype=jnp.int32)[:, None]).astype(
        jnp.float32
    )
    edge_ids = jnp.arange(edges, dtype=jnp.int32)
    same_source = source_cluster[:, None] == source_cluster[None, :]
    earlier = edge_ids[:, None] > edge_ids[None, :]
    slot_rank = jnp.sum((same_source & earlier).astype(jnp.int32), axis=1)
    slot_index = source_cluster * capacity + slot_rank
    slot_hot = (
        slot_index[:, None] == jnp.arange(clusters * capacity, dtype=jnp.int32)[None, :]
    ).astype(jnp.int32)
    wanted = jnp.sum(slot_hot * crack_source[:, None], axis=0)
    requested = lax.all_to_all(wanted, "clu", split_axis=0, concat_axis=0, tiled=True)

    def fetch(vec_low):
        picked = jnp.take(vec_low, requested, axis=2)
        received = lax.all_to_all(picked, "clu", split_axis=2, concat_axis=2, tiled=True)
        return jnp.take(received, slot_index, axis=2)

    def apply(vector):
        vec_low = vector.astype(jnp.bfloat16).reshape(freq_dev, 2, nblocks, block_width, directions)
        extended = with_halo(vec_low, (("clu", 2),), nblocks)
        columns = jnp.take(extended, near_flat, axis=2).reshape(
            freq_dev, 2, nblocks, near_span, block_width, directions
        )
        products = jnp.einsum(
            "bsfcpq,fdbsqk->fcdbpk", near_blocks, columns, preferred_element_type=jnp.float32
        )
        near_real = products[:, 0, 0] - products[:, 1, 1]
        near_imag = products[:, 0, 1] + products[:, 1, 0]
        chosen = fetch(vec_low)
        crack_prod = jnp.einsum(
            "efcpq,fdeqk->fcdepk", crack_blocks, chosen, preferred_element_type=jnp.float32
        )
        crack_real = crack_prod[:, 0, 0] - crack_prod[:, 1, 1]
        crack_imag = crack_prod[:, 0, 1] + crack_prod[:, 1, 0]
        added_real = jnp.einsum(
            "be,fepk->fbpk", target_hot, crack_real, precision=lax.Precision.HIGHEST
        )
        added_imag = jnp.einsum(
            "be,fepk->fbpk", target_hot, crack_imag, precision=lax.Precision.HIGHEST
        )
        result = jnp.stack([near_real + added_real, near_imag + added_imag], axis=1)
        return 0.5 * vector + result.reshape(freq_dev, 2, panels, directions)

    residual = incident - apply(initial)
    beta_norm = jnp.sqrt(lax.psum(square_local(residual), "clu") + epsilon)
    basis_one = residual / beta_norm[:, None, None, :]
    heights, image, sub_one = arnoldi_column([basis_one], apply(basis_one))
    first_h = heights[0]
    basis_two = image / sub_one[:, None, None, :]
    heights, image, sub_two = arnoldi_column([basis_one, basis_two], apply(basis_two))
    early, later = least_squares(beta_norm, first_h, sub_one, heights[0], heights[1], sub_two)
    scattered = initial + complex_times(early, basis_one) + complex_times(later, basis_two)
    total_times = FR_DEV * lax.axis_size("frq")
    times = jnp.arange(FR_DEV * lax.axis_size("frq"), dtype=jnp.int32).astype(jnp.float32)[:, None]
    freqs = (lax.axis_index("frq") * freq_dev + jnp.arange(freq_dev, dtype=jnp.int32)).astype(
        jnp.float32
    )[None, :]
    angle = 2.0 * jnp.pi * times * freqs / total_times
    coef_real = pulse_spectrum[None, :, 0] * jnp.cos(angle) - pulse_spectrum[None, :, 1] * jnp.sin(
        angle
    )
    coef_imag = -(
        pulse_spectrum[None, :, 0] * jnp.sin(angle) + pulse_spectrum[None, :, 1] * jnp.cos(angle)
    )
    term = jnp.einsum("tf,fpk->tpk", coef_real, scattered[:, 0], precision=lax.Precision.HIGHEST)
    time_trace = lax.psum_scatter(
        term
        + jnp.einsum("tf,fpk->tpk", coef_imag, scattered[:, 1], precision=lax.Precision.HIGHEST),
        "frq",
        scatter_dimension=0,
        tiled=True,
    )
    return (scattered, time_trace)


def solution(mesh):
    in_specs = (
        P("frq", None, "clu", None),
        P("frq", None, "clu", None),
        P("clu", None, "frq", None, None, None),
        P("clu", None),
        P("clu", "frq", None, None, None),
        P("clu", None),
        P("clu"),
        P("clu"),
        P("frq", None),
    )
    out_specs = (P("frq", None, "clu", None), P("frq", "clu", None))
    return jax.shard_map(local, mesh=mesh, in_specs=in_specs, out_specs=out_specs, check_vma=False)
```

profile of v0, /device:TPU:0, one launch (start us, length us, event | category | flops | bytes accessed | tf_op | source)
XLA Modules:
  0.0 733.1 jit_solution(3434305039883475400)
XLA Ops:
  10.3 7.3 all-to-all-start
  19.2 4.7 all-to-all-done
  28.2 4.6 fusion.11
  32.8 4.7 all-to-all-start.1
  42.5 89.0 %collective-permute-done = bf16[1,2,16,128,128]{4,3,2,1,0:T(8,128)(2,1)} collective-permute-done((bf16[1,2,16,128,128]{4,3,2,1,0:T(8,128)(2,1)S(1)}, bf16[1,2,16,128,128]{4,3,2,1,0:T(8,128)(2,1)}, u32[]{:S(2)}, u32[]{:S(2)}) %collective-permute-start) | collective-permute-done | bytes 1048608 | tf_op jit(solution)/shard_map/ppermute | solution.py:18
  134.6 8.5 %gather_fusion = bf16[128,2,128,128]{3,2,1,0:T(8,128)(2,1)} fusion(bf16[2,48,128,128]{3,2,1,0:T(8,128)(2,1)} %maximum_bitcast_fusion, s32[1024]{0:T(1024)S(1)} %pad_clamp_fusion.2), kind=kCustom, calls=%fused_computation.clone | custom fusion | bytes 16777728 | tf_op jit(solution)/shard_map/jit(_take)/gather | solution.py:127
  143.0 7.4 %bitcast_select_fusion.2 = bf16[1,2,128,128,128]{4,3,1,2,0:T(8,128)(2,1)} fusion(bf16[128,2,128,128]{3,2,1,0:T(8,128)(2,1)} %gather_fusion, pred[128]{0:T(512)(128)(4,1)S(1)} %compare_and_fusion.2), kind=kLoop, calls=%fused_computation.11 | loop fusion | flops 4194304 | bytes 16777344 | tf_op jit(solution)/shard_map/jit(_take)/select_n | solution.py:127
  150.5 10.0 %fusion.12 = f32[1,2,2,16,128,128]{5,4,1,2,3,0:T(8,128)} fusion(bf16[2,16,8,128,128,1]{4,3,0,2,1,5:T(8,128)(2,1)} %bitcast.313, bf16[16,8,1,2,128,128]{5,4,3,2,1,0:T(8,128)(2,1)} %param.17), kind=kOutput, calls=%fused_computation.37 | convolution fusion | flops 2147483648 | bytes 20971520 | tf_op jit(solution)/shard_map/bsfcpq,fdbsqk->fcdbpk/dot_general | solution.py:130
  160.5 4.7 copy.213
  189.7 36.7 %psum.75 = f32[1,128]{1,0:T(1,128)S(1)} all-reduce(f32[1,128]{1,0:T(1,128)S(1)} %bitcast.333), channel_id=1, replica_groups=mesh['clu'=8,'frq'=4] {'clu'}, use_global_device_ids=true, to_apply=%region_3.0 | all-reduce | flops 128 | bytes 1024 | tf_op jit(solution)/shard_map/psum | solution.py:151
  232.6 4.6 fusion.10
  237.2 4.6 all-to-all-start.2
  246.6 85.1 %collective-permute-done.2 = bf16[1,2,16,128,128]{4,3,2,1,0:T(8,128)(2,1)S(1)} collective-permute-done((bf16[1,2,16,128,128]{4,3,2,1,0:T(8,128)(2,1)S(1)}, bf16[1,2,16,128,128]{4,3,2,1,0:T(8,128)(2,1)S(1)}, u32[]{:S(2)}, u32[]{:S(2)}) %collective-permute-start.2) | collective-permute-done | bytes 1048608 | tf_op jit(solution)/shard_map/ppermute | solution.py:18
  333.6 8.5 %gather_fusion.3 = bf16[128,2,128,128]{3,2,1,0:T(8,128)(2,1)} fusion(bf16[2,48,128,128]{3,2,1,0:T(8,128)(2,1)} %maximum_bitcast_fusion.1, s32[1024]{0:T(1024)S(1)} %pad_clamp_fusion.2), kind=kCustom, calls=%fused_computation.3.clone | custom fusion | bytes 16777728 | tf_op jit(solution)/shard_map/jit(_take)/gather | solution.py:127
  342.0 7.4 %bitcast_select_fusion.1 = bf16[1,2,128,128,128]{4,3,1,2,0:T(8,128)(2,1)} fusion(bf16[128,2,128,128]{3,2,1,0:T(8,128)(2,1)} %gather_fusion.3, pred[128]{0:T(512)(128)(4,1)S(1)} %compare_and_fusion.2), kind=kLoop, calls=%fused_computation.10 | loop fusion | flops 4194304 | bytes 16777344 | tf_op jit(solution)/shard_map/jit(_take)/select_n | solution.py:127
  349.4 10.1 %fusion.17 = f32[1,2,2,16,128,128]{5,4,1,2,3,0:T(8,128)} fusion(bf16[2,16,8,128,128,1]{4,3,0,2,1,5:T(8,128)(2,1)} %bitcast.314, bf16[16,8,1,2,128,128]{5,4,3,2,1,0:T(8,128)(2,1)} %param.17), kind=kOutput, calls=%fused_computation.38 | convolution fusion | flops 2147483648 | bytes 20971520 | tf_op jit(solution)/shard_map/bsfcpq,fdbsqk->fcdbpk/dot_general | solution.py:130
  359.5 4.7 copy.212
  364.2 4.3 gather_fusion.5
  391.6 36.8 %all-reduce.1 = (f32[1,128]{1,0:T(1,128)S(1)}, f32[1,128]{1,0:T(1,128)S(1)}) all-reduce(f32[1,128]{1,0:T(1,128)S(1)} %bitcast.330, f32[1,128]{1,0:T(1,128)S(1)} %bitcast.329), channel_id=1, replica_groups=mesh['clu'=8,'frq'=4] {'clu'}, use_global_device_ids=true, to_apply=%region_7.11 | all-reduce | flops 256 | bytes 2048 | tf_op jit(solution)/shard_map/psum | solution.py:67
  432.0 17.5 %psum.80 = f32[1,128]{1,0:T(1,128)S(1)} all-reduce(f32[1,128]{1,0:T(1,128)S(1)} %bitcast.331), channel_id=1, replica_groups=mesh['clu'=8,'frq'=4] {'clu'}, use_global_device_ids=true, to_apply=%region_9.13 | all-reduce | flops 128 | bytes 1024 | tf_op jit(solution)/shard_map/psum | solution.py:72
  449.5 4.6 fusion.97
  457.1 4.6 fusion.9
  461.6 4.7 all-to-all-start.3
  473.1 81.5 %collective-permute-done.4 = bf16[1,2,16,128,128]{4,3,2,1,0:T(8,128)(2,1)} collective-permute-done((bf16[1,2,16,128,128]{4,3,2,1,0:T(8,128)(2,1)S(1)}, bf16[1,2,16,128,128]{4,3,2,1,0:T(8,128)(2,1)}, u32[]{:S(2)}, u32[]{:S(2)}) %collective-permute-start.4) | collective-permute-done | bytes 1048608 | tf_op jit(solution)/shard_map/ppermute | solution.py:18
  557.6 8.5 %gather_fusion.6 = bf16[128,2,128,128]{3,2,1,0:T(8,128)(2,1)} fusion(bf16[2,48,128,128]{3,2,1,0:T(8,128)(2,1)} %maximum_bitcast_fusion.2, s32[1024]{0:T(1024)S(1)} %pad_clamp_fusion.2), kind=kCustom, calls=%fused_computation.4.clone | custom fusion | bytes 16777728 | tf_op jit(solution)/shard_map/jit(_take)/gather | solution.py:127
  566.0 7.4 %bitcast_select_fusion = bf16[1,2,128,128,128]{4,3,1,2,0:T(8,128)(2,1)} fusion(bf16[128,2,128,128]{3,2,1,0:T(8,128)(2,1)} %gather_fusion.6, pred[128]{0:T(512)(128)(4,1)S(1)} %compare_and_fusion.2), kind=kLoop, calls=%fused_computation.9 | loop fusion | flops 4194304 | bytes 16777344 | tf_op jit(solution)/shard_map/jit(_take)/select_n | solution.py:127
  573.5 10.0 %fusion.22 = f32[1,2,2,16,128,128]{5,4,1,2,3,0:T(8,128)} fusion(bf16[2,16,8,128,128,1]{4,3,0,2,1,5:T(8,128)(2,1)} %bitcast.312, bf16[16,8,1,2,128,128]{5,4,3,2,1,0:T(8,128)(2,1)} %param.17), kind=kOutput, calls=%fused_computation.39 | convolution fusion | flops 2147483648 | bytes 20971520 | tf_op jit(solution)/shard_map/bsfcpq,fdbsqk->fcdbpk/dot_general | solution.py:130
  583.5 4.7 copy.211
  588.2 4.3 gather_fusion.8
  617.2 36.6 %all-reduce = (f32[1,128]{1,0:T(1,128)S(1)}, f32[1,128]{1,0:T(1,128)S(1)}, f32[1,128]{1,0:T(1,128)S(1)}, f32[1,128]{1,0:T(1,128)S(1)}) all-reduce(f32[1,128]{1,0:T(1,128)S(1)} %bitcast.326, f32[1,128]{1,0:T(1,128)S(1)} %bitcast.327, f32[1,128]{1,0:T(1,128)S(1)} %bitcast.328, ...), channel_id=1, replica_groups=mesh['clu'=8,'frq'=4] {'clu'}, use_global_device_ids=true, to_apply=%region_17.21 | all-reduce | flops 512 | bytes 4096 | tf_op jit(solution)/shard_map/psum | solution.py:67
  657.6 17.5 %psum.89 = f32[1,128]{1,0:T(1,128)S(1)} all-reduce(f32[1,128]{1,0:T(1,128)S(1)} %bitcast.332), channel_id=1, replica_groups=mesh['clu'=8,'frq'=4] {'clu'}, use_global_device_ids=true, to_apply=%region_19.23 | all-reduce | flops 128 | bytes 1024 | tf_op jit(solution)/shard_map/psum | solution.py:72
  683.1 43.0 %reduce-scatter.2.cloned.1.call-done = f32[1,2048,128]{2,1,0:T(8,128)} async-done(((f32[4,2048,128]{2,1,0:T(8,128)}), f32[1,2048,128]{2,1,0:T(8,128)}) %reduce-scatter.2.cloned.1.call-update) | async-done | bytes 1048592 | tf_op jit(solution)/shard_map/reduce_scatter | solution.py:172
  (139 shorter events, 130.0 us)
Async XLA Ops:
  7.2 162.4 %copy-start = (bf16[32,1,2,128,128]{4,3,2,1,0:T(8,128)(2,1)S(1)}, bf16[32,1,2,128,128]{4,3,2,1,0:T(8,128)(2,1)}, u32[]{:S(2)}) copy-start(bf16[32,1,2,128,128]{4,3,2,1,0:T(8,128)(2,1)} %param.19) | copy-start | bytes 6291460
  10.3 13.6 %all-to-all-start = ((s32[8,8,1]{1,2,0:T(1,128)}), s32[8,8,1]{1,2,0:T(1,128)S(1)}, u32[]{:S(2)}, u32[]{:S(2)}) async-start(s32[8,8,1]{1,2,0:T(1,128)} %bitcast.17), calls=%async_computation | async-start | bytes 8192 | tf_op jit(solution)/shard_map/all_to_all | solution.py:117
  32.8 9.5 %copy-start.24 = (s32[16,8]{0,1:T(8,128)S(1)}, s32[16,8]{0,1:T(8,128)}, u32[]{:S(2)}) copy-start(s32[16,8]{0,1:T(8,128)} %param.18) | copy-start | bytes 1540
  32.8 9.7 %copy-start.26 = (s32[32,1]{0,1:T(1,128)S(1)}, s32[32,1]{0,1:T(1,128)}, u32[]{:S(2)}) copy-start(s32[32,1]{0,1:T(1,128)} %param.20) | copy-start | bytes 388
  32.8 127.7 %all-to-all-start.1 = ((bf16[1,2,64,128,128]{4,3,1,0,2:T(8,128)(2,1)}), bf16[1,2,64,128,128]{4,3,1,0,2:T(8,128)(2,1)}, u32[]{:S(2)}, u32[]{:S(2)}) async-start(bf16[1,2,64,128,128]{4,3,1,0,2:T(8,128)(2,1)} %fusion.11), calls=%async_computation.1 | async-start | bytes 8388608 | tf_op jit(solution)/shard_map/all_to_all | solution.py:121
  37.5 94.0 %collective-permute-start = (bf16[1,2,16,128,128]{4,3,2,1,0:T(8,128)(2,1)S(1)}, bf16[1,2,16,128,128]{4,3,2,1,0:T(8,128)(2,1)}, u32[]{:S(2)}, u32[]{:S(2)}) collective-permute-start(bf16[1,2,16,128,128]{4,3,2,1,0:T(8,128)(2,1)S(1)} %bitcast.292), channel_id=1, source_target_pairs={{0,4},{4,8},{8,12},{12,16},{16,20},{20,24},{24,28},{28,0},{1,5},{5... | collective-permute-start | bytes 3145736 | tf_op jit(solution)/shard_map/ppermute | solution.py:18
  39.4 92.2 %collective-permute-start.1 = (bf16[1,2,16,128,128]{4,3,2,1,0:T(8,128)(2,1)S(1)}, bf16[1,2,16,128,128]{4,3,2,1,0:T(8,128)(2,1)}, u32[]{:S(2)}, u32[]{:S(2)}) collective-permute-start(bf16[1,2,16,128,128]{4,3,2,1,0:T(8,128)(2,1)S(1)} %bitcast.293), channel_id=1, source_target_pairs={{4,0},{8,4},{12,8},{16,12},{20,16},{24,20},{28,24},{0,28},{5,1},{9... | collective-permute-start | bytes 3145736 | tf_op jit(solution)/shard_map/ppermute | solution.py:21
  179.1 3.1 copy-start.23
  182.2 2.6 copy-start.17
  182.2 3.5 copy-start.19
  185.6 1.6 copy-start.8
  185.6 2.2 copy-start.22
  237.2 122.3 %all-to-all-start.2 = ((bf16[1,2,64,128,128]{4,3,1,0,2:T(8,128)(2,1)}), bf16[1,2,64,128,128]{4,3,1,0,2:T(8,128)(2,1)}, u32[]{:S(2)}, u32[]{:S(2)}) async-start(bf16[1,2,64,128,128]{4,3,1,0,2:T(8,128)(2,1)} %fusion.10), calls=%async_computation.2 | async-start | bytes 8388608 | tf_op jit(solution)/shard_map/all_to_all | solution.py:121
  241.8 89.9 %collective-permute-start.2 = (bf16[1,2,16,128,128]{4,3,2,1,0:T(8,128)(2,1)S(1)}, bf16[1,2,16,128,128]{4,3,2,1,0:T(8,128)(2,1)S(1)}, u32[]{:S(2)}, u32[]{:S(2)}) collective-permute-start(bf16[1,2,16,128,128]{4,3,2,1,0:T(8,128)(2,1)S(1)} %bitcast.296), channel_id=1, source_target_pairs={{0,4},{4,8},{8,12},{12,16},{16,20},{20,24},{24,28},{28,0},{1,5},{5... | collective-permute-start | bytes 3145736 | tf_op jit(solution)/shard_map/ppermute | solution.py:18
  243.7 88.0 %collective-permute-start.3 = (bf16[1,2,16,128,128]{4,3,2,1,0:T(8,128)(2,1)S(1)}, bf16[1,2,16,128,128]{4,3,2,1,0:T(8,128)(2,1)S(1)}, u32[]{:S(2)}, u32[]{:S(2)}) collective-permute-start(bf16[1,2,16,128,128]{4,3,2,1,0:T(8,128)(2,1)S(1)} %bitcast.297), channel_id=1, source_target_pairs={{4,0},{8,4},{12,8},{16,12},{20,16},{24,20},{28,24},{0,28},{5,1},{9... | collective-permute-start | bytes 3145736 | tf_op jit(solution)/shard_map/ppermute | solution.py:21
  384.6 2.5 copy-start.20
  387.1 3.3 copy-start.1
  390.3 40.0 %copy-start.10 = (f32[1,16,128,128]{3,2,1,0:T(8,128)}, f32[1,16,128,128]{3,2,1,0:T(8,128)S(1)}, u32[]{:S(2)}) copy-start(f32[1,16,128,128]{3,2,1,0:T(8,128)S(1)} %get-tuple-element.43) | copy-start | bytes 3145732
  428.4 2.2 copy-start.2
  428.4 2.5 copy-start.12
  461.6 9.6 %copy-start.25 = (f32[1,2]{1,0:T(1,128)S(1)}, f32[1,2]{1,0:T(1,128)}, u32[]{:S(2)}) copy-start(f32[1,2]{1,0:T(1,128)} %param.23) | copy-start | bytes 28
  461.6 121.8 %all-to-all-start.3 = ((bf16[1,2,64,128,128]{4,3,1,0,2:T(8,128)(2,1)}), bf16[1,2,64,128,128]{4,3,1,0,2:T(8,128)(2,1)}, u32[]{:S(2)}, u32[]{:S(2)}) async-start(bf16[1,2,64,128,128]{4,3,1,0,2:T(8,128)(2,1)} %fusion.9), calls=%async_computation.3 | async-start | bytes 8388608 | tf_op jit(solution)/shard_map/all_to_all | solution.py:121
  466.4 259.7 %reduce-scatter.2.cloned.1.call-start = ((), (), s32[]{:S(2)}) async-start(), calls=%async_computation.5 | async-start | bytes 5242880 | tf_op jit(solution)/shard_map/reduce_scatter | solution.py:172
  466.4 88.1 %collective-permute-start.4 = (bf16[1,2,16,128,128]{4,3,2,1,0:T(8,128)(2,1)S(1)}, bf16[1,2,16,128,128]{4,3,2,1,0:T(8,128)(2,1)}, u32[]{:S(2)}, u32[]{:S(2)}) collective-permute-start(bf16[1,2,16,128,128]{4,3,2,1,0:T(8,128)(2,1)S(1)} %bitcast.288), channel_id=1, source_target_pairs={{0,4},{4,8},{8,12},{12,16},{16,20},{20,24},{24,28},{28,0},{1,5},{5... | collective-permute-start | bytes 3145736 | tf_op jit(solution)/shard_map/ppermute | solution.py:18
  468.3 86.3 %collective-permute-start.5 = (bf16[1,2,16,128,128]{4,3,2,1,0:T(8,128)(2,1)S(1)}, bf16[1,2,16,128,128]{4,3,2,1,0:T(8,128)(2,1)}, u32[]{:S(2)}, u32[]{:S(2)}) collective-permute-start(bf16[1,2,16,128,128]{4,3,2,1,0:T(8,128)(2,1)S(1)} %bitcast.289), channel_id=1, source_target_pairs={{4,0},{8,4},{12,8},{16,12},{20,16},{24,20},{28,24},{0,28},{5,1},{9... | collective-permute-start | bytes 3145736 | tf_op jit(solution)/shard_map/ppermute | solution.py:21
  608.7 2.5 copy-start.21
  611.2 3.3 copy-start.5
  614.4 2.0 copy-start.3
  653.8 2.9 copy-start.6
  653.8 3.1 copy-start.16
  675.2 2.2 copy-start.4
  677.4 1.6 copy-start.9
  (6 other events, 7.0 us)
Sparse Core Ops, SparseCore 0:
  683.2 42.8 reduce-scatter.1
where the time goes:
time: 745 us; the launch traced here: 733 us
  waiting for transfers between devices  303 us (41%)
  blocking collectives  145 us (19%)
  local copies, waits for them, and re-layouts  92.1 us (12%)
  other arithmetic  86.2 us (12%)
  matrix products  56.2 us (8%)
  starting transfers between devices  35.6 us (5%)
  between operations  14.7 us (2%)
    ppermute x3, waiting for transfers between devices, with_halo(): lax.ppermute(lax.slice_in_dim(block, block.shape[dim] - width, None, axis...  256 us
    psum x2, blocking collectives, project(): summed = lax.psum(tuple(terms), 'clu')  73.4 us
    reduce_scatter x1, waiting for transfers between devices, local(): lax.psum_scatter(term + jnp.einsum('tf,fpk->tpk', coef_imag, scattered[:,...  43 us
    psum x1, blocking collectives, local(): beta_norm = jnp.sqrt(lax.psum(square_local(residual), 'clu') + epsilon)  36.7 us
    psum x2, blocking collectives, lengths(): return lax.psum(square_local(vector), 'clu')  35 us
    dot_general x3, matrix products, apply(): jnp.einsum('bsfcpq,fdbsqk->fcdbpk', near_blocks, columns, preferred_eleme...  30.1 us
    gather x3, local copies, waits for them, and re-layouts, apply(): jnp.take(extended, near_flat, axis=2)  25.4 us
    select_n x4, other arithmetic, apply(): jnp.take(extended, near_flat, axis=2)  22.3 us
  transfers between devices with their start and end apart: 11, of which 5 were waited for; matrix products, arithmetic and copies ran while one was open for 12% of the time, Pallas kernels for 0%

commit v1 on v0

v1 whole, which is shorter than its diff:
```python
import functools

import jax
import jax.numpy as jnp
from jax import lax
from jax.experimental import pallas as pl
from jax.experimental.pallas import tpu as pltpu
from jax.sharding import PartitionSpec as P

EPS = 1e-06
STREAMS = 1
VMEM_LIMIT = 44 * 1024 * 1024


def turn(rows):
    half = rows.shape[1] // 2
    if half % 128 == 0:
        return jnp.concatenate([-rows[:, half:], rows[:, :half]], axis=1)
    lane = lax.broadcasted_iota(jnp.int32, rows.shape, 1)
    rolled = pltpu.roll(rows, half, 1)
    return jnp.where(lane < half, -rolled, rolled)


def join(real, imag, stream, streams):
    if streams == 1:
        return jnp.concatenate([real, imag], axis=1)
    half = real.shape[1] // 2
    lane = lax.broadcasted_iota(jnp.int32, real.shape, 1)
    if stream == 0:
        return jnp.where(lane < half, real, pltpu.roll(imag, half, 1))
    return jnp.where(lane < half, pltpu.roll(real, half, 1), imag)


def col_sum(rows):
    return jnp.sum(rows.reshape(rows.shape[0] // 8, 8, rows.shape[1]), axis=0)


def apply_kernel(step, stream, streams, sizes, offsets, *refs):
    nblocks, span, edges, width = sizes
    nparts = len(offsets)
    near_idx, crack_idx, crack_tgt, near_ref, crack_ref = refs[:5]
    parts = refs[5 : 5 + nparts]
    rest = refs[5 + nparts :]
    extras = rest[:2] if step != 2 else rest[:1]
    rest = rest[len(extras) :]
    nouts = (3, 3, 1)[step - 1]
    outs, rest = rest[:nouts], rest[nouts:]
    near_v, crack_v, source_v, extra_v, acc, part_sem, near_sem, crack_sem, extra_sem = rest

    part_copies = []
    for place, (part, offset) in enumerate(zip(parts, offsets)):
        part_copies.append(
            pltpu.make_async_copy(
                part, source_v.at[pl.ds(offset, part.shape[0])], part_sem.at[place]
            )
        )
    for copy in part_copies:
        copy.start()

    def near_copy(g):
        return pltpu.make_async_copy(near_ref.at[g], near_v.at[g], near_sem.at[g])

    for g in range(nblocks):
        near_copy(g).start()
    crack_copy = pltpu.make_async_copy(crack_ref, crack_v, crack_sem)
    crack_copy.start()
    extra_copies = [
        pltpu.make_async_copy(extra, extra_v.at[place], extra_sem.at[place])
        for place, extra in enumerate(extras)
    ]
    for copy in extra_copies:
        copy.start()
    for copy in part_copies:
        copy.wait()

    def near_row(g, carry):
        near_copy(g).wait()
        left = jnp.concatenate([near_v[g, s] for s in range(span)], axis=1)
        right = jnp.concatenate([source_v[near_idx[g * span + s]] for s in range(span)], axis=0)
        acc[g] = jnp.dot(left, right, preferred_element_type=jnp.float32)
        return carry

    lax.fori_loop(0, nblocks, near_row, 0)
    crack_copy.wait()

    def crack_edge(e, carry):
        target = crack_tgt[e]
        acc[target] += jnp.dot(
            crack_v[e], source_v[crack_idx[e]], preferred_element_type=jnp.float32
        )
        return carry

    lax.fori_loop(0, edges, crack_edge, 0)
    for copy in extra_copies:
        copy.wait()

    def image(g):
        total = acc[g]
        return total[:width] + turn(total[width:])

    lanes = acc.shape[2]
    nsums = (1, 3, 5)[step - 1]
    zero = jnp.zeros((8, lanes), jnp.float32)

    def finish(g, sums):
        rows = pl.ds(pl.multiple_of(g * width, width), width)
        new = image(g)
        if step == 1:
            incident = join(extra_v[0, 0, rows], extra_v[0, 1, rows], stream, streams)
            initial = join(extra_v[1, 0, rows], extra_v[1, 1, rows], stream, streams)
            new = incident - 0.5 * initial - new
            terms = (new * new,)
        elif step == 2:
            first = extra_v[0, rows]
            terms = (first * new, first * turn(new), new * new)
        else:
            first, second, turned = extra_v[0, rows], extra_v[1, rows], turn(new)
            terms = (first * new, first * turned, second * new, second * turned, new * new)
        if step != 3:
            outs[0][rows, :] = new
            outs[1][rows, :] = new.astype(jnp.bfloat16)
        return tuple(total + col_sum(term) for total, term in zip(sums, terms))

    sums = lax.fori_loop(0, nblocks, finish, (zero,) * nsums)
    sums = [jnp.sum(total, axis=0, keepdims=True) for total in sums]
    sums.append(jnp.zeros((8 - nsums, lanes), jnp.float32))
    outs[-1][...] = jnp.concatenate(sums, axis=0)


def apply_call(step, stream, streams, tables, near, crack, parts, extras):
    nblocks, span = near.shape[:2]
    edges, width = crack.shape[0], near.shape[3]
    lanes = parts[0].shape[2]
    rows = nblocks * width
    offsets, total = [], 0
    for part in parts:
        offsets.append(total)
        total += part.shape[0]
    vector = jax.ShapeDtypeStruct((rows, lanes), jnp.float32)
    gram = jax.ShapeDtypeStruct((8, lanes), jnp.float32)
    if step == 3:
        out_shape = (gram,)
    else:
        out_shape = (vector, jax.ShapeDtypeStruct((rows, lanes), jnp.bfloat16), gram)
    smem = pl.BlockSpec(memory_space=pltpu.SMEM)
    anywhere = pl.BlockSpec(memory_space=pl.ANY)
    whole = pl.BlockSpec(memory_space=pltpu.VMEM)
    body = functools.partial(
        apply_kernel, step, stream, streams, (nblocks, span, edges, width), tuple(offsets)
    )
    return pl.pallas_call(
        body,
        out_shape=out_shape,
        in_specs=[smem] * 3 + [anywhere] * (2 + len(parts) + len(extras)),
        out_specs=tuple(whole for _ in out_shape),
        scratch_shapes=[
            pltpu.VMEM(near.shape, near.dtype),
            pltpu.VMEM(crack.shape, crack.dtype),
            pltpu.VMEM((total, width, lanes), jnp.bfloat16),
            pltpu.VMEM((len(extras), *extras[0].shape), jnp.float32),
            pltpu.VMEM((nblocks, 2 * width, lanes), jnp.float32),
            pltpu.SemaphoreType.DMA((len(parts),)),
            pltpu.SemaphoreType.DMA((nblocks,)),
            pltpu.SemaphoreType.DMA,
            pltpu.SemaphoreType.DMA((len(extras),)),
        ],
        compiler_params=pltpu.CompilerParams(vmem_limit_bytes=VMEM_LIMIT),
        cost_estimate=pl.CostEstimate(
            flops=4 * width * width * lanes * (nblocks * span + edges),
            bytes_accessed=near.size * 2 + crack.size * 2,
            transcendentals=0,
        ),
        name=f"operator_{step}_{stream}",
    )(*tables, near, crack, *parts, *extras)


def swap(value, axis, distance):
    count = lax.axis_size(axis)
    return lax.ppermute(value, axis, [(i, i ^ distance) for i in range(count)])


def shift(value, axis, distance):
    count = lax.axis_size(axis)
    return lax.ppermute(value, axis, [(i, (i + distance) % count) for i in range(count)])


def tuned():
    return lax.axis_size("clu") == 8


def exchange(low, front):
    count = lax.axis_size("clu")
    head = low[:front]
    if not tuned():
        every = lax.all_gather(head, "clu", axis=0, tiled=True)
        return [low, shift(low, "clu", -1), shift(low, "clu", 1), every]
    even = lax.axis_index("clu") % 2 == 0
    beside = swap(low, "clu", 1)
    before, across, after = (shift(head, "clu", d) for d in (2, 4, 6))
    ring = [(i, (i + 2) % count if i % 2 == 0 else (i - 2) % count) for i in range(count)]
    beyond = lax.ppermute(beside, "clu", ring)
    near_side = jnp.where(even, before, after)
    others = swap(jnp.concatenate([near_side, across], axis=0), "clu", 1)
    return [low, beside, beyond, before, across, after, others]


def source_tables(near_pattern, crack_cluster, crack_source, nblocks, front):
    count = lax.axis_size("clu")
    me = lax.axis_index("clu")
    side, block = near_pattern.reshape(-1) // nblocks, near_pattern.reshape(-1) % nblocks
    if not tuned():
        place = jnp.where(side == 1, 0, jnp.where(side == 2, 1, 2))
        return place * nblocks + block, 3 * nblocks + crack_cluster * front + crack_source
    odd = me % 2
    place = jnp.where(side == 1, 0, jnp.where((side == 2) ^ (odd == 1), 1, 2))
    offset = (crack_cluster - me) % count
    offset = jnp.where(odd == 1, (-offset) % count, offset)
    base = 3 * nblocks
    before = jnp.where(odd == 1, base + 2 * front, base)
    after = jnp.where(odd == 1, base, base + 2 * front)
    start = jnp.select(
        [offset == d for d in (0, 1, 7, 6, 4, 2, 3)],
        [
            jnp.zeros_like(offset),
            jnp.full_like(offset, nblocks),
            jnp.full_like(offset, 2 * nblocks),
            jnp.zeros_like(offset) + before,
            jnp.full_like(offset, base + front),
            jnp.zeros_like(offset) + after,
            jnp.full_like(offset, base + 3 * front),
        ],
        jnp.full_like(offset, base + 4 * front),
    )
    return place * nblocks + block, start + crack_source


def sum_over_clusters(value):
    if not tuned():
        return [lax.psum(value, "clu")]
    value = value + swap(value, "clu", 1)
    return [value, *(shift(value, "clu", d) for d in (2, 4, 6))]


def cmul(a, b):
    return (a[0] * b[0] - a[1] * b[1], a[0] * b[1] + a[1] * b[0])


def cjmul(a, b):
    return (a[0] * b[0] + a[1] * b[1], a[0] * b[1] - a[1] * b[0])


def cadd(*terms):
    return (sum(t[0] for t in terms), sum(t[1] for t in terms))


def scale(factor, a):
    return (factor * a[0], factor * a[1])


def norm2(a):
    return a[0] * a[0] + a[1] * a[1]


def least_squares(beta_norm, first_h, sub_one, second_h, third_h, sub_two):
    r_one = jnp.sqrt(first_h[0] ** 2 + first_h[1] ** 2 + sub_one**2)
    q_real = first_h[0] / r_one
    q_imag = first_h[1] / r_one
    q_low = sub_one / r_one
    mix_real = q_real * second_h[0] + q_imag * second_h[1] + q_low * third_h[0]
    mix_imag = q_real * second_h[1] - q_imag * second_h[0] + q_low * third_h[1]
    top_real = second_h[0] - (mix_real * q_real - mix_imag * q_imag)
    top_imag = second_h[1] - (mix_real * q_imag + mix_imag * q_real)
    mid_real = third_h[0] - mix_real * q_low
    mid_imag = third_h[1] - mix_imag * q_low
    r_two_sq = top_real**2 + top_imag**2 + mid_real**2 + mid_imag**2 + sub_two**2
    later_real = beta_norm * top_real / r_two_sq
    later_imag = -beta_norm * top_imag / r_two_sq
    early_real = (beta_norm * q_real - (mix_real * later_real - mix_imag * later_imag)) / r_one
    early_imag = (-beta_norm * q_imag - (mix_real * later_imag + mix_imag * later_real)) / r_one
    return ((early_real, early_imag), (later_real, later_imag))


def combine(g00, g01, g11, g02, g12, g22):
    beta2 = g00 + EPS
    beta = jnp.sqrt(beta2)
    h11 = ((0.5 * g00 + g01[0]) / beta2, g01[1] / beta2)
    s = (0.5 - h11[0], -h11[1])
    s01 = cjmul(s, g01)
    w2w2 = g11 + 2.0 * s01[0] + norm2(s) * g00
    h21 = jnp.sqrt(jnp.maximum(w2w2 / beta2, 0.0) + EPS)
    k = 1.0 / (beta * h21)
    d = (s[0] + 0.5, s[1])
    e = scale(0.5, s)
    r0u = cadd(g02, cmul(d, g01), scale(g00, e))
    z1u = cadd(g12, scale(g11, d), cmul(e, (g01[0], -g01[1])))
    h12 = scale(k / beta, r0u)
    h22 = scale(k * k, cadd(z1u, cjmul(s, r0u)))
    uu = (
        g22
        + norm2(d) * g11
        + norm2(e) * g00
        + 2.0 * cjmul(d, g12)[0]
        + 2.0 * cjmul(e, g02)[0]
        + 2.0 * cjmul(e, cmul(d, g01))[0]
    )
    n11 = g00 / beta2
    n22 = k * k * w2w2
    n12 = scale(k / beta, cadd(g01, scale(g00, s)))
    rest = (
        k * k * uu
        + norm2(h12) * (n11 - 2.0)
        + norm2(h22) * (n22 - 2.0)
        + 2.0 * cmul(cjmul(h12, h22), n12)[0]
    )
    h32 = jnp.sqrt(jnp.maximum(rest, 0.0) + EPS)
    early, later = least_squares(beta, h11, h21, h12, h22, h32)
    b = scale(k, later)
    a = cadd(scale(1.0 / beta, early), cmul(b, s))
    return a, b


def result_kernel(stream, streams, nsums, *refs):
    phases, rows_of = refs[0], refs[1 : 1 + nsums]
    initial, first, second, scattered, send, keep = refs[1 + nsums :]
    sums = rows_of[0][...]
    for other in rows_of[1:]:
        sums = sums + other[...]
    half = sums.shape[1] // 2
    if half % 128 == 0:
        sums = sums[:, :half] + sums[:, half:]
    else:
        sums = sums + pltpu.roll(sums, half, 1)

    def row(i):
        return sums[i : i + 1]

    a, b = combine(
        row(0),
        (row(8), -row(9)),
        row(10),
        (row(16), -row(17)),
        (row(18), -row(19)),
        row(20),
    )
    width = 128
    blocks = first.shape[0] // width

    def one(g, carry):
        rows = pl.ds(pl.multiple_of(g * width, width), width)
        x, y = first[rows, :], second[rows, :]
        xr, xi, yr, yi = x[:, :half], x[:, half:], y[:, :half], y[:, half:]
        real = initial[0, rows] + a[0] * xr - a[1] * xi + b[0] * yr - b[1] * yi
        imag = initial[1, rows] + a[0] * xi + a[1] * xr + b[0] * yi + b[1] * yr
        scattered[0, rows, :] = real
        scattered[1, rows, :] = imag
        send[rows, :] = phases[0] * real - phases[1] * imag
        keep[rows, :] = phases[2] * real - phases[3] * imag
        return carry

    lax.fori_loop(0, blocks, one, 0)


def result_call(phases, sums, initial, first, second):
    rows = initial.shape[1]
    real = jax.ShapeDtypeStruct((rows, 128), jnp.float32)
    whole = pl.BlockSpec(memory_space=pltpu.VMEM)
    return pl.pallas_call(
        functools.partial(result_kernel, 0, 1, len(sums)),
        out_shape=(jax.ShapeDtypeStruct(initial.shape, jnp.float32), real, real),
        in_specs=[pl.BlockSpec(memory_space=pltpu.SMEM)] + [whole] * (len(sums) + 3),
        out_specs=(whole, whole, whole),
        compiler_params=pltpu.CompilerParams(vmem_limit_bytes=VMEM_LIMIT),
        name="result",
    )(phases, *sums, initial, first, second)


def mix_kernel(signs, keep, taken, here, away):
    here[...] = signs[0] * keep[...] + signs[1] * taken[...]
    away[...] = (signs[2] * keep[...] + signs[3] * taken[...]).astype(jnp.bfloat16)


def mix_call(signs, keep, taken):
    whole = pl.BlockSpec(memory_space=pltpu.VMEM)
    return pl.pallas_call(
        mix_kernel,
        out_shape=(
            jax.ShapeDtypeStruct(keep.shape, jnp.float32),
            jax.ShapeDtypeStruct(keep.shape, jnp.bfloat16),
        ),
        in_specs=[pl.BlockSpec(memory_space=pltpu.SMEM), whole, whole],
        out_specs=(whole, whole),
        name="mix",
    )(signs, keep, taken)


def power_of_i(exponent):
    exponent = exponent % 4
    real = jnp.where(exponent == 0, 1.0, jnp.where(exponent == 2, -1.0, 0.0))
    imag = jnp.where(exponent == 1, 1.0, jnp.where(exponent == 3, -1.0, 0.0))
    return real, imag


def local(
    incident,
    initial,
    near_blocks,
    near_pattern,
    crack_blocks,
    crack_cluster,
    crack_source,
    crack_target,
    pulse_spectrum,
):
    panels, directions = incident.shape[2:]
    nblocks, span = near_blocks.shape[:2]
    width = near_blocks.shape[4]
    edges = crack_blocks.shape[0]
    front = 4
    near = near_blocks.reshape(nblocks, span, 2 * width, width)
    crack = crack_blocks.reshape(edges, 2 * width, width)
    near_idx, crack_idx = source_tables(
        near_pattern, crack_cluster[:, 0], crack_source, nblocks, front
    )
    tables = (near_idx.astype(jnp.int32), crack_idx.astype(jnp.int32), crack_target)
    incident, initial = incident[0], initial[0]

    def blocks_of(low):
        return low.reshape(nblocks, width, low.shape[1])

    low = jnp.concatenate([initial[0], initial[1]], axis=1).astype(jnp.bfloat16)
    parts = exchange(blocks_of(low), front)
    first, low, sums_one = apply_call(1, 0, 1, tables, near, crack, parts, (incident, initial))
    parts = exchange(blocks_of(low), front)
    second, low, sums_two = apply_call(2, 0, 1, tables, near, crack, parts, (first,))
    parts = exchange(blocks_of(low), front)
    (sums_three,) = apply_call(3, 0, 1, tables, near, crack, parts, (first, second))
    sums = sum_over_clusters(jnp.concatenate([sums_one, sums_two, sums_three], axis=0))

    f = lax.axis_index("frq")
    side, core = f // 2, f % 2
    pulse = (pulse_spectrum[0, 0], pulse_spectrum[0, 1])
    phase_send = cmul(pulse, power_of_i((1 - core) * f))
    phase_keep = cmul(pulse, power_of_i(core * f))
    phases = jnp.stack([*phase_send, *phase_keep])
    scattered, send, keep = result_call(phases, sums, initial, first, second)
    taken = swap(send, "frq", 1)
    sign_keep = jnp.where(core == 0, 1.0, -1.0)
    signs = jnp.stack(
        [
            jnp.where(side == 1, sign_keep, 1.0),
            jnp.where(side == 1, -sign_keep, 1.0),
            jnp.where(side == 0, sign_keep, 1.0),
            jnp.where(side == 0, -sign_keep, 1.0),
        ]
    )
    here, away = mix_call(signs, keep, taken)
    time_trace = here + swap(away, "frq", 2).astype(jnp.float32)
    return (scattered[None], time_trace[None])


def solution(mesh):
    in_specs = (
        P("frq", None, "clu", None),
        P("frq", None, "clu", None),
        P("clu", None, "frq", None, None, None),
        P("clu", None),
        P("clu", "frq", None, None, None),
        P("clu", None),
        P("clu"),
        P("clu"),
        P("frq", None),
    )
    out_specs = (P("frq", None, "clu", None), P("frq", "clu", None))
    return jax.shard_map(local, mesh=mesh, in_specs=in_specs, out_specs=out_specs, check_vma=False)
```

time: 745 us -> 307 us (0.41); the launches traced: 733 us -> 307 us
  blocking collectives: 145 us -> 0 us
  waiting for transfers between devices: 303 us -> 209 us
  local copies, waits for them, and re-layouts: 92.1 us -> 10.3 us
  other arithmetic: 86.2 us -> 6.37 us
  matrix products: 56.2 us -> 0 us
  Pallas kernels: 0 us -> 49.3 us
  starting transfers between devices: 35.6 us -> 25.1 us
  between operations: 14.7 us -> 6.13 us
    psum x5 -> x0, blocking collectives: 145 us -> none  [the longest x2 73.4 us: project(): summed = lax.psum(tuple(terms), 'clu')]
    dot_general x12 -> x0, matrix products: 56.2 us -> none  [the longest x3 30.1 us: apply(): jnp.einsum('bsfcpq,fdbsqk->fcdbpk', near_blocks, columns, preferred_eleme...]
    pallas_call x0 -> x5, Pallas kernels: none -> 49.3 us  [the longest x3 43.6 us: apply_call(): pl.pallas_call(body, out_shape=out_shape, in_specs=[smem] * 3 + [anywhere...]
    gather x9 -> x0, local copies, waits for them, and re-layouts: 47.4 us -> none  [the longest x3 25.4 us: apply(): jnp.take(extended, near_flat, axis=2)]
    ppermute x6 -> x24, waiting for transfers between devices: 256 us -> 209 us  [the longest x9 114 us: swap(): return lax.ppermute(value, axis, [(i, i ^ distance) for i in range(count)])]
    reduce_scatter x1 -> x0, waiting for transfers between devices: 43 us -> none  [local(): lax.psum_scatter(term + jnp.einsum('tf,fpk->tpk', coef_imag, scattered[:,...]
    select_n x8 -> x3, other arithmetic: 36 us -> 0.1 us  [exchange(): near_side = jnp.where(even, before, after)]
    all_to_all x4 -> x0, starting transfers between devices: 21.3 us -> none  [the longest x3 14 us: fetch(): lax.all_to_all(picked, 'clu', split_axis=2, concat_axis=2, tiled=True)]
  transfers between devices with their start and end apart: 11 -> 24, of which waited for: 5 -> 13; matrix products, arithmetic and copies ran while one was open for 12% -> 2% of each run, Pallas kernels for 0% -> 0%
where the time goes in v1:
time: 307 us
  waiting for transfers between devices  209 us (68%)
  Pallas kernels  49.3 us (16%)
  starting transfers between devices  25.1 us (8%)
  local copies, waits for them, and re-layouts  10.3 us (3%)
  other arithmetic  6.37 us (2%)
  between operations  6.13 us (2%)
    ppermute x9, waiting for transfers between devices, swap(): return lax.ppermute(value, axis, [(i, i ^ distance) for i in range(count)])  114 us
    ppermute x12, waiting for transfers between devices, shift(): lax.ppermute(value, axis, [(i, (i + distance) % count) for i in range(cou...  95.6 us
    pallas_call x3, Pallas kernels, apply_call(): pl.pallas_call(body, out_shape=out_shape, in_specs=[smem] * 3 + [anywhere...  43.6 us
    ppermute x12, starting transfers between devices, shift(): lax.ppermute(value, axis, [(i, (i + distance) % count) for i in range(cou...  17.7 us
    unnamed x29, local copies, waits for them, and re-layouts  7.9 us
  transfers between devices with their start and end apart: 24, of which 13 were waited for; matrix products, arithmetic and copies ran while one was open for 2% of the time, Pallas kernels for 0%

profile of v1, /device:TPU:0, one launch (start us, length us, event | category | flops | bytes accessed | tf_op | source)
XLA Modules:
  0.0 306.5 jit_solution(1185892782837895367)
XLA Ops:
  0.6 1.7 fusion.5
  2.5 3.0 collective-permute-start
  6.3 1.6 collective-permute-start.2
  7.8 2.2 collective-permute-start.4
  10.9 17.9 %collective-permute-done.refs_6_ = bf16[16,128,256]{2,1,0:T(8,128)(2,1)} collective-permute-done((bf16[16,128,256]{2,1,0:T(8,128)(2,1)S(1)}, bf16[16,128,256]{2,1,0:T(8,128)(2,1)}, u32[]{:S(2)}, u32[]{:S(2)}) %collective-permute-start) | collective-permute-done | bytes 1048608 | tf_op jit(solution)/shard_map/ppermute | solution.py:179
  28.8 1.8 collective-permute-start.1
  30.9 24.7 %collective-permute-done.3.refs_9_ = bf16[4,128,256]{2,1,0:T(8,128)(2,1)} collective-permute-done((bf16[4,128,256]{2,1,0:T(8,128)(2,1)}, bf16[4,128,256]{2,1,0:T(8,128)(2,1)}, u32[]{:S(2)}, u32[]{:S(2)}) %collective-permute-start.3) | collective-permute-done | bytes 262176 | tf_op jit(solution)/shard_map/ppermute | solution.py:184
  55.5 1.8 pad_maximum_fusion.1
  57.9 13.5 %collective-permute-done.5.refs_11_ = bf16[8,128,256]{2,1,0:T(8,128)(2,1)} collective-permute-done((bf16[8,128,256]{2,1,0:T(8,128)(2,1)}, bf16[8,128,256]{2,1,0:T(8,128)(2,1)}, u32[]{:S(2)}, u32[]{:S(2)}) %collective-permute-start.5) | collective-permute-done | bytes 524320 | tf_op jit(solution)/shard_map/ppermute | solution.py:179
  71.5 16.2 %operator_1_0.1 = (f32[2048,256]{1,0:T(8,128)S(1)}, bf16[2048,256]{1,0:T(8,128)(2,1)S(1)}, f32[8,256]{1,0:T(8,128)S(1)}) custom-call(s32[128]{0:T(128)S(1)} %fusion.refs_0_, s32[32]{0:T(128)S(1)} %fusion.1.refs_1_, s32[32]{0:T(128)S(1)} %copy-done.8, bf16[16,8,256,128]{3,2,1,0:T(8,128)(2,1)} %bitcast.38, bf16[32,256,128]{2,1,0:T(8,128)(2,1)S(1)} %bitcast.29, ...), custom_call_target="tpu_custom_call" | custom-call | flops 2684354560 | bytes 10485760 | tf_op jit(solution)/shard_map/operator_1_0/pallas_call | solution.py:151
  89.3 2.0 collective-permute-start.8
  91.4 21.8 %collective-permute-done.6.refs_6_ = bf16[16,128,256]{2,1,0:T(8,128)(2,1)S(1)} collective-permute-done((bf16[16,128,256]{2,1,0:T(8,128)(2,1)S(1)}, bf16[16,128,256]{2,1,0:T(8,128)(2,1)S(1)}, u32[]{:S(2)}, u32[]{:S(2)}) %collective-permute-start.6) | collective-permute-done | bytes 1048608 | tf_op jit(solution)/shard_map/ppermute | solution.py:179
  113.3 35.4 %collective-permute-done.9.refs_9_ = bf16[4,128,256]{2,1,0:T(8,128)(2,1)S(1)} collective-permute-done((bf16[4,128,256]{2,1,0:T(8,128)(2,1)S(1)}, bf16[4,128,256]{2,1,0:T(8,128)(2,1)S(1)}, u32[]{:S(2)}, u32[]{:S(2)}) %collective-permute-start.9) | collective-permute-done | bytes 262176 | tf_op jit(solution)/shard_map/ppermute | solution.py:184
  148.8 12.9 %collective-permute-done.11.refs_11_ = bf16[8,128,256]{2,1,0:T(8,128)(2,1)S(1)} collective-permute-done((bf16[8,128,256]{2,1,0:T(8,128)(2,1)S(1)}, bf16[8,128,256]{2,1,0:T(8,128)(2,1)S(1)}, u32[]{:S(2)}, u32[]{:S(2)}) %collective-permute-start.11) | collective-permute-done | bytes 524320 | tf_op jit(solution)/shard_map/ppermute | solution.py:179
  161.7 13.4 %operator_2_0.1 = (f32[2048,256]{1,0:T(8,128)S(1)}, bf16[2048,256]{1,0:T(8,128)(2,1)S(1)}, f32[8,256]{1,0:T(8,128)S(1)}) custom-call(s32[128]{0:T(128)S(1)} %fusion.refs_0_, s32[32]{0:T(128)S(1)} %fusion.1.refs_1_, s32[32]{0:T(128)S(1)} %copy-done.8, bf16[16,8,256,128]{3,2,1,0:T(8,128)(2,1)} %bitcast.39, bf16[32,256,128]{2,1,0:T(8,128)(2,1)S(1)} %bitcast.30, ...), custom_call_target="tpu_custom_call" | custom-call | flops 2684354560 | bytes 10485760 | tf_op jit(solution)/shard_map/operator_2_0/pallas_call | solution.py:151
  175.1 1.3 copy-done.5
  176.8 3.8 %collective-permute-start.16 = (bf16[4,128,256]{2,1,0:T(8,128)(2,1)S(1)}, bf16[4,128,256]{2,1,0:T(8,128)(2,1)S(1)}, u32[]{:S(2)}, u32[]{:S(2)}) collective-permute-start(bf16[4,128,256]{2,1,0:T(8,128)(2,1)S(1)} %bitcast.47), channel_id=1, source_target_pairs={{0,24},{4,28},{8,0},{12,4},{16,8},{20,12},{24,16},{28,20},{1,25},{... | collective-permute-start | bytes 786440 | tf_op jit(solution)/shard_map/ppermute | solution.py:184
  180.6 19.0 %collective-permute-done.12.refs_6_ = bf16[16,128,256]{2,1,0:T(8,128)(2,1)S(1)} collective-permute-done((bf16[16,128,256]{2,1,0:T(8,128)(2,1)S(1)}, bf16[16,128,256]{2,1,0:T(8,128)(2,1)S(1)}, u32[]{:S(2)}, u32[]{:S(2)}) %collective-permute-start.12) | collective-permute-done | bytes 1048608 | tf_op jit(solution)/shard_map/ppermute | solution.py:179
  199.6 3.2 %collective-permute-start.15 = (bf16[4,128,256]{2,1,0:T(8,128)(2,1)S(1)}, bf16[4,128,256]{2,1,0:T(8,128)(2,1)S(1)}, u32[]{:S(2)}, u32[]{:S(2)}) collective-permute-start(bf16[4,128,256]{2,1,0:T(8,128)(2,1)S(1)} %bitcast.48), channel_id=1, source_target_pairs={{0,16},{4,20},{8,24},{12,28},{16,0},{20,4},{24,8},{28,12},{1,17},{... | collective-permute-start | bytes 786440 | tf_op jit(solution)/shard_map/ppermute | solution.py:184
  202.9 32.5 %collective-permute-done.15.refs_9_ = bf16[4,128,256]{2,1,0:T(8,128)(2,1)S(1)} collective-permute-done((bf16[4,128,256]{2,1,0:T(8,128)(2,1)S(1)}, bf16[4,128,256]{2,1,0:T(8,128)(2,1)S(1)}, u32[]{:S(2)}, u32[]{:S(2)}) %collective-permute-start.15) | collective-permute-done | bytes 262176 | tf_op jit(solution)/shard_map/ppermute | solution.py:184
  235.5 13.8 %collective-permute-done.17.refs_11_ = bf16[8,128,256]{2,1,0:T(8,128)(2,1)S(1)} collective-permute-done((bf16[8,128,256]{2,1,0:T(8,128)(2,1)S(1)}, bf16[8,128,256]{2,1,0:T(8,128)(2,1)S(1)}, u32[]{:S(2)}, u32[]{:S(2)}) %collective-permute-start.17) | collective-permute-done | bytes 524320 | tf_op jit(solution)/shard_map/ppermute | solution.py:179
  249.4 14.1 %operator_3_0.1 = f32[8,256]{1,0:T(8,128)S(1)} custom-call(s32[128]{0:T(128)S(1)} %fusion.refs_0_, s32[32]{0:T(128)S(1)} %fusion.1.refs_1_, s32[32]{0:T(128)S(1)} %copy-done.8, bf16[16,8,256,128]{3,2,1,0:T(8,128)(2,1)} %bitcast.40, bf16[32,256,128]{2,1,0:T(8,128)(2,1)S(1)} %bitcast.31, bf16[16,128,256]{2,1,0:T(8,128)(2,1)S(1)} %bitcast.37, ...), custom_call_target="tpu_custom_call" | custom-call | flops 2684354560 | bytes 10485760 | tf_op jit(solution)/shard_map/operator_3_0/pallas_call | solution.py:151
  269.8 3.0 collective-permute-start.20
  273.6 1.7 collective-permute-done.19.refs_2_
  276.6 1.6 copy-done.4
  278.2 1.6 copy-done.6
  279.8 2.9 result.1
  284.2 2.1 collective-permute-done.22.taken
  287.3 2.8 mix.1
  290.1 1.5 collective-permute-start.23
  291.6 12.6 %collective-permute-done.23 = bf16[2048,128]{1,0:T(8,128)(2,1)S(1)} collective-permute-done((bf16[2048,128]{1,0:T(8,128)(2,1)}, bf16[2048,128]{1,0:T(8,128)(2,1)S(1)}, u32[]{:S(2)}, u32[]{:S(2)}) %collective-permute-start.23) | collective-permute-done | bytes 524320 | tf_op jit(solution)/shard_map/ppermute | solution.py:179
  304.3 2.3 add_bitcast_fusion
  (75 shorter events, 10.6 us)
Async XLA Ops:
  2.3 8.6 %copy-start.12 = (s32[32,1]{0,1:T(1,128)S(1)}, s32[32,1]{0,1:T(1,128)}, u32[]{:S(2)}) copy-start(s32[32,1]{0,1:T(1,128)} %param.14) | copy-start | bytes 388
  2.3 28.3 %copy-start.10 = (s32[16,8]{0,1:T(8,128)S(1)}, s32[16,8]{0,1:T(8,128)}, u32[]{:S(2)}) copy-start(s32[16,8]{0,1:T(8,128)} %param.12) | copy-start | bytes 1540
  2.5 55.4 %copy-start.13 = (s32[32]{0:T(128)S(1)}, s32[32]{0:T(128)}, u32[]{:S(2)}) copy-start(s32[32]{0:T(128)} %param.15) | copy-start | bytes 388
  2.5 69.0 %copy-start.2 = (bf16[32,1,2,128,128]{4,3,2,1,0:T(8,128)(2,1)S(1)}, bf16[32,1,2,128,128]{4,3,2,1,0:T(8,128)(2,1)}, u32[]{:S(2)}) copy-start(bf16[32,1,2,128,128]{4,3,2,1,0:T(8,128)(2,1)} %param.13) | copy-start | bytes 6291460
  2.5 69.0 %copy-start.8 = (s32[32]{0:T(128)S(1)}, s32[32]{0:T(128)}, u32[]{:S(2)}) copy-start(s32[32]{0:T(128)} %refs_2_.5) | copy-start | bytes 388
  2.5 26.3 %collective-permute-start = (bf16[16,128,256]{2,1,0:T(8,128)(2,1)S(1)}, bf16[16,128,256]{2,1,0:T(8,128)(2,1)}, u32[]{:S(2)}, u32[]{:S(2)}) collective-permute-start(bf16[16,128,256]{2,1,0:T(8,128)(2,1)S(1)} %pad_maximum_fusion.refs_5_), channel_id=1, source_target_pairs={{0,4},{4,0},{8,12},{12,8},{16,20},{20,16},{24,28},{28,24},{1,5},{5... | collective-permute-start | bytes 3145736 | tf_op jit(solution)/shard_map/ppermute | solution.py:179
  6.3 24.5 %collective-permute-start.2 = (bf16[4,128,256]{2,1,0:T(8,128)(2,1)}, bf16[4,128,256]{2,1,0:T(8,128)(2,1)S(1)}, u32[]{:S(2)}, u32[]{:S(2)}) collective-permute-start(bf16[4,128,256]{2,1,0:T(8,128)(2,1)} %bitcast.13), channel_id=1, source_target_pairs={{0,8},{4,12},{8,16},{12,20},{16,24},{20,28},{24,0},{28,4},{1,9},{5... | collective-permute-start | bytes 786440 | tf_op jit(solution)/shard_map/ppermute | solution.py:184
  7.8 23.0 %collective-permute-start.4 = (bf16[4,128,256]{2,1,0:T(8,128)(2,1)}, bf16[4,128,256]{2,1,0:T(8,128)(2,1)}, u32[]{:S(2)}, u32[]{:S(2)}) collective-permute-start(bf16[4,128,256]{2,1,0:T(8,128)(2,1)} %bitcast.13), channel_id=1, source_target_pairs={{0,24},{4,28},{8,0},{12,4},{16,8},{20,12},{24,16},{28,20},{1,25},{... | collective-permute-start | bytes 786440 | tf_op jit(solution)/shard_map/ppermute | solution.py:184
  10.1 45.4 %collective-permute-start.3 = (bf16[4,128,256]{2,1,0:T(8,128)(2,1)}, bf16[4,128,256]{2,1,0:T(8,128)(2,1)}, u32[]{:S(2)}, u32[]{:S(2)}) collective-permute-start(bf16[4,128,256]{2,1,0:T(8,128)(2,1)} %bitcast.13), channel_id=1, source_target_pairs={{0,16},{4,20},{8,24},{12,28},{16,0},{20,4},{24,8},{28,12},{1,17},{... | collective-permute-start | bytes 786440 | tf_op jit(solution)/shard_map/ppermute | solution.py:184
  28.8 42.7 %collective-permute-start.1 = (bf16[16,128,256]{2,1,0:T(8,128)(2,1)}, bf16[16,128,256]{2,1,0:T(8,128)(2,1)}, u32[]{:S(2)}, u32[]{:S(2)}) collective-permute-start(bf16[16,128,256]{2,1,0:T(8,128)(2,1)} %collective-permute-done.refs_6_), channel_id=1, source_target_pairs={{0,8},{4,28},{8,16},{12,4},{16,24},{20,12},{24,0},{28,20},{1,9},{5... | collective-permute-start | bytes 3145736 | tf_op jit(solution)/shard_map/ppermute | solution.py:201
  57.3 14.2 %collective-permute-start.5 = (bf16[8,128,256]{2,1,0:T(8,128)(2,1)}, bf16[8,128,256]{2,1,0:T(8,128)(2,1)}, u32[]{:S(2)}, u32[]{:S(2)}) collective-permute-start(bf16[8,128,256]{2,1,0:T(8,128)(2,1)} %pad_maximum_fusion.1), channel_id=1, source_target_pairs={{0,4},{4,0},{8,12},{12,8},{16,20},{20,16},{24,28},{28,24},{1,5},{5... | collective-permute-start | bytes 1572872 | tf_op jit(solution)/shard_map/ppermute | solution.py:179
  89.0 24.2 %collective-permute-start.6 = (bf16[16,128,256]{2,1,0:T(8,128)(2,1)S(1)}, bf16[16,128,256]{2,1,0:T(8,128)(2,1)S(1)}, u32[]{:S(2)}, u32[]{:S(2)}) collective-permute-start(bf16[16,128,256]{2,1,0:T(8,128)(2,1)S(1)} %bitcast.34), channel_id=1, source_target_pairs={{0,4},{4,0},{8,12},{12,8},{16,20},{20,16},{24,28},{28,24},{1,5},{5... | collective-permute-start | bytes 3145736 | tf_op jit(solution)/shard_map/ppermute | solution.py:179
  89.3 23.9 %collective-permute-start.10 = (bf16[4,128,256]{2,1,0:T(8,128)(2,1)S(1)}, bf16[4,128,256]{2,1,0:T(8,128)(2,1)S(1)}, u32[]{:S(2)}, u32[]{:S(2)}) collective-permute-start(bf16[4,128,256]{2,1,0:T(8,128)(2,1)S(1)} %bitcast.49), channel_id=1, source_target_pairs={{0,24},{4,28},{8,0},{12,4},{16,8},{20,12},{24,16},{28,20},{1,25},{... | collective-permute-start | bytes 786440 | tf_op jit(solution)/shard_map/ppermute | solution.py:184
  89.3 23.9 %collective-permute-start.8 = (bf16[4,128,256]{2,1,0:T(8,128)(2,1)S(1)}, bf16[4,128,256]{2,1,0:T(8,128)(2,1)S(1)}, u32[]{:S(2)}, u32[]{:S(2)}) collective-permute-start(bf16[4,128,256]{2,1,0:T(8,128)(2,1)S(1)} %bitcast.50), channel_id=1, source_target_pairs={{0,8},{4,12},{8,16},{12,20},{16,24},{20,28},{24,0},{28,4},{1,9},{5... | collective-permute-start | bytes 786440 | tf_op jit(solution)/shard_map/ppermute | solution.py:184
  113.2 48.5 %collective-permute-start.7 = (bf16[16,128,256]{2,1,0:T(8,128)(2,1)S(1)}, bf16[16,128,256]{2,1,0:T(8,128)(2,1)S(1)}, u32[]{:S(2)}, u32[]{:S(2)}) collective-permute-start(bf16[16,128,256]{2,1,0:T(8,128)(2,1)S(1)} %collective-permute-done.6.refs_6_), channel_id=1, source_target_pairs={{0,8},{4,28},{8,16},{12,4},{16,24},{20,12},{24,0},{28,20},{1,9},{5... | collective-permute-start | bytes 3145736 | tf_op jit(solution)/shard_map/ppermute | solution.py:201
  113.2 35.5 %collective-permute-start.9 = (bf16[4,128,256]{2,1,0:T(8,128)(2,1)S(1)}, bf16[4,128,256]{2,1,0:T(8,128)(2,1)S(1)}, u32[]{:S(2)}, u32[]{:S(2)}) collective-permute-start(bf16[4,128,256]{2,1,0:T(8,128)(2,1)S(1)} %bitcast.51), channel_id=1, source_target_pairs={{0,16},{4,20},{8,24},{12,28},{16,0},{20,4},{24,8},{28,12},{1,17},{... | collective-permute-start | bytes 786440 | tf_op jit(solution)/shard_map/ppermute | solution.py:184
  148.7 12.9 %collective-permute-start.11 = (bf16[8,128,256]{2,1,0:T(8,128)(2,1)S(1)}, bf16[8,128,256]{2,1,0:T(8,128)(2,1)S(1)}, u32[]{:S(2)}, u32[]{:S(2)}) collective-permute-start(bf16[8,128,256]{2,1,0:T(8,128)(2,1)S(1)} %pad_maximum_fusion.2), channel_id=1, source_target_pairs={{0,4},{4,0},{8,12},{12,8},{16,20},{20,16},{24,28},{28,24},{1,5},{5... | collective-permute-start | bytes 1572872 | tf_op jit(solution)/shard_map/ppermute | solution.py:179
  161.7 87.7 %copy-start.3 = (bf16[32,1,2,128,128]{4,3,2,1,0:T(8,128)(2,1)S(1)}, bf16[32,1,2,128,128]{4,3,2,1,0:T(8,128)(2,1)}, u32[]{:S(2)}) copy-start(bf16[32,1,2,128,128]{4,3,2,1,0:T(8,128)(2,1)} %param.13) | copy-start | bytes 6291460
  176.4 73.0 %copy-start.1 = (f32[2048,256]{1,0:T(8,128)S(1)}, f32[2048,256]{1,0:T(8,128)}, u32[]{:S(2)}) copy-start(f32[2048,256]{1,0:T(8,128)} %copy-done) | copy-start | bytes 6291460
  176.4 23.2 %collective-permute-start.12 = (bf16[16,128,256]{2,1,0:T(8,128)(2,1)S(1)}, bf16[16,128,256]{2,1,0:T(8,128)(2,1)S(1)}, u32[]{:S(2)}, u32[]{:S(2)}) collective-permute-start(bf16[16,128,256]{2,1,0:T(8,128)(2,1)S(1)} %bitcast.36), channel_id=1, source_target_pairs={{0,4},{4,0},{8,12},{12,8},{16,20},{20,16},{24,28},{28,24},{1,5},{5... | collective-permute-start | bytes 3145736 | tf_op jit(solution)/shard_map/ppermute | solution.py:179
  176.7 26.1 %collective-permute-start.14 = (bf16[4,128,256]{2,1,0:T(8,128)(2,1)S(1)}, bf16[4,128,256]{2,1,0:T(8,128)(2,1)S(1)}, u32[]{:S(2)}, u32[]{:S(2)}) collective-permute-start(bf16[4,128,256]{2,1,0:T(8,128)(2,1)S(1)} %bitcast.46), channel_id=1, source_target_pairs={{0,8},{4,12},{8,16},{12,20},{16,24},{20,28},{24,0},{28,4},{1,9},{5... | collective-permute-start | bytes 786440 | tf_op jit(solution)/shard_map/ppermute | solution.py:184
  176.8 26.1 %collective-permute-start.16 = (bf16[4,128,256]{2,1,0:T(8,128)(2,1)S(1)}, bf16[4,128,256]{2,1,0:T(8,128)(2,1)S(1)}, u32[]{:S(2)}, u32[]{:S(2)}) collective-permute-start(bf16[4,128,256]{2,1,0:T(8,128)(2,1)S(1)} %bitcast.47), channel_id=1, source_target_pairs={{0,24},{4,28},{8,0},{12,4},{16,8},{20,12},{24,16},{28,20},{1,25},{... | collective-permute-start | bytes 786440 | tf_op jit(solution)/shard_map/ppermute | solution.py:184
  199.6 49.8 %collective-permute-start.13 = (bf16[16,128,256]{2,1,0:T(8,128)(2,1)S(1)}, bf16[16,128,256]{2,1,0:T(8,128)(2,1)S(1)}, u32[]{:S(2)}, u32[]{:S(2)}) collective-permute-start(bf16[16,128,256]{2,1,0:T(8,128)(2,1)S(1)} %collective-permute-done.12.refs_6_), channel_id=1, source_target_pairs={{0,8},{4,28},{8,16},{12,4},{16,24},{20,12},{24,0},{28,20},{1,9},{5... | collective-permute-start | bytes 3145736 | tf_op jit(solution)/shard_map/ppermute | solution.py:201
  199.6 35.8 %collective-permute-start.15 = (bf16[4,128,256]{2,1,0:T(8,128)(2,1)S(1)}, bf16[4,128,256]{2,1,0:T(8,128)(2,1)S(1)}, u32[]{:S(2)}, u32[]{:S(2)}) collective-permute-start(bf16[4,128,256]{2,1,0:T(8,128)(2,1)S(1)} %bitcast.48), channel_id=1, source_target_pairs={{0,16},{4,20},{8,24},{12,28},{16,0},{20,4},{24,8},{28,12},{1,17},{... | collective-permute-start | bytes 786440 | tf_op jit(solution)/shard_map/ppermute | solution.py:184
  235.5 13.9 %collective-permute-start.17 = (bf16[8,128,256]{2,1,0:T(8,128)(2,1)S(1)}, bf16[8,128,256]{2,1,0:T(8,128)(2,1)S(1)}, u32[]{:S(2)}, u32[]{:S(2)}) collective-permute-start(bf16[8,128,256]{2,1,0:T(8,128)(2,1)S(1)} %pad_maximum_fusion.3), channel_id=1, source_target_pairs={{0,4},{4,0},{8,12},{12,8},{16,20},{20,16},{24,28},{28,24},{1,5},{5... | collective-permute-start | bytes 1572872 | tf_op jit(solution)/shard_map/ppermute | solution.py:179
  249.4 14.5 %copy-start.11 = (f32[1,2]{1,0:T(1,128)S(1)}, f32[1,2]{1,0:T(1,128)}, u32[]{:S(2)}) copy-start(f32[1,2]{1,0:T(1,128)} %param.17) | copy-start | bytes 28
  263.5 6.2 %collective-permute-start.18 = (f32[24,256]{1,0:T(8,128)S(1)}, f32[24,256]{1,0:T(8,128)S(1)}, u32[]{:S(2)}, u32[]{:S(2)}) collective-permute-start(f32[24,256]{1,0:T(8,128)S(1)} %pad_maximum_fusion.5), channel_id=1, source_target_pairs={{0,4},{4,0},{8,12},{12,8},{16,20},{20,16},{24,28},{28,24},{1,5},{5... | collective-permute-start | bytes 73736 | tf_op jit(solution)/shard_map/ppermute | solution.py:179
  269.7 5.7 %collective-permute-start.19 = (f32[24,256]{1,0:T(8,128)S(1)}, f32[24,256]{1,0:T(8,128)S(1)}, u32[]{:S(2)}, u32[]{:S(2)}) collective-permute-start(f32[24,256]{1,0:T(8,128)S(1)} %fusion.4.refs_1_), channel_id=1, source_target_pairs={{0,8},{4,12},{8,16},{12,20},{16,24},{20,28},{24,0},{28,4},{1,9},{5... | collective-permute-start | bytes 73736 | tf_op jit(solution)/shard_map/ppermute | solution.py:184
  269.8 5.6 %collective-permute-start.20 = (f32[24,256]{1,0:T(8,128)S(1)}, f32[24,256]{1,0:T(8,128)S(1)}, u32[]{:S(2)}, u32[]{:S(2)}) collective-permute-start(f32[24,256]{1,0:T(8,128)S(1)} %fusion.4.refs_1_), channel_id=1, source_target_pairs={{0,16},{4,20},{8,24},{12,28},{16,0},{20,4},{24,8},{28,12},{1,17},{... | collective-permute-start | bytes 73736 | tf_op jit(solution)/shard_map/ppermute | solution.py:184
  272.8 3.8 %collective-permute-start.21 = (f32[24,256]{1,0:T(8,128)S(1)}, f32[24,256]{1,0:T(8,128)S(1)}, u32[]{:S(2)}, u32[]{:S(2)}) collective-permute-start(f32[24,256]{1,0:T(8,128)S(1)} %fusion.4.refs_1_), channel_id=1, source_target_pairs={{0,24},{4,28},{8,0},{12,4},{16,8},{20,12},{24,16},{28,20},{1,25},{... | collective-permute-start | bytes 73736 | tf_op jit(solution)/shard_map/ppermute | solution.py:184
  283.6 2.7 collective-permute-start.22
  290.1 14.2 %collective-permute-start.23 = (bf16[2048,128]{1,0:T(8,128)(2,1)}, bf16[2048,128]{1,0:T(8,128)(2,1)S(1)}, u32[]{:S(2)}, u32[]{:S(2)}) collective-permute-start(bf16[2048,128]{1,0:T(8,128)(2,1)} %get-tuple-element.25), channel_id=1, source_target_pairs={{0,2},{1,3},{2,0},{3,1},{4,6},{5,7},{6,4},{7,5},{8,10},{9,11},{10,... | collective-permute-start | bytes 1572872 | tf_op jit(solution)/shard_map/ppermute | solution.py:179
  (6 other events, 7.8 us)

commit v2 on v1

v2 whole, which is shorter than its diff:
```python
import functools

import jax
import jax.numpy as jnp
from jax import lax
from jax.experimental import pallas as pl
from jax.experimental.pallas import tpu as pltpu
from jax.sharding import PartitionSpec as P

EPS = 1e-06
MIB = 1024 * 1024
PLAIN_VMEM = 10 * MIB


def turn(rows):
    half = rows.shape[1] // 2
    return jnp.concatenate([-rows[:, half:], rows[:, :half]], axis=1)


def col_sum(rows):
    return jnp.sum(rows.reshape(rows.shape[0] // 8, 8, rows.shape[1]), axis=0)


def apply_kernel(step, sizes, moves, *refs):
    nblocks, span, edges, width, group, front = sizes
    early, late, nparts = moves
    near_idx, crack_idx, crack_tgt, near_in, crack_in = refs[:5]
    parts = refs[5 : 5 + nparts]
    rest = refs[5 + nparts :]
    extras = rest[:2] if step != 2 else rest[:1]
    rest = rest[len(extras) :]
    nouts = (5, 5, 1)[step - 1]
    outs, rest = rest[:nouts], rest[nouts:]
    front_v, source_v, acc, front_sem, source_sem = rest[:5]
    near_v, crack_v = near_in, crack_in
    matrix_copies, extra_copies = [], []
    if step == 1:
        near_v, crack_v, extra_v, matrix_sem, extra_sem = rest[5:]
        matrix_copies = [pltpu.make_async_copy(crack_in, crack_v, matrix_sem.at[nblocks])]
        for g in range(nblocks):
            matrix_copies.append(
                pltpu.make_async_copy(near_in.at[g], near_v.at[g], matrix_sem.at[g])
            )
        extra_copies = [
            pltpu.make_async_copy(extra, extra_v.at[place], extra_sem.at[place])
            for place, extra in enumerate(extras)
        ]
        extras = [extra_v.at[place] for place in range(2)]

    def copies(which, target, sems):
        return [
            pltpu.make_async_copy(
                parts[part].at[pl.ds(begin, count)],
                target.at[pl.ds(offset, count)],
                sems.at[place],
            )
            for place, (part, begin, count, offset) in enumerate(which)
        ]

    front_copies = copies(early, front_v, front_sem)
    source_copies = copies(late, source_v, source_sem)
    for copy in front_copies + matrix_copies[:1] + source_copies + extra_copies:
        copy.start()
    for copy in matrix_copies[1:]:
        copy.start()
    acc[...] = jnp.zeros(acc.shape, jnp.float32)
    for copy in front_copies + matrix_copies[:1]:
        copy.wait()

    def crack_edges(i, carry):
        products = [
            jnp.dot(
                crack_v[i * group + k],
                front_v[crack_idx[i * group + k]],
                preferred_element_type=jnp.float32,
            )
            for k in range(group)
        ]
        for k in range(group):
            acc[crack_tgt[i * group + k]] += products[k]
        return carry

    lax.fori_loop(0, edges // group, crack_edges, 0)
    for copy in source_copies + extra_copies:
        copy.wait()

    lanes = acc.shape[2]
    nsums = (1, 3, 5)[step - 1]
    zero = jnp.zeros((8, lanes), jnp.float32)

    def row(part, start, g, sums):
        if step == 1:
            pltpu.make_async_copy(near_in.at[g], near_v.at[g], matrix_sem.at[g]).wait()
        left = jnp.concatenate([near_v[g, s] for s in range(span)], axis=1)
        right = jnp.concatenate([source_v[near_idx[g * span + s]] for s in range(span)], axis=0)
        total = acc[g] + jnp.dot(left, right, preferred_element_type=jnp.float32)
        new = total[:width] + turn(total[width:])
        rows = pl.ds(pl.multiple_of(g * width, width), width)
        if step == 1:
            incident = jnp.concatenate([extras[0][0, rows], extras[0][1, rows]], axis=1)
            initial = jnp.concatenate([extras[1][0, rows], extras[1][1, rows]], axis=1)
            new = incident - 0.5 * initial - new
            terms = (new * new,)
        elif step == 2:
            first = extras[0][rows, :]
            terms = (first * new, first * turn(new), new * new)
        else:
            first, second, turned = extras[0][rows, :], extras[1][rows, :], turn(new)
            terms = (first * new, first * turned, second * new, second * turned, new * new)
        if step != 3:
            outs[0][rows, :] = new
            rounded = new.astype(jnp.bfloat16)
            outs[1 + part][g - start] = rounded
            if part == 0:

                @pl.when(g < front)
                def _():
                    outs[3][g] = rounded

        return tuple(total + col_sum(term) for total, term in zip(sums, terms))

    sums = (zero,) * nsums
    cut = nblocks // 2
    for part, (start, end) in enumerate(((0, cut), (cut, nblocks))):
        sums = lax.fori_loop(start, end, functools.partial(row, part, start), sums, unroll=2)
    sums = [jnp.sum(total, axis=0, keepdims=True) for total in sums]
    sums.append(jnp.zeros((8 - nsums, lanes), jnp.float32))
    outs[-1][...] = jnp.concatenate(sums, axis=0)


def low_shapes(nblocks, width, lanes, front):
    cut = nblocks // 2
    return tuple(
        jax.ShapeDtypeStruct((count, width, lanes), jnp.bfloat16)
        for count in (cut, nblocks - cut, front)
    )


def apply_call(step, front, tables, near, crack, found, extras):
    parts, early, late = found
    nblocks, span = near.shape[:2]
    edges, width = crack.shape[0], near.shape[3]
    lanes = parts[0].shape[2]
    group = 4 if edges % 4 == 0 else 1
    gram = jax.ShapeDtypeStruct((8, lanes), jnp.float32)
    out_shape = (gram,)
    if step != 3:
        vector = jax.ShapeDtypeStruct((nblocks * width, lanes), jnp.float32)
        out_shape = (vector, *low_shapes(nblocks, width, lanes, front), gram)
    smem = pl.BlockSpec(memory_space=pltpu.SMEM)
    anywhere = pl.BlockSpec(memory_space=pltpu.HBM if step == 1 else pl.ANY)
    whole = pl.BlockSpec(memory_space=pltpu.VMEM)
    scratch = []
    if step == 1:
        scratch = [
            pltpu.VMEM(near.shape, near.dtype),
            pltpu.VMEM(crack.shape, crack.dtype),
            pltpu.VMEM((2, *extras[0].shape), jnp.float32),
            pltpu.SemaphoreType.DMA((nblocks + 1,)),
            pltpu.SemaphoreType.DMA((2,)),
        ]
    nearby = sum(move[2] for move in early), sum(move[2] for move in late)
    held = 2 * sum(nearby) * width * lanes + 8 * nblocks * width * lanes
    if step == 1:
        held += 8 * extras[0].size + 2 * (near.size + crack.size)
    body = functools.partial(
        apply_kernel,
        step,
        (nblocks, span, edges, width, group, front),
        (early, late, len(parts)),
    )
    return pl.pallas_call(
        body,
        out_shape=out_shape,
        in_specs=[smem] * 3
        + [anywhere if step == 1 else whole] * 2
        + [anywhere] * len(parts)
        + [anywhere if step == 1 else whole] * len(extras),
        out_specs=tuple(whole for _ in out_shape),
        scratch_shapes=[
            pltpu.VMEM((nearby[0], width, lanes), jnp.bfloat16),
            pltpu.VMEM((nearby[1], width, lanes), jnp.bfloat16),
            pltpu.VMEM((nblocks, 2 * width, lanes), jnp.float32),
            pltpu.SemaphoreType.DMA((len(early),)),
            pltpu.SemaphoreType.DMA((len(late),)),
            *scratch,
        ],
        compiler_params=pltpu.CompilerParams(vmem_limit_bytes=44 * MIB if step == 1 else held + 2 * MIB),
        cost_estimate=pl.CostEstimate(
            flops=4 * width * width * lanes * (nblocks * span + edges),
            bytes_accessed=near.size * 2 + crack.size * 2,
            transcendentals=0,
        ),
        name=f"operator_{step}",
    )(*tables, near, crack, *parts, *extras)


def prepare_kernel(initial, low_a, low_b, head):
    width = low_a.shape[1]

    def one(target, start, g, carry):
        rows = pl.ds(pl.multiple_of((start + g) * width, width), width)
        rounded = jnp.concatenate([initial[0, rows], initial[1, rows]], axis=1)
        target[g] = rounded.astype(jnp.bfloat16)
        return carry

    cut = low_a.shape[0]
    lax.fori_loop(0, cut, functools.partial(one, low_a, 0), 0)
    lax.fori_loop(0, low_b.shape[0], functools.partial(one, low_b, cut), 0)
    lax.fori_loop(0, head.shape[0], functools.partial(one, head, 0), 0)


def swap(value, axis, distance):
    count = lax.axis_size(axis)
    return lax.ppermute(value, axis, [(i, i ^ distance) for i in range(count)])


def shift(value, axis, distance):
    count = lax.axis_size(axis)
    return lax.ppermute(value, axis, [(i, (i + distance) % count) for i in range(count)])


def ring(value, distance):
    count = lax.axis_size("clu")
    pairs = [(i, (i + (-distance if i % 2 else distance)) % count) for i in range(count)]
    return lax.ppermute(value, "clu", pairs)


def tuned():
    return lax.axis_size("clu") == 8


def tie(*values):
    return lax.optimization_barrier(values)


def exchange(lows, early_ties=(), late_ties=()):
    low_a, low_b, head = lows
    cut, rest, front = (low.shape[0] for low in lows)
    nblocks = cut + rest
    if not tuned():
        count = lax.axis_size("clu")
        low = jnp.concatenate([low_a, low_b], axis=0)
        every = lax.all_gather(head, "clu", axis=0, tiled=True)
        parts = [low, shift(low, "clu", -1), shift(low, "clu", 1), every]
        late = tuple((k, 0, nblocks, k * nblocks) for k in range(3))
        return (parts, ((3, 0, count * front, 0),), late), early_ties, late_ties
    beside_a = swap(low_a, "clu", 1)
    same = ring(head, 2)
    other = ring(head, -2)
    tail, beside_a, same, other, *early_ties = tie(low_b, beside_a, same, other, *early_ties)
    beyond_a = ring(jnp.concatenate([beside_a, same], axis=0), 2)
    beside_b = swap(tail, "clu", 1)
    same_pair = swap(same, "clu", 1)
    beside_b, *late_ties = tie(beside_b, *late_ties)
    beyond_b = ring(beside_b, 2)
    far_pair = swap(beyond_a[cut:], "clu", 1)
    parts = [low_a, low_b, beside_a, beside_b, beyond_a, beyond_b]
    parts += [same, other, same_pair, far_pair]
    early = tuple(
        (part, begin, front, place * front)
        for place, (part, begin) in enumerate(
            [(0, 0), (2, 0), (4, 0), (6, 0), (7, 0), (4, cut), (8, 0), (9, 0)]
        )
    )
    late = tuple(
        (2 * k + half, 0, (cut, rest)[half], k * nblocks + half * cut)
        for k in range(3)
        for half in range(2)
    )
    return (parts, early, late), early_ties, late_ties


def source_tables(near_pattern, crack_cluster, crack_source, nblocks, front):
    count = lax.axis_size("clu")
    me = lax.axis_index("clu")
    side, block = near_pattern.reshape(-1) // nblocks, near_pattern.reshape(-1) % nblocks
    if not tuned():
        place = jnp.where(side == 1, 0, jnp.where(side == 2, 1, 2))
        return place * nblocks + block, crack_cluster * front + crack_source
    odd = me % 2 == 1
    place = jnp.where(side == 1, 0, jnp.where((side == 2) ^ odd, 1, 2))
    offset = (crack_cluster - me) % count
    offset = jnp.where(odd, (-offset) % count, offset)
    slot = jnp.zeros_like(offset)
    for position, distance in enumerate((0, 1, 7, 6, 2, 4, 3, 5)):
        slot = jnp.where(offset == distance, position, slot)
    return place * nblocks + block, slot * front + crack_source


def sum_over_clusters(value):
    if not tuned():
        return [lax.psum(value, "clu")]
    value = value + swap(value, "clu", 1)
    return [value, *(shift(value, "clu", d) for d in (2, 4, 6))]


def cmul(a, b):
    return (a[0] * b[0] - a[1] * b[1], a[0] * b[1] + a[1] * b[0])


def cjmul(a, b):
    return (a[0] * b[0] + a[1] * b[1], a[0] * b[1] - a[1] * b[0])


def cadd(*terms):
    return (sum(t[0] for t in terms), sum(t[1] for t in terms))


def scale(factor, a):
    return (factor * a[0], factor * a[1])


def norm2(a):
    return a[0] * a[0] + a[1] * a[1]


def least_squares(beta_norm, first_h, sub_one, second_h, third_h, sub_two):
    r_one = jnp.sqrt(first_h[0] ** 2 + first_h[1] ** 2 + sub_one**2)
    q_real = first_h[0] / r_one
    q_imag = first_h[1] / r_one
    q_low = sub_one / r_one
    mix_real = q_real * second_h[0] + q_imag * second_h[1] + q_low * third_h[0]
    mix_imag = q_real * second_h[1] - q_imag * second_h[0] + q_low * third_h[1]
    top_real = second_h[0] - (mix_real * q_real - mix_imag * q_imag)
    top_imag = second_h[1] - (mix_real * q_imag + mix_imag * q_real)
    mid_real = third_h[0] - mix_real * q_low
    mid_imag = third_h[1] - mix_imag * q_low
    r_two_sq = top_real**2 + top_imag**2 + mid_real**2 + mid_imag**2 + sub_two**2
    later_real = beta_norm * top_real / r_two_sq
    later_imag = -beta_norm * top_imag / r_two_sq
    early_real = (beta_norm * q_real - (mix_real * later_real - mix_imag * later_imag)) / r_one
    early_imag = (-beta_norm * q_imag - (mix_real * later_imag + mix_imag * later_real)) / r_one
    return ((early_real, early_imag), (later_real, later_imag))


def combine(g00, g01, g11, g02, g12, g22):
    beta2 = g00 + EPS
    beta = jnp.sqrt(beta2)
    h11 = ((0.5 * g00 + g01[0]) / beta2, g01[1] / beta2)
    s = (0.5 - h11[0], -h11[1])
    s01 = cjmul(s, g01)
    w2w2 = g11 + 2.0 * s01[0] + norm2(s) * g00
    h21 = jnp.sqrt(jnp.maximum(w2w2 / beta2, 0.0) + EPS)
    k = 1.0 / (beta * h21)
    d = (s[0] + 0.5, s[1])
    e = scale(0.5, s)
    r0u = cadd(g02, cmul(d, g01), scale(g00, e))
    z1u = cadd(g12, scale(g11, d), cmul(e, (g01[0], -g01[1])))
    h12 = scale(k / beta, r0u)
    h22 = scale(k * k, cadd(z1u, cjmul(s, r0u)))
    uu = (
        g22
        + norm2(d) * g11
        + norm2(e) * g00
        + 2.0 * cjmul(d, g12)[0]
        + 2.0 * cjmul(e, g02)[0]
        + 2.0 * cjmul(e, cmul(d, g01))[0]
    )
    n11 = g00 / beta2
    n22 = k * k * w2w2
    n12 = scale(k / beta, cadd(g01, scale(g00, s)))
    rest = (
        k * k * uu
        + norm2(h12) * (n11 - 2.0)
        + norm2(h22) * (n22 - 2.0)
        + 2.0 * cmul(cjmul(h12, h22), n12)[0]
    )
    h32 = jnp.sqrt(jnp.maximum(rest, 0.0) + EPS)
    early, later = least_squares(beta, h11, h21, h12, h22, h32)
    b = scale(k, later)
    a = cadd(scale(1.0 / beta, early), cmul(b, s))
    return a, b


def small_kernel(nsums, pulse, *refs):
    coefs, sent = refs[nsums:]
    sums = refs[0][...]
    for other in refs[1:nsums]:
        sums = sums + other[...]
    half = sums.shape[1] // 2
    sums = sums[:, :half] + sums[:, half:]

    def row(i):
        return sums[i : i + 1]

    a, b = combine(
        row(0),
        (row(8), -row(9)),
        row(10),
        (row(16), -row(17)),
        (row(18), -row(19)),
        row(20),
    )
    zero = jnp.zeros((4, half), jnp.float32)
    coefs[...] = jnp.concatenate([*a, *b, zero], axis=0)
    factor = (pulse[0, 0], pulse[0, 1])
    sent[...] = jnp.concatenate([*cmul(factor, a), *cmul(factor, b), zero], axis=0)


def scattered_kernel(coefs, initial, first, second, scattered):
    half = initial.shape[2]
    a = (coefs[0:1], coefs[1:2])
    b = (coefs[2:3], coefs[3:4])
    width = 256

    def one(g, carry):
        rows = pl.ds(pl.multiple_of(g * width, width), width)
        x, y = first[rows, :], second[rows, :]
        xr, xi, yr, yi = x[:, :half], x[:, half:], y[:, :half], y[:, half:]
        scattered[0, rows, :] = initial[0, rows] + a[0] * xr - a[1] * xi + b[0] * yr - b[1] * yi
        scattered[1, rows, :] = initial[1, rows] + a[0] * xi + a[1] * xr + b[0] * yi + b[1] * yr
        return carry

    lax.fori_loop(0, first.shape[0] // width, one, 0)


def power_of_i(exponent):
    exponent = lax.rem(exponent, 4)
    real = jnp.where(exponent == 0, 1.0, jnp.where(exponent == 2, -1.0, 0.0))
    imag = jnp.where(exponent == 1, 1.0, jnp.where(exponent == 3, -1.0, 0.0))
    return real, imag


def terms_kernel(place, pulse, initial, send, keep):
    width = 256
    f, core = place[0], lax.rem(place[0], 2)
    factor = (pulse[0, 0], pulse[0, 1])
    sent = cmul(factor, power_of_i((1 - core) * f))
    kept = cmul(factor, power_of_i(core * f))

    def one(g, carry):
        rows = pl.ds(pl.multiple_of(g * width, width), width)
        real, imag = initial[0, rows], initial[1, rows]
        send[rows, :] = sent[0] * real - sent[1] * imag
        keep[rows, :] = kept[0] * real - kept[1] * imag
        return carry

    lax.fori_loop(0, initial.shape[1] // width, one, 0)


def mix_kernel(place, keep, taken, here, away):
    side, sign = place[0] // 2, 1.0 - 2.0 * lax.rem(place[0], 2).astype(jnp.float32)
    near_sign, far_sign = jnp.where(side == 1, sign, 1.0), jnp.where(side == 0, sign, 1.0)
    near_other, far_other = jnp.where(side == 1, -sign, 1.0), jnp.where(side == 0, -sign, 1.0)
    here[...] = near_sign * keep[...] + near_other * taken[...]
    away[...] = far_sign * keep[...] + far_other * taken[...]


def trace_kernel(count, place, here, away, *refs):
    coefs, firsts, seconds = refs[:count], refs[count : 2 * count], refs[2 * count : 3 * count]
    trace = refs[3 * count]
    half = trace.shape[1]
    width = 256
    weights = []
    for k in range(count):
        turned = power_of_i(place[0] * place[k])
        values = coefs[k][...]
        weights.append(
            (
                cmul(turned, (values[0:1], values[1:2])),
                cmul(turned, (values[2:3], values[3:4])),
            )
        )

    def one(g, carry):
        rows = pl.ds(pl.multiple_of(g * width, width), width)
        total = here[rows, :] + away[rows, :]
        for k in range(count):
            a, b = weights[k]
            x, y = firsts[k][rows, :], seconds[k][rows, :]
            total = total + (a[0] * x[:, :half] - a[1] * x[:, half:])
            total = total + (b[0] * y[:, :half] - b[1] * y[:, half:])
        trace[rows, :] = total
        return carry

    lax.fori_loop(0, trace.shape[0] // width, one, 0)


def on_vmem(body, out_shape, smem_args, args, name):
    outs = jax.tree.leaves(out_shape)
    moved = sum(a.size * a.dtype.itemsize for a in (*args, *outs))
    whole = pl.BlockSpec(memory_space=pltpu.VMEM)
    smem = pl.BlockSpec(memory_space=pltpu.SMEM)
    return pl.pallas_call(
        body,
        out_shape=out_shape,
        in_specs=[smem] * len(smem_args) + [whole] * len(args),
        out_specs=jax.tree.map(lambda _: whole, out_shape),
        compiler_params=pltpu.CompilerParams(vmem_limit_bytes=PLAIN_VMEM),
        cost_estimate=pl.CostEstimate(flops=0, bytes_accessed=moved, transcendentals=0),
        name=name,
    )(*smem_args, *args)


def local(
    incident,
    initial,
    near_blocks,
    near_pattern,
    crack_blocks,
    crack_cluster,
    crack_source,
    crack_target,
    pulse_spectrum,
):
    panels, directions = incident.shape[2:]
    nblocks, span = near_blocks.shape[:2]
    width = near_blocks.shape[4]
    edges = crack_blocks.shape[0]
    front = 4
    near = near_blocks.reshape(nblocks, span, 2 * width, width)
    crack = crack_blocks.reshape(edges, 2 * width, width)
    near_idx, crack_idx = source_tables(
        near_pattern, crack_cluster[:, 0], crack_source, nblocks, front
    )
    tables = (near_idx.astype(jnp.int32), crack_idx.astype(jnp.int32), crack_target)
    incident, initial = incident[0], initial[0]
    lows = on_vmem(
        prepare_kernel,
        low_shapes(nblocks, width, 2 * directions, front),
        (),
        (initial,),
        "prepare",
    )

    place = lax.axis_index("frq") ^ jnp.arange(4, dtype=jnp.int32)
    real = jax.ShapeDtypeStruct((panels, directions), jnp.float32)
    send, keep = on_vmem(
        terms_kernel, (real, real), (place, pulse_spectrum), (initial,), "terms"
    )
    taken = swap(send, "frq", 1)
    here, away = on_vmem(mix_kernel, (real, real), (place,), (keep, taken), "mix")

    found, _, (here, away) = exchange(lows, (), (here, away))
    away = swap(away, "frq", 2)
    first, *lows, sums_one = apply_call(1, front, tables, near, crack, found, (incident, initial))

    first_sent, away, *lows = tie(first, away, *lows)
    first_across = swap(first_sent, "frq", 2)
    first_one = swap(first, "frq", 1)
    found, _, _ = exchange(lows)
    second, *lows, sums_two = apply_call(2, front, tables, near, crack, found, (first,))

    second_sent, first_across, *lows = tie(second, first_across, *lows)
    second_across = swap(second_sent, "frq", 2)
    found, (first_across,), _ = exchange(lows, (first_across,))
    parts, early, late = found
    first_three = swap(first_across, "frq", 1)
    second_across, first_three, *parts = tie(second_across, first_three, *parts)
    second_one, second_three = swap(second, "frq", 1), swap(second_across, "frq", 1)
    (sums_three,) = apply_call(
        3, front, tables, near, crack, (parts, early, late), (first, second)
    )
    sums_three, second_one, second_three = tie(sums_three, second_one, second_three)
    firsts = [first, first_one, first_across, first_three]
    seconds = [second, second_one, second_across, second_three]

    sums = sum_over_clusters(jnp.concatenate([sums_one, sums_two, sums_three], axis=0))
    row = jax.ShapeDtypeStruct((8, directions), jnp.float32)
    coefs, sent = on_vmem(
        functools.partial(small_kernel, len(sums)), (row, row), (pulse_spectrum,), sums, "small"
    )
    every = [sent, *(swap(sent, "frq", d) for d in (1, 2, 3))]
    scattered = on_vmem(
        scattered_kernel,
        jax.ShapeDtypeStruct(initial.shape, jnp.float32),
        (),
        (coefs, initial, first, second),
        "scattered",
    )
    trace = on_vmem(
        functools.partial(trace_kernel, len(firsts)),
        real,
        (place,),
        (here, away, *every, *firsts, *seconds),
        "trace",
    )
    return (scattered[None], trace[None])


def solution(mesh):
    in_specs = (
        P("frq", None, "clu", None),
        P("frq", None, "clu", None),
        P("clu", None, "frq", None, None, None),
        P("clu", None),
        P("clu", "frq", None, None, None),
        P("clu", None),
        P("clu"),
        P("clu"),
        P("frq", None),
    )
    out_specs = (P("frq", None, "clu", None), P("frq", "clu", None))
    return jax.shard_map(local, mesh=mesh, in_specs=in_specs, out_specs=out_specs, check_vma=False)
```

time: 307 us -> 205 us (0.67)
  waiting for transfers between devices: 209 us -> 110 us
  starting transfers between devices: 25.1 us -> 43.1 us
  Pallas kernels: 49.3 us -> 41.1 us
  other arithmetic: 6.37 us -> 1.14 us
  between operations: 6.13 us -> 1 us
    ppermute x12 -> x3, waiting for transfers between devices: 95.6 us -> 1.52 us  [shift(): lax.ppermute(value, axis, [(i, (i + distance) % count) for i in range(cou...]
    ppermute x9 -> x24, waiting for transfers between devices: 114 us -> 41.4 us  [swap(): return lax.ppermute(value, axis, [(i, i ^ distance) for i in range(count)])]
    ppermute x3 -> x12, waiting for transfers between devices: 0.01 us -> 67.5 us  [ring(): return lax.ppermute(value, 'clu', pairs)]
    ppermute x9 -> x24, starting transfers between devices: 5.62 us -> 21.1 us  [swap(): return lax.ppermute(value, axis, [(i, i ^ distance) for i in range(count)])]
    ppermute x3 -> x12, starting transfers between devices: 1.83 us -> 17 us  [ring(): return lax.ppermute(value, 'clu', pairs)]
    ppermute x12 -> x3, starting transfers between devices: 17.7 us -> 5.01 us  [shift(): lax.ppermute(value, axis, [(i, (i + distance) % count) for i in range(cou...]
    pallas_call x3, Pallas kernels: 43.6 us -> 31.2 us  [apply_call(): pl.pallas_call(body, out_shape=out_shape, in_specs=[smem] * 3 + [anywhere...]
    pallas_call x2 -> x6, Pallas kernels: 5.68 us -> 9.9 us  [on_vmem(): pl.pallas_call(body, out_shape=out_shape, in_specs=[smem] * len(smem_args...]
  transfers between devices with their start and end apart: 24 -> 39, of which waited for: 13 -> 22; matrix products, arithmetic and copies ran while one was open for 2% -> 1% of each run, Pallas kernels for 0% -> 18%
where the time goes in v2:
time: 205 us
  waiting for transfers between devices  110 us (54%)
  starting transfers between devices  43.1 us (21%)
  Pallas kernels  41.1 us (20%)
  local copies, waits for them, and re-layouts  8.03 us (4%)
    ppermute x12, waiting for transfers between devices, ring(): return lax.ppermute(value, 'clu', pairs)  67.5 us
    ppermute x24, waiting for transfers between devices, swap(): return lax.ppermute(value, axis, [(i, i ^ distance) for i in range(count)])  41.4 us
    pallas_call x3, Pallas kernels, apply_call(): pl.pallas_call(body, out_shape=out_shape, in_specs=[smem] * 3 + [anywhere...  31.2 us
    ppermute x24, starting transfers between devices, swap(): return lax.ppermute(value, axis, [(i, i ^ distance) for i in range(count)])  21.1 us
    ppermute x12, starting transfers between devices, ring(): return lax.ppermute(value, 'clu', pairs)  17 us
    pallas_call x6, Pallas kernels, on_vmem(): pl.pallas_call(body, out_shape=out_shape, in_specs=[smem] * len(smem_args...  9.9 us
    unnamed x43, local copies, waits for them, and re-layouts  6.93 us
    ppermute x3, starting transfers between devices, shift(): lax.ppermute(value, axis, [(i, (i + distance) % count) for i in range(cou...  5.01 us
  transfers between devices with their start and end apart: 39, of which 22 were waited for; matrix products, arithmetic and copies ran while one was open for 1% of the time, Pallas kernels for 18%

profile of v2, /device:TPU:0, one launch (start us, length us, event | category | flops | bytes accessed | tf_op | source)
XLA Modules:
  0.0 204.8 jit_solution(7731354213690130081)
XLA Ops:
  4.1 2.9 %collective-permute-start = (bf16[8,128,256]{2,1,0:T(8,128)(2,1)}, bf16[8,128,256]{2,1,0:T(8,128)(2,1)S(1)}, u32[]{:S(2)}, u32[]{:S(2)}) collective-permute-start(bf16[8,128,256]{2,1,0:T(8,128)(2,1)} %get-tuple-element.62.refs_5_), channel_id=1, source_target_pairs={{0,4},{4,0},{8,12},{12,8},{16,20},{20,16},{24,28},{28,24},{1,5},{5... | collective-permute-start | bytes 1572872 | tf_op jit(solution)/shard_map/ppermute | solution.py:215
  9.6 2.2 %collective-permute-start.2 = (bf16[4,128,256]{2,1,0:T(8,128)(2,1)}, bf16[4,128,256]{2,1,0:T(8,128)(2,1)S(1)}, u32[]{:S(2)}, u32[]{:S(2)}) collective-permute-start(bf16[4,128,256]{2,1,0:T(8,128)(2,1)} %get-tuple-element.64), channel_id=1, source_target_pairs={{0,24},{4,12},{8,0},{12,20},{16,8},{20,28},{24,16},{28,4},{1,25},{... | collective-permute-start | bytes 786440 | tf_op jit(solution)/shard_map/ppermute | solution.py:226
  11.9 7.3 %collective-permute-done.1.refs_11_ = bf16[4,128,256]{2,1,0:T(8,128)(2,1)S(1)} collective-permute-done((bf16[4,128,256]{2,1,0:T(8,128)(2,1)}, bf16[4,128,256]{2,1,0:T(8,128)(2,1)S(1)}, u32[]{:S(2)}, u32[]{:S(2)}) %collective-permute-start.1) | collective-permute-done | bytes 262176 | tf_op jit(solution)/shard_map/ppermute | solution.py:226
  19.2 4.6 %collective-permute-done.2.refs_12_ = bf16[4,128,256]{2,1,0:T(8,128)(2,1)S(1)} collective-permute-done((bf16[4,128,256]{2,1,0:T(8,128)(2,1)}, bf16[4,128,256]{2,1,0:T(8,128)(2,1)S(1)}, u32[]{:S(2)}, u32[]{:S(2)}) %collective-permute-start.2) | collective-permute-done | bytes 262176 | tf_op jit(solution)/shard_map/ppermute | solution.py:226
  27.8 1.7 mix.1
  30.5 6.9 %collective-permute-done.3.refs_8_ = bf16[8,128,256]{2,1,0:T(8,128)(2,1)} collective-permute-done((bf16[8,128,256]{2,1,0:T(8,128)(2,1)S(1)}, bf16[8,128,256]{2,1,0:T(8,128)(2,1)}, u32[]{:S(2)}, u32[]{:S(2)}) %collective-permute-start.3) | collective-permute-done | bytes 524320 | tf_op jit(solution)/shard_map/ppermute | solution.py:215
  38.9 1.7 collective-permute-start.6
  42.0 6.8 %collective-permute-done.5.refs_9_ = bf16[12,128,256]{2,1,0:T(8,128)(2,1)} collective-permute-done((bf16[12,128,256]{2,1,0:T(8,128)(2,1)}, bf16[12,128,256]{2,1,0:T(8,128)(2,1)}, u32[]{:S(2)}, u32[]{:S(2)}) %collective-permute-start.5) | collective-permute-done | bytes 786464 | tf_op jit(solution)/shard_map/ppermute | solution.py:226
  49.9 8.4 %collective-permute-done.6.refs_10_ = bf16[8,128,256]{2,1,0:T(8,128)(2,1)} collective-permute-done((bf16[8,128,256]{2,1,0:T(8,128)(2,1)}, bf16[8,128,256]{2,1,0:T(8,128)(2,1)}, u32[]{:S(2)}, u32[]{:S(2)}) %collective-permute-start.6) | collective-permute-done | bytes 524320 | tf_op jit(solution)/shard_map/ppermute | solution.py:226
  61.8 13.5 %operator_1.1 = (f32[2048,256]{1,0:T(8,128)S(1)}, bf16[8,128,256]{2,1,0:T(8,128)(2,1)S(1)}, bf16[8,128,256]{2,1,0:T(8,128)(2,1)S(1)}, bf16[4,128,256]{2,1,0:T(8,128)(2,1)S(1)}, f32[8,256]{1,0:T(8,128)S(1)}) custom-call(s32[128]{0:T(128)S(1)} %fusion.refs_0_, s32[32]{0:T(128)S(1)} %fusion.2.refs_1_, s32[32]{0:T(128)S(1)} %copy-done.13, ...), custom_call_target="tpu_custom_call" | custom-call | flops 2684354560 | bytes 10485760 | tf_op jit(solution)/shard_map/operator_1/pallas_call | solution.py:172
  77.3 3.4 %collective-permute-start.12 = (bf16[4,128,256]{2,1,0:T(8,128)(2,1)S(1)}, bf16[4,128,256]{2,1,0:T(8,128)(2,1)S(1)}, u32[]{:S(2)}, u32[]{:S(2)}) collective-permute-start(bf16[4,128,256]{2,1,0:T(8,128)(2,1)S(1)} %get-tuple-element.82), channel_id=1, source_target_pairs={{0,24},{4,12},{8,0},{12,20},{16,8},{20,28},{24,16},{28,4},{1,25},{... | collective-permute-start | bytes 786440 | tf_op jit(solution)/shard_map/ppermute | solution.py:226
  80.7 7.2 %collective-permute-done.11.refs_11_ = bf16[4,128,256]{2,1,0:T(8,128)(2,1)S(1)} collective-permute-done((bf16[4,128,256]{2,1,0:T(8,128)(2,1)S(1)}, bf16[4,128,256]{2,1,0:T(8,128)(2,1)S(1)}, u32[]{:S(2)}, u32[]{:S(2)}) %collective-permute-start.11) | collective-permute-done | bytes 262176 | tf_op jit(solution)/shard_map/ppermute | solution.py:226
  91.8 11.4 %collective-permute-done.13.refs_8_ = bf16[8,128,256]{2,1,0:T(8,128)(2,1)S(1)} collective-permute-done((bf16[8,128,256]{2,1,0:T(8,128)(2,1)S(1)}, bf16[8,128,256]{2,1,0:T(8,128)(2,1)S(1)}, u32[]{:S(2)}, u32[]{:S(2)}) %collective-permute-start.13) | collective-permute-done | bytes 524320 | tf_op jit(solution)/shard_map/ppermute | solution.py:215
  103.5 3.3 %collective-permute-start.16 = (bf16[4,128,256]{2,1,0:T(8,128)(2,1)S(1)}, bf16[4,128,256]{2,1,0:T(8,128)(2,1)S(1)}, u32[]{:S(2)}, u32[]{:S(2)}) collective-permute-start(bf16[4,128,256]{2,1,0:T(8,128)(2,1)S(1)} %collective-permute-done.11.refs_11_), channel_id=1, source_target_pairs={{0,4},{4,0},{8,12},{12,8},{16,20},{20,16},{24,28},{28,24},{1,5},{5... | collective-permute-start | bytes 786440 | tf_op jit(solution)/shard_map/ppermute | solution.py:215
  106.8 4.8 %collective-permute-done.14.refs_9_ = bf16[12,128,256]{2,1,0:T(8,128)(2,1)S(1)} collective-permute-done((bf16[12,128,256]{2,1,0:T(8,128)(2,1)S(1)}, bf16[12,128,256]{2,1,0:T(8,128)(2,1)S(1)}, u32[]{:S(2)}, u32[]{:S(2)}) %collective-permute-start.14) | collective-permute-done | bytes 786464 | tf_op jit(solution)/shard_map/ppermute | solution.py:226
  111.7 2.3 %collective-permute-done.16.refs_13_ = bf16[4,128,256]{2,1,0:T(8,128)(2,1)S(1)} collective-permute-done((bf16[4,128,256]{2,1,0:T(8,128)(2,1)S(1)}, bf16[4,128,256]{2,1,0:T(8,128)(2,1)S(1)}, u32[]{:S(2)}, u32[]{:S(2)}) %collective-permute-start.16) | collective-permute-done | bytes 262176 | tf_op jit(solution)/shard_map/ppermute | solution.py:215
  114.0 4.1 %collective-permute-done.17.refs_14_ = bf16[4,128,256]{2,1,0:T(8,128)(2,1)S(1)} collective-permute-done((bf16[4,128,256]{2,1,0:T(8,128)(2,1)S(1)}, bf16[4,128,256]{2,1,0:T(8,128)(2,1)S(1)}, u32[]{:S(2)}, u32[]{:S(2)}) %collective-permute-start.17) | collective-permute-done | bytes 262176 | tf_op jit(solution)/shard_map/ppermute | solution.py:215
  118.1 1.7 collective-permute-done.15.refs_10_
  119.8 9.4 %operator_2.1 = (f32[2048,256]{1,0:T(8,128)S(1)}, bf16[8,128,256]{2,1,0:T(8,128)(2,1)S(1)}, bf16[8,128,256]{2,1,0:T(8,128)(2,1)S(1)}, bf16[4,128,256]{2,1,0:T(8,128)(2,1)S(1)}, f32[8,256]{1,0:T(8,128)S(1)}) custom-call(s32[128]{0:T(128)S(1)} %fusion.refs_0_, s32[32]{0:T(128)S(1)} %fusion.2.refs_1_, s32[32]{0:T(128)S(1)} %copy-done.13, ...), custom_call_target="tpu_custom_call" | custom-call | flops 2684354560 | bytes 10485760 | tf_op jit(solution)/shard_map/operator_2/pallas_call | solution.py:172
  130.8 2.4 %collective-permute-start.22 = (bf16[4,128,256]{2,1,0:T(8,128)(2,1)S(1)}, bf16[4,128,256]{2,1,0:T(8,128)(2,1)S(1)}, u32[]{:S(2)}, u32[]{:S(2)}) collective-permute-start(bf16[4,128,256]{2,1,0:T(8,128)(2,1)S(1)} %get-tuple-element.96), channel_id=1, source_target_pairs={{0,24},{4,12},{8,0},{12,20},{16,8},{20,28},{24,16},{28,4},{1,25},{... | collective-permute-start | bytes 786440 | tf_op jit(solution)/shard_map/ppermute | solution.py:226
  133.8 5.7 %collective-permute-done.21.refs_11_ = bf16[4,128,256]{2,1,0:T(8,128)(2,1)S(1)} collective-permute-done((bf16[4,128,256]{2,1,0:T(8,128)(2,1)S(1)}, bf16[4,128,256]{2,1,0:T(8,128)(2,1)S(1)}, u32[]{:S(2)}, u32[]{:S(2)}) %collective-permute-start.21) | collective-permute-done | bytes 262176 | tf_op jit(solution)/shard_map/ppermute | solution.py:226
  139.5 2.6 %collective-permute-done.22.refs_12_ = bf16[4,128,256]{2,1,0:T(8,128)(2,1)S(1)} collective-permute-done((bf16[4,128,256]{2,1,0:T(8,128)(2,1)S(1)}, bf16[4,128,256]{2,1,0:T(8,128)(2,1)S(1)}, u32[]{:S(2)}, u32[]{:S(2)}) %collective-permute-start.22) | collective-permute-done | bytes 262176 | tf_op jit(solution)/shard_map/ppermute | solution.py:226
  142.1 1.9 collective-permute-start.24
  144.1 12.5 %collective-permute-done.24.refs_8_ = bf16[8,128,256]{2,1,0:T(8,128)(2,1)S(1)} collective-permute-done((bf16[8,128,256]{2,1,0:T(8,128)(2,1)S(1)}, bf16[8,128,256]{2,1,0:T(8,128)(2,1)S(1)}, u32[]{:S(2)}, u32[]{:S(2)}) %collective-permute-start.24) | collective-permute-done | bytes 524320 | tf_op jit(solution)/shard_map/ppermute | solution.py:215
  157.0 2.6 %collective-permute-start.27 = (bf16[4,128,256]{2,1,0:T(8,128)(2,1)S(1)}, bf16[4,128,256]{2,1,0:T(8,128)(2,1)S(1)}, u32[]{:S(2)}, u32[]{:S(2)}) collective-permute-start(bf16[4,128,256]{2,1,0:T(8,128)(2,1)S(1)} %collective-permute-done.21.refs_11_), channel_id=1, source_target_pairs={{0,4},{4,0},{8,12},{12,8},{16,20},{20,16},{24,28},{28,24},{1,5},{5... | collective-permute-start | bytes 786440 | tf_op jit(solution)/shard_map/ppermute | solution.py:215
  159.7 6.6 %collective-permute-done.25.refs_9_ = bf16[12,128,256]{2,1,0:T(8,128)(2,1)S(1)} collective-permute-done((bf16[12,128,256]{2,1,0:T(8,128)(2,1)S(1)}, bf16[12,128,256]{2,1,0:T(8,128)(2,1)S(1)}, u32[]{:S(2)}, u32[]{:S(2)}) %collective-permute-start.25) | collective-permute-done | bytes 786464 | tf_op jit(solution)/shard_map/ppermute | solution.py:226
  166.5 10.3 %collective-permute-done.26.refs_10_ = bf16[8,128,256]{2,1,0:T(8,128)(2,1)S(1)} collective-permute-done((bf16[8,128,256]{2,1,0:T(8,128)(2,1)S(1)}, bf16[8,128,256]{2,1,0:T(8,128)(2,1)S(1)}, u32[]{:S(2)}, u32[]{:S(2)}) %collective-permute-start.26) | collective-permute-done | bytes 524320 | tf_op jit(solution)/shard_map/ppermute | solution.py:226
  177.8 8.2 %operator_3.1 = f32[8,256]{1,0:T(8,128)S(1)} custom-call(s32[128]{0:T(128)S(1)} %fusion.refs_0_, s32[32]{0:T(128)S(1)} %fusion.2.refs_1_, s32[32]{0:T(128)S(1)} %copy-done.13, bf16[16,8,256,128]{3,2,1,0:T(8,128)(2,1)S(1)} %bitcast.12, bf16[32,256,128]{2,1,0:T(8,128)(2,1)S(1)} %bitcast.19, bf16[8,128,256]{2,1,0:T(8,128)(2,1)S(1)} %get-tuple-element.103.refs_5_, ...), custom_call_target="tpu_custom_call" | custom-call | flops 2684354560 | bytes 10485760 | tf_op jit(solution)/shard_map/operator_3/pallas_call | solution.py:172
  186.2 3.8 %collective-permute-done.31 = f32[24,256]{1,0:T(8,128)S(1)} collective-permute-done((f32[24,256]{1,0:T(8,128)S(1)}, f32[24,256]{1,0:T(8,128)S(1)}, u32[]{:S(2)}, u32[]{:S(2)}) %collective-permute-start.31) | collective-permute-done | bytes 24608 | tf_op jit(solution)/shard_map/ppermute | solution.py:215
  192.3 2.7 %collective-permute-start.34 = (f32[24,256]{1,0:T(8,128)S(1)}, f32[24,256]{1,0:T(8,128)S(1)}, u32[]{:S(2)}, u32[]{:S(2)}) collective-permute-start(f32[24,256]{1,0:T(8,128)S(1)} %add.36.refs_0_), channel_id=1, source_target_pairs={{0,24},{4,28},{8,0},{12,4},{16,8},{20,12},{24,16},{28,20},{1,25},{... | collective-permute-start | bytes 73736 | tf_op jit(solution)/shard_map/ppermute | solution.py:220
  199.1 2.1 %scattered.1 = f32[2,2048,128]{2,1,0:T(8,128)} custom-call(f32[8,128]{1,0:T(8,128)S(1)} %get-tuple-element.115.coefs, f32[2,2048,128]{2,1,0:T(8,128)S(1)} %bitcast.16, f32[2048,256]{1,0:T(8,128)S(1)} %get-tuple-element.89.refs_15_.first.refs_4_, f32[2048,256]{1,0:T(8,128)S(1)} %get-tuple-element.93.refs_16_.second.refs_8_), custom_call_target="tpu_custom_call" | custom-call | bytes 8392704 | tf_op jit(solution)/shard_map/scattered/pallas_call | solution.py:485
  201.2 3.6 %trace.1 = f32[2048,128]{1,0:T(8,128)} custom-call(s32[4]{0:T(128)S(1)} %iota_xor_fusion.place, f32[2048,128]{1,0:T(8,128)S(1)} %copy-done.7, f32[2048,128]{1,0:T(8,128)} %collective-permute-done.9.away, f32[8,128]{1,0:T(8,128)S(1)} %get-tuple-element.118.refs_0_, f32[8,128]{1,0:T(8,128)S(1)} %collective-permute-done.35.refs_1_, ...), custom_call_target="tpu_custom_call" | custom-call | bytes 19939328 | tf_op jit(solution)/shard_map/trace/pallas_call | solution.py:485
  (111 shorter events, 35.1 us)
Async XLA Ops:
  4.1 19.7 %collective-permute-start = (bf16[8,128,256]{2,1,0:T(8,128)(2,1)}, bf16[8,128,256]{2,1,0:T(8,128)(2,1)S(1)}, u32[]{:S(2)}, u32[]{:S(2)}) collective-permute-start(bf16[8,128,256]{2,1,0:T(8,128)(2,1)} %get-tuple-element.62.refs_5_), channel_id=1, source_target_pairs={{0,4},{4,0},{8,12},{12,8},{16,20},{20,16},{24,28},{28,24},{1,5},{5... | collective-permute-start | bytes 1572872 | tf_op jit(solution)/shard_map/ppermute | solution.py:215
  7.9 19.9 %collective-permute-start.4 = (f32[2048,128]{1,0:T(8,128)S(1)}, f32[2048,128]{1,0:T(8,128)S(1)}, u32[]{:S(2)}, u32[]{:S(2)}) collective-permute-start(f32[2048,128]{1,0:T(8,128)S(1)} %get-tuple-element.68), channel_id=1, source_target_pairs={{0,1},{1,0},{2,3},{3,2},{4,5},{5,4},{6,7},{7,6},{8,9},{9,8},{10,11... | collective-permute-start | bytes 3145736 | tf_op jit(solution)/shard_map/ppermute | solution.py:215
  8.0 11.2 %collective-permute-start.1 = (bf16[4,128,256]{2,1,0:T(8,128)(2,1)}, bf16[4,128,256]{2,1,0:T(8,128)(2,1)S(1)}, u32[]{:S(2)}, u32[]{:S(2)}) collective-permute-start(bf16[4,128,256]{2,1,0:T(8,128)(2,1)} %get-tuple-element.64), channel_id=1, source_target_pairs={{0,8},{4,28},{8,16},{12,4},{16,24},{20,12},{24,0},{28,20},{1,9},{5... | collective-permute-start | bytes 786440 | tf_op jit(solution)/shard_map/ppermute | solution.py:226
  9.6 14.2 %collective-permute-start.2 = (bf16[4,128,256]{2,1,0:T(8,128)(2,1)}, bf16[4,128,256]{2,1,0:T(8,128)(2,1)S(1)}, u32[]{:S(2)}, u32[]{:S(2)}) collective-permute-start(bf16[4,128,256]{2,1,0:T(8,128)(2,1)} %get-tuple-element.64), channel_id=1, source_target_pairs={{0,24},{4,12},{8,0},{12,20},{16,8},{20,28},{24,16},{28,4},{1,25},{... | collective-permute-start | bytes 786440 | tf_op jit(solution)/shard_map/ppermute | solution.py:226
  23.9 13.5 %collective-permute-start.3 = (bf16[8,128,256]{2,1,0:T(8,128)(2,1)S(1)}, bf16[8,128,256]{2,1,0:T(8,128)(2,1)}, u32[]{:S(2)}, u32[]{:S(2)}) collective-permute-start(bf16[8,128,256]{2,1,0:T(8,128)(2,1)S(1)} %copy-done.9), channel_id=1, source_target_pairs={{0,4},{4,0},{8,12},{12,8},{16,20},{20,16},{24,28},{28,24},{1,5},{5... | collective-permute-start | bytes 1572872 | tf_op jit(solution)/shard_map/ppermute | solution.py:215
  26.2 22.6 %collective-permute-start.5 = (bf16[12,128,256]{2,1,0:T(8,128)(2,1)}, bf16[12,128,256]{2,1,0:T(8,128)(2,1)}, u32[]{:S(2)}, u32[]{:S(2)}) collective-permute-start(bf16[12,128,256]{2,1,0:T(8,128)(2,1)} %pad_maximum_fusion), channel_id=1, source_target_pairs={{0,8},{4,28},{8,16},{12,4},{16,24},{20,12},{24,0},{28,20},{1,9},{5... | collective-permute-start | bytes 2359304 | tf_op jit(solution)/shard_map/ppermute | solution.py:226
  37.4 37.9 %collective-permute-start.9 = (f32[2048,128]{1,0:T(8,128)}, f32[2048,128]{1,0:T(8,128)}, u32[]{:S(2)}, u32[]{:S(2)}) collective-permute-start(f32[2048,128]{1,0:T(8,128)} %get-tuple-element.76), channel_id=1, source_target_pairs={{0,2},{1,3},{2,0},{3,1},{4,6},{5,7},{6,4},{7,5},{8,10},{9,11},{10,... | collective-permute-start | bytes 3145736 | tf_op jit(solution)/shard_map/ppermute | solution.py:215
  38.9 19.5 %collective-permute-start.6 = (bf16[8,128,256]{2,1,0:T(8,128)(2,1)}, bf16[8,128,256]{2,1,0:T(8,128)(2,1)}, u32[]{:S(2)}, u32[]{:S(2)}) collective-permute-start(bf16[8,128,256]{2,1,0:T(8,128)(2,1)} %collective-permute-done.3.refs_8_), channel_id=1, source_target_pairs={{0,8},{4,28},{8,16},{12,4},{16,24},{20,12},{24,0},{28,20},{1,9},{5... | collective-permute-start | bytes 1572872 | tf_op jit(solution)/shard_map/ppermute | solution.py:226
  40.7 9.2 %collective-permute-start.7 = (bf16[4,128,256]{2,1,0:T(8,128)(2,1)S(1)}, bf16[4,128,256]{2,1,0:T(8,128)(2,1)S(1)}, u32[]{:S(2)}, u32[]{:S(2)}) collective-permute-start(bf16[4,128,256]{2,1,0:T(8,128)(2,1)S(1)} %collective-permute-done.1.refs_11_), channel_id=1, source_target_pairs={{0,4},{4,0},{8,12},{12,8},{16,20},{20,16},{24,28},{28,24},{1,5},{5... | collective-permute-start | bytes 786440 | tf_op jit(solution)/shard_map/ppermute | solution.py:215
  49.7 8.6 %collective-permute-start.8 = (bf16[4,128,256]{2,1,0:T(8,128)(2,1)S(1)}, bf16[4,128,256]{2,1,0:T(8,128)(2,1)S(1)}, u32[]{:S(2)}, u32[]{:S(2)}) collective-permute-start(bf16[4,128,256]{2,1,0:T(8,128)(2,1)S(1)} %slice.12), channel_id=1, source_target_pairs={{0,4},{4,0},{8,12},{12,8},{16,20},{20,16},{24,28},{28,24},{1,5},{5... | collective-permute-start | bytes 786440 | tf_op jit(solution)/shard_map/ppermute | solution.py:215
  75.3 54.0 %collective-permute-start.18 = (f32[2048,256]{1,0:T(8,128)S(1)}, f32[2048,256]{1,0:T(8,128)S(1)}, u32[]{:S(2)}, u32[]{:S(2)}) collective-permute-start(f32[2048,256]{1,0:T(8,128)S(1)} %get-tuple-element.89.refs_15_.first.refs_4_), channel_id=1, source_target_pairs={{0,2},{1,3},{2,0},{3,1},{4,6},{5,7},{6,4},{7,5},{8,10},{9,11},{10,... | collective-permute-start | bytes 6291464 | tf_op jit(solution)/shard_map/ppermute | solution.py:215
  76.9 12.3 %collective-permute-start.10 = (bf16[8,128,256]{2,1,0:T(8,128)(2,1)S(1)}, bf16[8,128,256]{2,1,0:T(8,128)(2,1)S(1)}, u32[]{:S(2)}, u32[]{:S(2)}) collective-permute-start(bf16[8,128,256]{2,1,0:T(8,128)(2,1)S(1)} %get-tuple-element.80.refs_5_), channel_id=1, source_target_pairs={{0,4},{4,0},{8,12},{12,8},{16,20},{20,16},{24,28},{28,24},{1,5},{5... | collective-permute-start | bytes 1572872 | tf_op jit(solution)/shard_map/ppermute | solution.py:215
  76.9 11.0 %collective-permute-start.11 = (bf16[4,128,256]{2,1,0:T(8,128)(2,1)S(1)}, bf16[4,128,256]{2,1,0:T(8,128)(2,1)S(1)}, u32[]{:S(2)}, u32[]{:S(2)}) collective-permute-start(bf16[4,128,256]{2,1,0:T(8,128)(2,1)S(1)} %get-tuple-element.82), channel_id=1, source_target_pairs={{0,8},{4,28},{8,16},{12,4},{16,24},{20,12},{24,0},{28,20},{1,9},{5... | collective-permute-start | bytes 786440 | tf_op jit(solution)/shard_map/ppermute | solution.py:226
  77.3 11.9 %collective-permute-start.12 = (bf16[4,128,256]{2,1,0:T(8,128)(2,1)S(1)}, bf16[4,128,256]{2,1,0:T(8,128)(2,1)S(1)}, u32[]{:S(2)}, u32[]{:S(2)}) collective-permute-start(bf16[4,128,256]{2,1,0:T(8,128)(2,1)S(1)} %get-tuple-element.82), channel_id=1, source_target_pairs={{0,24},{4,12},{8,0},{12,20},{16,8},{20,28},{24,16},{28,4},{1,25},{... | collective-permute-start | bytes 786440 | tf_op jit(solution)/shard_map/ppermute | solution.py:226
  89.3 22.3 %collective-permute-start.14 = (bf16[12,128,256]{2,1,0:T(8,128)(2,1)S(1)}, bf16[12,128,256]{2,1,0:T(8,128)(2,1)S(1)}, u32[]{:S(2)}, u32[]{:S(2)}) collective-permute-start(bf16[12,128,256]{2,1,0:T(8,128)(2,1)S(1)} %pad_maximum_fusion.1), channel_id=1, source_target_pairs={{0,8},{4,28},{8,16},{12,4},{16,24},{20,12},{24,0},{28,20},{1,9},{5... | collective-permute-start | bytes 2359304 | tf_op jit(solution)/shard_map/ppermute | solution.py:226
  90.5 12.6 %collective-permute-start.13 = (bf16[8,128,256]{2,1,0:T(8,128)(2,1)S(1)}, bf16[8,128,256]{2,1,0:T(8,128)(2,1)S(1)}, u32[]{:S(2)}, u32[]{:S(2)}) collective-permute-start(bf16[8,128,256]{2,1,0:T(8,128)(2,1)S(1)} %get-tuple-element.84.refs_6_), channel_id=1, source_target_pairs={{0,4},{4,0},{8,12},{12,8},{16,20},{20,16},{24,28},{28,24},{1,5},{5... | collective-permute-start | bytes 1572872 | tf_op jit(solution)/shard_map/ppermute | solution.py:215
  103.2 16.6 %collective-permute-start.15 = (bf16[8,128,256]{2,1,0:T(8,128)(2,1)S(1)}, bf16[8,128,256]{2,1,0:T(8,128)(2,1)S(1)}, u32[]{:S(2)}, u32[]{:S(2)}) collective-permute-start(bf16[8,128,256]{2,1,0:T(8,128)(2,1)S(1)} %collective-permute-done.13.refs_8_), channel_id=1, source_target_pairs={{0,8},{4,28},{8,16},{12,4},{16,24},{20,12},{24,0},{28,20},{1,9},{5... | collective-permute-start | bytes 1572872 | tf_op jit(solution)/shard_map/ppermute | solution.py:226
  103.5 10.5 %collective-permute-start.16 = (bf16[4,128,256]{2,1,0:T(8,128)(2,1)S(1)}, bf16[4,128,256]{2,1,0:T(8,128)(2,1)S(1)}, u32[]{:S(2)}, u32[]{:S(2)}) collective-permute-start(bf16[4,128,256]{2,1,0:T(8,128)(2,1)S(1)} %collective-permute-done.11.refs_11_), channel_id=1, source_target_pairs={{0,4},{4,0},{8,12},{12,8},{16,20},{20,16},{24,28},{28,24},{1,5},{5... | collective-permute-start | bytes 786440 | tf_op jit(solution)/shard_map/ppermute | solution.py:215
  111.6 6.4 %collective-permute-start.17 = (bf16[4,128,256]{2,1,0:T(8,128)(2,1)S(1)}, bf16[4,128,256]{2,1,0:T(8,128)(2,1)S(1)}, u32[]{:S(2)}, u32[]{:S(2)}) collective-permute-start(bf16[4,128,256]{2,1,0:T(8,128)(2,1)S(1)} %slice.13), channel_id=1, source_target_pairs={{0,4},{4,0},{8,12},{12,8},{16,20},{20,16},{24,28},{28,24},{1,5},{5... | collective-permute-start | bytes 786440 | tf_op jit(solution)/shard_map/ppermute | solution.py:215
  129.3 12.8 %collective-permute-start.20 = (bf16[8,128,256]{2,1,0:T(8,128)(2,1)S(1)}, bf16[8,128,256]{2,1,0:T(8,128)(2,1)S(1)}, u32[]{:S(2)}, u32[]{:S(2)}) collective-permute-start(bf16[8,128,256]{2,1,0:T(8,128)(2,1)S(1)} %get-tuple-element.103.refs_5_), channel_id=1, source_target_pairs={{0,4},{4,0},{8,12},{12,8},{16,20},{20,16},{24,28},{28,24},{1,5},{5... | collective-permute-start | bytes 1572872 | tf_op jit(solution)/shard_map/ppermute | solution.py:215
  129.3 10.1 %collective-permute-start.21 = (bf16[4,128,256]{2,1,0:T(8,128)(2,1)S(1)}, bf16[4,128,256]{2,1,0:T(8,128)(2,1)S(1)}, u32[]{:S(2)}, u32[]{:S(2)}) collective-permute-start(bf16[4,128,256]{2,1,0:T(8,128)(2,1)S(1)} %get-tuple-element.96), channel_id=1, source_target_pairs={{0,8},{4,28},{8,16},{12,4},{16,24},{20,12},{24,0},{28,20},{1,9},{5... | collective-permute-start | bytes 786440 | tf_op jit(solution)/shard_map/ppermute | solution.py:226
  130.8 11.3 %collective-permute-start.22 = (bf16[4,128,256]{2,1,0:T(8,128)(2,1)S(1)}, bf16[4,128,256]{2,1,0:T(8,128)(2,1)S(1)}, u32[]{:S(2)}, u32[]{:S(2)}) collective-permute-start(bf16[4,128,256]{2,1,0:T(8,128)(2,1)S(1)} %get-tuple-element.96), channel_id=1, source_target_pairs={{0,24},{4,12},{8,0},{12,20},{16,8},{20,28},{24,16},{28,4},{1,25},{... | collective-permute-start | bytes 786440 | tf_op jit(solution)/shard_map/ppermute | solution.py:226
  133.2 44.1 %collective-permute-start.19 = (f32[2048,256]{1,0:T(8,128)S(1)}, f32[2048,256]{1,0:T(8,128)S(1)}, u32[]{:S(2)}, u32[]{:S(2)}) collective-permute-start(f32[2048,256]{1,0:T(8,128)S(1)} %get-tuple-element.93.refs_16_.second.refs_8_), channel_id=1, source_target_pairs={{0,2},{1,3},{2,0},{3,1},{4,6},{5,7},{6,4},{7,5},{8,10},{9,11},{10,... | collective-permute-start | bytes 6291464 | tf_op jit(solution)/shard_map/ppermute | solution.py:215
  142.1 35.2 %collective-permute-start.23 = (f32[2048,256]{1,0:T(8,128)S(1)}, f32[2048,256]{1,0:T(8,128)S(1)}, u32[]{:S(2)}, u32[]{:S(2)}) collective-permute-start(f32[2048,256]{1,0:T(8,128)S(1)} %collective-permute-done.18.refs_6_), channel_id=1, source_target_pairs={{0,1},{1,0},{2,3},{3,2},{4,5},{5,4},{6,7},{7,6},{8,9},{9,8},{10,11... | collective-permute-start | bytes 6291464 | tf_op jit(solution)/shard_map/ppermute | solution.py:215
  142.1 14.5 %collective-permute-start.24 = (bf16[8,128,256]{2,1,0:T(8,128)(2,1)S(1)}, bf16[8,128,256]{2,1,0:T(8,128)(2,1)S(1)}, u32[]{:S(2)}, u32[]{:S(2)}) collective-permute-start(bf16[8,128,256]{2,1,0:T(8,128)(2,1)S(1)} %get-tuple-element.104.refs_6_), channel_id=1, source_target_pairs={{0,4},{4,0},{8,12},{12,8},{16,20},{20,16},{24,28},{28,24},{1,5},{5... | collective-permute-start | bytes 1572872 | tf_op jit(solution)/shard_map/ppermute | solution.py:215
  144.1 22.2 %collective-permute-start.25 = (bf16[12,128,256]{2,1,0:T(8,128)(2,1)S(1)}, bf16[12,128,256]{2,1,0:T(8,128)(2,1)S(1)}, u32[]{:S(2)}, u32[]{:S(2)}) collective-permute-start(bf16[12,128,256]{2,1,0:T(8,128)(2,1)S(1)} %pad_maximum_fusion.2), channel_id=1, source_target_pairs={{0,8},{4,28},{8,16},{12,4},{16,24},{20,12},{24,0},{28,20},{1,9},{5... | collective-permute-start | bytes 2359304 | tf_op jit(solution)/shard_map/ppermute | solution.py:226
  156.6 20.2 %collective-permute-start.26 = (bf16[8,128,256]{2,1,0:T(8,128)(2,1)S(1)}, bf16[8,128,256]{2,1,0:T(8,128)(2,1)S(1)}, u32[]{:S(2)}, u32[]{:S(2)}) collective-permute-start(bf16[8,128,256]{2,1,0:T(8,128)(2,1)S(1)} %collective-permute-done.24.refs_8_), channel_id=1, source_target_pairs={{0,8},{4,28},{8,16},{12,4},{16,24},{20,12},{24,0},{28,20},{1,9},{5... | collective-permute-start | bytes 1572872 | tf_op jit(solution)/shard_map/ppermute | solution.py:226
  157.0 9.4 %collective-permute-start.27 = (bf16[4,128,256]{2,1,0:T(8,128)(2,1)S(1)}, bf16[4,128,256]{2,1,0:T(8,128)(2,1)S(1)}, u32[]{:S(2)}, u32[]{:S(2)}) collective-permute-start(bf16[4,128,256]{2,1,0:T(8,128)(2,1)S(1)} %collective-permute-done.21.refs_11_), channel_id=1, source_target_pairs={{0,4},{4,0},{8,12},{12,8},{16,20},{20,16},{24,28},{28,24},{1,5},{5... | collective-permute-start | bytes 786440 | tf_op jit(solution)/shard_map/ppermute | solution.py:215
  166.3 10.5 %collective-permute-start.28 = (bf16[4,128,256]{2,1,0:T(8,128)(2,1)S(1)}, bf16[4,128,256]{2,1,0:T(8,128)(2,1)S(1)}, u32[]{:S(2)}, u32[]{:S(2)}) collective-permute-start(bf16[4,128,256]{2,1,0:T(8,128)(2,1)S(1)} %slice.14), channel_id=1, source_target_pairs={{0,4},{4,0},{8,12},{12,8},{16,20},{20,16},{24,28},{28,24},{1,5},{5... | collective-permute-start | bytes 786440 | tf_op jit(solution)/shard_map/ppermute | solution.py:215
  166.4 19.7 %collective-permute-start.29 = (f32[2048,256]{1,0:T(8,128)S(1)}, f32[2048,256]{1,0:T(8,128)S(1)}, u32[]{:S(2)}, u32[]{:S(2)}) collective-permute-start(f32[2048,256]{1,0:T(8,128)S(1)} %get-tuple-element.93.refs_16_.second.refs_8_), channel_id=1, source_target_pairs={{0,1},{1,0},{2,3},{3,2},{4,5},{5,4},{6,7},{7,6},{8,9},{9,8},{10,11... | collective-permute-start | bytes 6291464 | tf_op jit(solution)/shard_map/ppermute | solution.py:215
  177.3 8.8 %collective-permute-start.30 = (f32[2048,256]{1,0:T(8,128)S(1)}, f32[2048,256]{1,0:T(8,128)S(1)}, u32[]{:S(2)}, u32[]{:S(2)}) collective-permute-start(f32[2048,256]{1,0:T(8,128)S(1)} %collective-permute-done.19.refs_10_), channel_id=1, source_target_pairs={{0,1},{1,0},{2,3},{3,2},{4,5},{5,4},{6,7},{7,6},{8,9},{9,8},{10,11... | collective-permute-start | bytes 6291464 | tf_op jit(solution)/shard_map/ppermute | solution.py:215
  177.3 23.9 %collective-permute-start.38 = (f32[2048,256]{1,0:T(8,128)S(1)}, f32[2048,256]{1,0:T(8,128)S(1)}, u32[]{:S(2)}, u32[]{:S(2)}) collective-permute-start(f32[2048,256]{1,0:T(8,128)S(1)} %get-tuple-element.89.refs_15_.first.refs_4_), channel_id=1, source_target_pairs={{0,1},{1,0},{2,3},{3,2},{4,5},{5,4},{6,7},{7,6},{8,9},{9,8},{10,11... | collective-permute-start | bytes 6291464 | tf_op jit(solution)/shard_map/ppermute | solution.py:215
  (27 other events, 413.4 us)

commit v3 on v2

--- a/solution.py
+++ b/solution.py
@@ -21,85 +21,270 @@
     return jnp.sum(rows.reshape(rows.shape[0] // 8, 8, rows.shape[1]), axis=0)
 
 
-def apply_kernel(step, sizes, moves, *refs):
-    nblocks, span, edges, width, group, front = sizes
-    early, late, nparts = moves
-    near_idx, crack_idx, crack_tgt, near_in, crack_in = refs[:5]
+def table_kernel(sizes, place, pattern, cluster, source, target, *outs):
+    nblocks, span, edges, front, count, tuned_here = sizes
+    near_a, crack_a, near_rows, near_mats, near_srcs, edge_rows, edge_mats, edge_srcs, numbers = outs
+    me = place[0]
+    odd = lax.rem(me, 2)
+    cut = nblocks // 2
+    limits = (2 * nblocks + cut, 6 * front) if tuned_here else (3 * nblocks, count * front)
+    zeros = (nblocks - cut, 2 * front)
+
+    def fill(i, carry):
+        for rows, mats, srcs, zero in (
+            (near_rows, near_mats, near_srcs, zeros[0]),
+            (edge_rows, edge_mats, edge_srcs, zeros[1]),
+        ):
+
+            @pl.when(i < rows.shape[0])
+            def _():
+                rows[i] = 0
+                mats[i] = 0
+                srcs[i] = zero
+
+        return carry
+
+    lax.fori_loop(0, max(near_rows.shape[0], edge_rows.shape[0]), fill, 0)
+
+    def note(lists, half, row, mat, src, late, found):
+        rows, mats, srcs = lists
+        spot = half * (rows.shape[0] // 2) + jnp.where(half == 0, found[0], found[1])
+
+        @pl.when(late)
+        def _():
+            rows[spot] = row - half * cut
+            mats[spot] = mat
+            srcs[spot] = src
+
+        step = jnp.where(late, 1, 0)
+        return (
+            found[0] + jnp.where(half == 0, step, 0),
+            found[1] + jnp.where(half == 1, step, 0),
+        )
+
+    def near_one(i, found):
+        value = pattern[i]
+        side, block = value // nblocks, lax.rem(value, nblocks)
+        beside = jnp.where(side == 2, 1 - odd, odd) if tuned_here else jnp.where(side == 2, 1, 0)
+        spot = jnp.where(side == 1, 0, jnp.where(beside == 1, 1, 2)) * nblocks + block
+        late = spot >= limits[0]
+        near_a[i] = jnp.where(late, limits[0], spot)
+        row = i // span
+        half = jnp.where(row >= cut, 1, 0)
+        lists = (near_rows, near_mats, near_srcs)
+        return note(lists, half, row, i, spot - limits[0], late, found)
+
+    none = (jnp.int32(0), jnp.int32(0))
+    near_found = lax.fori_loop(0, nblocks * span, near_one, none)
+
+    def edge_one(e, found):
+        if tuned_here:
+            offset = lax.rem(cluster[e] - me + count, count)
+            offset = jnp.where(odd == 1, lax.rem(count - offset, count), offset)
+            slot = jnp.int32(0)
+            for position, distance in enumerate((0, 1, 7, 6, 2, 4, 3, 5)):
+                slot = jnp.where(offset == distance, position, slot)
+        else:
+            slot = cluster[e]
+        spot = slot * front + source[e]
+        late = spot >= limits[1]
+        crack_a[e] = jnp.where(late, limits[1], spot)
+        row = target[e]
+        half = jnp.where(row >= cut, 1, 0)
+        lists = (edge_rows, edge_mats, edge_srcs)
+        return note(lists, half, row, e, spot - limits[1], late, found)
+
+    edge_found = lax.fori_loop(0, edges, edge_one, none)
+    for half in range(2):
+        numbers[half] = near_found[half]
+        numbers[2 + half] = edge_found[half]
+
+
+def table_call(me, pattern, cluster, source, target, nblocks, span, front):
+    edges = cluster.shape[0]
+    cut = nblocks // 2
+    near_list = 2 * max(cut, nblocks - cut) * span
+    lengths = (nblocks * span, edges, *(near_list,) * 3, *(2 * edges,) * 3, 4)
+    smem = pl.BlockSpec(memory_space=pltpu.SMEM)
+    sizes = (nblocks, span, edges, front, lax.axis_size("clu"), tuned())
+    return pl.pallas_call(
+        functools.partial(table_kernel, sizes),
+        out_shape=tuple(jax.ShapeDtypeStruct((length,), jnp.int32) for length in lengths),
+        in_specs=[smem] * 5,
+        out_specs=tuple(smem for _ in lengths),
+        name="tables",
+    )(me, pattern, cluster, source, target)
+
+
+def block_copies(parts, moves, target, sems):
+    return [
+        pltpu.make_async_copy(
+            parts[part].at[pl.ds(begin, count)], target.at[pl.ds(offset, count)], sems.at[place]
+        )
+        for place, (part, begin, count, offset) in enumerate(moves)
+    ]
+
+
+def total_of(moves):
+    return sum(move[2] for move in moves)
+
+
+GROUP = 4
+REST_COST = 3
+
+
+def main_kernel(sizes, moves, *refs):
+    nblocks, span, edges, front_moves, source_moves, nparts = (*sizes, *moves)
+    near_idx, crack_idx, crack_tgt, near_v, crack_v = refs[:5]
     parts = refs[5 : 5 + nparts]
-    rest = refs[5 + nparts :]
-    extras = rest[:2] if step != 2 else rest[:1]
-    rest = rest[len(extras) :]
-    nouts = (5, 5, 1)[step - 1]
-    outs, rest = rest[:nouts], rest[nouts:]
-    front_v, source_v, acc, front_sem, source_sem = rest[:5]
-    near_v, crack_v = near_in, crack_in
-    matrix_copies, extra_copies = [], []
-    if step == 1:
-        near_v, crack_v, extra_v, matrix_sem, extra_sem = rest[5:]
-        matrix_copies = [pltpu.make_async_copy(crack_in, crack_v, matrix_sem.at[nblocks])]
-        for g in range(nblocks):
-            matrix_copies.append(
-                pltpu.make_async_copy(near_in.at[g], near_v.at[g], matrix_sem.at[g])
-            )
-        extra_copies = [
-            pltpu.make_async_copy(extra, extra_v.at[place], extra_sem.at[place])
-            for place, extra in enumerate(extras)
-        ]
-        extras = [extra_v.at[place] for place in range(2)]
-
-    def copies(which, target, sems):
-        return [
-            pltpu.make_async_copy(
-                parts[part].at[pl.ds(begin, count)],
-                target.at[pl.ds(offset, count)],
-                sems.at[place],
-            )
-            for place, (part, begin, count, offset) in enumerate(which)
-        ]
-
-    front_copies = copies(early, front_v, front_sem)
-    source_copies = copies(late, source_v, source_sem)
-    for copy in front_copies + matrix_copies[:1] + source_copies + extra_copies:
+    acc_a, acc_b, front_v, source_v, front_sem, source_sem = refs[5 + nparts :]
+    cut = acc_a.shape[0]
+    front_copies = block_copies(parts, front_moves, front_v, front_sem)
+    source_copies = block_copies(parts, source_moves, source_v, source_sem)
+    for copy in source_copies + front_copies:
         copy.start()
-    for copy in matrix_copies[1:]:
-        copy.start()
-    acc[...] = jnp.zeros(acc.shape, jnp.float32)
-    for copy in front_copies + matrix_copies[:1]:
+    for store in (front_v, source_v):
+        store[store.shape[0] - 1] = jnp.zeros(store.shape[1:], store.dtype)
+    for copy in source_copies:
+        copy.wait()
+
+    def row(acc, start, g, carry):
+        left = jnp.concatenate([near_v[g, s] for s in range(span)], axis=1)
+        right = jnp.concatenate([source_v[near_idx[g * span + s]] for s in range(span)], axis=0)
+        acc[g - start] = jnp.dot(left, right, preferred_element_type=jnp.float32)
+        return carry
+
+    lax.fori_loop(0, cut, functools.partial(row, acc_a, 0), 0, unroll=2)
+    lax.fori_loop(cut, nblocks, functools.partial(row, acc_b, cut), 0, unroll=2)
+    for copy in front_copies:
         copy.wait()
 
     def crack_edges(i, carry):
         products = [
             jnp.dot(
-                crack_v[i * group + k],
-                front_v[crack_idx[i * group + k]],
+                crack_v[i * GROUP + k],
+                front_v[crack_idx[i * GROUP + k]],
                 preferred_element_type=jnp.float32,
             )
-            for k in range(group)
+            for k in range(GROUP)
         ]
-        for k in range(group):
-            acc[crack_tgt[i * group + k]] += products[k]
+        for k in range(GROUP):
+            target = crack_tgt[i * GROUP + k]
+
+            @pl.when(target < cut)
+            def _():
+                acc_a[target] += products[k]
+
+            @pl.when(target >= cut)
+            def _():
+                acc_b[target - cut] += products[k]
+
         return carry
 
-    lax.fori_loop(0, edges // group, crack_edges, 0)
-    for copy in source_copies + extra_copies:
-        copy.wait()
-
+    lax.fori_loop(0, edges // GROUP, crack_edges, 0)
+
+
+def main_call(step, tables, near, crack, found):
+    parts, front_moves, source_moves = found[:3]
+    nblocks, span = near.shape[:2]
+    edges, width = crack.shape[0], near.shape[3]
+    lanes = parts[0].shape[2]
+    cut = nblocks // 2
+    smem = pl.BlockSpec(memory_space=pltpu.SMEM)
+    anywhere = pl.BlockSpec(memory_space=pl.ANY)
+    whole = pl.BlockSpec(memory_space=pltpu.VMEM)
+    blocks = total_of(front_moves) + total_of(source_moves) + 2
+    return pl.pallas_call(
+        functools.partial(
+            main_kernel, (nblocks, span, edges), (front_moves, source_moves, len(parts))
+        ),
+        out_shape=tuple(
+            jax.ShapeDtypeStruct((rows, 2 * width, lanes), jnp.float32)
+            for rows in (cut, nblocks - cut)
+        ),
+        in_specs=[smem] * 3 + [whole] * 2 + [anywhere] * len(parts),
+        out_specs=(whole, whole),
+        scratch_shapes=[
+            pltpu.VMEM((total_of(front_moves) + 1, width, lanes), jnp.bfloat16),
+            pltpu.VMEM((total_of(source_moves) + 1, width, lanes), jnp.bfloat16),
+            pltpu.SemaphoreType.DMA((len(front_moves),)),
+            pltpu.SemaphoreType.DMA((len(source_moves),)),
+        ],
+        compiler_params=pltpu.CompilerParams(
+            vmem_limit_bytes=2 * blocks * width * lanes + 2 * MIB
+        ),
+        cost_estimate=pl.CostEstimate(
+            flops=4 * width * width * lanes * (nblocks * span + edges),
+            bytes_accessed=near.size * 2 + crack.size * 2,
+            transcendentals=0,
+        ),
+        name=f"operator_{step}",
+    )(tables[0], tables[1], tables[-1], near, crack, *parts)
+
+
+def rest_kernel(step, part, sizes, moves, *refs):
+    nblocks, span, width, front, start, nrows = sizes
+    near_moves, edge_moves, nparts = moves
+    lists, rest = refs[:7], refs[7:]
+    near_v, crack_v, acc = rest[:3]
+    parts, rest = rest[3 : 3 + nparts], rest[3 + nparts :]
+    nextra = 2 if step == 3 else 1
+    extras, rest = rest[:nextra], rest[nextra:]
+    before = ()
+    if part == 1:
+        nbefore = 1 if step == 3 else 2
+        before, rest = rest[:nbefore], rest[nbefore:]
+    nouts = 1 if step == 3 else (4, 3)[part]
+    outs, rest = rest[:nouts], rest[nouts:]
+    numbers = lists[6]
     lanes = acc.shape[2]
+    late = nparts > 0
+    if late:
+        near_src, edge_src, extra, near_sem, edge_sem = rest
+        copies = block_copies(parts, near_moves, near_src, near_sem)
+        copies += block_copies(parts, edge_moves, edge_src, edge_sem)
+        for copy in copies:
+            copy.start()
+        extra[...] = jnp.zeros(extra.shape, jnp.float32)
+        for store in (near_src, edge_src):
+            store[store.shape[0] - 1] = jnp.zeros(store.shape[1:], store.dtype)
+        for copy in copies:
+            copy.wait()
+
+        def add(rows, mats, srcs, number, matrix, source):
+            offset = part * (rows.shape[0] // 2)
+
+            def some(i, carry):
+                spots = [offset + i * GROUP + k for k in range(GROUP)]
+                products = [
+                    jnp.dot(
+                        matrix(mats[spot]), source[srcs[spot]], preferred_element_type=jnp.float32
+                    )
+                    for spot in spots
+                ]
+                for spot, product in zip(spots, products):
+                    extra[rows[spot]] += product
+                return carry
+
+            lax.fori_loop(0, (number + GROUP - 1) // GROUP, some, 0)
+
+        add(
+            *lists[:3],
+            numbers[part],
+            lambda i: near_v[i // span, lax.rem(i, span)],
+            near_src,
+        )
+        add(*lists[3:6], numbers[2 + part], lambda i: crack_v[i], edge_src)
+
     nsums = (1, 3, 5)[step - 1]
     zero = jnp.zeros((8, lanes), jnp.float32)
 
-    def row(part, start, g, sums):
+    def row(g, sums):
+        total = acc[g] + extra[g] if late else acc[g]
+        new = total[:width] + turn(total[width:])
+        rows = pl.ds(pl.multiple_of((start + g) * width, width), width)
         if step == 1:
-            pltpu.make_async_copy(near_in.at[g], near_v.at[g], matrix_sem.at[g]).wait()
-        left = jnp.concatenate([near_v[g, s] for s in range(span)], axis=1)
-        right = jnp.concatenate([source_v[near_idx[g * span + s]] for s in range(span)], axis=0)
-        total = acc[g] + jnp.dot(left, right, preferred_element_type=jnp.float32)
-        new = total[:width] + turn(total[width:])
-        rows = pl.ds(pl.multiple_of(g * width, width), width)
-        if step == 1:
-            incident = jnp.concatenate([extras[0][0, rows], extras[0][1, rows]], axis=1)
-            initial = jnp.concatenate([extras[1][0, rows], extras[1][1, rows]], axis=1)
-            new = incident - 0.5 * initial - new
+            new = extras[0][rows, :] - new
             terms = (new * new,)
         elif step == 2:
             first = extras[0][rows, :]
@@ -110,22 +295,74 @@
         if step != 3:
             outs[0][rows, :] = new
             rounded = new.astype(jnp.bfloat16)
-            outs[1 + part][g - start] = rounded
+            outs[1][g] = rounded
             if part == 0:
 
                 @pl.when(g < front)
                 def _():
-                    outs[3][g] = rounded
+                    outs[2][g] = rounded
 
         return tuple(total + col_sum(term) for total, term in zip(sums, terms))
 
-    sums = (zero,) * nsums
-    cut = nblocks // 2
-    for part, (start, end) in enumerate(((0, cut), (cut, nblocks))):
-        sums = lax.fori_loop(start, end, functools.partial(row, part, start), sums, unroll=2)
+    sums = lax.fori_loop(0, nrows, row, (zero,) * nsums, unroll=2)
     sums = [jnp.sum(total, axis=0, keepdims=True) for total in sums]
     sums.append(jnp.zeros((8 - nsums, lanes), jnp.float32))
-    outs[-1][...] = jnp.concatenate(sums, axis=0)
+    sums = jnp.concatenate(sums, axis=0)
+    if part == 1:
+        sums = sums + before[-1][...]
+        if step != 3:
+            outs[0][: before[0].shape[0], :] = before[0][...]
+    outs[-1][...] = sums
+
+
+def rest_call(step, part, front, tables, near, crack, found, acc, extras, before=()):
+    _, _, _, parts, near_moves, edge_moves = found
+    nblocks, span = near.shape[:2]
+    width, lanes = near.shape[3], acc.shape[2]
+    nrows = acc.shape[0]
+    start = part * (nblocks // 2)
+    out_shape = [jax.ShapeDtypeStruct((8, lanes), jnp.float32)]
+    if step != 3:
+        ends = start + nrows
+        vector = jax.ShapeDtypeStruct((ends * width, lanes), jnp.float32)
+        low_a, low_b, head = low_shapes(nblocks, width, lanes, front)
+        out_shape = [vector, *((low_a, head), (low_b,))[part], *out_shape]
+    smem = pl.BlockSpec(memory_space=pltpu.SMEM)
+    anywhere = pl.BlockSpec(memory_space=pl.ANY)
+    whole = pl.BlockSpec(memory_space=pltpu.VMEM)
+    scratch, held = [], 0
+    if parts:
+        shapes = (total_of(near_moves) + 1, total_of(edge_moves) + 1)
+        scratch = [pltpu.VMEM((n, width, lanes), jnp.bfloat16) for n in shapes]
+        scratch += [
+            pltpu.VMEM(acc.shape, jnp.float32),
+            pltpu.SemaphoreType.DMA((len(near_moves),)),
+            pltpu.SemaphoreType.DMA((len(edge_moves),)),
+        ]
+        held = 2 * sum(shapes) * width * lanes + 4 * acc.size
+    return pl.pallas_call(
+        functools.partial(
+            rest_kernel,
+            step,
+            part,
+            (nblocks, span, width, front, start, nrows),
+            (near_moves, edge_moves, len(parts)),
+        ),
+        out_shape=tuple(out_shape),
+        in_specs=[smem] * 7
+        + [whole] * 3
+        + [anywhere] * len(parts)
+        + [whole] * (len(extras) + len(before)),
+        out_specs=tuple(whole for _ in out_shape),
+        scratch_shapes=scratch,
+        compiler_params=pltpu.CompilerParams(vmem_limit_bytes=held + 2 * MIB),
+        cost_estimate=pl.CostEstimate(
+            flops=4 * width * width * lanes * nrows * span // 4,
+            bytes_accessed=REST_COST * acc.size * 4,
+            transcendentals=0,
+        ),
+        name=f"rest_{step}_{part}",
+    )(*tables[2:9], near, crack, acc, *parts, *extras, *before)
 
 
 def low_shapes(nblocks, width, lanes, front):
@@ -134,65 +371,6 @@
         jax.ShapeDtypeStruct((count, width, lanes), jnp.bfloat16)
         for count in (cut, nblocks - cut, front)
     )
-
-
-def apply_call(step, front, tables, near, crack, found, extras):
-    parts, early, late = found
-    nblocks, span = near.shape[:2]
-    edges, width = crack.shape[0], near.shape[3]
-    lanes = parts[0].shape[2]
-    group = 4 if edges % 4 == 0 else 1
-    gram = jax.ShapeDtypeStruct((8, lanes), jnp.float32)
-    out_shape = (gram,)
-    if step != 3:
-        vector = jax.ShapeDtypeStruct((nblocks * width, lanes), jnp.float32)
-        out_shape = (vector, *low_shapes(nblocks, width, lanes, front), gram)
-    smem = pl.BlockSpec(memory_space=pltpu.SMEM)
-    anywhere = pl.BlockSpec(memory_space=pltpu.HBM if step == 1 else pl.ANY)
-    whole = pl.BlockSpec(memory_space=pltpu.VMEM)
-    scratch = []
-    if step == 1:
-        scratch = [
-            pltpu.VMEM(near.shape, near.dtype),
-            pltpu.VMEM(crack.shape, crack.dtype),
-            pltpu.VMEM((2, *extras[0].shape), jnp.float32),
-            pltpu.SemaphoreType.DMA((nblocks + 1,)),
-            pltpu.SemaphoreType.DMA((2,)),
-        ]
-    nearby = sum(move[2] for move in early), sum(move[2] for move in late)
-    held = 2 * sum(nearby) * width * lanes + 8 * nblocks * width * lanes
-    if step == 1:
-        held += 8 * extras[0].size + 2 * (near.size + crack.size)
-    body = functools.partial(
-        apply_kernel,
-        step,
-        (nblocks, span, edges, width, group, front),
-        (early, late, len(parts)),
-    )
-    return pl.pallas_call(
-        body,
-        out_shape=out_shape,
-        in_specs=[smem] * 3
-        + [anywhere if step == 1 else whole] * 2
-        + [anywhere] * len(parts)
-        + [anywhere if step == 1 else whole] * len(extras),
-        out_specs=tuple(whole for _ in out_shape),
-        scratch_shapes=[
-            pltpu.VMEM((nearby[0], width, lanes), jnp.bfloat16),
-            pltpu.VMEM((nearby[1], width, lanes), jnp.bfloat16),
-            pltpu.VMEM((nblocks, 2 * width, lanes), jnp.float32),
-            pltpu.SemaphoreType.DMA((len(early),)),
-            pltpu.SemaphoreType.DMA((len(late),)),
-            *scratch,
-        ],
-        compiler_params=pltpu.CompilerParams(vmem_limit_bytes=44 * MIB if step == 1 else held + 2 * MIB),
-        cost_estimate=pl.CostEstimate(
-            flops=4 * width * width * lanes * (nblocks * span + edges),
-            bytes_accessed=near.size * 2 + crack.size * 2,
-            transcendentals=0,
-        ),
-        name=f"operator_{step}",
-    )(*tables, near, crack, *parts, *extras)
 
 
 def prepare_kernel(initial, low_a, low_b, head):
@@ -240,59 +418,50 @@
     nblocks = cut + rest
     if not tuned():
         count = lax.axis_size("clu")
+        if callable(late_ties):
+            late_ties = late_ties(early_ties)
         low = jnp.concatenate([low_a, low_b], axis=0)
         every = lax.all_gather(head, "clu", axis=0, tiled=True)
         parts = [low, shift(low, "clu", -1), shift(low, "clu", 1), every]
-        late = tuple((k, 0, nblocks, k * nblocks) for k in range(3))
-        return (parts, ((3, 0, count * front, 0),), late), early_ties, late_ties
+        source_moves = tuple((k, 0, nblocks, k * nblocks) for k in range(3))
+        found = (parts, ((3, 0, count * front, 0),), source_moves, [], (), ())
+        return found, early_ties, late_ties
     beside_a = swap(low_a, "clu", 1)
     same = ring(head, 2)
     other = ring(head, -2)
     tail, beside_a, same, other, *early_ties = tie(low_b, beside_a, same, other, *early_ties)
-    beyond_a = ring(jnp.concatenate([beside_a, same], axis=0), 2)
+    onward = jnp.concatenate([beside_a, same], axis=0)
+    beyond_a = ring(onward, 2)
     beside_b = swap(tail, "clu", 1)
-    same_pair = swap(same, "clu", 1)
+    if callable(late_ties):
+        late_ties = late_ties(early_ties)
     beside_b, *late_ties = tie(beside_b, *late_ties)
     beyond_b = ring(beside_b, 2)
-    far_pair = swap(beyond_a[cut:], "clu", 1)
-    parts = [low_a, low_b, beside_a, beside_b, beyond_a, beyond_b]
-    parts += [same, other, same_pair, far_pair]
-    early = tuple(
+    pairs = swap(jnp.concatenate([same, beyond_a[cut:]], axis=0), "clu", 1)
+    parts = [low_a, low_b, beside_a, beside_b, beyond_a, same, other]
+    front_moves = tuple(
         (part, begin, front, place * front)
         for place, (part, begin) in enumerate(
-            [(0, 0), (2, 0), (4, 0), (6, 0), (7, 0), (4, cut), (8, 0), (9, 0)]
+            [(0, 0), (2, 0), (4, 0), (5, 0), (6, 0), (4, cut)]
         )
     )
-    late = tuple(
-        (2 * k + half, 0, (cut, rest)[half], k * nblocks + half * cut)
-        for k in range(3)
-        for half in range(2)
-    )
-    return (parts, early, late), early_ties, late_ties
-
-
-def source_tables(near_pattern, crack_cluster, crack_source, nblocks, front):
-    count = lax.axis_size("clu")
-    me = lax.axis_index("clu")
-    side, block = near_pattern.reshape(-1) // nblocks, near_pattern.reshape(-1) % nblocks
+    source_moves = (
+        (0, 0, cut, 0),
+        (1, 0, rest, cut),
+        (2, 0, cut, nblocks),
+        (3, 0, rest, nblocks + cut),
+        (4, 0, cut, 2 * nblocks),
+    )
+    last = [beyond_b, pairs]
+    found = (parts, front_moves, source_moves, last, ((0, 0, rest, 0),), ((1, 0, 2 * front, 0),))
+    return found, early_ties, late_ties
+
+
+def sum_over_clusters(value, *tied):
     if not tuned():
-        place = jnp.where(side == 1, 0, jnp.where(side == 2, 1, 2))
-        return place * nblocks + block, crack_cluster * front + crack_source
-    odd = me % 2 == 1
-    place = jnp.where(side == 1, 0, jnp.where((side == 2) ^ odd, 1, 2))
-    offset = (crack_cluster - me) % count
-    offset = jnp.where(odd, (-offset) % count, offset)
-    slot = jnp.zeros_like(offset)
-    for position, distance in enumerate((0, 1, 7, 6, 2, 4, 3, 5)):
-        slot = jnp.where(offset == distance, position, slot)
-    return place * nblocks + block, slot * front + crack_source
-
-
-def sum_over_clusters(value):
-    if not tuned():
-        return [lax.psum(value, "clu")]
-    value = value + swap(value, "clu", 1)
-    return [value, *(shift(value, "clu", d) for d in (2, 4, 6))]
+        return [lax.psum(value, "clu")], tied
+    value, *tied = tie(value + swap(value, "clu", 1), *tied)
+    return [value, *(shift(value, "clu", d) for d in (2, 4, 6))], tied
 
 
 def cmul(a, b):
@@ -439,6 +608,19 @@
     lax.fori_loop(0, initial.shape[1] // width, one, 0)
 
 
+def base_kernel(incident, initial, base):
+    width = 256
+
+    def one(g, carry):
+        rows = pl.ds(pl.multiple_of(g * width, width), width)
+        base[rows, :] = jnp.concatenate(
+            [incident[half, rows] - 0.5 * initial[half, rows] for half in range(2)], axis=1
+        )
+        return carry
+
+    lax.fori_loop(0, base.shape[0] // width, one, 0)
+
+
 def mix_kernel(place, keep, taken, here, away):
     side, sign = place[0] // 2, 1.0 - 2.0 * lax.rem(place[0], 2).astype(jnp.float32)
     near_sign, far_sign = jnp.where(side == 1, sign, 1.0), jnp.where(side == 0, sign, 1.0)
@@ -511,10 +693,6 @@
     front = 4
     near = near_blocks.reshape(nblocks, span, 2 * width, width)
     crack = crack_blocks.reshape(edges, 2 * width, width)
-    near_idx, crack_idx = source_tables(
-        near_pattern, crack_cluster[:, 0], crack_source, nblocks, front
-    )
-    tables = (near_idx.astype(jnp.int32), crack_idx.astype(jnp.int32), crack_target)
     incident, initial = incident[0], initial[0]
     lows = on_vmem(
         prepare_kernel,
@@ -526,37 +704,62 @@
 
     place = lax.axis_index("frq") ^ jnp.arange(4, dtype=jnp.int32)
     real = jax.ShapeDtypeStruct((panels, directions), jnp.float32)
+    both = jax.ShapeDtypeStruct((panels, 2 * directions), jnp.float32)
+
+    tables = table_call(
+        lax.axis_index("clu").reshape(1),
+        near_pattern.reshape(-1),
+        crack_cluster[:, 0],
+        crack_source,
+        crack_target,
+        nblocks,
+        span,
+        front,
+    )
+
+    found, (from_start, *tables), base = exchange(
+        lows,
+        (initial, *tables),
+        lambda early: [on_vmem(base_kernel, both, (), (incident, early[0]), "base")],
+    )
+    base = base[0]
+    tables = (*tables, crack_target)
     send, keep = on_vmem(
-        terms_kernel, (real, real), (place, pulse_spectrum), (initial,), "terms"
-    )
-    taken = swap(send, "frq", 1)
-    here, away = on_vmem(mix_kernel, (real, real), (place,), (keep, taken), "mix")
-
-    found, _, (here, away) = exchange(lows, (), (here, away))
+        terms_kernel, (real, real), (place, pulse_spectrum), (from_start,), "terms"
+    )
+    here, away = on_vmem(
+        mix_kernel, (real, real), (place,), (keep, swap(send, "frq", 1)), "mix"
+    )
     away = swap(away, "frq", 2)
-    first, *lows, sums_one = apply_call(1, front, tables, near, crack, found, (incident, initial))
-
-    first_sent, away, *lows = tie(first, away, *lows)
-    first_across = swap(first_sent, "frq", 2)
-    first_one = swap(first, "frq", 1)
-    found, _, _ = exchange(lows)
-    second, *lows, sums_two = apply_call(2, front, tables, near, crack, found, (first,))
-
-    second_sent, first_across, *lows = tie(second, first_across, *lows)
-    second_across = swap(second_sent, "frq", 2)
-    found, (first_across,), _ = exchange(lows, (first_across,))
-    parts, early, late = found
-    first_three = swap(first_across, "frq", 1)
-    second_across, first_three, *parts = tie(second_across, first_three, *parts)
-    second_one, second_three = swap(second, "frq", 1), swap(second_across, "frq", 1)
-    (sums_three,) = apply_call(
-        3, front, tables, near, crack, (parts, early, late), (first, second)
-    )
-    sums_three, second_one, second_three = tie(sums_three, second_one, second_three)
+
+    def operate(step, found, extras, *tied):
+        acc_a, acc_b = main_call(step, tables, near, crack, found)
+        both_halves = (front, tables, near, crack, found)
+        if step == 3:
+            (sums,) = rest_call(3, 0, *both_halves, acc_a, extras)
+            (sums,) = rest_call(3, 1, *both_halves, acc_b, extras, (sums,))
+            return sums, *tied
+        upper, low_a, head, sums = rest_call(step, 0, *both_halves, acc_a, extras)
+        vector, low_b, sums = rest_call(step, 1, *both_halves, acc_b, extras, (upper, sums))
+        return vector, low_a, low_b, head, sums
+
+    first, *lows, sums_one = operate(1, found, (base,))
+    found, (first_sent, away), _ = exchange(lows, (first, away))
+    first_across, first_one = swap(first_sent, "frq", 2), swap(first, "frq", 1)
+
+    second, *lows, sums_two = operate(2, found, (first,))
+    found, (second_sent, first_across), _ = exchange(lows, (second, first_across))
+    second_across, first_three = swap(second_sent, "frq", 2), swap(first_across, "frq", 1)
+    (sums_three,) = operate(3, found, (first, second))
+    second_one = swap(second, "frq", 1)
+    sums = jnp.concatenate([sums_one, sums_two, sums_three], axis=0)
+    sums, (second_across, second_one, first_three) = sum_over_clusters(
+        sums, second_across, second_one, first_three
+    )
+    second_three = swap(second_across, "frq", 1)
     firsts = [first, first_one, first_across, first_three]
     seconds = [second, second_one, second_across, second_three]
 
-    sums = sum_over_clusters(jnp.concatenate([sums_one, sums_two, sums_three], axis=0))
     row = jax.ShapeDtypeStruct((8, directions), jnp.float32)
     coefs, sent = on_vmem(
         functools.partial(small_kernel, len(sums)), (row, row), (pulse_spectrum,), sums, "small"

time: 205 us -> 182 us (0.89)
  waiting for transfers between devices: 110 us -> 86.6 us
  Pallas kernels: 41.1 us -> 54.5 us
  starting transfers between devices: 43.1 us -> 36.2 us
  local copies, waits for them, and re-layouts: 8.03 us -> 3.25 us
    ppermute x12, waiting for transfers between devices: 67.5 us -> 39 us  [ring(): return lax.ppermute(value, 'clu', pairs)]
    pallas_call x3 -> x10, Pallas kernels: 31.2 us -> 46.1 us  [the longest x3 24.3 us: main_call(): pl.pallas_call(functools.partial(main_kernel, (nblocks, span, edges), (fr...]
    ppermute x24 -> x21, starting transfers between devices: 21.1 us -> 15.2 us  [swap(): return lax.ppermute(value, axis, [(i, i ^ distance) for i in range(count)])]
    unnamed x43 -> x39, local copies, waits for them, and re-layouts: 6.93 us -> 2.53 us
    ppermute x24 -> x21, waiting for transfers between devices: 41.4 us -> 45.4 us  [swap(): return lax.ppermute(value, axis, [(i, i ^ distance) for i in range(count)])]
    pallas_call x6 -> x7, Pallas kernels: 9.9 us -> 8.39 us  [on_vmem(): pl.pallas_call(body, out_shape=out_shape, in_specs=[smem] * len(smem_args...]
  transfers between devices with their start and end apart: 39 -> 36, of which waited for: 22 -> 22; matrix products, arithmetic and copies ran while one was open for 1% -> 1% of each run, Pallas kernels for 18% -> 27%
where the time goes in v3:
time: 182 us
  waiting for transfers between devices  86.6 us (48%)
  Pallas kernels  54.5 us (30%)
  starting transfers between devices  36.2 us (20%)
  local copies, waits for them, and re-layouts  3.25 us (2%)
    ppermute x21, waiting for transfers between devices, swap(): return lax.ppermute(value, axis, [(i, i ^ distance) for i in range(count)])  45.4 us
    ppermute x12, waiting for transfers between devices, ring(): return lax.ppermute(value, 'clu', pairs)  39 us
    pallas_call x3, Pallas kernels, main_call(): pl.pallas_call(functools.partial(main_kernel, (nblocks, span, edges), (fr...  24.3 us
    ppermute x12, starting transfers between devices, ring(): return lax.ppermute(value, 'clu', pairs)  17 us
    pallas_call x6, Pallas kernels, rest_call(): pl.pallas_call(functools.partial(rest_kernel, step, part, (nblocks, span,...  15.4 us
    ppermute x21, starting transfers between devices, swap(): return lax.ppermute(value, axis, [(i, i ^ distance) for i in range(count)])  15.2 us
    pallas_call x7, Pallas kernels, on_vmem(): pl.pallas_call(body, out_shape=out_shape, in_specs=[smem] * len(smem_args...  8.39 us
    pallas_call x1, Pallas kernels, table_call(): pl.pallas_call(functools.partial(table_kernel, sizes), out_shape=tuple((j...  6.41 us
  transfers between devices with their start and end apart: 36, of which 22 were waited for; matrix products, arithmetic and copies ran while one was open for 1% of the time, Pallas kernels for 27%

profile of v3, /device:TPU:0, one launch (start us, length us, event | category | flops | bytes accessed | tf_op | source)
XLA Modules:
  0.0 182.0 jit_solution(15362900979576713396)
XLA Ops:
  3.9 2.9 %collective-permute-start = (bf16[8,128,256]{2,1,0:T(8,128)(2,1)S(1)}, bf16[8,128,256]{2,1,0:T(8,128)(2,1)S(1)}, u32[]{:S(2)}, u32[]{:S(2)}) collective-permute-start(bf16[8,128,256]{2,1,0:T(8,128)(2,1)S(1)} %get-tuple-element.73.refs_5_), channel_id=1, source_target_pairs={{0,4},{4,0},{8,12},{12,8},{16,20},{20,16},{24,28},{28,24},{1,5},{5... | collective-permute-start | bytes 1572872 | tf_op jit(solution)/shard_map/ppermute | solution.py:393
  8.4 2.2 %collective-permute-start.2 = (bf16[4,128,256]{2,1,0:T(8,128)(2,1)}, bf16[4,128,256]{2,1,0:T(8,128)(2,1)}, u32[]{:S(2)}, u32[]{:S(2)}) collective-permute-start(bf16[4,128,256]{2,1,0:T(8,128)(2,1)} %get-tuple-element.74), channel_id=1, source_target_pairs={{0,24},{4,12},{8,0},{12,20},{16,8},{20,28},{24,16},{28,4},{1,25},{... | collective-permute-start | bytes 786440 | tf_op jit(solution)/shard_map/ppermute | solution.py:404
  11.4 6.4 %tables.1 = (s32[128]{0:T(128)}, s32[32]{0:T(128)}, s32[128]{0:T(128)}, s32[128]{0:T(128)}, s32[128]{0:T(128)}, /*index=5*/s32[64]{0:T(128)}, s32[64]{0:T(128)}, s32[64]{0:T(128)}, s32[4]{0:T(128)}) custom-call(s32[1]{0:T(128)} %bitcast.1.place, s32[128]{0:T(128)} %reshape.17.pattern, s32[32]{0:T(128)} %bitcast.33, s32[32]{0:T(128)} %source.1, s32[32]{0:T(128)} %refs_2_.5), custom_call_target="tpu_custom_call" | custom-call | tf_op jit(solution)/shard_map/tables/pallas_call | solution.py:110
  18.2 3.7 %collective-permute-done.2.refs_11_ = bf16[4,128,256]{2,1,0:T(8,128)(2,1)} collective-permute-done((bf16[4,128,256]{2,1,0:T(8,128)(2,1)}, bf16[4,128,256]{2,1,0:T(8,128)(2,1)}, u32[]{:S(2)}, u32[]{:S(2)}) %collective-permute-start.2) | collective-permute-done | bytes 262176 | tf_op jit(solution)/shard_map/ppermute | solution.py:404
  26.4 11.9 %collective-permute-done.3.refs_8_ = bf16[8,128,256]{2,1,0:T(8,128)(2,1)S(1)} collective-permute-done((bf16[8,128,256]{2,1,0:T(8,128)(2,1)S(1)}, bf16[8,128,256]{2,1,0:T(8,128)(2,1)S(1)}, u32[]{:S(2)}, u32[]{:S(2)}) %collective-permute-start.3) | collective-permute-done | bytes 524320 | tf_op jit(solution)/shard_map/ppermute | solution.py:393
  38.7 6.3 %collective-permute-done.4.refs_9_ = bf16[12,128,256]{2,1,0:T(8,128)(2,1)S(1)} collective-permute-done((bf16[12,128,256]{2,1,0:T(8,128)(2,1)S(1)}, bf16[12,128,256]{2,1,0:T(8,128)(2,1)S(1)}, u32[]{:S(2)}, u32[]{:S(2)}) %collective-permute-start.4) | collective-permute-done | bytes 786464 | tf_op jit(solution)/shard_map/ppermute | solution.py:404
  47.7 8.1 %operator_1.1 = (f32[8,256,256]{2,1,0:T(8,128)S(1)}, f32[8,256,256]{2,1,0:T(8,128)S(1)}) custom-call(s32[128]{0:T(128)S(1)} %copy-done.15, s32[32]{0:T(128)S(1)} %copy-done.16, s32[32]{0:T(128)S(1)} %copy-done.14, bf16[16,8,256,128]{3,2,1,0:T(8,128)(2,1)S(1)} %bitcast.8, bf16[32,256,128]{2,1,0:T(8,128)(2,1)S(1)} %bitcast.17, ...), custom_call_target="tpu_custom_call" | custom-call | flops 2684354560 | bytes 10485760 | tf_op jit(solution)/shard_map/operator_1/pallas_call | solution.py:197
  55.9 2.4 %collective-permute-done.6.refs_11_ = bf16[8,128,256]{2,1,0:T(8,128)(2,1)S(1)} collective-permute-done((bf16[8,128,256]{2,1,0:T(8,128)(2,1)S(1)}, bf16[8,128,256]{2,1,0:T(8,128)(2,1)S(1)}, u32[]{:S(2)}, u32[]{:S(2)}) %collective-permute-start.6) | collective-permute-done | bytes 524320 | tf_op jit(solution)/shard_map/ppermute | solution.py:393
  58.4 2.2 %rest_1_0.1 = (f32[1024,256]{1,0:T(8,128)S(1)}, bf16[8,128,256]{2,1,0:T(8,128)(2,1)S(1)}, bf16[4,128,256]{2,1,0:T(8,128)(2,1)S(1)}, f32[8,256]{1,0:T(8,128)S(1)}) custom-call(s32[128]{0:T(128)S(1)} %copy-done.7, s32[128]{0:T(128)S(1)} %copy-done.8, s32[128]{0:T(128)S(1)} %copy-done.9, s32[64]{0:T(128)S(1)} %copy-done.10, s32[64]{0:T(128)S(1)} %copy-done.11, ...), custom_call_target="tpu_custom_call" | custom-call | flops 268435456 | bytes 6291456 | tf_op jit(solution)/shard_map/rest_1_0/pallas_call | solution.py:343
  62.7 2.1 %collective-permute-start.9 = (bf16[4,128,256]{2,1,0:T(8,128)(2,1)S(1)}, bf16[4,128,256]{2,1,0:T(8,128)(2,1)S(1)}, u32[]{:S(2)}, u32[]{:S(2)}) collective-permute-start(bf16[4,128,256]{2,1,0:T(8,128)(2,1)S(1)} %get-tuple-element.107), channel_id=1, source_target_pairs={{0,24},{4,12},{8,0},{12,20},{16,8},{20,28},{24,16},{28,4},{1,25},{... | collective-permute-start | bytes 786440 | tf_op jit(solution)/shard_map/ppermute | solution.py:404
  64.8 2.6 %rest_1_1.1 = (f32[2048,256]{1,0:T(8,128)S(1)}, bf16[8,128,256]{2,1,0:T(8,128)(2,1)S(1)}, f32[8,256]{1,0:T(8,128)S(1)}) custom-call(s32[128]{0:T(128)S(1)} %copy-done.7, s32[128]{0:T(128)S(1)} %copy-done.8, s32[128]{0:T(128)S(1)} %copy-done.9, s32[64]{0:T(128)S(1)} %copy-done.10, s32[64]{0:T(128)S(1)} %copy-done.11, s32[64]{0:T(128)S(1)} %copy-done.12, ...), custom_call_target="tpu_custom_call" | custom-call | flops 268435456 | bytes 6291456 | tf_op jit(solution)/shard_map/rest_1_1/pallas_call | solution.py:343
  67.4 4.6 %collective-permute-done.8.refs_10_ = bf16[4,128,256]{2,1,0:T(8,128)(2,1)S(1)} collective-permute-done((bf16[4,128,256]{2,1,0:T(8,128)(2,1)S(1)}, bf16[4,128,256]{2,1,0:T(8,128)(2,1)S(1)}, u32[]{:S(2)}, u32[]{:S(2)}) %collective-permute-start.8) | collective-permute-done | bytes 262176 | tf_op jit(solution)/shard_map/ppermute | solution.py:404
  72.0 2.3 %collective-permute-done.9.refs_11_ = bf16[4,128,256]{2,1,0:T(8,128)(2,1)S(1)} collective-permute-done((bf16[4,128,256]{2,1,0:T(8,128)(2,1)S(1)}, bf16[4,128,256]{2,1,0:T(8,128)(2,1)S(1)}, u32[]{:S(2)}, u32[]{:S(2)}) %collective-permute-start.9) | collective-permute-done | bytes 262176 | tf_op jit(solution)/shard_map/ppermute | solution.py:404
  78.5 10.9 %collective-permute-done.12.refs_8_ = bf16[8,128,256]{2,1,0:T(8,128)(2,1)S(1)} collective-permute-done((bf16[8,128,256]{2,1,0:T(8,128)(2,1)S(1)}, bf16[8,128,256]{2,1,0:T(8,128)(2,1)S(1)}, u32[]{:S(2)}, u32[]{:S(2)}) %collective-permute-start.12) | collective-permute-done | bytes 524320 | tf_op jit(solution)/shard_map/ppermute | solution.py:393
  89.7 8.5 %collective-permute-done.13.refs_9_ = bf16[12,128,256]{2,1,0:T(8,128)(2,1)S(1)} collective-permute-done((bf16[12,128,256]{2,1,0:T(8,128)(2,1)S(1)}, bf16[12,128,256]{2,1,0:T(8,128)(2,1)S(1)}, u32[]{:S(2)}, u32[]{:S(2)}) %collective-permute-start.13) | collective-permute-done | bytes 786464 | tf_op jit(solution)/shard_map/ppermute | solution.py:404
  98.4 8.1 %operator_2.1 = (f32[8,256,256]{2,1,0:T(8,128)S(1)}, f32[8,256,256]{2,1,0:T(8,128)S(1)}) custom-call(s32[128]{0:T(128)S(1)} %copy-done.15, s32[32]{0:T(128)S(1)} %copy-done.16, s32[32]{0:T(128)S(1)} %copy-done.14, bf16[16,8,256,128]{3,2,1,0:T(8,128)(2,1)S(1)} %bitcast.11, bf16[32,256,128]{2,1,0:T(8,128)(2,1)S(1)} %bitcast.20, ...), custom_call_target="tpu_custom_call" | custom-call | flops 2684354560 | bytes 10485760 | tf_op jit(solution)/shard_map/operator_2/pallas_call | solution.py:197
  108.2 2.4 %rest_2_0.1 = (f32[1024,256]{1,0:T(8,128)S(1)}, bf16[8,128,256]{2,1,0:T(8,128)(2,1)S(1)}, bf16[4,128,256]{2,1,0:T(8,128)(2,1)S(1)}, f32[8,256]{1,0:T(8,128)S(1)}) custom-call(s32[128]{0:T(128)S(1)} %copy-done.7, s32[128]{0:T(128)S(1)} %copy-done.8, s32[128]{0:T(128)S(1)} %copy-done.9, s32[64]{0:T(128)S(1)} %copy-done.10, s32[64]{0:T(128)S(1)} %copy-done.11, ...), custom_call_target="tpu_custom_call" | custom-call | flops 268435456 | bytes 6291456 | tf_op jit(solution)/shard_map/rest_2_0/pallas_call | solution.py:343
  111.7 3.2 %collective-permute-start.18 = (bf16[4,128,256]{2,1,0:T(8,128)(2,1)S(1)}, bf16[4,128,256]{2,1,0:T(8,128)(2,1)S(1)}, u32[]{:S(2)}, u32[]{:S(2)}) collective-permute-start(bf16[4,128,256]{2,1,0:T(8,128)(2,1)S(1)} %get-tuple-element.123), channel_id=1, source_target_pairs={{0,24},{4,12},{8,0},{12,20},{16,8},{20,28},{24,16},{28,4},{1,25},{... | collective-permute-start | bytes 786440 | tf_op jit(solution)/shard_map/ppermute | solution.py:404
  114.9 2.7 %rest_2_1.1 = (f32[2048,256]{1,0:T(8,128)S(1)}, bf16[8,128,256]{2,1,0:T(8,128)(2,1)S(1)}, f32[8,256]{1,0:T(8,128)S(1)}) custom-call(s32[128]{0:T(128)S(1)} %copy-done.7, s32[128]{0:T(128)S(1)} %copy-done.8, s32[128]{0:T(128)S(1)} %copy-done.9, s32[64]{0:T(128)S(1)} %copy-done.10, s32[64]{0:T(128)S(1)} %copy-done.11, s32[64]{0:T(128)S(1)} %copy-done.12, ...), custom_call_target="tpu_custom_call" | custom-call | flops 268435456 | bytes 6291456 | tf_op jit(solution)/shard_map/rest_2_1/pallas_call | solution.py:343
  117.6 3.4 %collective-permute-done.17.refs_10_ = bf16[4,128,256]{2,1,0:T(8,128)(2,1)S(1)} collective-permute-done((bf16[4,128,256]{2,1,0:T(8,128)(2,1)S(1)}, bf16[4,128,256]{2,1,0:T(8,128)(2,1)S(1)}, u32[]{:S(2)}, u32[]{:S(2)}) %collective-permute-start.17) | collective-permute-done | bytes 262176 | tf_op jit(solution)/shard_map/ppermute | solution.py:404
  124.9 12.8 %collective-permute-done.20.refs_8_ = bf16[8,128,256]{2,1,0:T(8,128)(2,1)S(1)} collective-permute-done((bf16[8,128,256]{2,1,0:T(8,128)(2,1)S(1)}, bf16[8,128,256]{2,1,0:T(8,128)(2,1)S(1)}, u32[]{:S(2)}, u32[]{:S(2)}) %collective-permute-start.20) | collective-permute-done | bytes 524320 | tf_op jit(solution)/shard_map/ppermute | solution.py:393
  139.6 5.4 %collective-permute-done.21.refs_9_ = bf16[12,128,256]{2,1,0:T(8,128)(2,1)S(1)} collective-permute-done((bf16[12,128,256]{2,1,0:T(8,128)(2,1)S(1)}, bf16[12,128,256]{2,1,0:T(8,128)(2,1)S(1)}, u32[]{:S(2)}, u32[]{:S(2)}) %collective-permute-start.21) | collective-permute-done | bytes 786464 | tf_op jit(solution)/shard_map/ppermute | solution.py:404
  145.1 8.1 %operator_3.1 = (f32[8,256,256]{2,1,0:T(8,128)S(1)}, f32[8,256,256]{2,1,0:T(8,128)S(1)}) custom-call(s32[128]{0:T(128)S(1)} %copy-done.15, s32[32]{0:T(128)S(1)} %copy-done.16, s32[32]{0:T(128)S(1)} %copy-done.14, bf16[16,8,256,128]{3,2,1,0:T(8,128)(2,1)S(1)} %bitcast.14, bf16[32,256,128]{2,1,0:T(8,128)(2,1)S(1)} %bitcast.23, ...), custom_call_target="tpu_custom_call" | custom-call | flops 2684354560 | bytes 10485760 | tf_op jit(solution)/shard_map/operator_3/pallas_call | solution.py:197
  153.2 2.6 %collective-permute-done.22.refs_10_ = bf16[8,128,256]{2,1,0:T(8,128)(2,1)S(1)} collective-permute-done((bf16[8,128,256]{2,1,0:T(8,128)(2,1)S(1)}, bf16[8,128,256]{2,1,0:T(8,128)(2,1)S(1)}, u32[]{:S(2)}, u32[]{:S(2)}) %collective-permute-start.22) | collective-permute-done | bytes 524320 | tf_op jit(solution)/shard_map/ppermute | solution.py:404
  155.8 2.5 %collective-permute-done.23.refs_11_ = bf16[8,128,256]{2,1,0:T(8,128)(2,1)S(1)} collective-permute-done((bf16[8,128,256]{2,1,0:T(8,128)(2,1)S(1)}, bf16[8,128,256]{2,1,0:T(8,128)(2,1)S(1)}, u32[]{:S(2)}, u32[]{:S(2)}) %collective-permute-start.23) | collective-permute-done | bytes 524320 | tf_op jit(solution)/shard_map/ppermute | solution.py:393
  158.2 2.6 %rest_3_0.1.refs_14_ = f32[8,256]{1,0:T(8,128)S(1)} custom-call(s32[128]{0:T(128)S(1)} %copy-done.7, s32[128]{0:T(128)S(1)} %copy-done.8, s32[128]{0:T(128)S(1)} %copy-done.9, s32[64]{0:T(128)S(1)} %copy-done.10, s32[64]{0:T(128)S(1)} %copy-done.11, s32[64]{0:T(128)S(1)} %copy-done.12, s32[4]{0:T(128)S(1)} %copy-done.13, ...), custom_call_target="tpu_custom_call" | custom-call | flops 268435456 | bytes 6291456 | tf_op jit(solution)/shard_map/rest_3_0/pallas_call | solution.py:343
  160.8 2.9 %rest_3_1.1 = f32[8,256]{1,0:T(8,128)S(1)} custom-call(s32[128]{0:T(128)S(1)} %copy-done.7, s32[128]{0:T(128)S(1)} %copy-done.8, s32[128]{0:T(128)S(1)} %copy-done.9, s32[64]{0:T(128)S(1)} %copy-done.10, s32[64]{0:T(128)S(1)} %copy-done.11, s32[64]{0:T(128)S(1)} %copy-done.12, s32[4]{0:T(128)S(1)} %copy-done.13, bf16[16,8,256,128]{3,2,1,0:T(8,128)(2,1)S(1)} %bitcast.16, ...), custom_call_target="tpu_custom_call" | custom-call | flops 268435456 | bytes 6291456 | tf_op jit(solution)/shard_map/rest_3_1/pallas_call | solution.py:343
  164.1 3.5 %collective-permute-done.24 = f32[24,256]{1,0:T(8,128)S(1)} collective-permute-done((f32[24,256]{1,0:T(8,128)S(1)}, f32[24,256]{1,0:T(8,128)S(1)}, u32[]{:S(2)}, u32[]{:S(2)}) %collective-permute-start.24) | collective-permute-done | bytes 24608 | tf_op jit(solution)/shard_map/ppermute | solution.py:393
  169.5 2.2 %collective-permute-start.30 = (f32[24,256]{1,0:T(8,128)S(1)}, f32[24,256]{1,0:T(8,128)S(1)}, u32[]{:S(2)}, u32[]{:S(2)}) collective-permute-start(f32[24,256]{1,0:T(8,128)S(1)} %fusion.refs_0_), channel_id=1, source_target_pairs={{0,24},{4,28},{8,0},{12,4},{16,8},{20,12},{24,16},{28,20},{1,25},{... | collective-permute-start | bytes 73736 | tf_op jit(solution)/shard_map/ppermute | solution.py:398
  171.7 1.9 %collective-permute-done.28.refs_1_ = f32[24,256]{1,0:T(8,128)S(1)} collective-permute-done((f32[24,256]{1,0:T(8,128)S(1)}, f32[24,256]{1,0:T(8,128)S(1)}, u32[]{:S(2)}, u32[]{:S(2)}) %collective-permute-start.28) | collective-permute-done | bytes 24608 | tf_op jit(solution)/shard_map/ppermute | solution.py:398
  176.6 2.0 %scattered.1 = f32[2,2048,128]{2,1,0:T(8,128)} custom-call(f32[8,128]{1,0:T(8,128)S(1)} %get-tuple-element.135.coefs, f32[2,2048,128]{2,1,0:T(8,128)S(1)} %bitcast.29, f32[2048,256]{1,0:T(8,128)S(1)} %get-tuple-element.125.refs_12_.first.refs_4_, f32[2048,256]{1,0:T(8,128)S(1)} %get-tuple-element.132.refs_13_.second.refs_8_), custom_call_target="tpu_custom_call" | custom-call | bytes 8392704 | tf_op jit(solution)/shard_map/scattered/pallas_call | solution.py:667
  179.1 2.9 %trace.1 = f32[2048,128]{1,0:T(8,128)} custom-call(s32[4]{0:T(128)S(1)} %iota_xor_fusion.place, f32[2048,128]{1,0:T(8,128)S(1)} %get-tuple-element.136.here, f32[2048,128]{1,0:T(8,128)S(1)} %collective-permute-done.11.away, f32[8,128]{1,0:T(8,128)S(1)} %get-tuple-element.138.refs_0_, f32[8,128]{1,0:T(8,128)S(1)} %collective-permute-done.31.refs_1_, ...), custom_call_target="tpu_custom_call" | custom-call | bytes 19939328 | tf_op jit(solution)/shard_map/trace/pallas_call | solution.py:667
  (109 shorter events, 34.4 us)
Async XLA Ops:
  3.9 17.9 %collective-permute-start = (bf16[8,128,256]{2,1,0:T(8,128)(2,1)S(1)}, bf16[8,128,256]{2,1,0:T(8,128)(2,1)S(1)}, u32[]{:S(2)}, u32[]{:S(2)}) collective-permute-start(bf16[8,128,256]{2,1,0:T(8,128)(2,1)S(1)} %get-tuple-element.73.refs_5_), channel_id=1, source_target_pairs={{0,4},{4,0},{8,12},{12,8},{16,20},{20,16},{24,28},{28,24},{1,5},{5... | collective-permute-start | bytes 1572872 | tf_op jit(solution)/shard_map/ppermute | solution.py:393
  6.9 11.3 %collective-permute-start.1 = (bf16[4,128,256]{2,1,0:T(8,128)(2,1)}, bf16[4,128,256]{2,1,0:T(8,128)(2,1)S(1)}, u32[]{:S(2)}, u32[]{:S(2)}) collective-permute-start(bf16[4,128,256]{2,1,0:T(8,128)(2,1)} %get-tuple-element.74), channel_id=1, source_target_pairs={{0,8},{4,28},{8,16},{12,4},{16,24},{20,12},{24,0},{28,20},{1,9},{5... | collective-permute-start | bytes 786440 | tf_op jit(solution)/shard_map/ppermute | solution.py:404
  8.4 13.4 %collective-permute-start.2 = (bf16[4,128,256]{2,1,0:T(8,128)(2,1)}, bf16[4,128,256]{2,1,0:T(8,128)(2,1)}, u32[]{:S(2)}, u32[]{:S(2)}) collective-permute-start(bf16[4,128,256]{2,1,0:T(8,128)(2,1)} %get-tuple-element.74), channel_id=1, source_target_pairs={{0,24},{4,12},{8,0},{12,20},{16,8},{20,28},{24,16},{28,4},{1,25},{... | collective-permute-start | bytes 786440 | tf_op jit(solution)/shard_map/ppermute | solution.py:404
  22.7 22.5 %collective-permute-start.10 = (f32[2048,128]{1,0:T(8,128)S(1)}, f32[2048,128]{1,0:T(8,128)S(1)}, u32[]{:S(2)}, u32[]{:S(2)}) collective-permute-start(f32[2048,128]{1,0:T(8,128)S(1)} %get-tuple-element.110), channel_id=1, source_target_pairs={{0,1},{1,0},{2,3},{3,2},{4,5},{5,4},{6,7},{7,6},{8,9},{9,8},{10,11... | collective-permute-start | bytes 3145736 | tf_op jit(solution)/shard_map/ppermute | solution.py:393
  22.9 22.2 %collective-permute-start.4 = (bf16[12,128,256]{2,1,0:T(8,128)(2,1)S(1)}, bf16[12,128,256]{2,1,0:T(8,128)(2,1)S(1)}, u32[]{:S(2)}, u32[]{:S(2)}) collective-permute-start(bf16[12,128,256]{2,1,0:T(8,128)(2,1)S(1)} %pad_maximum_fusion), channel_id=1, source_target_pairs={{0,8},{4,28},{8,16},{12,4},{16,24},{20,12},{24,0},{28,20},{1,9},{5... | collective-permute-start | bytes 2359304 | tf_op jit(solution)/shard_map/ppermute | solution.py:404
  24.1 14.2 %collective-permute-start.3 = (bf16[8,128,256]{2,1,0:T(8,128)(2,1)S(1)}, bf16[8,128,256]{2,1,0:T(8,128)(2,1)S(1)}, u32[]{:S(2)}, u32[]{:S(2)}) collective-permute-start(bf16[8,128,256]{2,1,0:T(8,128)(2,1)S(1)} %copy-done.6), channel_id=1, source_target_pairs={{0,4},{4,0},{8,12},{12,8},{16,20},{20,16},{24,28},{28,24},{1,5},{5... | collective-permute-start | bytes 1572872 | tf_op jit(solution)/shard_map/ppermute | solution.py:393
  38.2 17.7 %collective-permute-start.5 = (bf16[8,128,256]{2,1,0:T(8,128)(2,1)S(1)}, bf16[8,128,256]{2,1,0:T(8,128)(2,1)S(1)}, u32[]{:S(2)}, u32[]{:S(2)}) collective-permute-start(bf16[8,128,256]{2,1,0:T(8,128)(2,1)S(1)} %collective-permute-done.3.refs_8_), channel_id=1, source_target_pairs={{0,8},{4,28},{8,16},{12,4},{16,24},{20,12},{24,0},{28,20},{1,9},{5... | collective-permute-start | bytes 1572872 | tf_op jit(solution)/shard_map/ppermute | solution.py:404
  45.2 13.2 %collective-permute-start.6 = (bf16[8,128,256]{2,1,0:T(8,128)(2,1)S(1)}, bf16[8,128,256]{2,1,0:T(8,128)(2,1)S(1)}, u32[]{:S(2)}, u32[]{:S(2)}) collective-permute-start(bf16[8,128,256]{2,1,0:T(8,128)(2,1)S(1)} %pad_maximum_fusion.3), channel_id=1, source_target_pairs={{0,4},{4,0},{8,12},{12,8},{16,20},{20,16},{24,28},{28,24},{1,5},{5... | collective-permute-start | bytes 1572872 | tf_op jit(solution)/shard_map/ppermute | solution.py:393
  46.0 28.3 %collective-permute-start.11 = (f32[2048,128]{1,0:T(8,128)S(1)}, f32[2048,128]{1,0:T(8,128)S(1)}, u32[]{:S(2)}, u32[]{:S(2)}) collective-permute-start(f32[2048,128]{1,0:T(8,128)S(1)} %get-tuple-element.111), channel_id=1, source_target_pairs={{0,2},{1,3},{2,0},{3,1},{4,6},{5,7},{6,4},{7,5},{8,10},{9,11},{10,... | collective-permute-start | bytes 3145736 | tf_op jit(solution)/shard_map/ppermute | solution.py:393
  60.6 13.7 %collective-permute-start.7 = (bf16[8,128,256]{2,1,0:T(8,128)(2,1)S(1)}, bf16[8,128,256]{2,1,0:T(8,128)(2,1)S(1)}, u32[]{:S(2)}, u32[]{:S(2)}) collective-permute-start(bf16[8,128,256]{2,1,0:T(8,128)(2,1)S(1)} %get-tuple-element.105.refs_5_), channel_id=1, source_target_pairs={{0,4},{4,0},{8,12},{12,8},{16,20},{20,16},{24,28},{28,24},{1,5},{5... | collective-permute-start | bytes 1572872 | tf_op jit(solution)/shard_map/ppermute | solution.py:393
  61.0 11.0 %collective-permute-start.8 = (bf16[4,128,256]{2,1,0:T(8,128)(2,1)S(1)}, bf16[4,128,256]{2,1,0:T(8,128)(2,1)S(1)}, u32[]{:S(2)}, u32[]{:S(2)}) collective-permute-start(bf16[4,128,256]{2,1,0:T(8,128)(2,1)S(1)} %get-tuple-element.107), channel_id=1, source_target_pairs={{0,8},{4,28},{8,16},{12,4},{16,24},{20,12},{24,0},{28,20},{1,9},{5... | collective-permute-start | bytes 786440 | tf_op jit(solution)/shard_map/ppermute | solution.py:404
  62.7 11.6 %collective-permute-start.9 = (bf16[4,128,256]{2,1,0:T(8,128)(2,1)S(1)}, bf16[4,128,256]{2,1,0:T(8,128)(2,1)S(1)}, u32[]{:S(2)}, u32[]{:S(2)}) collective-permute-start(bf16[4,128,256]{2,1,0:T(8,128)(2,1)S(1)} %get-tuple-element.107), channel_id=1, source_target_pairs={{0,24},{4,12},{8,0},{12,20},{16,8},{20,28},{24,16},{28,4},{1,25},{... | collective-permute-start | bytes 786440 | tf_op jit(solution)/shard_map/ppermute | solution.py:404
  74.3 47.6 %collective-permute-start.19 = (f32[2048,256]{1,0:T(8,128)S(1)}, f32[2048,256]{1,0:T(8,128)S(1)}, u32[]{:S(2)}, u32[]{:S(2)}) collective-permute-start(f32[2048,256]{1,0:T(8,128)S(1)} %get-tuple-element.125.refs_12_.first.refs_4_), channel_id=1, source_target_pairs={{0,2},{1,3},{2,0},{3,1},{4,6},{5,7},{6,4},{7,5},{8,10},{9,11},{10,... | collective-permute-start | bytes 6291464 | tf_op jit(solution)/shard_map/ppermute | solution.py:393
  75.9 22.3 %collective-permute-start.13 = (bf16[12,128,256]{2,1,0:T(8,128)(2,1)S(1)}, bf16[12,128,256]{2,1,0:T(8,128)(2,1)S(1)}, u32[]{:S(2)}, u32[]{:S(2)}) collective-permute-start(bf16[12,128,256]{2,1,0:T(8,128)(2,1)S(1)} %pad_maximum_fusion.1), channel_id=1, source_target_pairs={{0,8},{4,28},{8,16},{12,4},{16,24},{20,12},{24,0},{28,20},{1,9},{5... | collective-permute-start | bytes 2359304 | tf_op jit(solution)/shard_map/ppermute | solution.py:404
  76.7 12.7 %collective-permute-start.12 = (bf16[8,128,256]{2,1,0:T(8,128)(2,1)S(1)}, bf16[8,128,256]{2,1,0:T(8,128)(2,1)S(1)}, u32[]{:S(2)}, u32[]{:S(2)}) collective-permute-start(bf16[8,128,256]{2,1,0:T(8,128)(2,1)S(1)} %get-tuple-element.113.refs_6_), channel_id=1, source_target_pairs={{0,4},{4,0},{8,12},{12,8},{16,20},{20,16},{24,28},{28,24},{1,5},{5... | collective-permute-start | bytes 1572872 | tf_op jit(solution)/shard_map/ppermute | solution.py:393
  89.4 18.1 %collective-permute-start.14 = (bf16[8,128,256]{2,1,0:T(8,128)(2,1)S(1)}, bf16[8,128,256]{2,1,0:T(8,128)(2,1)S(1)}, u32[]{:S(2)}, u32[]{:S(2)}) collective-permute-start(bf16[8,128,256]{2,1,0:T(8,128)(2,1)S(1)} %collective-permute-done.12.refs_8_), channel_id=1, source_target_pairs={{0,8},{4,28},{8,16},{12,4},{16,24},{20,12},{24,0},{28,20},{1,9},{5... | collective-permute-start | bytes 1572872 | tf_op jit(solution)/shard_map/ppermute | solution.py:404
  98.3 9.9 %collective-permute-start.15 = (bf16[8,128,256]{2,1,0:T(8,128)(2,1)S(1)}, bf16[8,128,256]{2,1,0:T(8,128)(2,1)S(1)}, u32[]{:S(2)}, u32[]{:S(2)}) collective-permute-start(bf16[8,128,256]{2,1,0:T(8,128)(2,1)S(1)} %pad_maximum_fusion.4), channel_id=1, source_target_pairs={{0,4},{4,0},{8,12},{12,8},{16,20},{20,16},{24,28},{28,24},{1,5},{5... | collective-permute-start | bytes 1572872 | tf_op jit(solution)/shard_map/ppermute | solution.py:393
  110.6 11.3 %collective-permute-start.16 = (bf16[8,128,256]{2,1,0:T(8,128)(2,1)S(1)}, bf16[8,128,256]{2,1,0:T(8,128)(2,1)S(1)}, u32[]{:S(2)}, u32[]{:S(2)}) collective-permute-start(bf16[8,128,256]{2,1,0:T(8,128)(2,1)S(1)} %get-tuple-element.121.refs_5_), channel_id=1, source_target_pairs={{0,4},{4,0},{8,12},{12,8},{16,20},{20,16},{24,28},{28,24},{1,5},{5... | collective-permute-start | bytes 1572872 | tf_op jit(solution)/shard_map/ppermute | solution.py:393
  111.0 10.0 %collective-permute-start.17 = (bf16[4,128,256]{2,1,0:T(8,128)(2,1)S(1)}, bf16[4,128,256]{2,1,0:T(8,128)(2,1)S(1)}, u32[]{:S(2)}, u32[]{:S(2)}) collective-permute-start(bf16[4,128,256]{2,1,0:T(8,128)(2,1)S(1)} %get-tuple-element.123), channel_id=1, source_target_pairs={{0,8},{4,28},{8,16},{12,4},{16,24},{20,12},{24,0},{28,20},{1,9},{5... | collective-permute-start | bytes 786440 | tf_op jit(solution)/shard_map/ppermute | solution.py:404
  111.7 10.2 %collective-permute-start.18 = (bf16[4,128,256]{2,1,0:T(8,128)(2,1)S(1)}, bf16[4,128,256]{2,1,0:T(8,128)(2,1)S(1)}, u32[]{:S(2)}, u32[]{:S(2)}) collective-permute-start(bf16[4,128,256]{2,1,0:T(8,128)(2,1)S(1)} %get-tuple-element.123), channel_id=1, source_target_pairs={{0,24},{4,12},{8,0},{12,20},{16,8},{20,28},{24,16},{28,4},{1,25},{... | collective-permute-start | bytes 786440 | tf_op jit(solution)/shard_map/ppermute | solution.py:404
  117.5 50.1 %collective-permute-start.26 = (f32[2048,256]{1,0:T(8,128)S(1)}, f32[2048,256]{1,0:T(8,128)S(1)}, u32[]{:S(2)}, u32[]{:S(2)}) collective-permute-start(f32[2048,256]{1,0:T(8,128)S(1)} %get-tuple-element.132.refs_13_.second.refs_8_), channel_id=1, source_target_pairs={{0,1},{1,0},{2,3},{3,2},{4,5},{5,4},{6,7},{7,6},{8,9},{9,8},{10,11... | collective-permute-start | bytes 6291464 | tf_op jit(solution)/shard_map/ppermute | solution.py:393
  121.9 45.8 %collective-permute-start.25 = (f32[2048,256]{1,0:T(8,128)S(1)}, f32[2048,256]{1,0:T(8,128)S(1)}, u32[]{:S(2)}, u32[]{:S(2)}) collective-permute-start(f32[2048,256]{1,0:T(8,128)S(1)} %get-tuple-element.132.refs_13_.second.refs_8_), channel_id=1, source_target_pairs={{0,2},{1,3},{2,0},{3,1},{4,6},{5,7},{6,4},{7,5},{8,10},{9,11},{10,... | collective-permute-start | bytes 6291464 | tf_op jit(solution)/shard_map/ppermute | solution.py:393
  122.6 45.0 %collective-permute-start.27 = (f32[2048,256]{1,0:T(8,128)S(1)}, f32[2048,256]{1,0:T(8,128)S(1)}, u32[]{:S(2)}, u32[]{:S(2)}) collective-permute-start(f32[2048,256]{1,0:T(8,128)S(1)} %collective-permute-done.19.refs_6_), channel_id=1, source_target_pairs={{0,1},{1,0},{2,3},{3,2},{4,5},{5,4},{6,7},{7,6},{8,9},{9,8},{10,11... | collective-permute-start | bytes 6291464 | tf_op jit(solution)/shard_map/ppermute | solution.py:393
  122.7 22.2 %collective-permute-start.21 = (bf16[12,128,256]{2,1,0:T(8,128)(2,1)S(1)}, bf16[12,128,256]{2,1,0:T(8,128)(2,1)S(1)}, u32[]{:S(2)}, u32[]{:S(2)}) collective-permute-start(bf16[12,128,256]{2,1,0:T(8,128)(2,1)S(1)} %pad_maximum_fusion.2), channel_id=1, source_target_pairs={{0,8},{4,28},{8,16},{12,4},{16,24},{20,12},{24,0},{28,20},{1,9},{5... | collective-permute-start | bytes 2359304 | tf_op jit(solution)/shard_map/ppermute | solution.py:404
  123.6 14.1 %collective-permute-start.20 = (bf16[8,128,256]{2,1,0:T(8,128)(2,1)S(1)}, bf16[8,128,256]{2,1,0:T(8,128)(2,1)S(1)}, u32[]{:S(2)}, u32[]{:S(2)}) collective-permute-start(bf16[8,128,256]{2,1,0:T(8,128)(2,1)S(1)} %get-tuple-element.127.refs_6_), channel_id=1, source_target_pairs={{0,4},{4,0},{8,12},{12,8},{16,20},{20,16},{24,28},{28,24},{1,5},{5... | collective-permute-start | bytes 1572872 | tf_op jit(solution)/shard_map/ppermute | solution.py:393
  137.7 18.1 %collective-permute-start.22 = (bf16[8,128,256]{2,1,0:T(8,128)(2,1)S(1)}, bf16[8,128,256]{2,1,0:T(8,128)(2,1)S(1)}, u32[]{:S(2)}, u32[]{:S(2)}) collective-permute-start(bf16[8,128,256]{2,1,0:T(8,128)(2,1)S(1)} %collective-permute-done.20.refs_8_), channel_id=1, source_target_pairs={{0,8},{4,28},{8,16},{12,4},{16,24},{20,12},{24,0},{28,20},{1,9},{5... | collective-permute-start | bytes 1572872 | tf_op jit(solution)/shard_map/ppermute | solution.py:404
  145.0 13.2 %collective-permute-start.23 = (bf16[8,128,256]{2,1,0:T(8,128)(2,1)S(1)}, bf16[8,128,256]{2,1,0:T(8,128)(2,1)S(1)}, u32[]{:S(2)}, u32[]{:S(2)}) collective-permute-start(bf16[8,128,256]{2,1,0:T(8,128)(2,1)S(1)} %pad_maximum_fusion.5), channel_id=1, source_target_pairs={{0,4},{4,0},{8,12},{12,8},{16,20},{20,16},{24,28},{28,24},{1,5},{5... | collective-permute-start | bytes 1572872 | tf_op jit(solution)/shard_map/ppermute | solution.py:393
  164.1 14.5 %collective-permute-start.34 = (f32[2048,256]{1,0:T(8,128)S(1)}, f32[2048,256]{1,0:T(8,128)S(1)}, u32[]{:S(2)}, u32[]{:S(2)}) collective-permute-start(f32[2048,256]{1,0:T(8,128)S(1)} %get-tuple-element.125.refs_12_.first.refs_4_), channel_id=1, source_target_pairs={{0,1},{1,0},{2,3},{3,2},{4,5},{5,4},{6,7},{7,6},{8,9},{9,8},{10,11... | collective-permute-start | bytes 6291464 | tf_op jit(solution)/shard_map/ppermute | solution.py:393
  167.7 11.4 %collective-permute-start.35 = (f32[2048,256]{1,0:T(8,128)S(1)}, f32[2048,256]{1,0:T(8,128)S(1)}, u32[]{:S(2)}, u32[]{:S(2)}) collective-permute-start(f32[2048,256]{1,0:T(8,128)S(1)} %collective-permute-done.25.refs_10_), channel_id=1, source_target_pairs={{0,1},{1,0},{2,3},{3,2},{4,5},{5,4},{6,7},{7,6},{8,9},{9,8},{10,11... | collective-permute-start | bytes 6291464 | tf_op jit(solution)/shard_map/ppermute | solution.py:393
  167.8 5.9 %collective-permute-start.28 = (f32[24,256]{1,0:T(8,128)S(1)}, f32[24,256]{1,0:T(8,128)S(1)}, u32[]{:S(2)}, u32[]{:S(2)}) collective-permute-start(f32[24,256]{1,0:T(8,128)S(1)} %fusion.refs_0_), channel_id=1, source_target_pairs={{0,8},{4,12},{8,16},{12,20},{16,24},{20,28},{24,0},{28,4},{1,9},{5... | collective-permute-start | bytes 73736 | tf_op jit(solution)/shard_map/ppermute | solution.py:398
  168.0 5.6 %collective-permute-start.29 = (f32[24,256]{1,0:T(8,128)S(1)}, f32[24,256]{1,0:T(8,128)S(1)}, u32[]{:S(2)}, u32[]{:S(2)}) collective-permute-start(f32[24,256]{1,0:T(8,128)S(1)} %fusion.refs_0_), channel_id=1, source_target_pairs={{0,16},{4,20},{8,24},{12,28},{16,0},{20,4},{24,8},{28,12},{1,17},{... | collective-permute-start | bytes 73736 | tf_op jit(solution)/shard_map/ppermute | solution.py:398
  169.5 4.5 %collective-permute-start.30 = (f32[24,256]{1,0:T(8,128)S(1)}, f32[24,256]{1,0:T(8,128)S(1)}, u32[]{:S(2)}, u32[]{:S(2)}) collective-permute-start(f32[24,256]{1,0:T(8,128)S(1)} %fusion.refs_0_), channel_id=1, source_target_pairs={{0,24},{4,28},{8,0},{12,4},{16,8},{20,12},{24,16},{28,20},{1,25},{... | collective-permute-start | bytes 73736 | tf_op jit(solution)/shard_map/ppermute | solution.py:398
  (23 other events, 265.9 us)

commit v4 on v3

--- a/solution.py
+++ b/solution.py
@@ -137,8 +137,11 @@
     nblocks, span, edges, front_moves, source_moves, nparts = (*sizes, *moves)
     near_idx, crack_idx, crack_tgt, near_v, crack_v = refs[:5]
     parts = refs[5 : 5 + nparts]
-    acc_a, acc_b, front_v, source_v, front_sem, source_sem = refs[5 + nparts :]
-    cut = acc_a.shape[0]
+    *accs, front_v, source_v, front_sem, source_sem = refs[5 + nparts :]
+    cut = nblocks // 2
+    if len(accs) == 1:
+        accs = [accs[0].at[pl.ds(0, cut)], accs[0].at[pl.ds(cut, nblocks - cut)]]
+    acc_a, acc_b = accs
     front_copies = block_copies(parts, front_moves, front_v, front_sem)
     source_copies = block_copies(parts, source_moves, source_v, source_sem)
     for copy in source_copies + front_copies:
@@ -194,16 +197,17 @@
     anywhere = pl.BlockSpec(memory_space=pl.ANY)
     whole = pl.BlockSpec(memory_space=pltpu.VMEM)
     blocks = total_of(front_moves) + total_of(source_moves) + 2
+    counts = (nblocks,) if step == 3 else (cut, nblocks - cut)
     return pl.pallas_call(
         functools.partial(
             main_kernel, (nblocks, span, edges), (front_moves, source_moves, len(parts))
         ),
         out_shape=tuple(
             jax.ShapeDtypeStruct((rows, 2 * width, lanes), jnp.float32)
-            for rows in (cut, nblocks - cut)
+            for rows in counts
         ),
         in_specs=[smem] * 3 + [whole] * 2 + [anywhere] * len(parts),
-        out_specs=(whole, whole),
+        out_specs=tuple(whole for _ in counts),
         scratch_shapes=[
             pltpu.VMEM((total_of(front_moves) + 1, width, lanes), jnp.bfloat16),
             pltpu.VMEM((total_of(source_moves) + 1, width, lanes), jnp.bfloat16),
@@ -232,7 +236,7 @@
     extras, rest = rest[:nextra], rest[nextra:]
     before = ()
     if part == 1:
-        nbefore = 1 if step == 3 else 2
+        nbefore = 2
         before, rest = rest[:nbefore], rest[nbefore:]
     nouts = 1 if step == 3 else (4, 3)[part]
     outs, rest = rest[:nouts], rest[nouts:]
@@ -251,8 +255,9 @@
         for copy in copies:
             copy.wait()
 
-        def add(rows, mats, srcs, number, matrix, source):
-            offset = part * (rows.shape[0] // 2)
+        def add(half, rows, mats, srcs, number, matrix, source):
+            offset = half * (rows.shape[0] // 2)
+            shift_by = half * (nblocks // 2) if step == 3 else 0
 
             def some(i, carry):
                 spots = [offset + i * GROUP + k for k in range(GROUP)]
@@ -263,18 +268,20 @@
                     for spot in spots
                 ]
                 for spot, product in zip(spots, products):
-                    extra[rows[spot]] += product
+                    extra[rows[spot] + shift_by] += product
                 return carry
 
             lax.fori_loop(0, (number + GROUP - 1) // GROUP, some, 0)
 
-        add(
-            *lists[:3],
-            numbers[part],
-            lambda i: near_v[i // span, lax.rem(i, span)],
-            near_src,
-        )
-        add(*lists[3:6], numbers[2 + part], lambda i: crack_v[i], edge_src)
+        for half in (0, 1) if step == 3 else (part,):
+            add(
+                half,
+                *lists[:3],
+                numbers[half],
+                lambda i: near_v[i // span, lax.rem(i, span)],
+                near_src,
+            )
+            add(half, *lists[3:6], numbers[2 + half], lambda i: crack_v[i], edge_src)
 
     nsums = (1, 3, 5)[step - 1]
     zero = jnp.zeros((8, lanes), jnp.float32)
@@ -429,8 +436,8 @@
     beside_a = swap(low_a, "clu", 1)
     same = ring(head, 2)
     other = ring(head, -2)
-    tail, beside_a, same, other, *early_ties = tie(low_b, beside_a, same, other, *early_ties)
-    onward = jnp.concatenate([beside_a, same], axis=0)
+    tail, beside_a, same, other = tie(low_b, beside_a, same, other)
+    onward, *early_ties = tie(jnp.concatenate([beside_a, same], axis=0), *early_ties)
     beyond_a = ring(onward, 2)
     beside_b = swap(tail, "clu", 1)
     if callable(late_ties):
@@ -732,15 +739,13 @@
     )
     away = swap(away, "frq", 2)
 
-    def operate(step, found, extras, *tied):
-        acc_a, acc_b = main_call(step, tables, near, crack, found)
-        both_halves = (front, tables, near, crack, found)
+    def operate(step, found, extras):
+        accs = main_call(step, tables, near, crack, found)
+        common = (front, tables, near, crack, found)
         if step == 3:
-            (sums,) = rest_call(3, 0, *both_halves, acc_a, extras)
-            (sums,) = rest_call(3, 1, *both_halves, acc_b, extras, (sums,))
-            return sums, *tied
-        upper, low_a, head, sums = rest_call(step, 0, *both_halves, acc_a, extras)
-        vector, low_b, sums = rest_call(step, 1, *both_halves, acc_b, extras, (upper, sums))
+            return rest_call(3, 0, *common, accs[0], extras)
+        upper, low_a, head, sums = rest_call(step, 0, *common, accs[0], extras)
+        vector, low_b, sums = rest_call(step, 1, *common, accs[1], extras, (upper, sums))
         return vector, low_a, low_b, head, sums
 
     first, *lows, sums_one = operate(1, found, (base,))

time: 182 us -> 178 us (0.978)
  waiting for transfers between devices: 86.6 us -> 76 us
  starting transfers between devices: 36.2 us -> 43.5 us
    ppermute x12, waiting for transfers between devices: 39 us -> 28.4 us  [ring(): return lax.ppermute(value, 'clu', pairs)]
    ppermute x21, starting transfers between devices: 15.2 us -> 21.8 us  [swap(): return lax.ppermute(value, axis, [(i, i ^ distance) for i in range(count)])]
    pallas_call x6 -> x5, Pallas kernels: 15.4 us -> 15.5 us  [rest_call(): pl.pallas_call(functools.partial(rest_kernel, step, part, (nblocks, span,...]
  transfers between devices with their start and end apart: 36 -> 36, of which waited for: 22 -> 24; matrix products, arithmetic and copies ran while one was open for 1% -> 1% of each run, Pallas kernels for 27% -> 28%
where the time goes in v4:
time: 178 us; the launch traced here: 179 us
  waiting for transfers between devices  76 us (43%)
  Pallas kernels  54.5 us (31%)
  starting transfers between devices  43.5 us (24%)
  local copies, waits for them, and re-layouts  3.2 us (2%)
    ppermute x21, waiting for transfers between devices, swap(): return lax.ppermute(value, axis, [(i, i ^ distance) for i in range(count)])  44.9 us
    ppermute x12, waiting for transfers between devices, ring(): return lax.ppermute(value, 'clu', pairs)  28.4 us
    pallas_call x3, Pallas kernels, main_call(): pl.pallas_call(functools.partial(main_kernel, (nblocks, span, edges), (fr...  24.3 us
    ppermute x21, starting transfers between devices, swap(): return lax.ppermute(value, axis, [(i, i ^ distance) for i in range(count)])  21.8 us
    ppermute x12, starting transfers between devices, ring(): return lax.ppermute(value, 'clu', pairs)  17.6 us
    pallas_call x5, Pallas kernels, rest_call(): pl.pallas_call(functools.partial(rest_kernel, step, part, (nblocks, span,...  15.5 us
    pallas_call x7, Pallas kernels, on_vmem(): pl.pallas_call(body, out_shape=out_shape, in_specs=[smem] * len(smem_args...  8.22 us
    pallas_call x1, Pallas kernels, table_call(): pl.pallas_call(functools.partial(table_kernel, sizes), out_shape=tuple((j...  6.41 us
  transfers between devices with their start and end apart: 36, of which 24 were waited for; matrix products, arithmetic and copies ran while one was open for 1% of the time, Pallas kernels for 28%

profile of v4, /device:TPU:0, one launch (start us, length us, event | category | flops | bytes accessed | tf_op | source)
XLA Modules:
  0.0 178.6 jit_solution(2282722272527030099)
XLA Ops:
  3.9 2.9 %collective-permute-start = (bf16[8,128,256]{2,1,0:T(8,128)(2,1)S(1)}, bf16[8,128,256]{2,1,0:T(8,128)(2,1)S(1)}, u32[]{:S(2)}, u32[]{:S(2)}) collective-permute-start(bf16[8,128,256]{2,1,0:T(8,128)(2,1)S(1)} %get-tuple-element.74.refs_5_), channel_id=1, source_target_pairs={{0,4},{4,0},{8,12},{12,8},{16,20},{20,16},{24,28},{28,24},{1,5},{5... | collective-permute-start | bytes 1572872 | tf_op jit(solution)/shard_map/ppermute | solution.py:400
  8.4 2.2 %collective-permute-start.2 = (bf16[4,128,256]{2,1,0:T(8,128)(2,1)}, bf16[4,128,256]{2,1,0:T(8,128)(2,1)}, u32[]{:S(2)}, u32[]{:S(2)}) collective-permute-start(bf16[4,128,256]{2,1,0:T(8,128)(2,1)} %get-tuple-element.75), channel_id=1, source_target_pairs={{0,24},{4,12},{8,0},{12,20},{16,8},{20,28},{24,16},{28,4},{1,25},{... | collective-permute-start | bytes 786440 | tf_op jit(solution)/shard_map/ppermute | solution.py:411
  11.4 6.4 %tables.1 = (s32[128]{0:T(128)}, s32[32]{0:T(128)}, s32[128]{0:T(128)}, s32[128]{0:T(128)}, s32[128]{0:T(128)}, /*index=5*/s32[64]{0:T(128)}, s32[64]{0:T(128)}, s32[64]{0:T(128)}, s32[4]{0:T(128)}) custom-call(s32[1]{0:T(128)} %bitcast.1.place, s32[128]{0:T(128)} %reshape.17.pattern, s32[32]{0:T(128)} %bitcast.31, s32[32]{0:T(128)} %source.1, s32[32]{0:T(128)} %refs_2_.5), custom_call_target="tpu_custom_call" | custom-call | tf_op jit(solution)/shard_map/tables/pallas_call | solution.py:110
  18.2 3.7 %collective-permute-done.2.refs_11_ = bf16[4,128,256]{2,1,0:T(8,128)(2,1)} collective-permute-done((bf16[4,128,256]{2,1,0:T(8,128)(2,1)}, bf16[4,128,256]{2,1,0:T(8,128)(2,1)}, u32[]{:S(2)}, u32[]{:S(2)}) %collective-permute-start.2) | collective-permute-done | bytes 262176 | tf_op jit(solution)/shard_map/ppermute | solution.py:411
  24.1 1.9 %collective-permute-start.3 = (bf16[8,128,256]{2,1,0:T(8,128)(2,1)S(1)}, bf16[8,128,256]{2,1,0:T(8,128)(2,1)S(1)}, u32[]{:S(2)}, u32[]{:S(2)}) collective-permute-start(bf16[8,128,256]{2,1,0:T(8,128)(2,1)S(1)} %copy-done.6), channel_id=1, source_target_pairs={{0,4},{4,0},{8,12},{12,8},{16,20},{20,16},{24,28},{28,24},{1,5},{5... | collective-permute-start | bytes 1572872 | tf_op jit(solution)/shard_map/ppermute | solution.py:400
  26.3 12.2 %collective-permute-done.3.refs_8_ = bf16[8,128,256]{2,1,0:T(8,128)(2,1)S(1)} collective-permute-done((bf16[8,128,256]{2,1,0:T(8,128)(2,1)S(1)}, bf16[8,128,256]{2,1,0:T(8,128)(2,1)S(1)}, u32[]{:S(2)}, u32[]{:S(2)}) %collective-permute-start.3) | collective-permute-done | bytes 524320 | tf_op jit(solution)/shard_map/ppermute | solution.py:400
  39.0 3.6 %collective-permute-done.4.refs_9_ = bf16[12,128,256]{2,1,0:T(8,128)(2,1)S(1)} collective-permute-done((bf16[12,128,256]{2,1,0:T(8,128)(2,1)S(1)}, bf16[12,128,256]{2,1,0:T(8,128)(2,1)S(1)}, u32[]{:S(2)}, u32[]{:S(2)}) %collective-permute-start.4) | collective-permute-done | bytes 786464 | tf_op jit(solution)/shard_map/ppermute | solution.py:411
  45.2 8.1 %operator_1.1 = (f32[8,256,256]{2,1,0:T(8,128)S(1)}, f32[8,256,256]{2,1,0:T(8,128)S(1)}) custom-call(s32[128]{0:T(128)S(1)} %copy-done.15, s32[32]{0:T(128)S(1)} %copy-done.16, s32[32]{0:T(128)S(1)} %copy-done.14, bf16[16,8,256,128]{3,2,1,0:T(8,128)(2,1)S(1)} %bitcast.8, bf16[32,256,128]{2,1,0:T(8,128)(2,1)S(1)} %bitcast.16, ...), custom_call_target="tpu_custom_call" | custom-call | flops 2684354560 | bytes 10485760 | tf_op jit(solution)/shard_map/operator_1/pallas_call | solution.py:201
  55.1 2.5 %rest_1_0.1 = (f32[1024,256]{1,0:T(8,128)S(1)}, bf16[8,128,256]{2,1,0:T(8,128)(2,1)S(1)}, bf16[4,128,256]{2,1,0:T(8,128)(2,1)S(1)}, f32[8,256]{1,0:T(8,128)S(1)}) custom-call(s32[128]{0:T(128)S(1)} %copy-done.7, s32[128]{0:T(128)S(1)} %copy-done.8, s32[128]{0:T(128)S(1)} %copy-done.9, s32[64]{0:T(128)S(1)} %copy-done.10, s32[64]{0:T(128)S(1)} %copy-done.11, ...), custom_call_target="tpu_custom_call" | custom-call | flops 268435456 | bytes 6291456 | tf_op jit(solution)/shard_map/rest_1_0/pallas_call | solution.py:350
  58.9 2.9 %collective-permute-start.9 = (bf16[4,128,256]{2,1,0:T(8,128)(2,1)S(1)}, bf16[4,128,256]{2,1,0:T(8,128)(2,1)S(1)}, u32[]{:S(2)}, u32[]{:S(2)}) collective-permute-start(bf16[4,128,256]{2,1,0:T(8,128)(2,1)S(1)} %get-tuple-element.109), channel_id=1, source_target_pairs={{0,24},{4,12},{8,0},{12,20},{16,8},{20,28},{24,16},{28,4},{1,25},{... | collective-permute-start | bytes 786440 | tf_op jit(solution)/shard_map/ppermute | solution.py:411
  61.9 2.6 %rest_1_1.1 = (f32[2048,256]{1,0:T(8,128)S(1)}, bf16[8,128,256]{2,1,0:T(8,128)(2,1)S(1)}, f32[8,256]{1,0:T(8,128)S(1)}) custom-call(s32[128]{0:T(128)S(1)} %copy-done.7, s32[128]{0:T(128)S(1)} %copy-done.8, s32[128]{0:T(128)S(1)} %copy-done.9, s32[64]{0:T(128)S(1)} %copy-done.10, s32[64]{0:T(128)S(1)} %copy-done.11, s32[64]{0:T(128)S(1)} %copy-done.12, ...), custom_call_target="tpu_custom_call" | custom-call | flops 268435456 | bytes 6291456 | tf_op jit(solution)/shard_map/rest_1_1/pallas_call | solution.py:350
  64.5 4.2 %collective-permute-done.8.refs_10_ = bf16[4,128,256]{2,1,0:T(8,128)(2,1)S(1)} collective-permute-done((bf16[4,128,256]{2,1,0:T(8,128)(2,1)S(1)}, bf16[4,128,256]{2,1,0:T(8,128)(2,1)S(1)}, u32[]{:S(2)}, u32[]{:S(2)}) %collective-permute-start.8) | collective-permute-done | bytes 262176 | tf_op jit(solution)/shard_map/ppermute | solution.py:411
  72.8 2.4 %collective-permute-start.10 = (bf16[8,128,256]{2,1,0:T(8,128)(2,1)S(1)}, bf16[8,128,256]{2,1,0:T(8,128)(2,1)S(1)}, u32[]{:S(2)}, u32[]{:S(2)}) collective-permute-start(bf16[8,128,256]{2,1,0:T(8,128)(2,1)S(1)} %get-tuple-element.111.refs_6_), channel_id=1, source_target_pairs={{0,4},{4,0},{8,12},{12,8},{16,20},{20,16},{24,28},{28,24},{1,5},{5... | collective-permute-start | bytes 1572872 | tf_op jit(solution)/shard_map/ppermute | solution.py:400
  75.2 10.8 %collective-permute-done.10.refs_8_ = bf16[8,128,256]{2,1,0:T(8,128)(2,1)S(1)} collective-permute-done((bf16[8,128,256]{2,1,0:T(8,128)(2,1)S(1)}, bf16[8,128,256]{2,1,0:T(8,128)(2,1)S(1)}, u32[]{:S(2)}, u32[]{:S(2)}) %collective-permute-start.10) | collective-permute-done | bytes 524320 | tf_op jit(solution)/shard_map/ppermute | solution.py:400
  86.0 3.3 %collective-permute-done.13.refs_9_ = bf16[12,128,256]{2,1,0:T(8,128)(2,1)S(1)} collective-permute-done((bf16[12,128,256]{2,1,0:T(8,128)(2,1)S(1)}, bf16[12,128,256]{2,1,0:T(8,128)(2,1)S(1)}, u32[]{:S(2)}, u32[]{:S(2)}) %collective-permute-start.13) | collective-permute-done | bytes 786464 | tf_op jit(solution)/shard_map/ppermute | solution.py:411
  89.4 2.4 %collective-permute-start.15 = (bf16[8,128,256]{2,1,0:T(8,128)(2,1)S(1)}, bf16[8,128,256]{2,1,0:T(8,128)(2,1)S(1)}, u32[]{:S(2)}, u32[]{:S(2)}) collective-permute-start(bf16[8,128,256]{2,1,0:T(8,128)(2,1)S(1)} %pad_maximum_fusion.4), channel_id=1, source_target_pairs={{0,4},{4,0},{8,12},{12,8},{16,20},{20,16},{24,28},{28,24},{1,5},{5... | collective-permute-start | bytes 1572872 | tf_op jit(solution)/shard_map/ppermute | solution.py:400
  91.8 8.1 %operator_2.1 = (f32[8,256,256]{2,1,0:T(8,128)S(1)}, f32[8,256,256]{2,1,0:T(8,128)S(1)}) custom-call(s32[128]{0:T(128)S(1)} %copy-done.15, s32[32]{0:T(128)S(1)} %copy-done.16, s32[32]{0:T(128)S(1)} %copy-done.14, bf16[16,8,256,128]{3,2,1,0:T(8,128)(2,1)S(1)} %bitcast.11, bf16[32,256,128]{2,1,0:T(8,128)(2,1)S(1)} %bitcast.19, ...), custom_call_target="tpu_custom_call" | custom-call | flops 2684354560 | bytes 10485760 | tf_op jit(solution)/shard_map/operator_2/pallas_call | solution.py:201
  100.5 2.7 %rest_2_0.1 = (f32[1024,256]{1,0:T(8,128)S(1)}, bf16[8,128,256]{2,1,0:T(8,128)(2,1)S(1)}, bf16[4,128,256]{2,1,0:T(8,128)(2,1)S(1)}, f32[8,256]{1,0:T(8,128)S(1)}) custom-call(s32[128]{0:T(128)S(1)} %copy-done.7, s32[128]{0:T(128)S(1)} %copy-done.8, s32[128]{0:T(128)S(1)} %copy-done.9, s32[64]{0:T(128)S(1)} %copy-done.10, s32[64]{0:T(128)S(1)} %copy-done.11, ...), custom_call_target="tpu_custom_call" | custom-call | flops 268435456 | bytes 6291456 | tf_op jit(solution)/shard_map/rest_2_0/pallas_call | solution.py:350
  105.3 4.0 %collective-permute-start.18 = (bf16[4,128,256]{2,1,0:T(8,128)(2,1)S(1)}, bf16[4,128,256]{2,1,0:T(8,128)(2,1)S(1)}, u32[]{:S(2)}, u32[]{:S(2)}) collective-permute-start(bf16[4,128,256]{2,1,0:T(8,128)(2,1)S(1)} %get-tuple-element.126), channel_id=1, source_target_pairs={{0,24},{4,12},{8,0},{12,20},{16,8},{20,28},{24,16},{28,4},{1,25},{... | collective-permute-start | bytes 786440 | tf_op jit(solution)/shard_map/ppermute | solution.py:411
  109.3 2.7 %rest_2_1.1 = (f32[2048,256]{1,0:T(8,128)S(1)}, bf16[8,128,256]{2,1,0:T(8,128)(2,1)S(1)}, f32[8,256]{1,0:T(8,128)S(1)}) custom-call(s32[128]{0:T(128)S(1)} %copy-done.7, s32[128]{0:T(128)S(1)} %copy-done.8, s32[128]{0:T(128)S(1)} %copy-done.9, s32[64]{0:T(128)S(1)} %copy-done.10, s32[64]{0:T(128)S(1)} %copy-done.11, s32[64]{0:T(128)S(1)} %copy-done.12, ...), custom_call_target="tpu_custom_call" | custom-call | flops 268435456 | bytes 6291456 | tf_op jit(solution)/shard_map/rest_2_1/pallas_call | solution.py:350
  112.0 3.7 %collective-permute-done.17.refs_10_ = bf16[4,128,256]{2,1,0:T(8,128)(2,1)S(1)} collective-permute-done((bf16[4,128,256]{2,1,0:T(8,128)(2,1)S(1)}, bf16[4,128,256]{2,1,0:T(8,128)(2,1)S(1)}, u32[]{:S(2)}, u32[]{:S(2)}) %collective-permute-start.17) | collective-permute-done | bytes 262176 | tf_op jit(solution)/shard_map/ppermute | solution.py:411
  116.0 1.8 %collective-permute-done.20.refs_6_ = f32[2048,256]{1,0:T(8,128)S(1)} collective-permute-done((f32[2048,256]{1,0:T(8,128)S(1)}, f32[2048,256]{1,0:T(8,128)S(1)}, u32[]{:S(2)}, u32[]{:S(2)}) %collective-permute-start.20) | collective-permute-done | bytes 2097184 | tf_op jit(solution)/shard_map/ppermute | solution.py:400
  122.2 12.5 %collective-permute-done.19.refs_8_ = bf16[8,128,256]{2,1,0:T(8,128)(2,1)S(1)} collective-permute-done((bf16[8,128,256]{2,1,0:T(8,128)(2,1)S(1)}, bf16[8,128,256]{2,1,0:T(8,128)(2,1)S(1)}, u32[]{:S(2)}, u32[]{:S(2)}) %collective-permute-start.19) | collective-permute-done | bytes 524320 | tf_op jit(solution)/shard_map/ppermute | solution.py:400
  136.1 5.4 %collective-permute-done.21.refs_9_ = bf16[12,128,256]{2,1,0:T(8,128)(2,1)S(1)} collective-permute-done((bf16[12,128,256]{2,1,0:T(8,128)(2,1)S(1)}, bf16[12,128,256]{2,1,0:T(8,128)(2,1)S(1)}, u32[]{:S(2)}, u32[]{:S(2)}) %collective-permute-start.21) | collective-permute-done | bytes 786464 | tf_op jit(solution)/shard_map/ppermute | solution.py:411
  142.3 8.1 %operator_3.1.refs_9_ = f32[16,256,256]{2,1,0:T(8,128)S(1)} custom-call(s32[128]{0:T(128)S(1)} %copy-done.15, s32[32]{0:T(128)S(1)} %copy-done.16, s32[32]{0:T(128)S(1)} %copy-done.14, bf16[16,8,256,128]{3,2,1,0:T(8,128)(2,1)S(1)} %bitcast.14, bf16[32,256,128]{2,1,0:T(8,128)(2,1)S(1)} %bitcast.22, bf16[8,128,256]{2,1,0:T(8,128)(2,1)S(1)} %get-tuple-element.124.refs_5_, ...), custom_call_target="tpu_custom_call" | custom-call | flops 2684354560 | bytes 10485760 | tf_op jit(solution)/shard_map/operator_3/pallas_call | solution.py:201
  150.4 2.0 %collective-permute-done.22.refs_10_ = bf16[8,128,256]{2,1,0:T(8,128)(2,1)S(1)} collective-permute-done((bf16[8,128,256]{2,1,0:T(8,128)(2,1)S(1)}, bf16[8,128,256]{2,1,0:T(8,128)(2,1)S(1)}, u32[]{:S(2)}, u32[]{:S(2)}) %collective-permute-start.22) | collective-permute-done | bytes 524320 | tf_op jit(solution)/shard_map/ppermute | solution.py:411
  152.3 2.5 %collective-permute-done.23.refs_11_ = bf16[8,128,256]{2,1,0:T(8,128)(2,1)S(1)} collective-permute-done((bf16[8,128,256]{2,1,0:T(8,128)(2,1)S(1)}, bf16[8,128,256]{2,1,0:T(8,128)(2,1)S(1)}, u32[]{:S(2)}, u32[]{:S(2)}) %collective-permute-start.23) | collective-permute-done | bytes 524320 | tf_op jit(solution)/shard_map/ppermute | solution.py:400
  154.8 5.1 %rest_3_0.1 = f32[8,256]{1,0:T(8,128)S(1)} custom-call(s32[128]{0:T(128)S(1)} %copy-done.7, s32[128]{0:T(128)S(1)} %copy-done.8, s32[128]{0:T(128)S(1)} %copy-done.9, s32[64]{0:T(128)S(1)} %copy-done.10, s32[64]{0:T(128)S(1)} %copy-done.11, s32[64]{0:T(128)S(1)} %copy-done.12, s32[4]{0:T(128)S(1)} %copy-done.13, bf16[16,8,256,128]{3,2,1,0:T(8,128)(2,1)S(1)} %bitcast.15, ...), custom_call_target="tpu_custom_call" | custom-call | flops 536870912 | bytes 12582912 | tf_op jit(solution)/shard_map/rest_3_0/pallas_call | solution.py:350
  160.6 3.2 %collective-permute-done.24 = f32[24,256]{1,0:T(8,128)S(1)} collective-permute-done((f32[24,256]{1,0:T(8,128)S(1)}, f32[24,256]{1,0:T(8,128)S(1)}, u32[]{:S(2)}, u32[]{:S(2)}) %collective-permute-start.24) | collective-permute-done | bytes 24608 | tf_op jit(solution)/shard_map/ppermute | solution.py:400
  165.7 2.3 %collective-permute-start.30 = (f32[24,256]{1,0:T(8,128)S(1)}, f32[24,256]{1,0:T(8,128)S(1)}, u32[]{:S(2)}, u32[]{:S(2)}) collective-permute-start(f32[24,256]{1,0:T(8,128)S(1)} %fusion.refs_0_), channel_id=1, source_target_pairs={{0,24},{4,28},{8,0},{12,4},{16,8},{20,12},{24,16},{28,20},{1,25},{... | collective-permute-start | bytes 73736 | tf_op jit(solution)/shard_map/ppermute | solution.py:405
  173.2 2.0 %scattered.1 = f32[2,2048,128]{2,1,0:T(8,128)} custom-call(f32[8,128]{1,0:T(8,128)S(1)} %get-tuple-element.137.coefs, f32[2,2048,128]{2,1,0:T(8,128)S(1)} %bitcast.27, f32[2048,256]{1,0:T(8,128)S(1)} %get-tuple-element.131.refs_12_.first.refs_4_, f32[2048,256]{1,0:T(8,128)S(1)} %get-tuple-element.134.refs_13_.second.refs_8_), custom_call_target="tpu_custom_call" | custom-call | bytes 8392704 | tf_op jit(solution)/shard_map/scattered/pallas_call | solution.py:674
  175.8 2.8 %trace.1 = f32[2048,128]{1,0:T(8,128)} custom-call(s32[4]{0:T(128)S(1)} %iota_xor_fusion.place, f32[2048,128]{1,0:T(8,128)S(1)} %get-tuple-element.138.here, f32[2048,128]{1,0:T(8,128)S(1)} %collective-permute-done.12.away, f32[8,128]{1,0:T(8,128)S(1)} %get-tuple-element.140.refs_0_, f32[8,128]{1,0:T(8,128)S(1)} %collective-permute-done.31.refs_1_, ...), custom_call_target="tpu_custom_call" | custom-call | bytes 19939328 | tf_op jit(solution)/shard_map/trace/pallas_call | solution.py:674
  (108 shorter events, 36.3 us)
Async XLA Ops:
  3.9 17.9 %collective-permute-start = (bf16[8,128,256]{2,1,0:T(8,128)(2,1)S(1)}, bf16[8,128,256]{2,1,0:T(8,128)(2,1)S(1)}, u32[]{:S(2)}, u32[]{:S(2)}) collective-permute-start(bf16[8,128,256]{2,1,0:T(8,128)(2,1)S(1)} %get-tuple-element.74.refs_5_), channel_id=1, source_target_pairs={{0,4},{4,0},{8,12},{12,8},{16,20},{20,16},{24,28},{28,24},{1,5},{5... | collective-permute-start | bytes 1572872 | tf_op jit(solution)/shard_map/ppermute | solution.py:400
  6.9 11.3 %collective-permute-start.1 = (bf16[4,128,256]{2,1,0:T(8,128)(2,1)}, bf16[4,128,256]{2,1,0:T(8,128)(2,1)S(1)}, u32[]{:S(2)}, u32[]{:S(2)}) collective-permute-start(bf16[4,128,256]{2,1,0:T(8,128)(2,1)} %get-tuple-element.75), channel_id=1, source_target_pairs={{0,8},{4,28},{8,16},{12,4},{16,24},{20,12},{24,0},{28,20},{1,9},{5... | collective-permute-start | bytes 786440 | tf_op jit(solution)/shard_map/ppermute | solution.py:411
  8.4 13.4 %collective-permute-start.2 = (bf16[4,128,256]{2,1,0:T(8,128)(2,1)}, bf16[4,128,256]{2,1,0:T(8,128)(2,1)}, u32[]{:S(2)}, u32[]{:S(2)}) collective-permute-start(bf16[4,128,256]{2,1,0:T(8,128)(2,1)} %get-tuple-element.75), channel_id=1, source_target_pairs={{0,24},{4,12},{8,0},{12,20},{16,8},{20,28},{24,16},{28,4},{1,25},{... | collective-permute-start | bytes 786440 | tf_op jit(solution)/shard_map/ppermute | solution.py:411
  21.9 20.7 %collective-permute-start.4 = (bf16[12,128,256]{2,1,0:T(8,128)(2,1)S(1)}, bf16[12,128,256]{2,1,0:T(8,128)(2,1)S(1)}, u32[]{:S(2)}, u32[]{:S(2)}) collective-permute-start(bf16[12,128,256]{2,1,0:T(8,128)(2,1)S(1)} %pad_maximum_fusion), channel_id=1, source_target_pairs={{0,8},{4,28},{8,16},{12,4},{16,24},{20,12},{24,0},{28,20},{1,9},{5... | collective-permute-start | bytes 2359304 | tf_op jit(solution)/shard_map/ppermute | solution.py:411
  24.0 18.8 %collective-permute-start.11 = (f32[2048,128]{1,0:T(8,128)S(1)}, f32[2048,128]{1,0:T(8,128)S(1)}, u32[]{:S(2)}, u32[]{:S(2)}) collective-permute-start(f32[2048,128]{1,0:T(8,128)S(1)} %get-tuple-element.115), channel_id=1, source_target_pairs={{0,1},{1,0},{2,3},{3,2},{4,5},{5,4},{6,7},{7,6},{8,9},{9,8},{10,11... | collective-permute-start | bytes 3145736 | tf_op jit(solution)/shard_map/ppermute | solution.py:400
  24.1 14.5 %collective-permute-start.3 = (bf16[8,128,256]{2,1,0:T(8,128)(2,1)S(1)}, bf16[8,128,256]{2,1,0:T(8,128)(2,1)S(1)}, u32[]{:S(2)}, u32[]{:S(2)}) collective-permute-start(bf16[8,128,256]{2,1,0:T(8,128)(2,1)S(1)} %copy-done.6), channel_id=1, source_target_pairs={{0,4},{4,0},{8,12},{12,8},{16,20},{20,16},{24,28},{28,24},{1,5},{5... | collective-permute-start | bytes 1572872 | tf_op jit(solution)/shard_map/ppermute | solution.py:400
  38.5 15.4 %collective-permute-start.5 = (bf16[8,128,256]{2,1,0:T(8,128)(2,1)S(1)}, bf16[8,128,256]{2,1,0:T(8,128)(2,1)S(1)}, u32[]{:S(2)}, u32[]{:S(2)}) collective-permute-start(bf16[8,128,256]{2,1,0:T(8,128)(2,1)S(1)} %collective-permute-done.3.refs_8_), channel_id=1, source_target_pairs={{0,8},{4,28},{8,16},{12,4},{16,24},{20,12},{24,0},{28,20},{1,9},{5... | collective-permute-start | bytes 1572872 | tf_op jit(solution)/shard_map/ppermute | solution.py:411
  42.7 12.3 %collective-permute-start.6 = (bf16[8,128,256]{2,1,0:T(8,128)(2,1)S(1)}, bf16[8,128,256]{2,1,0:T(8,128)(2,1)S(1)}, u32[]{:S(2)}, u32[]{:S(2)}) collective-permute-start(bf16[8,128,256]{2,1,0:T(8,128)(2,1)S(1)} %pad_maximum_fusion.3), channel_id=1, source_target_pairs={{0,4},{4,0},{8,12},{12,8},{16,20},{20,16},{24,28},{28,24},{1,5},{5... | collective-permute-start | bytes 1572872 | tf_op jit(solution)/shard_map/ppermute | solution.py:400
  43.6 26.4 %collective-permute-start.12 = (f32[2048,128]{1,0:T(8,128)S(1)}, f32[2048,128]{1,0:T(8,128)S(1)}, u32[]{:S(2)}, u32[]{:S(2)}) collective-permute-start(f32[2048,128]{1,0:T(8,128)S(1)} %get-tuple-element.116), channel_id=1, source_target_pairs={{0,2},{1,3},{2,0},{3,1},{4,6},{5,7},{6,4},{7,5},{8,10},{9,11},{10,... | collective-permute-start | bytes 3145736 | tf_op jit(solution)/shard_map/ppermute | solution.py:400
  57.6 12.3 %collective-permute-start.7 = (bf16[8,128,256]{2,1,0:T(8,128)(2,1)S(1)}, bf16[8,128,256]{2,1,0:T(8,128)(2,1)S(1)}, u32[]{:S(2)}, u32[]{:S(2)}) collective-permute-start(bf16[8,128,256]{2,1,0:T(8,128)(2,1)S(1)} %get-tuple-element.107.refs_5_), channel_id=1, source_target_pairs={{0,4},{4,0},{8,12},{12,8},{16,20},{20,16},{24,28},{28,24},{1,5},{5... | collective-permute-start | bytes 1572872 | tf_op jit(solution)/shard_map/ppermute | solution.py:400
  58.1 10.6 %collective-permute-start.8 = (bf16[4,128,256]{2,1,0:T(8,128)(2,1)S(1)}, bf16[4,128,256]{2,1,0:T(8,128)(2,1)S(1)}, u32[]{:S(2)}, u32[]{:S(2)}) collective-permute-start(bf16[4,128,256]{2,1,0:T(8,128)(2,1)S(1)} %get-tuple-element.109), channel_id=1, source_target_pairs={{0,8},{4,28},{8,16},{12,4},{16,24},{20,12},{24,0},{28,20},{1,9},{5... | collective-permute-start | bytes 786440 | tf_op jit(solution)/shard_map/ppermute | solution.py:411
  58.9 10.9 %collective-permute-start.9 = (bf16[4,128,256]{2,1,0:T(8,128)(2,1)S(1)}, bf16[4,128,256]{2,1,0:T(8,128)(2,1)S(1)}, u32[]{:S(2)}, u32[]{:S(2)}) collective-permute-start(bf16[4,128,256]{2,1,0:T(8,128)(2,1)S(1)} %get-tuple-element.109), channel_id=1, source_target_pairs={{0,24},{4,12},{8,0},{12,20},{16,8},{20,28},{24,16},{28,4},{1,25},{... | collective-permute-start | bytes 786440 | tf_op jit(solution)/shard_map/ppermute | solution.py:411
  70.0 19.4 %collective-permute-start.13 = (bf16[12,128,256]{2,1,0:T(8,128)(2,1)S(1)}, bf16[12,128,256]{2,1,0:T(8,128)(2,1)S(1)}, u32[]{:S(2)}, u32[]{:S(2)}) collective-permute-start(bf16[12,128,256]{2,1,0:T(8,128)(2,1)S(1)} %pad_maximum_fusion.1), channel_id=1, source_target_pairs={{0,8},{4,28},{8,16},{12,4},{16,24},{20,12},{24,0},{28,20},{1,9},{5... | collective-permute-start | bytes 2359304 | tf_op jit(solution)/shard_map/ppermute | solution.py:411
  71.3 46.5 %collective-permute-start.20 = (f32[2048,256]{1,0:T(8,128)S(1)}, f32[2048,256]{1,0:T(8,128)S(1)}, u32[]{:S(2)}, u32[]{:S(2)}) collective-permute-start(f32[2048,256]{1,0:T(8,128)S(1)} %get-tuple-element.131.refs_12_.first.refs_4_), channel_id=1, source_target_pairs={{0,2},{1,3},{2,0},{3,1},{4,6},{5,7},{6,4},{7,5},{8,10},{9,11},{10,... | collective-permute-start | bytes 6291464 | tf_op jit(solution)/shard_map/ppermute | solution.py:400
  72.8 13.2 %collective-permute-start.10 = (bf16[8,128,256]{2,1,0:T(8,128)(2,1)S(1)}, bf16[8,128,256]{2,1,0:T(8,128)(2,1)S(1)}, u32[]{:S(2)}, u32[]{:S(2)}) collective-permute-start(bf16[8,128,256]{2,1,0:T(8,128)(2,1)S(1)} %get-tuple-element.111.refs_6_), channel_id=1, source_target_pairs={{0,4},{4,0},{8,12},{12,8},{16,20},{20,16},{24,28},{28,24},{1,5},{5... | collective-permute-start | bytes 1572872 | tf_op jit(solution)/shard_map/ppermute | solution.py:400
  86.0 14.2 %collective-permute-start.14 = (bf16[8,128,256]{2,1,0:T(8,128)(2,1)S(1)}, bf16[8,128,256]{2,1,0:T(8,128)(2,1)S(1)}, u32[]{:S(2)}, u32[]{:S(2)}) collective-permute-start(bf16[8,128,256]{2,1,0:T(8,128)(2,1)S(1)} %collective-permute-done.10.refs_8_), channel_id=1, source_target_pairs={{0,8},{4,28},{8,16},{12,4},{16,24},{20,12},{24,0},{28,20},{1,9},{5... | collective-permute-start | bytes 1572872 | tf_op jit(solution)/shard_map/ppermute | solution.py:411
  89.4 11.1 %collective-permute-start.15 = (bf16[8,128,256]{2,1,0:T(8,128)(2,1)S(1)}, bf16[8,128,256]{2,1,0:T(8,128)(2,1)S(1)}, u32[]{:S(2)}, u32[]{:S(2)}) collective-permute-start(bf16[8,128,256]{2,1,0:T(8,128)(2,1)S(1)} %pad_maximum_fusion.4), channel_id=1, source_target_pairs={{0,4},{4,0},{8,12},{12,8},{16,20},{20,16},{24,28},{28,24},{1,5},{5... | collective-permute-start | bytes 1572872 | tf_op jit(solution)/shard_map/ppermute | solution.py:400
  103.2 12.7 %collective-permute-start.16 = (bf16[8,128,256]{2,1,0:T(8,128)(2,1)S(1)}, bf16[8,128,256]{2,1,0:T(8,128)(2,1)S(1)}, u32[]{:S(2)}, u32[]{:S(2)}) collective-permute-start(bf16[8,128,256]{2,1,0:T(8,128)(2,1)S(1)} %get-tuple-element.124.refs_5_), channel_id=1, source_target_pairs={{0,4},{4,0},{8,12},{12,8},{16,20},{20,16},{24,28},{28,24},{1,5},{5... | collective-permute-start | bytes 1572872 | tf_op jit(solution)/shard_map/ppermute | solution.py:400
  105.0 10.7 %collective-permute-start.17 = (bf16[4,128,256]{2,1,0:T(8,128)(2,1)S(1)}, bf16[4,128,256]{2,1,0:T(8,128)(2,1)S(1)}, u32[]{:S(2)}, u32[]{:S(2)}) collective-permute-start(bf16[4,128,256]{2,1,0:T(8,128)(2,1)S(1)} %get-tuple-element.126), channel_id=1, source_target_pairs={{0,8},{4,28},{8,16},{12,4},{16,24},{20,12},{24,0},{28,20},{1,9},{5... | collective-permute-start | bytes 786440 | tf_op jit(solution)/shard_map/ppermute | solution.py:411
  105.3 10.6 %collective-permute-start.18 = (bf16[4,128,256]{2,1,0:T(8,128)(2,1)S(1)}, bf16[4,128,256]{2,1,0:T(8,128)(2,1)S(1)}, u32[]{:S(2)}, u32[]{:S(2)}) collective-permute-start(bf16[4,128,256]{2,1,0:T(8,128)(2,1)S(1)} %get-tuple-element.126), channel_id=1, source_target_pairs={{0,24},{4,12},{8,0},{12,20},{16,8},{20,28},{24,16},{28,4},{1,25},{... | collective-permute-start | bytes 786440 | tf_op jit(solution)/shard_map/ppermute | solution.py:411
  111.9 51.9 %collective-permute-start.26 = (f32[2048,256]{1,0:T(8,128)S(1)}, f32[2048,256]{1,0:T(8,128)S(1)}, u32[]{:S(2)}, u32[]{:S(2)}) collective-permute-start(f32[2048,256]{1,0:T(8,128)S(1)} %get-tuple-element.134.refs_13_.second.refs_8_), channel_id=1, source_target_pairs={{0,1},{1,0},{2,3},{3,2},{4,5},{5,4},{6,7},{7,6},{8,9},{9,8},{10,11... | collective-permute-start | bytes 6291464 | tf_op jit(solution)/shard_map/ppermute | solution.py:400
  117.8 46.0 %collective-permute-start.25 = (f32[2048,256]{1,0:T(8,128)S(1)}, f32[2048,256]{1,0:T(8,128)S(1)}, u32[]{:S(2)}, u32[]{:S(2)}) collective-permute-start(f32[2048,256]{1,0:T(8,128)S(1)} %get-tuple-element.134.refs_13_.second.refs_8_), channel_id=1, source_target_pairs={{0,2},{1,3},{2,0},{3,1},{4,6},{5,7},{6,4},{7,5},{8,10},{9,11},{10,... | collective-permute-start | bytes 6291464 | tf_op jit(solution)/shard_map/ppermute | solution.py:400
  119.4 44.5 %collective-permute-start.27 = (f32[2048,256]{1,0:T(8,128)S(1)}, f32[2048,256]{1,0:T(8,128)S(1)}, u32[]{:S(2)}, u32[]{:S(2)}) collective-permute-start(f32[2048,256]{1,0:T(8,128)S(1)} %collective-permute-done.20.refs_6_), channel_id=1, source_target_pairs={{0,1},{1,0},{2,3},{3,2},{4,5},{5,4},{6,7},{7,6},{8,9},{9,8},{10,11... | collective-permute-start | bytes 6291464 | tf_op jit(solution)/shard_map/ppermute | solution.py:400
  119.4 22.1 %collective-permute-start.21 = (bf16[12,128,256]{2,1,0:T(8,128)(2,1)S(1)}, bf16[12,128,256]{2,1,0:T(8,128)(2,1)S(1)}, u32[]{:S(2)}, u32[]{:S(2)}) collective-permute-start(bf16[12,128,256]{2,1,0:T(8,128)(2,1)S(1)} %pad_maximum_fusion.2), channel_id=1, source_target_pairs={{0,8},{4,28},{8,16},{12,4},{16,24},{20,12},{24,0},{28,20},{1,9},{5... | collective-permute-start | bytes 2359304 | tf_op jit(solution)/shard_map/ppermute | solution.py:411
  120.6 14.1 %collective-permute-start.19 = (bf16[8,128,256]{2,1,0:T(8,128)(2,1)S(1)}, bf16[8,128,256]{2,1,0:T(8,128)(2,1)S(1)}, u32[]{:S(2)}, u32[]{:S(2)}) collective-permute-start(bf16[8,128,256]{2,1,0:T(8,128)(2,1)S(1)} %get-tuple-element.128.refs_6_), channel_id=1, source_target_pairs={{0,4},{4,0},{8,12},{12,8},{16,20},{20,16},{24,28},{28,24},{1,5},{5... | collective-permute-start | bytes 1572872 | tf_op jit(solution)/shard_map/ppermute | solution.py:400
  134.7 17.7 %collective-permute-start.22 = (bf16[8,128,256]{2,1,0:T(8,128)(2,1)S(1)}, bf16[8,128,256]{2,1,0:T(8,128)(2,1)S(1)}, u32[]{:S(2)}, u32[]{:S(2)}) collective-permute-start(bf16[8,128,256]{2,1,0:T(8,128)(2,1)S(1)} %collective-permute-done.19.refs_8_), channel_id=1, source_target_pairs={{0,8},{4,28},{8,16},{12,4},{16,24},{20,12},{24,0},{28,20},{1,9},{5... | collective-permute-start | bytes 1572872 | tf_op jit(solution)/shard_map/ppermute | solution.py:411
  141.6 13.2 %collective-permute-start.23 = (bf16[8,128,256]{2,1,0:T(8,128)(2,1)S(1)}, bf16[8,128,256]{2,1,0:T(8,128)(2,1)S(1)}, u32[]{:S(2)}, u32[]{:S(2)}) collective-permute-start(bf16[8,128,256]{2,1,0:T(8,128)(2,1)S(1)} %pad_maximum_fusion.5), channel_id=1, source_target_pairs={{0,4},{4,0},{8,12},{12,8},{16,20},{20,16},{24,28},{28,24},{1,5},{5... | collective-permute-start | bytes 1572872 | tf_op jit(solution)/shard_map/ppermute | solution.py:400
  160.6 14.6 %collective-permute-start.34 = (f32[2048,256]{1,0:T(8,128)S(1)}, f32[2048,256]{1,0:T(8,128)S(1)}, u32[]{:S(2)}, u32[]{:S(2)}) collective-permute-start(f32[2048,256]{1,0:T(8,128)S(1)} %get-tuple-element.131.refs_12_.first.refs_4_), channel_id=1, source_target_pairs={{0,1},{1,0},{2,3},{3,2},{4,5},{5,4},{6,7},{7,6},{8,9},{9,8},{10,11... | collective-permute-start | bytes 6291464 | tf_op jit(solution)/shard_map/ppermute | solution.py:400
  163.9 11.9 %collective-permute-start.35 = (f32[2048,256]{1,0:T(8,128)S(1)}, f32[2048,256]{1,0:T(8,128)S(1)}, u32[]{:S(2)}, u32[]{:S(2)}) collective-permute-start(f32[2048,256]{1,0:T(8,128)S(1)} %collective-permute-done.25.refs_10_), channel_id=1, source_target_pairs={{0,1},{1,0},{2,3},{3,2},{4,5},{5,4},{6,7},{7,6},{8,9},{9,8},{10,11... | collective-permute-start | bytes 6291464 | tf_op jit(solution)/shard_map/ppermute | solution.py:400
  163.9 5.7 %collective-permute-start.28 = (f32[24,256]{1,0:T(8,128)S(1)}, f32[24,256]{1,0:T(8,128)S(1)}, u32[]{:S(2)}, u32[]{:S(2)}) collective-permute-start(f32[24,256]{1,0:T(8,128)S(1)} %fusion.refs_0_), channel_id=1, source_target_pairs={{0,8},{4,12},{8,16},{12,20},{16,24},{20,28},{24,0},{28,4},{1,9},{5... | collective-permute-start | bytes 73736 | tf_op jit(solution)/shard_map/ppermute | solution.py:405
  165.4 5.0 %collective-permute-start.29 = (f32[24,256]{1,0:T(8,128)S(1)}, f32[24,256]{1,0:T(8,128)S(1)}, u32[]{:S(2)}, u32[]{:S(2)}) collective-permute-start(f32[24,256]{1,0:T(8,128)S(1)} %fusion.refs_0_), channel_id=1, source_target_pairs={{0,16},{4,20},{8,24},{12,28},{16,0},{20,4},{24,8},{28,12},{1,17},{... | collective-permute-start | bytes 73736 | tf_op jit(solution)/shard_map/ppermute | solution.py:405
  165.7 4.9 %collective-permute-start.30 = (f32[24,256]{1,0:T(8,128)S(1)}, f32[24,256]{1,0:T(8,128)S(1)}, u32[]{:S(2)}, u32[]{:S(2)}) collective-permute-start(f32[24,256]{1,0:T(8,128)S(1)} %fusion.refs_0_), channel_id=1, source_target_pairs={{0,24},{4,28},{8,0},{12,4},{16,8},{20,12},{24,16},{28,20},{1,25},{... | collective-permute-start | bytes 73736 | tf_op jit(solution)/shard_map/ppermute | solution.py:405
  (23 other events, 250.3 us)

commit v5 on v4

--- a/solution.py
+++ b/solution.py
@@ -419,7 +419,7 @@
     return lax.optimization_barrier(values)
 
 
-def exchange(lows, early_ties=(), late_ties=()):
+def exchange(lows, early_ties=(), late_ties=(), first_ties=()):
     low_a, low_b, head = lows
     cut, rest, front = (low.shape[0] for low in lows)
     nblocks = cut + rest
@@ -432,9 +432,9 @@
         parts = [low, shift(low, "clu", -1), shift(low, "clu", 1), every]
         source_moves = tuple((k, 0, nblocks, k * nblocks) for k in range(3))
         found = (parts, ((3, 0, count * front, 0),), source_moves, [], (), ())
-        return found, early_ties, late_ties
+        return found, early_ties, late_ties, first_ties
     beside_a = swap(low_a, "clu", 1)
-    same = ring(head, 2)
+    same, *first_ties = tie(ring(head, 2), *first_ties)
     other = ring(head, -2)
     tail, beside_a, same, other = tie(low_b, beside_a, same, other)
     onward, *early_ties = tie(jnp.concatenate([beside_a, same], axis=0), *early_ties)
@@ -461,7 +461,7 @@
     )
     last = [beyond_b, pairs]
     found = (parts, front_moves, source_moves, last, ((0, 0, rest, 0),), ((1, 0, 2 * front, 0),))
-    return found, early_ties, late_ties
+    return found, early_ties, late_ties, first_ties
 
 
 def sum_over_clusters(value, *tied):
@@ -514,7 +514,7 @@
     beta2 = g00 + EPS
     beta = jnp.sqrt(beta2)
     h11 = ((0.5 * g00 + g01[0]) / beta2, g01[1] / beta2)
-    s = (0.5 - h11[0], -h11[1])
+    s = ((0.5 * EPS - g01[0]) / beta2, -g01[1] / beta2)
     s01 = cjmul(s, g01)
     w2w2 = g11 + 2.0 * s01[0] + norm2(s) * g00
     h21 = jnp.sqrt(jnp.maximum(w2w2 / beta2, 0.0) + EPS)
@@ -724,7 +724,7 @@
         front,
     )
 
-    found, (from_start, *tables), base = exchange(
+    found, (from_start, *tables), base, _ = exchange(
         lows,
         (initial, *tables),
         lambda early: [on_vmem(base_kernel, both, (), (incident, early[0]), "base")],
@@ -749,11 +749,12 @@
         return vector, low_a, low_b, head, sums
 
     first, *lows, sums_one = operate(1, found, (base,))
-    found, (first_sent, away), _ = exchange(lows, (first, away))
+    found, (away,), _, (first_sent,) = exchange(lows, (away,), (), (first,))
     first_across, first_one = swap(first_sent, "frq", 2), swap(first, "frq", 1)
 
     second, *lows, sums_two = operate(2, found, (first,))
-    found, (second_sent, first_across), _ = exchange(lows, (second, first_across))
+    second_sent, first_across = tie(second, first_across)
+    found, _, _, _ = exchange(lows)
     second_across, first_three = swap(second_sent, "frq", 2), swap(first_across, "frq", 1)
     (sums_three,) = operate(3, found, (first, second))
     second_one = swap(second, "frq", 1)

time: 178 us -> 175 us (0.983)
  starting transfers between devices: 43.5 us -> 40.9 us
    ppermute x21, waiting for transfers between devices: 44.9 us -> 41.3 us  [swap(): return lax.ppermute(value, axis, [(i, i ^ distance) for i in range(count)])]
    ppermute x21, starting transfers between devices: 21.8 us -> 19.2 us  [swap(): return lax.ppermute(value, axis, [(i, i ^ distance) for i in range(count)])]
    ppermute x12, waiting for transfers between devices: 28.4 us -> 30.5 us  [ring(): return lax.ppermute(value, 'clu', pairs)]
  transfers between devices with their start and end apart: 36 -> 36, of which waited for: 24 -> 24; matrix products, arithmetic and copies ran while one was open for 1% -> 1% of each run, Pallas kernels for 28% -> 29%
where the time goes in v5:
time: 175 us; the launch traced here: 174 us
  waiting for transfers between devices  74.4 us (43%)
  Pallas kernels  54.5 us (31%)
  starting transfers between devices  40.9 us (23%)
  local copies, waits for them, and re-layouts  3.2 us (2%)
    ppermute x21, waiting for transfers between devices, swap(): return lax.ppermute(value, axis, [(i, i ^ distance) for i in range(count)])  41.3 us
    ppermute x12, waiting for transfers between devices, ring(): return lax.ppermute(value, 'clu', pairs)  30.5 us
    pallas_call x3, Pallas kernels, main_call(): pl.pallas_call(functools.partial(main_kernel, (nblocks, span, edges), (fr...  24.3 us
    ppermute x21, starting transfers between devices, swap(): return lax.ppermute(value, axis, [(i, i ^ distance) for i in range(count)])  19.2 us
    ppermute x12, starting transfers between devices, ring(): return lax.ppermute(value, 'clu', pairs)  17.6 us
    pallas_call x5, Pallas kernels, rest_call(): pl.pallas_call(functools.partial(rest_kernel, step, part, (nblocks, span,...  15.6 us
    pallas_call x7, Pallas kernels, on_vmem(): pl.pallas_call(body, out_shape=out_shape, in_specs=[smem] * len(smem_args...  8.22 us
    pallas_call x1, Pallas kernels, table_call(): pl.pallas_call(functools.partial(table_kernel, sizes), out_shape=tuple((j...  6.41 us
  transfers between devices with their start and end apart: 36, of which 24 were waited for; matrix products, arithmetic and copies ran while one was open for 1% of the time, Pallas kernels for 29%

profile of v5, /device:TPU:0, one launch (start us, length us, event | category | flops | bytes accessed | tf_op | source)
XLA Modules:
  0.0 174.4 jit_solution(9440428103435141257)
XLA Ops:
  3.9 2.9 %collective-permute-start = (bf16[8,128,256]{2,1,0:T(8,128)(2,1)S(1)}, bf16[8,128,256]{2,1,0:T(8,128)(2,1)S(1)}, u32[]{:S(2)}, u32[]{:S(2)}) collective-permute-start(bf16[8,128,256]{2,1,0:T(8,128)(2,1)S(1)} %get-tuple-element.74.refs_5_), channel_id=1, source_target_pairs={{0,4},{4,0},{8,12},{12,8},{16,20},{20,16},{24,28},{28,24},{1,5},{5... | collective-permute-start | bytes 1572872 | tf_op jit(solution)/shard_map/ppermute | solution.py:400
  8.4 2.2 %collective-permute-start.2 = (bf16[4,128,256]{2,1,0:T(8,128)(2,1)}, bf16[4,128,256]{2,1,0:T(8,128)(2,1)}, u32[]{:S(2)}, u32[]{:S(2)}) collective-permute-start(bf16[4,128,256]{2,1,0:T(8,128)(2,1)} %get-tuple-element.75), channel_id=1, source_target_pairs={{0,24},{4,12},{8,0},{12,20},{16,8},{20,28},{24,16},{28,4},{1,25},{... | collective-permute-start | bytes 786440 | tf_op jit(solution)/shard_map/ppermute | solution.py:411
  11.4 6.4 %tables.1 = (s32[128]{0:T(128)}, s32[32]{0:T(128)}, s32[128]{0:T(128)}, s32[128]{0:T(128)}, s32[128]{0:T(128)}, /*index=5*/s32[64]{0:T(128)}, s32[64]{0:T(128)}, s32[64]{0:T(128)}, s32[4]{0:T(128)}) custom-call(s32[1]{0:T(128)} %bitcast.1.place, s32[128]{0:T(128)} %reshape.17.pattern, s32[32]{0:T(128)} %bitcast.31, s32[32]{0:T(128)} %source.1, s32[32]{0:T(128)} %refs_2_.5), custom_call_target="tpu_custom_call" | custom-call | tf_op jit(solution)/shard_map/tables/pallas_call | solution.py:110
  18.2 3.7 %collective-permute-done.2.refs_11_ = bf16[4,128,256]{2,1,0:T(8,128)(2,1)} collective-permute-done((bf16[4,128,256]{2,1,0:T(8,128)(2,1)}, bf16[4,128,256]{2,1,0:T(8,128)(2,1)}, u32[]{:S(2)}, u32[]{:S(2)}) %collective-permute-start.2) | collective-permute-done | bytes 262176 | tf_op jit(solution)/shard_map/ppermute | solution.py:411
  24.1 1.9 %collective-permute-start.3 = (bf16[8,128,256]{2,1,0:T(8,128)(2,1)S(1)}, bf16[8,128,256]{2,1,0:T(8,128)(2,1)S(1)}, u32[]{:S(2)}, u32[]{:S(2)}) collective-permute-start(bf16[8,128,256]{2,1,0:T(8,128)(2,1)S(1)} %copy-done.6), channel_id=1, source_target_pairs={{0,4},{4,0},{8,12},{12,8},{16,20},{20,16},{24,28},{28,24},{1,5},{5... | collective-permute-start | bytes 1572872 | tf_op jit(solution)/shard_map/ppermute | solution.py:400
  26.3 12.2 %collective-permute-done.3.refs_8_ = bf16[8,128,256]{2,1,0:T(8,128)(2,1)S(1)} collective-permute-done((bf16[8,128,256]{2,1,0:T(8,128)(2,1)S(1)}, bf16[8,128,256]{2,1,0:T(8,128)(2,1)S(1)}, u32[]{:S(2)}, u32[]{:S(2)}) %collective-permute-start.3) | collective-permute-done | bytes 524320 | tf_op jit(solution)/shard_map/ppermute | solution.py:400
  39.0 3.6 %collective-permute-done.4.refs_9_ = bf16[12,128,256]{2,1,0:T(8,128)(2,1)S(1)} collective-permute-done((bf16[12,128,256]{2,1,0:T(8,128)(2,1)S(1)}, bf16[12,128,256]{2,1,0:T(8,128)(2,1)S(1)}, u32[]{:S(2)}, u32[]{:S(2)}) %collective-permute-start.4) | collective-permute-done | bytes 786464 | tf_op jit(solution)/shard_map/ppermute | solution.py:411
  45.2 8.1 %operator_1.1 = (f32[8,256,256]{2,1,0:T(8,128)S(1)}, f32[8,256,256]{2,1,0:T(8,128)S(1)}) custom-call(s32[128]{0:T(128)S(1)} %copy-done.15, s32[32]{0:T(128)S(1)} %copy-done.16, s32[32]{0:T(128)S(1)} %copy-done.14, bf16[16,8,256,128]{3,2,1,0:T(8,128)(2,1)S(1)} %bitcast.8, bf16[32,256,128]{2,1,0:T(8,128)(2,1)S(1)} %bitcast.16, ...), custom_call_target="tpu_custom_call" | custom-call | flops 2684354560 | bytes 10485760 | tf_op jit(solution)/shard_map/operator_1/pallas_call | solution.py:201
  55.1 2.5 %rest_1_0.1 = (f32[1024,256]{1,0:T(8,128)S(1)}, bf16[8,128,256]{2,1,0:T(8,128)(2,1)S(1)}, bf16[4,128,256]{2,1,0:T(8,128)(2,1)S(1)}, f32[8,256]{1,0:T(8,128)S(1)}) custom-call(s32[128]{0:T(128)S(1)} %copy-done.7, s32[128]{0:T(128)S(1)} %copy-done.8, s32[128]{0:T(128)S(1)} %copy-done.9, s32[64]{0:T(128)S(1)} %copy-done.10, s32[64]{0:T(128)S(1)} %copy-done.11, ...), custom_call_target="tpu_custom_call" | custom-call | flops 268435456 | bytes 6291456 | tf_op jit(solution)/shard_map/rest_1_0/pallas_call | solution.py:350
  59.3 2.9 %collective-permute-start.9 = (bf16[4,128,256]{2,1,0:T(8,128)(2,1)S(1)}, bf16[4,128,256]{2,1,0:T(8,128)(2,1)S(1)}, u32[]{:S(2)}, u32[]{:S(2)}) collective-permute-start(bf16[4,128,256]{2,1,0:T(8,128)(2,1)S(1)} %get-tuple-element.109), channel_id=1, source_target_pairs={{0,24},{4,12},{8,0},{12,20},{16,8},{20,28},{24,16},{28,4},{1,25},{... | collective-permute-start | bytes 786440 | tf_op jit(solution)/shard_map/ppermute | solution.py:411
  62.2 2.6 %rest_1_1.1 = (f32[2048,256]{1,0:T(8,128)S(1)}, bf16[8,128,256]{2,1,0:T(8,128)(2,1)S(1)}, f32[8,256]{1,0:T(8,128)S(1)}) custom-call(s32[128]{0:T(128)S(1)} %copy-done.7, s32[128]{0:T(128)S(1)} %copy-done.8, s32[128]{0:T(128)S(1)} %copy-done.9, s32[64]{0:T(128)S(1)} %copy-done.10, s32[64]{0:T(128)S(1)} %copy-done.11, s32[64]{0:T(128)S(1)} %copy-done.12, ...), custom_call_target="tpu_custom_call" | custom-call | flops 268435456 | bytes 6291456 | tf_op jit(solution)/shard_map/rest_1_1/pallas_call | solution.py:350
  64.8 4.2 %collective-permute-done.8.refs_10_ = bf16[4,128,256]{2,1,0:T(8,128)(2,1)S(1)} collective-permute-done((bf16[4,128,256]{2,1,0:T(8,128)(2,1)S(1)}, bf16[4,128,256]{2,1,0:T(8,128)(2,1)S(1)}, u32[]{:S(2)}, u32[]{:S(2)}) %collective-permute-start.8) | collective-permute-done | bytes 262176 | tf_op jit(solution)/shard_map/ppermute | solution.py:411
  73.5 11.6 %collective-permute-done.10.refs_8_ = bf16[8,128,256]{2,1,0:T(8,128)(2,1)S(1)} collective-permute-done((bf16[8,128,256]{2,1,0:T(8,128)(2,1)S(1)}, bf16[8,128,256]{2,1,0:T(8,128)(2,1)S(1)}, u32[]{:S(2)}, u32[]{:S(2)}) %collective-permute-start.10) | collective-permute-done | bytes 524320 | tf_op jit(solution)/shard_map/ppermute | solution.py:400
  85.4 5.3 %collective-permute-done.13.refs_9_ = bf16[12,128,256]{2,1,0:T(8,128)(2,1)S(1)} collective-permute-done((bf16[12,128,256]{2,1,0:T(8,128)(2,1)S(1)}, bf16[12,128,256]{2,1,0:T(8,128)(2,1)S(1)}, u32[]{:S(2)}, u32[]{:S(2)}) %collective-permute-start.13) | collective-permute-done | bytes 786464 | tf_op jit(solution)/shard_map/ppermute | solution.py:411
  91.9 8.1 %operator_2.1 = (f32[8,256,256]{2,1,0:T(8,128)S(1)}, f32[8,256,256]{2,1,0:T(8,128)S(1)}) custom-call(s32[128]{0:T(128)S(1)} %copy-done.15, s32[32]{0:T(128)S(1)} %copy-done.16, s32[32]{0:T(128)S(1)} %copy-done.14, bf16[16,8,256,128]{3,2,1,0:T(8,128)(2,1)S(1)} %bitcast.11, bf16[32,256,128]{2,1,0:T(8,128)(2,1)S(1)} %bitcast.19, ...), custom_call_target="tpu_custom_call" | custom-call | flops 2684354560 | bytes 10485760 | tf_op jit(solution)/shard_map/operator_2/pallas_call | solution.py:201
  101.1 2.7 %rest_2_0.1 = (f32[1024,256]{1,0:T(8,128)S(1)}, bf16[8,128,256]{2,1,0:T(8,128)(2,1)S(1)}, bf16[4,128,256]{2,1,0:T(8,128)(2,1)S(1)}, f32[8,256]{1,0:T(8,128)S(1)}) custom-call(s32[128]{0:T(128)S(1)} %copy-done.7, s32[128]{0:T(128)S(1)} %copy-done.8, s32[128]{0:T(128)S(1)} %copy-done.9, s32[64]{0:T(128)S(1)} %copy-done.10, s32[64]{0:T(128)S(1)} %copy-done.11, ...), custom_call_target="tpu_custom_call" | custom-call | flops 268435456 | bytes 6291456 | tf_op jit(solution)/shard_map/rest_2_0/pallas_call | solution.py:350
  104.4 2.6 %collective-permute-start.17 = (bf16[4,128,256]{2,1,0:T(8,128)(2,1)S(1)}, bf16[4,128,256]{2,1,0:T(8,128)(2,1)S(1)}, u32[]{:S(2)}, u32[]{:S(2)}) collective-permute-start(bf16[4,128,256]{2,1,0:T(8,128)(2,1)S(1)} %get-tuple-element.127), channel_id=1, source_target_pairs={{0,8},{4,28},{8,16},{12,4},{16,24},{20,12},{24,0},{28,20},{1,9},{5... | collective-permute-start | bytes 786440 | tf_op jit(solution)/shard_map/ppermute | solution.py:411
  108.5 2.7 %rest_2_1.1 = (f32[2048,256]{1,0:T(8,128)S(1)}, bf16[8,128,256]{2,1,0:T(8,128)(2,1)S(1)}, f32[8,256]{1,0:T(8,128)S(1)}) custom-call(s32[128]{0:T(128)S(1)} %copy-done.7, s32[128]{0:T(128)S(1)} %copy-done.8, s32[128]{0:T(128)S(1)} %copy-done.9, s32[64]{0:T(128)S(1)} %copy-done.10, s32[64]{0:T(128)S(1)} %copy-done.11, s32[64]{0:T(128)S(1)} %copy-done.12, ...), custom_call_target="tpu_custom_call" | custom-call | flops 268435456 | bytes 6291456 | tf_op jit(solution)/shard_map/rest_2_1/pallas_call | solution.py:350
  115.0 2.4 %collective-permute-done.18.refs_11_ = bf16[4,128,256]{2,1,0:T(8,128)(2,1)S(1)} collective-permute-done((bf16[4,128,256]{2,1,0:T(8,128)(2,1)S(1)}, bf16[4,128,256]{2,1,0:T(8,128)(2,1)S(1)}, u32[]{:S(2)}, u32[]{:S(2)}) %collective-permute-start.18) | collective-permute-done | bytes 262176 | tf_op jit(solution)/shard_map/ppermute | solution.py:411
  117.9 1.8 %collective-permute-start.19 = (bf16[8,128,256]{2,1,0:T(8,128)(2,1)S(1)}, bf16[8,128,256]{2,1,0:T(8,128)(2,1)S(1)}, u32[]{:S(2)}, u32[]{:S(2)}) collective-permute-start(bf16[8,128,256]{2,1,0:T(8,128)(2,1)S(1)} %get-tuple-element.129.refs_6_), channel_id=1, source_target_pairs={{0,4},{4,0},{8,12},{12,8},{16,20},{20,16},{24,28},{28,24},{1,5},{5... | collective-permute-start | bytes 1572872 | tf_op jit(solution)/shard_map/ppermute | solution.py:400
  119.7 10.6 %collective-permute-done.19.refs_8_ = bf16[8,128,256]{2,1,0:T(8,128)(2,1)S(1)} collective-permute-done((bf16[8,128,256]{2,1,0:T(8,128)(2,1)S(1)}, bf16[8,128,256]{2,1,0:T(8,128)(2,1)S(1)}, u32[]{:S(2)}, u32[]{:S(2)}) %collective-permute-start.19) | collective-permute-done | bytes 524320 | tf_op jit(solution)/shard_map/ppermute | solution.py:400
  130.3 2.0 %collective-permute-start.21 = (bf16[8,128,256]{2,1,0:T(8,128)(2,1)S(1)}, bf16[8,128,256]{2,1,0:T(8,128)(2,1)S(1)}, u32[]{:S(2)}, u32[]{:S(2)}) collective-permute-start(bf16[8,128,256]{2,1,0:T(8,128)(2,1)S(1)} %collective-permute-done.19.refs_8_), channel_id=1, source_target_pairs={{0,8},{4,28},{8,16},{12,4},{16,24},{20,12},{24,0},{28,20},{1,9},{5... | collective-permute-start | bytes 1572872 | tf_op jit(solution)/shard_map/ppermute | solution.py:411
  132.2 7.6 %collective-permute-done.20.refs_9_ = bf16[12,128,256]{2,1,0:T(8,128)(2,1)S(1)} collective-permute-done((bf16[12,128,256]{2,1,0:T(8,128)(2,1)S(1)}, bf16[12,128,256]{2,1,0:T(8,128)(2,1)S(1)}, u32[]{:S(2)}, u32[]{:S(2)}) %collective-permute-start.20) | collective-permute-done | bytes 786464 | tf_op jit(solution)/shard_map/ppermute | solution.py:411
  140.0 8.1 %operator_3.1.refs_9_ = f32[16,256,256]{2,1,0:T(8,128)S(1)} custom-call(s32[128]{0:T(128)S(1)} %copy-done.15, s32[32]{0:T(128)S(1)} %copy-done.16, s32[32]{0:T(128)S(1)} %copy-done.14, bf16[16,8,256,128]{3,2,1,0:T(8,128)(2,1)S(1)} %bitcast.14, bf16[32,256,128]{2,1,0:T(8,128)(2,1)S(1)} %bitcast.22, bf16[8,128,256]{2,1,0:T(8,128)(2,1)S(1)} %get-tuple-element.125.refs_5_, ...), custom_call_target="tpu_custom_call" | custom-call | flops 2684354560 | bytes 10485760 | tf_op jit(solution)/shard_map/operator_3/pallas_call | solution.py:201
  149.5 5.1 %rest_3_0.1 = f32[8,256]{1,0:T(8,128)S(1)} custom-call(s32[128]{0:T(128)S(1)} %copy-done.7, s32[128]{0:T(128)S(1)} %copy-done.8, s32[128]{0:T(128)S(1)} %copy-done.9, s32[64]{0:T(128)S(1)} %copy-done.10, s32[64]{0:T(128)S(1)} %copy-done.11, s32[64]{0:T(128)S(1)} %copy-done.12, s32[4]{0:T(128)S(1)} %copy-done.13, bf16[16,8,256,128]{3,2,1,0:T(8,128)(2,1)S(1)} %bitcast.15, ...), custom_call_target="tpu_custom_call" | custom-call | flops 536870912 | bytes 12582912 | tf_op jit(solution)/shard_map/rest_3_0/pallas_call | solution.py:350
  154.6 1.8 %collective-permute-start.23 = (f32[24,256]{1,0:T(8,128)S(1)}, f32[24,256]{1,0:T(8,128)S(1)}, u32[]{:S(2)}, u32[]{:S(2)}) collective-permute-start(f32[24,256]{1,0:T(8,128)S(1)} %pad_maximum_fusion.6), channel_id=1, source_target_pairs={{0,4},{4,0},{8,12},{12,8},{16,20},{20,16},{24,28},{28,24},{1,5},{5... | collective-permute-start | bytes 73736 | tf_op jit(solution)/shard_map/ppermute | solution.py:400
  156.4 2.1 %collective-permute-done.23 = f32[24,256]{1,0:T(8,128)S(1)} collective-permute-done((f32[24,256]{1,0:T(8,128)S(1)}, f32[24,256]{1,0:T(8,128)S(1)}, u32[]{:S(2)}, u32[]{:S(2)}) %collective-permute-start.23) | collective-permute-done | bytes 24608 | tf_op jit(solution)/shard_map/ppermute | solution.py:400
  159.3 1.7 collective-permute-start.28
  163.4 1.6 collective-permute-done.28.refs_1_
  166.7 1.8 %collective-permute-start.32 = (f32[8,128]{1,0:T(8,128)S(1)}, f32[8,128]{1,0:T(8,128)S(1)}, u32[]{:S(2)}, u32[]{:S(2)}) collective-permute-start(f32[8,128]{1,0:T(8,128)S(1)} %get-tuple-element.140.refs_0_), channel_id=1, source_target_pairs={{0,2},{1,3},{2,0},{3,1},{4,6},{5,7},{6,4},{7,5},{8,10},{9,11},{10,... | collective-permute-start | bytes 12296 | tf_op jit(solution)/shard_map/ppermute | solution.py:400
  168.6 2.0 %scattered.1 = f32[2,2048,128]{2,1,0:T(8,128)} custom-call(f32[8,128]{1,0:T(8,128)S(1)} %get-tuple-element.137.coefs, f32[2,2048,128]{2,1,0:T(8,128)S(1)} %bitcast.27, f32[2048,256]{1,0:T(8,128)S(1)} %get-tuple-element.133.refs_12_.first.refs_4_, f32[2048,256]{1,0:T(8,128)S(1)} %get-tuple-element.134.refs_13_.second.refs_8_), custom_call_target="tpu_custom_call" | custom-call | bytes 8392704 | tf_op jit(solution)/shard_map/scattered/pallas_call | solution.py:674
  171.5 2.8 %trace.1 = f32[2048,128]{1,0:T(8,128)} custom-call(s32[4]{0:T(128)S(1)} %iota_xor_fusion.place, f32[2048,128]{1,0:T(8,128)S(1)} %get-tuple-element.138.here, f32[2048,128]{1,0:T(8,128)S(1)} %collective-permute-done.12.away, f32[8,128]{1,0:T(8,128)S(1)} %get-tuple-element.140.refs_0_, f32[8,128]{1,0:T(8,128)S(1)} %collective-permute-done.31.refs_1_, ...), custom_call_target="tpu_custom_call" | custom-call | bytes 19939328 | tf_op jit(solution)/shard_map/trace/pallas_call | solution.py:674
  (108 shorter events, 35.5 us)
Async XLA Ops:
  3.9 17.9 %collective-permute-start = (bf16[8,128,256]{2,1,0:T(8,128)(2,1)S(1)}, bf16[8,128,256]{2,1,0:T(8,128)(2,1)S(1)}, u32[]{:S(2)}, u32[]{:S(2)}) collective-permute-start(bf16[8,128,256]{2,1,0:T(8,128)(2,1)S(1)} %get-tuple-element.74.refs_5_), channel_id=1, source_target_pairs={{0,4},{4,0},{8,12},{12,8},{16,20},{20,16},{24,28},{28,24},{1,5},{5... | collective-permute-start | bytes 1572872 | tf_op jit(solution)/shard_map/ppermute | solution.py:400
  6.9 11.3 %collective-permute-start.1 = (bf16[4,128,256]{2,1,0:T(8,128)(2,1)}, bf16[4,128,256]{2,1,0:T(8,128)(2,1)S(1)}, u32[]{:S(2)}, u32[]{:S(2)}) collective-permute-start(bf16[4,128,256]{2,1,0:T(8,128)(2,1)} %get-tuple-element.75), channel_id=1, source_target_pairs={{0,8},{4,28},{8,16},{12,4},{16,24},{20,12},{24,0},{28,20},{1,9},{5... | collective-permute-start | bytes 786440 | tf_op jit(solution)/shard_map/ppermute | solution.py:411
  8.4 13.4 %collective-permute-start.2 = (bf16[4,128,256]{2,1,0:T(8,128)(2,1)}, bf16[4,128,256]{2,1,0:T(8,128)(2,1)}, u32[]{:S(2)}, u32[]{:S(2)}) collective-permute-start(bf16[4,128,256]{2,1,0:T(8,128)(2,1)} %get-tuple-element.75), channel_id=1, source_target_pairs={{0,24},{4,12},{8,0},{12,20},{16,8},{20,28},{24,16},{28,4},{1,25},{... | collective-permute-start | bytes 786440 | tf_op jit(solution)/shard_map/ppermute | solution.py:411
  21.9 20.7 %collective-permute-start.4 = (bf16[12,128,256]{2,1,0:T(8,128)(2,1)S(1)}, bf16[12,128,256]{2,1,0:T(8,128)(2,1)S(1)}, u32[]{:S(2)}, u32[]{:S(2)}) collective-permute-start(bf16[12,128,256]{2,1,0:T(8,128)(2,1)S(1)} %pad_maximum_fusion), channel_id=1, source_target_pairs={{0,8},{4,28},{8,16},{12,4},{16,24},{20,12},{24,0},{28,20},{1,9},{5... | collective-permute-start | bytes 2359304 | tf_op jit(solution)/shard_map/ppermute | solution.py:411
  24.0 18.8 %collective-permute-start.11 = (f32[2048,128]{1,0:T(8,128)S(1)}, f32[2048,128]{1,0:T(8,128)S(1)}, u32[]{:S(2)}, u32[]{:S(2)}) collective-permute-start(f32[2048,128]{1,0:T(8,128)S(1)} %get-tuple-element.116), channel_id=1, source_target_pairs={{0,1},{1,0},{2,3},{3,2},{4,5},{5,4},{6,7},{7,6},{8,9},{9,8},{10,11... | collective-permute-start | bytes 3145736 | tf_op jit(solution)/shard_map/ppermute | solution.py:400
  24.1 14.5 %collective-permute-start.3 = (bf16[8,128,256]{2,1,0:T(8,128)(2,1)S(1)}, bf16[8,128,256]{2,1,0:T(8,128)(2,1)S(1)}, u32[]{:S(2)}, u32[]{:S(2)}) collective-permute-start(bf16[8,128,256]{2,1,0:T(8,128)(2,1)S(1)} %copy-done.6), channel_id=1, source_target_pairs={{0,4},{4,0},{8,12},{12,8},{16,20},{20,16},{24,28},{28,24},{1,5},{5... | collective-permute-start | bytes 1572872 | tf_op jit(solution)/shard_map/ppermute | solution.py:400
  38.5 15.4 %collective-permute-start.5 = (bf16[8,128,256]{2,1,0:T(8,128)(2,1)S(1)}, bf16[8,128,256]{2,1,0:T(8,128)(2,1)S(1)}, u32[]{:S(2)}, u32[]{:S(2)}) collective-permute-start(bf16[8,128,256]{2,1,0:T(8,128)(2,1)S(1)} %collective-permute-done.3.refs_8_), channel_id=1, source_target_pairs={{0,8},{4,28},{8,16},{12,4},{16,24},{20,12},{24,0},{28,20},{1,9},{5... | collective-permute-start | bytes 1572872 | tf_op jit(solution)/shard_map/ppermute | solution.py:411
  42.7 12.3 %collective-permute-start.6 = (bf16[8,128,256]{2,1,0:T(8,128)(2,1)S(1)}, bf16[8,128,256]{2,1,0:T(8,128)(2,1)S(1)}, u32[]{:S(2)}, u32[]{:S(2)}) collective-permute-start(bf16[8,128,256]{2,1,0:T(8,128)(2,1)S(1)} %pad_maximum_fusion.3), channel_id=1, source_target_pairs={{0,4},{4,0},{8,12},{12,8},{16,20},{20,16},{24,28},{28,24},{1,5},{5... | collective-permute-start | bytes 1572872 | tf_op jit(solution)/shard_map/ppermute | solution.py:400
  43.6 26.9 %collective-permute-start.12 = (f32[2048,128]{1,0:T(8,128)S(1)}, f32[2048,128]{1,0:T(8,128)S(1)}, u32[]{:S(2)}, u32[]{:S(2)}) collective-permute-start(f32[2048,128]{1,0:T(8,128)S(1)} %get-tuple-element.117), channel_id=1, source_target_pairs={{0,2},{1,3},{2,0},{3,1},{4,6},{5,7},{6,4},{7,5},{8,10},{9,11},{10,... | collective-permute-start | bytes 3145736 | tf_op jit(solution)/shard_map/ppermute | solution.py:400
  57.6 12.7 %collective-permute-start.7 = (bf16[8,128,256]{2,1,0:T(8,128)(2,1)S(1)}, bf16[8,128,256]{2,1,0:T(8,128)(2,1)S(1)}, u32[]{:S(2)}, u32[]{:S(2)}) collective-permute-start(bf16[8,128,256]{2,1,0:T(8,128)(2,1)S(1)} %get-tuple-element.107.refs_5_), channel_id=1, source_target_pairs={{0,4},{4,0},{8,12},{12,8},{16,20},{20,16},{24,28},{28,24},{1,5},{5... | collective-permute-start | bytes 1572872 | tf_op jit(solution)/shard_map/ppermute | solution.py:400
  58.4 10.6 %collective-permute-start.8 = (bf16[4,128,256]{2,1,0:T(8,128)(2,1)S(1)}, bf16[4,128,256]{2,1,0:T(8,128)(2,1)S(1)}, u32[]{:S(2)}, u32[]{:S(2)}) collective-permute-start(bf16[4,128,256]{2,1,0:T(8,128)(2,1)S(1)} %get-tuple-element.109), channel_id=1, source_target_pairs={{0,8},{4,28},{8,16},{12,4},{16,24},{20,12},{24,0},{28,20},{1,9},{5... | collective-permute-start | bytes 786440 | tf_op jit(solution)/shard_map/ppermute | solution.py:411
  59.3 11.1 %collective-permute-start.9 = (bf16[4,128,256]{2,1,0:T(8,128)(2,1)S(1)}, bf16[4,128,256]{2,1,0:T(8,128)(2,1)S(1)}, u32[]{:S(2)}, u32[]{:S(2)}) collective-permute-start(bf16[4,128,256]{2,1,0:T(8,128)(2,1)S(1)} %get-tuple-element.109), channel_id=1, source_target_pairs={{0,24},{4,12},{8,0},{12,20},{16,8},{20,28},{24,16},{28,4},{1,25},{... | collective-permute-start | bytes 786440 | tf_op jit(solution)/shard_map/ppermute | solution.py:411
  69.0 43.1 %collective-permute-start.24 = (f32[2048,256]{1,0:T(8,128)S(1)}, f32[2048,256]{1,0:T(8,128)S(1)}, u32[]{:S(2)}, u32[]{:S(2)}) collective-permute-start(f32[2048,256]{1,0:T(8,128)S(1)} %get-tuple-element.133.refs_12_.first.refs_4_), channel_id=1, source_target_pairs={{0,2},{1,3},{2,0},{3,1},{4,6},{5,7},{6,4},{7,5},{8,10},{9,11},{10,... | collective-permute-start | bytes 6291464 | tf_op jit(solution)/shard_map/ppermute | solution.py:400
  70.5 20.3 %collective-permute-start.13 = (bf16[12,128,256]{2,1,0:T(8,128)(2,1)S(1)}, bf16[12,128,256]{2,1,0:T(8,128)(2,1)S(1)}, u32[]{:S(2)}, u32[]{:S(2)}) collective-permute-start(bf16[12,128,256]{2,1,0:T(8,128)(2,1)S(1)} %pad_maximum_fusion.1), channel_id=1, source_target_pairs={{0,8},{4,28},{8,16},{12,4},{16,24},{20,12},{24,0},{28,20},{1,9},{5... | collective-permute-start | bytes 2359304 | tf_op jit(solution)/shard_map/ppermute | solution.py:411
  71.9 13.1 %collective-permute-start.10 = (bf16[8,128,256]{2,1,0:T(8,128)(2,1)S(1)}, bf16[8,128,256]{2,1,0:T(8,128)(2,1)S(1)}, u32[]{:S(2)}, u32[]{:S(2)}) collective-permute-start(bf16[8,128,256]{2,1,0:T(8,128)(2,1)S(1)} %get-tuple-element.113.refs_6_), channel_id=1, source_target_pairs={{0,4},{4,0},{8,12},{12,8},{16,20},{20,16},{24,28},{28,24},{1,5},{5... | collective-permute-start | bytes 1572872 | tf_op jit(solution)/shard_map/ppermute | solution.py:400
  85.0 15.5 %collective-permute-start.14 = (bf16[8,128,256]{2,1,0:T(8,128)(2,1)S(1)}, bf16[8,128,256]{2,1,0:T(8,128)(2,1)S(1)}, u32[]{:S(2)}, u32[]{:S(2)}) collective-permute-start(bf16[8,128,256]{2,1,0:T(8,128)(2,1)S(1)} %collective-permute-done.10.refs_8_), channel_id=1, source_target_pairs={{0,8},{4,28},{8,16},{12,4},{16,24},{20,12},{24,0},{28,20},{1,9},{5... | collective-permute-start | bytes 1572872 | tf_op jit(solution)/shard_map/ppermute | solution.py:411
  90.8 10.3 %collective-permute-start.15 = (bf16[8,128,256]{2,1,0:T(8,128)(2,1)S(1)}, bf16[8,128,256]{2,1,0:T(8,128)(2,1)S(1)}, u32[]{:S(2)}, u32[]{:S(2)}) collective-permute-start(bf16[8,128,256]{2,1,0:T(8,128)(2,1)S(1)} %pad_maximum_fusion.4), channel_id=1, source_target_pairs={{0,4},{4,0},{8,12},{12,8},{16,20},{20,16},{24,28},{28,24},{1,5},{5... | collective-permute-start | bytes 1572872 | tf_op jit(solution)/shard_map/ppermute | solution.py:400
  103.7 13.7 %collective-permute-start.16 = (bf16[8,128,256]{2,1,0:T(8,128)(2,1)S(1)}, bf16[8,128,256]{2,1,0:T(8,128)(2,1)S(1)}, u32[]{:S(2)}, u32[]{:S(2)}) collective-permute-start(bf16[8,128,256]{2,1,0:T(8,128)(2,1)S(1)} %get-tuple-element.125.refs_5_), channel_id=1, source_target_pairs={{0,4},{4,0},{8,12},{12,8},{16,20},{20,16},{24,28},{28,24},{1,5},{5... | collective-permute-start | bytes 1572872 | tf_op jit(solution)/shard_map/ppermute | solution.py:400
  104.4 10.6 %collective-permute-start.17 = (bf16[4,128,256]{2,1,0:T(8,128)(2,1)S(1)}, bf16[4,128,256]{2,1,0:T(8,128)(2,1)S(1)}, u32[]{:S(2)}, u32[]{:S(2)}) collective-permute-start(bf16[4,128,256]{2,1,0:T(8,128)(2,1)S(1)} %get-tuple-element.127), channel_id=1, source_target_pairs={{0,8},{4,28},{8,16},{12,4},{16,24},{20,12},{24,0},{28,20},{1,9},{5... | collective-permute-start | bytes 786440 | tf_op jit(solution)/shard_map/ppermute | solution.py:411
  107.0 10.5 %collective-permute-start.18 = (bf16[4,128,256]{2,1,0:T(8,128)(2,1)S(1)}, bf16[4,128,256]{2,1,0:T(8,128)(2,1)S(1)}, u32[]{:S(2)}, u32[]{:S(2)}) collective-permute-start(bf16[4,128,256]{2,1,0:T(8,128)(2,1)S(1)} %get-tuple-element.127), channel_id=1, source_target_pairs={{0,24},{4,12},{8,0},{12,20},{16,8},{20,28},{24,16},{28,4},{1,25},{... | collective-permute-start | bytes 786440 | tf_op jit(solution)/shard_map/ppermute | solution.py:411
  111.1 47.4 %collective-permute-start.26 = (f32[2048,256]{1,0:T(8,128)S(1)}, f32[2048,256]{1,0:T(8,128)S(1)}, u32[]{:S(2)}, u32[]{:S(2)}) collective-permute-start(f32[2048,256]{1,0:T(8,128)S(1)} %get-tuple-element.134.refs_13_.second.refs_8_), channel_id=1, source_target_pairs={{0,1},{1,0},{2,3},{3,2},{4,5},{5,4},{6,7},{7,6},{8,9},{9,8},{10,11... | collective-permute-start | bytes 6291464 | tf_op jit(solution)/shard_map/ppermute | solution.py:400
  112.1 47.2 %collective-permute-start.25 = (f32[2048,256]{1,0:T(8,128)S(1)}, f32[2048,256]{1,0:T(8,128)S(1)}, u32[]{:S(2)}, u32[]{:S(2)}) collective-permute-start(f32[2048,256]{1,0:T(8,128)S(1)} %get-tuple-element.134.refs_13_.second.refs_8_), channel_id=1, source_target_pairs={{0,2},{1,3},{2,0},{3,1},{4,6},{5,7},{6,4},{7,5},{8,10},{9,11},{10,... | collective-permute-start | bytes 6291464 | tf_op jit(solution)/shard_map/ppermute | solution.py:400
  115.0 44.2 %collective-permute-start.27 = (f32[2048,256]{1,0:T(8,128)S(1)}, f32[2048,256]{1,0:T(8,128)S(1)}, u32[]{:S(2)}, u32[]{:S(2)}) collective-permute-start(f32[2048,256]{1,0:T(8,128)S(1)} %collective-permute-done.24.refs_6_), channel_id=1, source_target_pairs={{0,1},{1,0},{2,3},{3,2},{4,5},{5,4},{6,7},{7,6},{8,9},{9,8},{10,11... | collective-permute-start | bytes 6291464 | tf_op jit(solution)/shard_map/ppermute | solution.py:400
  117.5 22.3 %collective-permute-start.20 = (bf16[12,128,256]{2,1,0:T(8,128)(2,1)S(1)}, bf16[12,128,256]{2,1,0:T(8,128)(2,1)S(1)}, u32[]{:S(2)}, u32[]{:S(2)}) collective-permute-start(bf16[12,128,256]{2,1,0:T(8,128)(2,1)S(1)} %pad_maximum_fusion.2), channel_id=1, source_target_pairs={{0,8},{4,28},{8,16},{12,4},{16,24},{20,12},{24,0},{28,20},{1,9},{5... | collective-permute-start | bytes 2359304 | tf_op jit(solution)/shard_map/ppermute | solution.py:411
  117.9 12.3 %collective-permute-start.19 = (bf16[8,128,256]{2,1,0:T(8,128)(2,1)S(1)}, bf16[8,128,256]{2,1,0:T(8,128)(2,1)S(1)}, u32[]{:S(2)}, u32[]{:S(2)}) collective-permute-start(bf16[8,128,256]{2,1,0:T(8,128)(2,1)S(1)} %get-tuple-element.129.refs_6_), channel_id=1, source_target_pairs={{0,4},{4,0},{8,12},{12,8},{16,20},{20,16},{24,28},{28,24},{1,5},{5... | collective-permute-start | bytes 1572872 | tf_op jit(solution)/shard_map/ppermute | solution.py:400
  130.3 18.6 %collective-permute-start.21 = (bf16[8,128,256]{2,1,0:T(8,128)(2,1)S(1)}, bf16[8,128,256]{2,1,0:T(8,128)(2,1)S(1)}, u32[]{:S(2)}, u32[]{:S(2)}) collective-permute-start(bf16[8,128,256]{2,1,0:T(8,128)(2,1)S(1)} %collective-permute-done.19.refs_8_), channel_id=1, source_target_pairs={{0,8},{4,28},{8,16},{12,4},{16,24},{20,12},{24,0},{28,20},{1,9},{5... | collective-permute-start | bytes 1572872 | tf_op jit(solution)/shard_map/ppermute | solution.py:411
  139.9 9.5 %collective-permute-start.22 = (bf16[8,128,256]{2,1,0:T(8,128)(2,1)S(1)}, bf16[8,128,256]{2,1,0:T(8,128)(2,1)S(1)}, u32[]{:S(2)}, u32[]{:S(2)}) collective-permute-start(bf16[8,128,256]{2,1,0:T(8,128)(2,1)S(1)} %pad_maximum_fusion.5), channel_id=1, source_target_pairs={{0,4},{4,0},{8,12},{12,8},{16,20},{20,16},{24,28},{28,24},{1,5},{5... | collective-permute-start | bytes 1572872 | tf_op jit(solution)/shard_map/ppermute | solution.py:400
  156.4 14.2 %collective-permute-start.34 = (f32[2048,256]{1,0:T(8,128)S(1)}, f32[2048,256]{1,0:T(8,128)S(1)}, u32[]{:S(2)}, u32[]{:S(2)}) collective-permute-start(f32[2048,256]{1,0:T(8,128)S(1)} %get-tuple-element.133.refs_12_.first.refs_4_), channel_id=1, source_target_pairs={{0,1},{1,0},{2,3},{3,2},{4,5},{5,4},{6,7},{7,6},{8,9},{9,8},{10,11... | collective-permute-start | bytes 6291464 | tf_op jit(solution)/shard_map/ppermute | solution.py:400
  159.2 12.3 %collective-permute-start.35 = (f32[2048,256]{1,0:T(8,128)S(1)}, f32[2048,256]{1,0:T(8,128)S(1)}, u32[]{:S(2)}, u32[]{:S(2)}) collective-permute-start(f32[2048,256]{1,0:T(8,128)S(1)} %collective-permute-done.25.refs_10_), channel_id=1, source_target_pairs={{0,1},{1,0},{2,3},{3,2},{4,5},{5,4},{6,7},{7,6},{8,9},{9,8},{10,11... | collective-permute-start | bytes 6291464 | tf_op jit(solution)/shard_map/ppermute | solution.py:400
  159.3 5.7 %collective-permute-start.28 = (f32[24,256]{1,0:T(8,128)S(1)}, f32[24,256]{1,0:T(8,128)S(1)}, u32[]{:S(2)}, u32[]{:S(2)}) collective-permute-start(f32[24,256]{1,0:T(8,128)S(1)} %fusion.refs_0_), channel_id=1, source_target_pairs={{0,8},{4,12},{8,16},{12,20},{16,24},{20,28},{24,0},{28,4},{1,9},{5... | collective-permute-start | bytes 73736 | tf_op jit(solution)/shard_map/ppermute | solution.py:405
  161.0 4.9 %collective-permute-start.29 = (f32[24,256]{1,0:T(8,128)S(1)}, f32[24,256]{1,0:T(8,128)S(1)}, u32[]{:S(2)}, u32[]{:S(2)}) collective-permute-start(f32[24,256]{1,0:T(8,128)S(1)} %fusion.refs_0_), channel_id=1, source_target_pairs={{0,16},{4,20},{8,24},{12,28},{16,0},{20,4},{24,8},{28,12},{1,17},{... | collective-permute-start | bytes 73736 | tf_op jit(solution)/shard_map/ppermute | solution.py:405
  161.8 4.2 %collective-permute-start.30 = (f32[24,256]{1,0:T(8,128)S(1)}, f32[24,256]{1,0:T(8,128)S(1)}, u32[]{:S(2)}, u32[]{:S(2)}) collective-permute-start(f32[24,256]{1,0:T(8,128)S(1)} %fusion.refs_0_), channel_id=1, source_target_pairs={{0,24},{4,28},{8,0},{12,4},{16,8},{20,12},{24,16},{28,20},{1,25},{... | collective-permute-start | bytes 73736 | tf_op jit(solution)/shard_map/ppermute | solution.py:405
  (23 other events, 250.3 us)

commit v6 on v5

--- a/solution.py
+++ b/solution.py
@@ -28,19 +28,18 @@
     odd = lax.rem(me, 2)
     cut = nblocks // 2
     limits = (2 * nblocks + cut, 6 * front) if tuned_here else (3 * nblocks, count * front)
-    zeros = (nblocks - cut, 2 * front)
 
     def fill(i, carry):
-        for rows, mats, srcs, zero in (
-            (near_rows, near_mats, near_srcs, zeros[0]),
-            (edge_rows, edge_mats, edge_srcs, zeros[1]),
+        for rows, mats, srcs in (
+            (near_rows, near_mats, near_srcs),
+            (edge_rows, edge_mats, edge_srcs),
         ):
 
             @pl.when(i < rows.shape[0])
             def _():
                 rows[i] = 0
                 mats[i] = 0
-                srcs[i] = zero
+                srcs[i] = 0
 
         return carry
 
@@ -157,8 +156,8 @@
         acc[g - start] = jnp.dot(left, right, preferred_element_type=jnp.float32)
         return carry
 
-    lax.fori_loop(0, cut, functools.partial(row, acc_a, 0), 0, unroll=2)
-    lax.fori_loop(cut, nblocks, functools.partial(row, acc_b, cut), 0, unroll=2)
+    lax.fori_loop(0, cut, functools.partial(row, acc_a, 0), 0, unroll=4)
+    lax.fori_loop(cut, nblocks, functools.partial(row, acc_b, cut), 0, unroll=4)
     for copy in front_copies:
         copy.wait()
 
@@ -228,7 +227,7 @@
 
 def rest_kernel(step, part, sizes, moves, *refs):
     nblocks, span, width, front, start, nrows = sizes
-    near_moves, edge_moves, nparts = moves
+    nparts = moves
     lists, rest = refs[:7], refs[7:]
     near_v, crack_v, acc = rest[:3]
     parts, rest = rest[3 : 3 + nparts], rest[3 + nparts :]
@@ -244,16 +243,9 @@
     lanes = acc.shape[2]
     late = nparts > 0
     if late:
-        near_src, edge_src, extra, near_sem, edge_sem = rest
-        copies = block_copies(parts, near_moves, near_src, near_sem)
-        copies += block_copies(parts, edge_moves, edge_src, edge_sem)
-        for copy in copies:
-            copy.start()
+        near_src, edge_src = parts
+        (extra,) = rest
         extra[...] = jnp.zeros(extra.shape, jnp.float32)
-        for store in (near_src, edge_src):
-            store[store.shape[0] - 1] = jnp.zeros(store.shape[1:], store.dtype)
-        for copy in copies:
-            copy.wait()
 
         def add(half, rows, mats, srcs, number, matrix, source):
             offset = half * (rows.shape[0] // 2)
@@ -267,8 +259,9 @@
                     )
                     for spot in spots
                 ]
-                for spot, product in zip(spots, products):
-                    extra[rows[spot] + shift_by] += product
+                for k, (spot, product) in enumerate(zip(spots, products)):
+                    used = jnp.where(i * GROUP + k < number, 1.0, 0.0)
+                    extra[rows[spot] + shift_by] += used * product
                 return carry
 
             lax.fori_loop(0, (number + GROUP - 1) // GROUP, some, 0)
@@ -323,7 +316,7 @@
 
 
 def rest_call(step, part, front, tables, near, crack, found, acc, extras, before=()):
-    _, _, _, parts, near_moves, edge_moves = found
+    parts = found[3]
     nblocks, span = near.shape[:2]
     width, lanes = near.shape[3], acc.shape[2]
     nrows = acc.shape[0]
@@ -335,31 +328,22 @@
         low_a, low_b, head = low_shapes(nblocks, width, lanes, front)
         out_shape = [vector, *((low_a, head), (low_b,))[part], *out_shape]
     smem = pl.BlockSpec(memory_space=pltpu.SMEM)
-    anywhere = pl.BlockSpec(memory_space=pl.ANY)
     whole = pl.BlockSpec(memory_space=pltpu.VMEM)
     scratch, held = [], 0
     if parts:
-        shapes = (total_of(near_moves) + 1, total_of(edge_moves) + 1)
-        scratch = [pltpu.VMEM((n, width, lanes), jnp.bfloat16) for n in shapes]
-        scratch += [
-            pltpu.VMEM(acc.shape, jnp.float32),
-            pltpu.SemaphoreType.DMA((len(near_moves),)),
-            pltpu.SemaphoreType.DMA((len(edge_moves),)),
-        ]
-        held = 2 * sum(shapes) * width * lanes + 4 * acc.size
+        scratch = [pltpu.VMEM(acc.shape, jnp.float32)]
+        held = 4 * acc.size
     return pl.pallas_call(
         functools.partial(
             rest_kernel,
             step,
             part,
             (nblocks, span, width, front, start, nrows),
-            (near_moves, edge_moves, len(parts)),
+            len(parts),
         ),
         out_shape=tuple(out_shape),
         in_specs=[smem] * 7
-        + [whole] * 3
-        + [anywhere] * len(parts)
-        + [whole] * (len(extras) + len(before)),
+        + [whole] * (3 + len(parts) + len(extras) + len(before)),
         out_specs=tuple(whole for _ in out_shape),
         scratch_shapes=scratch,
         compiler_params=pltpu.CompilerParams(vmem_limit_bytes=held + 2 * MIB),
@@ -431,7 +415,7 @@
         every = lax.all_gather(head, "clu", axis=0, tiled=True)
         parts = [low, shift(low, "clu", -1), shift(low, "clu", 1), every]
         source_moves = tuple((k, 0, nblocks, k * nblocks) for k in range(3))
-        found = (parts, ((3, 0, count * front, 0),), source_moves, [], (), ())
+        found = (parts, ((3, 0, count * front, 0),), source_moves, [])
         return found, early_ties, late_ties, first_ties
     beside_a = swap(low_a, "clu", 1)
     same, *first_ties = tie(ring(head, 2), *first_ties)
@@ -460,7 +444,7 @@
         (4, 0, cut, 2 * nblocks),
     )
     last = [beyond_b, pairs]
-    found = (parts, front_moves, source_moves, last, ((0, 0, rest, 0),), ((1, 0, 2 * front, 0),))
+    found = (parts, front_moves, source_moves, last)
     return found, early_ties, late_ties, first_ties
 
 
@@ -759,9 +743,8 @@
     (sums_three,) = operate(3, found, (first, second))
     second_one = swap(second, "frq", 1)
     sums = jnp.concatenate([sums_one, sums_two, sums_three], axis=0)
-    sums, (second_across, second_one, first_three) = sum_over_clusters(
-        sums, second_across, second_one, first_three
-    )
+    sums, (second_one, first_three) = sum_over_clusters(sums, second_one, first_three)
+    *sums, second_across = tie(*sums, second_across)
     second_three = swap(second_across, "frq", 1)
     firsts = [first, first_one, first_across, first_three]
     seconds = [second, second_one, second_across, second_three]

time: 175 us -> 173 us (0.989)
  starting transfers between devices: 40.9 us -> 38.8 us
    pallas_call x3, Pallas kernels: 24.3 us -> 22.1 us  [main_call(): pl.pallas_call(functools.partial(main_kernel, (nblocks, span, edges), (fr...]
    ppermute x21, waiting for transfers between devices: 41.3 us -> 43.1 us  [swap(): return lax.ppermute(value, axis, [(i, i ^ distance) for i in range(count)])]
  transfers between devices with their start and end apart: 36 -> 36, of which waited for: 24 -> 22; matrix products, arithmetic and copies ran while one was open for 1% -> 1% of each run, Pallas kernels for 29% -> 29%
where the time goes in v6:
time: 173 us; the launch traced here: 172 us
  waiting for transfers between devices  75.4 us (44%)
  Pallas kernels  52.8 us (31%)
  starting transfers between devices  38.8 us (22%)
  local copies, waits for them, and re-layouts  3.2 us (2%)
    ppermute x21, waiting for transfers between devices, swap(): return lax.ppermute(value, axis, [(i, i ^ distance) for i in range(count)])  43.1 us
    ppermute x12, waiting for transfers between devices, ring(): return lax.ppermute(value, 'clu', pairs)  30 us
    pallas_call x3, Pallas kernels, main_call(): pl.pallas_call(functools.partial(main_kernel, (nblocks, span, edges), (fr...  22.1 us
    ppermute x21, starting transfers between devices, swap(): return lax.ppermute(value, axis, [(i, i ^ distance) for i in range(count)])  18.9 us
    ppermute x12, starting transfers between devices, ring(): return lax.ppermute(value, 'clu', pairs)  16.1 us
    pallas_call x5, Pallas kernels, rest_call(): pl.pallas_call(functools.partial(rest_kernel, step, part, (nblocks, span,...  16.1 us
    pallas_call x7, Pallas kernels, on_vmem(): pl.pallas_call(body, out_shape=out_shape, in_specs=[smem] * len(smem_args...  8.22 us
    pallas_call x1, Pallas kernels, table_call(): pl.pallas_call(functools.partial(table_kernel, sizes), out_shape=tuple((j...  6.41 us
  transfers between devices with their start and end apart: 36, of which 22 were waited for; matrix products, arithmetic and copies ran while one was open for 1% of the time, Pallas kernels for 29%

profile of v6, /device:TPU:0, one launch (start us, length us, event | category | flops | bytes accessed | tf_op | source)
XLA Modules:
  0.0 171.6 jit_solution(7834115729750972799)
XLA Ops:
  0.7 1.6 copy-done.2
  3.9 2.9 %collective-permute-start = (bf16[8,128,256]{2,1,0:T(8,128)(2,1)S(1)}, bf16[8,128,256]{2,1,0:T(8,128)(2,1)S(1)}, u32[]{:S(2)}, u32[]{:S(2)}) collective-permute-start(bf16[8,128,256]{2,1,0:T(8,128)(2,1)S(1)} %get-tuple-element.78.refs_5_), channel_id=1, source_target_pairs={{0,4},{4,0},{8,12},{12,8},{16,20},{20,16},{24,28},{28,24},{1,5},{5... | collective-permute-start | bytes 1572872 | tf_op jit(solution)/shard_map/ppermute | solution.py:384
  8.4 2.2 %collective-permute-start.2 = (bf16[4,128,256]{2,1,0:T(8,128)(2,1)}, bf16[4,128,256]{2,1,0:T(8,128)(2,1)}, u32[]{:S(2)}, u32[]{:S(2)}) collective-permute-start(bf16[4,128,256]{2,1,0:T(8,128)(2,1)} %get-tuple-element.79), channel_id=1, source_target_pairs={{0,24},{4,12},{8,0},{12,20},{16,8},{20,28},{24,16},{28,4},{1,25},{... | collective-permute-start | bytes 786440 | tf_op jit(solution)/shard_map/ppermute | solution.py:395
  11.4 6.4 %tables.1 = (s32[128]{0:T(128)}, s32[32]{0:T(128)}, s32[128]{0:T(128)}, s32[128]{0:T(128)}, s32[128]{0:T(128)}, /*index=5*/s32[64]{0:T(128)}, s32[64]{0:T(128)}, s32[64]{0:T(128)}, s32[4]{0:T(128)}) custom-call(s32[1]{0:T(128)} %bitcast.1.place, s32[128]{0:T(128)} %reshape.17.pattern, s32[32]{0:T(128)} %bitcast.31, s32[32]{0:T(128)} %source.1, s32[32]{0:T(128)} %refs_2_.5), custom_call_target="tpu_custom_call" | custom-call | tf_op jit(solution)/shard_map/tables/pallas_call | solution.py:109
  18.2 3.7 %collective-permute-done.2.refs_11_ = bf16[4,128,256]{2,1,0:T(8,128)(2,1)} collective-permute-done((bf16[4,128,256]{2,1,0:T(8,128)(2,1)}, bf16[4,128,256]{2,1,0:T(8,128)(2,1)}, u32[]{:S(2)}, u32[]{:S(2)}) %collective-permute-start.2) | collective-permute-done | bytes 262176 | tf_op jit(solution)/shard_map/ppermute | solution.py:395
  24.1 1.9 %collective-permute-start.3 = (bf16[8,128,256]{2,1,0:T(8,128)(2,1)S(1)}, bf16[8,128,256]{2,1,0:T(8,128)(2,1)S(1)}, u32[]{:S(2)}, u32[]{:S(2)}) collective-permute-start(bf16[8,128,256]{2,1,0:T(8,128)(2,1)S(1)} %copy-done.6), channel_id=1, source_target_pairs={{0,4},{4,0},{8,12},{12,8},{16,20},{20,16},{24,28},{28,24},{1,5},{5... | collective-permute-start | bytes 1572872 | tf_op jit(solution)/shard_map/ppermute | solution.py:384
  26.3 12.2 %collective-permute-done.3.refs_8_ = bf16[8,128,256]{2,1,0:T(8,128)(2,1)S(1)} collective-permute-done((bf16[8,128,256]{2,1,0:T(8,128)(2,1)S(1)}, bf16[8,128,256]{2,1,0:T(8,128)(2,1)S(1)}, u32[]{:S(2)}, u32[]{:S(2)}) %collective-permute-start.3) | collective-permute-done | bytes 524320 | tf_op jit(solution)/shard_map/ppermute | solution.py:384
  39.0 3.6 %collective-permute-done.4.refs_9_ = bf16[12,128,256]{2,1,0:T(8,128)(2,1)S(1)} collective-permute-done((bf16[12,128,256]{2,1,0:T(8,128)(2,1)S(1)}, bf16[12,128,256]{2,1,0:T(8,128)(2,1)S(1)}, u32[]{:S(2)}, u32[]{:S(2)}) %collective-permute-start.4) | collective-permute-done | bytes 786464 | tf_op jit(solution)/shard_map/ppermute | solution.py:395
  45.2 7.4 %operator_1.1 = (f32[8,256,256]{2,1,0:T(8,128)S(1)}, f32[8,256,256]{2,1,0:T(8,128)S(1)}) custom-call(s32[128]{0:T(128)S(1)} %copy-done.15, s32[32]{0:T(128)S(1)} %copy-done.16, s32[32]{0:T(128)S(1)} %copy-done.14, bf16[16,8,256,128]{3,2,1,0:T(8,128)(2,1)S(1)} %bitcast.8, bf16[32,256,128]{2,1,0:T(8,128)(2,1)S(1)} %bitcast.16, ...), custom_call_target="tpu_custom_call" | custom-call | flops 2684354560 | bytes 10485760 | tf_op jit(solution)/shard_map/operator_1/pallas_call | solution.py:200
  55.1 2.5 %rest_1_0.1 = (f32[1024,256]{1,0:T(8,128)S(1)}, bf16[8,128,256]{2,1,0:T(8,128)(2,1)S(1)}, bf16[4,128,256]{2,1,0:T(8,128)(2,1)S(1)}, f32[8,256]{1,0:T(8,128)S(1)}) custom-call(s32[128]{0:T(128)S(1)} %copy-done.7, s32[128]{0:T(128)S(1)} %copy-done.8, s32[128]{0:T(128)S(1)} %copy-done.9, s32[64]{0:T(128)S(1)} %copy-done.10, s32[64]{0:T(128)S(1)} %copy-done.11, ...), custom_call_target="tpu_custom_call" | custom-call | flops 268435456 | bytes 6291456 | tf_op jit(solution)/shard_map/rest_1_0/pallas_call | solution.py:336
  58.6 2.9 %collective-permute-start.9 = (bf16[4,128,256]{2,1,0:T(8,128)(2,1)S(1)}, bf16[4,128,256]{2,1,0:T(8,128)(2,1)S(1)}, u32[]{:S(2)}, u32[]{:S(2)}) collective-permute-start(bf16[4,128,256]{2,1,0:T(8,128)(2,1)S(1)} %get-tuple-element.113), channel_id=1, source_target_pairs={{0,24},{4,12},{8,0},{12,20},{16,8},{20,28},{24,16},{28,4},{1,25},{... | collective-permute-start | bytes 786440 | tf_op jit(solution)/shard_map/ppermute | solution.py:395
  61.5 2.8 %rest_1_1.1 = (f32[2048,256]{1,0:T(8,128)S(1)}, bf16[8,128,256]{2,1,0:T(8,128)(2,1)S(1)}, f32[8,256]{1,0:T(8,128)S(1)}) custom-call(s32[128]{0:T(128)S(1)} %copy-done.7, s32[128]{0:T(128)S(1)} %copy-done.8, s32[128]{0:T(128)S(1)} %copy-done.9, s32[64]{0:T(128)S(1)} %copy-done.10, s32[64]{0:T(128)S(1)} %copy-done.11, s32[64]{0:T(128)S(1)} %copy-done.12, ...), custom_call_target="tpu_custom_call" | custom-call | flops 268435456 | bytes 6291456 | tf_op jit(solution)/shard_map/rest_1_1/pallas_call | solution.py:336
  64.4 4.1 %collective-permute-done.8.refs_10_ = bf16[4,128,256]{2,1,0:T(8,128)(2,1)S(1)} collective-permute-done((bf16[4,128,256]{2,1,0:T(8,128)(2,1)S(1)}, bf16[4,128,256]{2,1,0:T(8,128)(2,1)S(1)}, u32[]{:S(2)}, u32[]{:S(2)}) %collective-permute-start.8) | collective-permute-done | bytes 262176 | tf_op jit(solution)/shard_map/ppermute | solution.py:395
  71.2 1.7 collective-permute-start.10
  72.9 11.1 %collective-permute-done.10.refs_8_ = bf16[8,128,256]{2,1,0:T(8,128)(2,1)S(1)} collective-permute-done((bf16[8,128,256]{2,1,0:T(8,128)(2,1)S(1)}, bf16[8,128,256]{2,1,0:T(8,128)(2,1)S(1)}, u32[]{:S(2)}, u32[]{:S(2)}) %collective-permute-start.10) | collective-permute-done | bytes 524320 | tf_op jit(solution)/shard_map/ppermute | solution.py:384
  84.4 5.1 %collective-permute-done.13.refs_9_ = bf16[12,128,256]{2,1,0:T(8,128)(2,1)S(1)} collective-permute-done((bf16[12,128,256]{2,1,0:T(8,128)(2,1)S(1)}, bf16[12,128,256]{2,1,0:T(8,128)(2,1)S(1)}, u32[]{:S(2)}, u32[]{:S(2)}) %collective-permute-start.13) | collective-permute-done | bytes 786464 | tf_op jit(solution)/shard_map/ppermute | solution.py:395
  89.6 2.3 %collective-permute-start.15 = (bf16[8,128,256]{2,1,0:T(8,128)(2,1)S(1)}, bf16[8,128,256]{2,1,0:T(8,128)(2,1)S(1)}, u32[]{:S(2)}, u32[]{:S(2)}) collective-permute-start(bf16[8,128,256]{2,1,0:T(8,128)(2,1)S(1)} %pad_maximum_fusion.4), channel_id=1, source_target_pairs={{0,4},{4,0},{8,12},{12,8},{16,20},{20,16},{24,28},{28,24},{1,5},{5... | collective-permute-start | bytes 1572872 | tf_op jit(solution)/shard_map/ppermute | solution.py:384
  91.9 7.4 %operator_2.1 = (f32[8,256,256]{2,1,0:T(8,128)S(1)}, f32[8,256,256]{2,1,0:T(8,128)S(1)}) custom-call(s32[128]{0:T(128)S(1)} %copy-done.15, s32[32]{0:T(128)S(1)} %copy-done.16, s32[32]{0:T(128)S(1)} %copy-done.14, bf16[16,8,256,128]{3,2,1,0:T(8,128)(2,1)S(1)} %bitcast.11, bf16[32,256,128]{2,1,0:T(8,128)(2,1)S(1)} %bitcast.19, ...), custom_call_target="tpu_custom_call" | custom-call | flops 2684354560 | bytes 10485760 | tf_op jit(solution)/shard_map/operator_2/pallas_call | solution.py:200
  99.8 2.6 %rest_2_0.1 = (f32[1024,256]{1,0:T(8,128)S(1)}, bf16[8,128,256]{2,1,0:T(8,128)(2,1)S(1)}, bf16[4,128,256]{2,1,0:T(8,128)(2,1)S(1)}, f32[8,256]{1,0:T(8,128)S(1)}) custom-call(s32[128]{0:T(128)S(1)} %copy-done.7, s32[128]{0:T(128)S(1)} %copy-done.8, s32[128]{0:T(128)S(1)} %copy-done.9, s32[64]{0:T(128)S(1)} %copy-done.10, s32[64]{0:T(128)S(1)} %copy-done.11, ...), custom_call_target="tpu_custom_call" | custom-call | flops 268435456 | bytes 6291456 | tf_op jit(solution)/shard_map/rest_2_0/pallas_call | solution.py:336
  103.4 2.6 %collective-permute-start.17 = (bf16[4,128,256]{2,1,0:T(8,128)(2,1)S(1)}, bf16[4,128,256]{2,1,0:T(8,128)(2,1)S(1)}, u32[]{:S(2)}, u32[]{:S(2)}) collective-permute-start(bf16[4,128,256]{2,1,0:T(8,128)(2,1)S(1)} %get-tuple-element.131), channel_id=1, source_target_pairs={{0,8},{4,28},{8,16},{12,4},{16,24},{20,12},{24,0},{28,20},{1,9},{5... | collective-permute-start | bytes 786440 | tf_op jit(solution)/shard_map/ppermute | solution.py:395
  107.2 2.9 %rest_2_1.1 = (f32[2048,256]{1,0:T(8,128)S(1)}, bf16[8,128,256]{2,1,0:T(8,128)(2,1)S(1)}, f32[8,256]{1,0:T(8,128)S(1)}) custom-call(s32[128]{0:T(128)S(1)} %copy-done.7, s32[128]{0:T(128)S(1)} %copy-done.8, s32[128]{0:T(128)S(1)} %copy-done.9, s32[64]{0:T(128)S(1)} %copy-done.10, s32[64]{0:T(128)S(1)} %copy-done.11, s32[64]{0:T(128)S(1)} %copy-done.12, ...), custom_call_target="tpu_custom_call" | custom-call | flops 268435456 | bytes 6291456 | tf_op jit(solution)/shard_map/rest_2_1/pallas_call | solution.py:336
  110.1 1.9 %collective-permute-done.25.refs_6_ = f32[2048,256]{1,0:T(8,128)S(1)} collective-permute-done((f32[2048,256]{1,0:T(8,128)S(1)}, f32[2048,256]{1,0:T(8,128)S(1)}, u32[]{:S(2)}, u32[]{:S(2)}) %collective-permute-start.25) | collective-permute-done | bytes 2097184 | tf_op jit(solution)/shard_map/ppermute | solution.py:384
  116.9 1.9 %collective-permute-start.19 = (bf16[8,128,256]{2,1,0:T(8,128)(2,1)S(1)}, bf16[8,128,256]{2,1,0:T(8,128)(2,1)S(1)}, u32[]{:S(2)}, u32[]{:S(2)}) collective-permute-start(bf16[8,128,256]{2,1,0:T(8,128)(2,1)S(1)} %get-tuple-element.133.refs_6_), channel_id=1, source_target_pairs={{0,4},{4,0},{8,12},{12,8},{16,20},{20,16},{24,28},{28,24},{1,5},{5... | collective-permute-start | bytes 1572872 | tf_op jit(solution)/shard_map/ppermute | solution.py:384
  118.8 10.5 %collective-permute-done.19.refs_8_ = bf16[8,128,256]{2,1,0:T(8,128)(2,1)S(1)} collective-permute-done((bf16[8,128,256]{2,1,0:T(8,128)(2,1)S(1)}, bf16[8,128,256]{2,1,0:T(8,128)(2,1)S(1)}, u32[]{:S(2)}, u32[]{:S(2)}) %collective-permute-start.19) | collective-permute-done | bytes 524320 | tf_op jit(solution)/shard_map/ppermute | solution.py:384
  129.7 8.5 %collective-permute-done.20.refs_9_ = bf16[12,128,256]{2,1,0:T(8,128)(2,1)S(1)} collective-permute-done((bf16[12,128,256]{2,1,0:T(8,128)(2,1)S(1)}, bf16[12,128,256]{2,1,0:T(8,128)(2,1)S(1)}, u32[]{:S(2)}, u32[]{:S(2)}) %collective-permute-start.20) | collective-permute-done | bytes 786464 | tf_op jit(solution)/shard_map/ppermute | solution.py:395
  138.4 7.3 %operator_3.1.refs_9_ = f32[16,256,256]{2,1,0:T(8,128)S(1)} custom-call(s32[128]{0:T(128)S(1)} %copy-done.15, s32[32]{0:T(128)S(1)} %copy-done.16, s32[32]{0:T(128)S(1)} %copy-done.14, bf16[16,8,256,128]{3,2,1,0:T(8,128)(2,1)S(1)} %bitcast.14, bf16[32,256,128]{2,1,0:T(8,128)(2,1)S(1)} %bitcast.22, bf16[8,128,256]{2,1,0:T(8,128)(2,1)S(1)} %get-tuple-element.129.refs_5_, ...), custom_call_target="tpu_custom_call" | custom-call | flops 2684354560 | bytes 10485760 | tf_op jit(solution)/shard_map/operator_3/pallas_call | solution.py:200
  147.5 5.3 %rest_3_0.1 = f32[8,256]{1,0:T(8,128)S(1)} custom-call(s32[128]{0:T(128)S(1)} %copy-done.7, s32[128]{0:T(128)S(1)} %copy-done.8, s32[128]{0:T(128)S(1)} %copy-done.9, s32[64]{0:T(128)S(1)} %copy-done.10, s32[64]{0:T(128)S(1)} %copy-done.11, s32[64]{0:T(128)S(1)} %copy-done.12, s32[4]{0:T(128)S(1)} %copy-done.13, bf16[16,8,256,128]{3,2,1,0:T(8,128)(2,1)S(1)} %bitcast.15, ...), custom_call_target="tpu_custom_call" | custom-call | flops 536870912 | bytes 12582912 | tf_op jit(solution)/shard_map/rest_3_0/pallas_call | solution.py:336
  153.0 3.8 %collective-permute-done.23 = f32[24,256]{1,0:T(8,128)S(1)} collective-permute-done((f32[24,256]{1,0:T(8,128)S(1)}, f32[24,256]{1,0:T(8,128)S(1)}, u32[]{:S(2)}, u32[]{:S(2)}) %collective-permute-start.23) | collective-permute-done | bytes 24608 | tf_op jit(solution)/shard_map/ppermute | solution.py:384
  158.3 2.4 %collective-permute-start.29 = (f32[24,256]{1,0:T(8,128)S(1)}, f32[24,256]{1,0:T(8,128)S(1)}, u32[]{:S(2)}, u32[]{:S(2)}) collective-permute-start(f32[24,256]{1,0:T(8,128)S(1)} %fusion.refs_0_), channel_id=1, source_target_pairs={{0,24},{4,28},{8,0},{12,4},{16,8},{20,12},{24,16},{28,20},{1,25},{... | collective-permute-start | bytes 73736 | tf_op jit(solution)/shard_map/ppermute | solution.py:389
  160.7 1.8 %collective-permute-done.27.refs_1_ = f32[24,256]{1,0:T(8,128)S(1)} collective-permute-done((f32[24,256]{1,0:T(8,128)S(1)}, f32[24,256]{1,0:T(8,128)S(1)}, u32[]{:S(2)}, u32[]{:S(2)}) %collective-permute-start.27) | collective-permute-done | bytes 24608 | tf_op jit(solution)/shard_map/ppermute | solution.py:389
  165.8 2.0 %scattered.1 = f32[2,2048,128]{2,1,0:T(8,128)} custom-call(f32[8,128]{1,0:T(8,128)S(1)} %get-tuple-element.145.coefs, f32[2,2048,128]{2,1,0:T(8,128)S(1)} %bitcast.27, f32[2048,256]{1,0:T(8,128)S(1)} %get-tuple-element.137.refs_12_.first.refs_4_, f32[2048,256]{1,0:T(8,128)S(1)} %get-tuple-element.140.refs_13_.second.refs_8_), custom_call_target="tpu_custom_call" | custom-call | bytes 8392704 | tf_op jit(solution)/shard_map/scattered/pallas_call | solution.py:658
  168.8 2.8 %trace.1 = f32[2048,128]{1,0:T(8,128)} custom-call(s32[4]{0:T(128)S(1)} %iota_xor_fusion.place, f32[2048,128]{1,0:T(8,128)S(1)} %get-tuple-element.146.here, f32[2048,128]{1,0:T(8,128)S(1)} %collective-permute-done.12.away, f32[8,128]{1,0:T(8,128)S(1)} %get-tuple-element.148.refs_0_, f32[8,128]{1,0:T(8,128)S(1)} %collective-permute-done.31.refs_1_, ...), custom_call_target="tpu_custom_call" | custom-call | bytes 19939328 | tf_op jit(solution)/shard_map/trace/pallas_call | solution.py:658
  (108 shorter events, 32.3 us)
Async XLA Ops:
  3.9 17.9 %collective-permute-start = (bf16[8,128,256]{2,1,0:T(8,128)(2,1)S(1)}, bf16[8,128,256]{2,1,0:T(8,128)(2,1)S(1)}, u32[]{:S(2)}, u32[]{:S(2)}) collective-permute-start(bf16[8,128,256]{2,1,0:T(8,128)(2,1)S(1)} %get-tuple-element.78.refs_5_), channel_id=1, source_target_pairs={{0,4},{4,0},{8,12},{12,8},{16,20},{20,16},{24,28},{28,24},{1,5},{5... | collective-permute-start | bytes 1572872 | tf_op jit(solution)/shard_map/ppermute | solution.py:384
  6.9 11.3 %collective-permute-start.1 = (bf16[4,128,256]{2,1,0:T(8,128)(2,1)}, bf16[4,128,256]{2,1,0:T(8,128)(2,1)S(1)}, u32[]{:S(2)}, u32[]{:S(2)}) collective-permute-start(bf16[4,128,256]{2,1,0:T(8,128)(2,1)} %get-tuple-element.79), channel_id=1, source_target_pairs={{0,8},{4,28},{8,16},{12,4},{16,24},{20,12},{24,0},{28,20},{1,9},{5... | collective-permute-start | bytes 786440 | tf_op jit(solution)/shard_map/ppermute | solution.py:395
  8.4 13.4 %collective-permute-start.2 = (bf16[4,128,256]{2,1,0:T(8,128)(2,1)}, bf16[4,128,256]{2,1,0:T(8,128)(2,1)}, u32[]{:S(2)}, u32[]{:S(2)}) collective-permute-start(bf16[4,128,256]{2,1,0:T(8,128)(2,1)} %get-tuple-element.79), channel_id=1, source_target_pairs={{0,24},{4,12},{8,0},{12,20},{16,8},{20,28},{24,16},{28,4},{1,25},{... | collective-permute-start | bytes 786440 | tf_op jit(solution)/shard_map/ppermute | solution.py:395
  21.9 20.7 %collective-permute-start.4 = (bf16[12,128,256]{2,1,0:T(8,128)(2,1)S(1)}, bf16[12,128,256]{2,1,0:T(8,128)(2,1)S(1)}, u32[]{:S(2)}, u32[]{:S(2)}) collective-permute-start(bf16[12,128,256]{2,1,0:T(8,128)(2,1)S(1)} %pad_maximum_fusion), channel_id=1, source_target_pairs={{0,8},{4,28},{8,16},{12,4},{16,24},{20,12},{24,0},{28,20},{1,9},{5... | collective-permute-start | bytes 2359304 | tf_op jit(solution)/shard_map/ppermute | solution.py:395
  24.0 18.8 %collective-permute-start.11 = (f32[2048,128]{1,0:T(8,128)S(1)}, f32[2048,128]{1,0:T(8,128)S(1)}, u32[]{:S(2)}, u32[]{:S(2)}) collective-permute-start(f32[2048,128]{1,0:T(8,128)S(1)} %get-tuple-element.120), channel_id=1, source_target_pairs={{0,1},{1,0},{2,3},{3,2},{4,5},{5,4},{6,7},{7,6},{8,9},{9,8},{10,11... | collective-permute-start | bytes 3145736 | tf_op jit(solution)/shard_map/ppermute | solution.py:384
  24.1 14.5 %collective-permute-start.3 = (bf16[8,128,256]{2,1,0:T(8,128)(2,1)S(1)}, bf16[8,128,256]{2,1,0:T(8,128)(2,1)S(1)}, u32[]{:S(2)}, u32[]{:S(2)}) collective-permute-start(bf16[8,128,256]{2,1,0:T(8,128)(2,1)S(1)} %copy-done.6), channel_id=1, source_target_pairs={{0,4},{4,0},{8,12},{12,8},{16,20},{20,16},{24,28},{28,24},{1,5},{5... | collective-permute-start | bytes 1572872 | tf_op jit(solution)/shard_map/ppermute | solution.py:384
  38.5 15.4 %collective-permute-start.5 = (bf16[8,128,256]{2,1,0:T(8,128)(2,1)S(1)}, bf16[8,128,256]{2,1,0:T(8,128)(2,1)S(1)}, u32[]{:S(2)}, u32[]{:S(2)}) collective-permute-start(bf16[8,128,256]{2,1,0:T(8,128)(2,1)S(1)} %collective-permute-done.3.refs_8_), channel_id=1, source_target_pairs={{0,8},{4,28},{8,16},{12,4},{16,24},{20,12},{24,0},{28,20},{1,9},{5... | collective-permute-start | bytes 1572872 | tf_op jit(solution)/shard_map/ppermute | solution.py:395
  42.7 12.3 %collective-permute-start.6 = (bf16[8,128,256]{2,1,0:T(8,128)(2,1)S(1)}, bf16[8,128,256]{2,1,0:T(8,128)(2,1)S(1)}, u32[]{:S(2)}, u32[]{:S(2)}) collective-permute-start(bf16[8,128,256]{2,1,0:T(8,128)(2,1)S(1)} %pad_maximum_fusion.3), channel_id=1, source_target_pairs={{0,4},{4,0},{8,12},{12,8},{16,20},{20,16},{24,28},{28,24},{1,5},{5... | collective-permute-start | bytes 1572872 | tf_op jit(solution)/shard_map/ppermute | solution.py:384
  43.6 26.5 %collective-permute-start.12 = (f32[2048,128]{1,0:T(8,128)S(1)}, f32[2048,128]{1,0:T(8,128)S(1)}, u32[]{:S(2)}, u32[]{:S(2)}) collective-permute-start(f32[2048,128]{1,0:T(8,128)S(1)} %get-tuple-element.121), channel_id=1, source_target_pairs={{0,2},{1,3},{2,0},{3,1},{4,6},{5,7},{6,4},{7,5},{8,10},{9,11},{10,... | collective-permute-start | bytes 3145736 | tf_op jit(solution)/shard_map/ppermute | solution.py:384
  57.6 12.4 %collective-permute-start.7 = (bf16[8,128,256]{2,1,0:T(8,128)(2,1)S(1)}, bf16[8,128,256]{2,1,0:T(8,128)(2,1)S(1)}, u32[]{:S(2)}, u32[]{:S(2)}) collective-permute-start(bf16[8,128,256]{2,1,0:T(8,128)(2,1)S(1)} %get-tuple-element.111.refs_5_), channel_id=1, source_target_pairs={{0,4},{4,0},{8,12},{12,8},{16,20},{20,16},{24,28},{28,24},{1,5},{5... | collective-permute-start | bytes 1572872 | tf_op jit(solution)/shard_map/ppermute | solution.py:384
  57.6 10.8 %collective-permute-start.8 = (bf16[4,128,256]{2,1,0:T(8,128)(2,1)S(1)}, bf16[4,128,256]{2,1,0:T(8,128)(2,1)S(1)}, u32[]{:S(2)}, u32[]{:S(2)}) collective-permute-start(bf16[4,128,256]{2,1,0:T(8,128)(2,1)S(1)} %get-tuple-element.113), channel_id=1, source_target_pairs={{0,8},{4,28},{8,16},{12,4},{16,24},{20,12},{24,0},{28,20},{1,9},{5... | collective-permute-start | bytes 786440 | tf_op jit(solution)/shard_map/ppermute | solution.py:395
  58.6 11.4 %collective-permute-start.9 = (bf16[4,128,256]{2,1,0:T(8,128)(2,1)S(1)}, bf16[4,128,256]{2,1,0:T(8,128)(2,1)S(1)}, u32[]{:S(2)}, u32[]{:S(2)}) collective-permute-start(bf16[4,128,256]{2,1,0:T(8,128)(2,1)S(1)} %get-tuple-element.113), channel_id=1, source_target_pairs={{0,24},{4,12},{8,0},{12,20},{16,8},{20,28},{24,16},{28,4},{1,25},{... | collective-permute-start | bytes 786440 | tf_op jit(solution)/shard_map/ppermute | solution.py:395
  68.4 43.6 %collective-permute-start.25 = (f32[2048,256]{1,0:T(8,128)S(1)}, f32[2048,256]{1,0:T(8,128)S(1)}, u32[]{:S(2)}, u32[]{:S(2)}) collective-permute-start(f32[2048,256]{1,0:T(8,128)S(1)} %get-tuple-element.137.refs_12_.first.refs_4_), channel_id=1, source_target_pairs={{0,2},{1,3},{2,0},{3,1},{4,6},{5,7},{6,4},{7,5},{8,10},{9,11},{10,... | collective-permute-start | bytes 6291464 | tf_op jit(solution)/shard_map/ppermute | solution.py:384
  70.1 19.5 %collective-permute-start.13 = (bf16[12,128,256]{2,1,0:T(8,128)(2,1)S(1)}, bf16[12,128,256]{2,1,0:T(8,128)(2,1)S(1)}, u32[]{:S(2)}, u32[]{:S(2)}) collective-permute-start(bf16[12,128,256]{2,1,0:T(8,128)(2,1)S(1)} %pad_maximum_fusion.1), channel_id=1, source_target_pairs={{0,8},{4,28},{8,16},{12,4},{16,24},{20,12},{24,0},{28,20},{1,9},{5... | collective-permute-start | bytes 2359304 | tf_op jit(solution)/shard_map/ppermute | solution.py:395
  71.2 12.8 %collective-permute-start.10 = (bf16[8,128,256]{2,1,0:T(8,128)(2,1)S(1)}, bf16[8,128,256]{2,1,0:T(8,128)(2,1)S(1)}, u32[]{:S(2)}, u32[]{:S(2)}) collective-permute-start(bf16[8,128,256]{2,1,0:T(8,128)(2,1)S(1)} %get-tuple-element.117.refs_6_), channel_id=1, source_target_pairs={{0,4},{4,0},{8,12},{12,8},{16,20},{20,16},{24,28},{28,24},{1,5},{5... | collective-permute-start | bytes 1572872 | tf_op jit(solution)/shard_map/ppermute | solution.py:384
  84.1 15.2 %collective-permute-start.14 = (bf16[8,128,256]{2,1,0:T(8,128)(2,1)S(1)}, bf16[8,128,256]{2,1,0:T(8,128)(2,1)S(1)}, u32[]{:S(2)}, u32[]{:S(2)}) collective-permute-start(bf16[8,128,256]{2,1,0:T(8,128)(2,1)S(1)} %collective-permute-done.10.refs_8_), channel_id=1, source_target_pairs={{0,8},{4,28},{8,16},{12,4},{16,24},{20,12},{24,0},{28,20},{1,9},{5... | collective-permute-start | bytes 1572872 | tf_op jit(solution)/shard_map/ppermute | solution.py:395
  89.6 10.2 %collective-permute-start.15 = (bf16[8,128,256]{2,1,0:T(8,128)(2,1)S(1)}, bf16[8,128,256]{2,1,0:T(8,128)(2,1)S(1)}, u32[]{:S(2)}, u32[]{:S(2)}) collective-permute-start(bf16[8,128,256]{2,1,0:T(8,128)(2,1)S(1)} %pad_maximum_fusion.4), channel_id=1, source_target_pairs={{0,4},{4,0},{8,12},{12,8},{16,20},{20,16},{24,28},{28,24},{1,5},{5... | collective-permute-start | bytes 1572872 | tf_op jit(solution)/shard_map/ppermute | solution.py:384
  102.4 13.4 %collective-permute-start.16 = (bf16[8,128,256]{2,1,0:T(8,128)(2,1)S(1)}, bf16[8,128,256]{2,1,0:T(8,128)(2,1)S(1)}, u32[]{:S(2)}, u32[]{:S(2)}) collective-permute-start(bf16[8,128,256]{2,1,0:T(8,128)(2,1)S(1)} %get-tuple-element.129.refs_5_), channel_id=1, source_target_pairs={{0,4},{4,0},{8,12},{12,8},{16,20},{20,16},{24,28},{28,24},{1,5},{5... | collective-permute-start | bytes 1572872 | tf_op jit(solution)/shard_map/ppermute | solution.py:384
  103.4 10.3 %collective-permute-start.17 = (bf16[4,128,256]{2,1,0:T(8,128)(2,1)S(1)}, bf16[4,128,256]{2,1,0:T(8,128)(2,1)S(1)}, u32[]{:S(2)}, u32[]{:S(2)}) collective-permute-start(bf16[4,128,256]{2,1,0:T(8,128)(2,1)S(1)} %get-tuple-element.131), channel_id=1, source_target_pairs={{0,8},{4,28},{8,16},{12,4},{16,24},{20,12},{24,0},{28,20},{1,9},{5... | collective-permute-start | bytes 786440 | tf_op jit(solution)/shard_map/ppermute | solution.py:395
  105.9 9.9 %collective-permute-start.18 = (bf16[4,128,256]{2,1,0:T(8,128)(2,1)S(1)}, bf16[4,128,256]{2,1,0:T(8,128)(2,1)S(1)}, u32[]{:S(2)}, u32[]{:S(2)}) collective-permute-start(bf16[4,128,256]{2,1,0:T(8,128)(2,1)S(1)} %get-tuple-element.131), channel_id=1, source_target_pairs={{0,24},{4,12},{8,0},{12,20},{16,8},{20,28},{24,16},{28,4},{1,25},{... | collective-permute-start | bytes 786440 | tf_op jit(solution)/shard_map/ppermute | solution.py:395
  110.1 46.7 %collective-permute-start.24 = (f32[2048,256]{1,0:T(8,128)S(1)}, f32[2048,256]{1,0:T(8,128)S(1)}, u32[]{:S(2)}, u32[]{:S(2)}) collective-permute-start(f32[2048,256]{1,0:T(8,128)S(1)} %get-tuple-element.140.refs_13_.second.refs_8_), channel_id=1, source_target_pairs={{0,1},{1,0},{2,3},{3,2},{4,5},{5,4},{6,7},{7,6},{8,9},{9,8},{10,11... | collective-permute-start | bytes 6291464 | tf_op jit(solution)/shard_map/ppermute | solution.py:384
  112.1 44.7 %collective-permute-start.26 = (f32[2048,256]{1,0:T(8,128)S(1)}, f32[2048,256]{1,0:T(8,128)S(1)}, u32[]{:S(2)}, u32[]{:S(2)}) collective-permute-start(f32[2048,256]{1,0:T(8,128)S(1)} %collective-permute-done.25.refs_6_), channel_id=1, source_target_pairs={{0,1},{1,0},{2,3},{3,2},{4,5},{5,4},{6,7},{7,6},{8,9},{9,8},{10,11... | collective-permute-start | bytes 6291464 | tf_op jit(solution)/shard_map/ppermute | solution.py:384
  113.7 47.0 %collective-permute-start.30 = (f32[2048,256]{1,0:T(8,128)S(1)}, f32[2048,256]{1,0:T(8,128)S(1)}, u32[]{:S(2)}, u32[]{:S(2)}) collective-permute-start(f32[2048,256]{1,0:T(8,128)S(1)} %get-tuple-element.140.refs_13_.second.refs_8_), channel_id=1, source_target_pairs={{0,2},{1,3},{2,0},{3,1},{4,6},{5,7},{6,4},{7,5},{8,10},{9,11},{10,... | collective-permute-start | bytes 6291464 | tf_op jit(solution)/shard_map/ppermute | solution.py:384
  115.9 22.3 %collective-permute-start.20 = (bf16[12,128,256]{2,1,0:T(8,128)(2,1)S(1)}, bf16[12,128,256]{2,1,0:T(8,128)(2,1)S(1)}, u32[]{:S(2)}, u32[]{:S(2)}) collective-permute-start(bf16[12,128,256]{2,1,0:T(8,128)(2,1)S(1)} %pad_maximum_fusion.2), channel_id=1, source_target_pairs={{0,8},{4,28},{8,16},{12,4},{16,24},{20,12},{24,0},{28,20},{1,9},{5... | collective-permute-start | bytes 2359304 | tf_op jit(solution)/shard_map/ppermute | solution.py:395
  116.9 12.4 %collective-permute-start.19 = (bf16[8,128,256]{2,1,0:T(8,128)(2,1)S(1)}, bf16[8,128,256]{2,1,0:T(8,128)(2,1)S(1)}, u32[]{:S(2)}, u32[]{:S(2)}) collective-permute-start(bf16[8,128,256]{2,1,0:T(8,128)(2,1)S(1)} %get-tuple-element.133.refs_6_), channel_id=1, source_target_pairs={{0,4},{4,0},{8,12},{12,8},{16,20},{20,16},{24,28},{28,24},{1,5},{5... | collective-permute-start | bytes 1572872 | tf_op jit(solution)/shard_map/ppermute | solution.py:384
  129.3 17.4 %collective-permute-start.21 = (bf16[8,128,256]{2,1,0:T(8,128)(2,1)S(1)}, bf16[8,128,256]{2,1,0:T(8,128)(2,1)S(1)}, u32[]{:S(2)}, u32[]{:S(2)}) collective-permute-start(bf16[8,128,256]{2,1,0:T(8,128)(2,1)S(1)} %collective-permute-done.19.refs_8_), channel_id=1, source_target_pairs={{0,8},{4,28},{8,16},{12,4},{16,24},{20,12},{24,0},{28,20},{1,9},{5... | collective-permute-start | bytes 1572872 | tf_op jit(solution)/shard_map/ppermute | solution.py:395
  138.3 9.2 %collective-permute-start.22 = (bf16[8,128,256]{2,1,0:T(8,128)(2,1)S(1)}, bf16[8,128,256]{2,1,0:T(8,128)(2,1)S(1)}, u32[]{:S(2)}, u32[]{:S(2)}) collective-permute-start(bf16[8,128,256]{2,1,0:T(8,128)(2,1)S(1)} %pad_maximum_fusion.5), channel_id=1, source_target_pairs={{0,4},{4,0},{8,12},{12,8},{16,20},{20,16},{24,28},{28,24},{1,5},{5... | collective-permute-start | bytes 1572872 | tf_op jit(solution)/shard_map/ppermute | solution.py:384
  156.8 5.7 %collective-permute-start.27 = (f32[24,256]{1,0:T(8,128)S(1)}, f32[24,256]{1,0:T(8,128)S(1)}, u32[]{:S(2)}, u32[]{:S(2)}) collective-permute-start(f32[24,256]{1,0:T(8,128)S(1)} %fusion.refs_0_), channel_id=1, source_target_pairs={{0,8},{4,12},{8,16},{12,20},{16,24},{20,28},{24,0},{28,4},{1,9},{5... | collective-permute-start | bytes 73736 | tf_op jit(solution)/shard_map/ppermute | solution.py:389
  156.9 5.6 %collective-permute-start.28 = (f32[24,256]{1,0:T(8,128)S(1)}, f32[24,256]{1,0:T(8,128)S(1)}, u32[]{:S(2)}, u32[]{:S(2)}) collective-permute-start(f32[24,256]{1,0:T(8,128)S(1)} %fusion.refs_0_), channel_id=1, source_target_pairs={{0,16},{4,20},{8,24},{12,28},{16,0},{20,4},{24,8},{28,12},{1,17},{... | collective-permute-start | bytes 73736 | tf_op jit(solution)/shard_map/ppermute | solution.py:389
  158.3 4.8 %collective-permute-start.29 = (f32[24,256]{1,0:T(8,128)S(1)}, f32[24,256]{1,0:T(8,128)S(1)}, u32[]{:S(2)}, u32[]{:S(2)}) collective-permute-start(f32[24,256]{1,0:T(8,128)S(1)} %fusion.refs_0_), channel_id=1, source_target_pairs={{0,24},{4,28},{8,0},{12,4},{16,8},{20,12},{24,16},{28,20},{1,25},{... | collective-permute-start | bytes 73736 | tf_op jit(solution)/shard_map/ppermute | solution.py:389
  160.7 7.1 %collective-permute-start.34 = (f32[2048,256]{1,0:T(8,128)S(1)}, f32[2048,256]{1,0:T(8,128)S(1)}, u32[]{:S(2)}, u32[]{:S(2)}) collective-permute-start(f32[2048,256]{1,0:T(8,128)S(1)} %get-tuple-element.137.refs_12_.first.refs_4_), channel_id=1, source_target_pairs={{0,1},{1,0},{2,3},{3,2},{4,5},{5,4},{6,7},{7,6},{8,9},{9,8},{10,11... | collective-permute-start | bytes 6291464 | tf_op jit(solution)/shard_map/ppermute | solution.py:384
  163.1 5.8 %collective-permute-start.35 = (f32[2048,256]{1,0:T(8,128)S(1)}, f32[2048,256]{1,0:T(8,128)S(1)}, u32[]{:S(2)}, u32[]{:S(2)}) collective-permute-start(f32[2048,256]{1,0:T(8,128)S(1)} %collective-permute-done.30.refs_10_), channel_id=1, source_target_pairs={{0,1},{1,0},{2,3},{3,2},{4,5},{5,4},{6,7},{7,6},{8,9},{9,8},{10,11... | collective-permute-start | bytes 6291464 | tf_op jit(solution)/shard_map/ppermute | solution.py:384
  (23 other events, 250.1 us)

commit v7 on v6

--- a/solution.py
+++ b/solution.py
@@ -306,8 +306,10 @@
 
     sums = lax.fori_loop(0, nrows, row, (zero,) * nsums, unroll=2)
     sums = [jnp.sum(total, axis=0, keepdims=True) for total in sums]
-    sums.append(jnp.zeros((8 - nsums, lanes), jnp.float32))
-    sums = jnp.concatenate(sums, axis=0)
+    sums = [total[:, : lanes // 2] + total[:, lanes // 2 :] for total in sums]
+    blank = jnp.zeros((1, lanes // 2), jnp.float32)
+    place = (0, 1, 4)[step - 1]
+    sums = jnp.concatenate([blank] * place + sums + [blank] * (16 - place - nsums), axis=0)
     if part == 1:
         sums = sums + before[-1][...]
         if step != 3:
@@ -321,7 +323,7 @@
     width, lanes = near.shape[3], acc.shape[2]
     nrows = acc.shape[0]
     start = part * (nblocks // 2)
-    out_shape = [jax.ShapeDtypeStruct((8, lanes), jnp.float32)]
+    out_shape = [jax.ShapeDtypeStruct((16, lanes // 2), jnp.float32)]
     if step != 3:
         ends = start + nrows
         vector = jax.ShapeDtypeStruct((ends * width, lanes), jnp.float32)
@@ -538,19 +540,18 @@
     sums = refs[0][...]
     for other in refs[1:nsums]:
         sums = sums + other[...]
-    half = sums.shape[1] // 2
-    sums = sums[:, :half] + sums[:, half:]
+    half = sums.shape[1]
 
     def row(i):
         return sums[i : i + 1]
 
     a, b = combine(
         row(0),
-        (row(8), -row(9)),
-        row(10),
-        (row(16), -row(17)),
-        (row(18), -row(19)),
-        row(20),
+        (row(1), -row(2)),
+        row(3),
+        (row(4), -row(5)),
+        (row(6), -row(7)),
+        row(8),
     )
     zero = jnp.zeros((4, half), jnp.float32)
     coefs[...] = jnp.concatenate([*a, *b, zero], axis=0)
@@ -742,7 +743,7 @@
     second_across, first_three = swap(second_sent, "frq", 2), swap(first_across, "frq", 1)
     (sums_three,) = operate(3, found, (first, second))
     second_one = swap(second, "frq", 1)
-    sums = jnp.concatenate([sums_one, sums_two, sums_three], axis=0)
+    sums = sums_one + sums_two + sums_three
     sums, (second_one, first_three) = sum_over_clusters(sums, second_one, first_three)
     *sums, second_across = tie(*sums, second_across)
     second_three = swap(second_across, "frq", 1)

time: 173 us -> 172 us (level)
  transfers between devices with their start and end apart: 36 -> 36, of which waited for: 22 -> 23; matrix products, arithmetic and copies ran while one was open for 1% -> 1% of each run, Pallas kernels for 29% -> 29%
where the time goes in v7:
time: 172 us
  waiting for transfers between devices  76.5 us (44%)
  Pallas kernels  52.8 us (31%)
  starting transfers between devices  37.9 us (22%)
  local copies, waits for them, and re-layouts  3.2 us (2%)
    ppermute x21, waiting for transfers between devices, swap(): return lax.ppermute(value, axis, [(i, i ^ distance) for i in range(count)])  43.3 us
    ppermute x12, waiting for transfers between devices, ring(): return lax.ppermute(value, 'clu', pairs)  30.9 us
    pallas_call x3, Pallas kernels, main_call(): pl.pallas_call(functools.partial(main_kernel, (nblocks, span, edges), (fr...  22.1 us
    ppermute x21, starting transfers between devices, swap(): return lax.ppermute(value, axis, [(i, i ^ distance) for i in range(count)])  17.8 us
    ppermute x12, starting transfers between devices, ring(): return lax.ppermute(value, 'clu', pairs)  16.2 us
    pallas_call x5, Pallas kernels, rest_call(): pl.pallas_call(functools.partial(rest_kernel, step, part, (nblocks, span,...  16.1 us
    pallas_call x7, Pallas kernels, on_vmem(): pl.pallas_call(body, out_shape=out_shape, in_specs=[smem] * len(smem_args...  8.22 us
    pallas_call x1, Pallas kernels, table_call(): pl.pallas_call(functools.partial(table_kernel, sizes), out_shape=tuple((j...  6.41 us
  transfers between devices with their start and end apart: 36, of which 23 were waited for; matrix products, arithmetic and copies ran while one was open for 1% of the time, Pallas kernels for 29%

profile of v7, /device:TPU:0, one launch (start us, length us, event | category | flops | bytes accessed | tf_op | source)
XLA Modules:
  0.0 171.8 jit_solution(3551917279130670837)
XLA Ops:
  3.9 2.9 %collective-permute-start = (bf16[8,128,256]{2,1,0:T(8,128)(2,1)S(1)}, bf16[8,128,256]{2,1,0:T(8,128)(2,1)S(1)}, u32[]{:S(2)}, u32[]{:S(2)}) collective-permute-start(bf16[8,128,256]{2,1,0:T(8,128)(2,1)S(1)} %get-tuple-element.78.refs_5_), channel_id=1, source_target_pairs={{0,4},{4,0},{8,12},{12,8},{16,20},{20,16},{24,28},{28,24},{1,5},{5... | collective-permute-start | bytes 1572872 | tf_op jit(solution)/shard_map/ppermute | solution.py:386
  8.4 2.2 %collective-permute-start.2 = (bf16[4,128,256]{2,1,0:T(8,128)(2,1)}, bf16[4,128,256]{2,1,0:T(8,128)(2,1)}, u32[]{:S(2)}, u32[]{:S(2)}) collective-permute-start(bf16[4,128,256]{2,1,0:T(8,128)(2,1)} %get-tuple-element.79), channel_id=1, source_target_pairs={{0,24},{4,12},{8,0},{12,20},{16,8},{20,28},{24,16},{28,4},{1,25},{... | collective-permute-start | bytes 786440 | tf_op jit(solution)/shard_map/ppermute | solution.py:397
  11.4 6.4 %tables.1 = (s32[128]{0:T(128)}, s32[32]{0:T(128)}, s32[128]{0:T(128)}, s32[128]{0:T(128)}, s32[128]{0:T(128)}, /*index=5*/s32[64]{0:T(128)}, s32[64]{0:T(128)}, s32[64]{0:T(128)}, s32[4]{0:T(128)}) custom-call(s32[1]{0:T(128)} %bitcast.1.place, s32[128]{0:T(128)} %reshape.17.pattern, s32[32]{0:T(128)} %bitcast.31, s32[32]{0:T(128)} %source.1, s32[32]{0:T(128)} %refs_2_.5), custom_call_target="tpu_custom_call" | custom-call | tf_op jit(solution)/shard_map/tables/pallas_call | solution.py:109
  18.2 3.7 %collective-permute-done.2.refs_11_ = bf16[4,128,256]{2,1,0:T(8,128)(2,1)} collective-permute-done((bf16[4,128,256]{2,1,0:T(8,128)(2,1)}, bf16[4,128,256]{2,1,0:T(8,128)(2,1)}, u32[]{:S(2)}, u32[]{:S(2)}) %collective-permute-start.2) | collective-permute-done | bytes 262176 | tf_op jit(solution)/shard_map/ppermute | solution.py:397
  24.1 1.9 %collective-permute-start.3 = (bf16[8,128,256]{2,1,0:T(8,128)(2,1)S(1)}, bf16[8,128,256]{2,1,0:T(8,128)(2,1)S(1)}, u32[]{:S(2)}, u32[]{:S(2)}) collective-permute-start(bf16[8,128,256]{2,1,0:T(8,128)(2,1)S(1)} %copy-done.6), channel_id=1, source_target_pairs={{0,4},{4,0},{8,12},{12,8},{16,20},{20,16},{24,28},{28,24},{1,5},{5... | collective-permute-start | bytes 1572872 | tf_op jit(solution)/shard_map/ppermute | solution.py:386
  26.3 12.2 %collective-permute-done.3.refs_8_ = bf16[8,128,256]{2,1,0:T(8,128)(2,1)S(1)} collective-permute-done((bf16[8,128,256]{2,1,0:T(8,128)(2,1)S(1)}, bf16[8,128,256]{2,1,0:T(8,128)(2,1)S(1)}, u32[]{:S(2)}, u32[]{:S(2)}) %collective-permute-start.3) | collective-permute-done | bytes 524320 | tf_op jit(solution)/shard_map/ppermute | solution.py:386
  39.0 3.6 %collective-permute-done.4.refs_9_ = bf16[12,128,256]{2,1,0:T(8,128)(2,1)S(1)} collective-permute-done((bf16[12,128,256]{2,1,0:T(8,128)(2,1)S(1)}, bf16[12,128,256]{2,1,0:T(8,128)(2,1)S(1)}, u32[]{:S(2)}, u32[]{:S(2)}) %collective-permute-start.4) | collective-permute-done | bytes 786464 | tf_op jit(solution)/shard_map/ppermute | solution.py:397
  45.2 7.4 %operator_1.1 = (f32[8,256,256]{2,1,0:T(8,128)S(1)}, f32[8,256,256]{2,1,0:T(8,128)S(1)}) custom-call(s32[128]{0:T(128)S(1)} %copy-done.15, s32[32]{0:T(128)S(1)} %copy-done.16, s32[32]{0:T(128)S(1)} %copy-done.14, bf16[16,8,256,128]{3,2,1,0:T(8,128)(2,1)S(1)} %bitcast.8, bf16[32,256,128]{2,1,0:T(8,128)(2,1)S(1)} %bitcast.16, ...), custom_call_target="tpu_custom_call" | custom-call | flops 2684354560 | bytes 10485760 | tf_op jit(solution)/shard_map/operator_1/pallas_call | solution.py:200
  55.1 2.5 %rest_1_0.1 = (f32[1024,256]{1,0:T(8,128)S(1)}, bf16[8,128,256]{2,1,0:T(8,128)(2,1)S(1)}, bf16[4,128,256]{2,1,0:T(8,128)(2,1)S(1)}, f32[16,128]{1,0:T(8,128)S(1)}) custom-call(s32[128]{0:T(128)S(1)} %copy-done.7, s32[128]{0:T(128)S(1)} %copy-done.8, s32[128]{0:T(128)S(1)} %copy-done.9, s32[64]{0:T(128)S(1)} %copy-done.10, s32[64]{0:T(128)S(1)} %copy-done.11, ...), custom_call_target="tpu_custom_call" | custom-call | flops 268435456 | bytes 6291456 | tf_op jit(solution)/shard_map/rest_1_0/pallas_call | solution.py:338
  58.6 2.9 %collective-permute-start.9 = (bf16[4,128,256]{2,1,0:T(8,128)(2,1)S(1)}, bf16[4,128,256]{2,1,0:T(8,128)(2,1)S(1)}, u32[]{:S(2)}, u32[]{:S(2)}) collective-permute-start(bf16[4,128,256]{2,1,0:T(8,128)(2,1)S(1)} %get-tuple-element.113), channel_id=1, source_target_pairs={{0,24},{4,12},{8,0},{12,20},{16,8},{20,28},{24,16},{28,4},{1,25},{... | collective-permute-start | bytes 786440 | tf_op jit(solution)/shard_map/ppermute | solution.py:397
  61.5 2.8 %rest_1_1.1 = (f32[2048,256]{1,0:T(8,128)S(1)}, bf16[8,128,256]{2,1,0:T(8,128)(2,1)S(1)}, f32[16,128]{1,0:T(8,128)S(1)}) custom-call(s32[128]{0:T(128)S(1)} %copy-done.7, s32[128]{0:T(128)S(1)} %copy-done.8, s32[128]{0:T(128)S(1)} %copy-done.9, s32[64]{0:T(128)S(1)} %copy-done.10, s32[64]{0:T(128)S(1)} %copy-done.11, s32[64]{0:T(128)S(1)} %copy-done.12, ...), custom_call_target="tpu_custom_call" | custom-call | flops 268435456 | bytes 6291456 | tf_op jit(solution)/shard_map/rest_1_1/pallas_call | solution.py:338
  64.3 4.1 %collective-permute-done.8.refs_10_ = bf16[4,128,256]{2,1,0:T(8,128)(2,1)S(1)} collective-permute-done((bf16[4,128,256]{2,1,0:T(8,128)(2,1)S(1)}, bf16[4,128,256]{2,1,0:T(8,128)(2,1)S(1)}, u32[]{:S(2)}, u32[]{:S(2)}) %collective-permute-start.8) | collective-permute-done | bytes 262176 | tf_op jit(solution)/shard_map/ppermute | solution.py:397
  71.5 1.8 %collective-permute-start.10 = (bf16[8,128,256]{2,1,0:T(8,128)(2,1)S(1)}, bf16[8,128,256]{2,1,0:T(8,128)(2,1)S(1)}, u32[]{:S(2)}, u32[]{:S(2)}) collective-permute-start(bf16[8,128,256]{2,1,0:T(8,128)(2,1)S(1)} %get-tuple-element.117.refs_6_), channel_id=1, source_target_pairs={{0,4},{4,0},{8,12},{12,8},{16,20},{20,16},{24,28},{28,24},{1,5},{5... | collective-permute-start | bytes 1572872 | tf_op jit(solution)/shard_map/ppermute | solution.py:386
  73.3 11.4 %collective-permute-done.10.refs_8_ = bf16[8,128,256]{2,1,0:T(8,128)(2,1)S(1)} collective-permute-done((bf16[8,128,256]{2,1,0:T(8,128)(2,1)S(1)}, bf16[8,128,256]{2,1,0:T(8,128)(2,1)S(1)}, u32[]{:S(2)}, u32[]{:S(2)}) %collective-permute-start.10) | collective-permute-done | bytes 524320 | tf_op jit(solution)/shard_map/ppermute | solution.py:386
  85.0 4.5 %collective-permute-done.13.refs_9_ = bf16[12,128,256]{2,1,0:T(8,128)(2,1)S(1)} collective-permute-done((bf16[12,128,256]{2,1,0:T(8,128)(2,1)S(1)}, bf16[12,128,256]{2,1,0:T(8,128)(2,1)S(1)}, u32[]{:S(2)}, u32[]{:S(2)}) %collective-permute-start.13) | collective-permute-done | bytes 786464 | tf_op jit(solution)/shard_map/ppermute | solution.py:397
  89.6 2.0 %collective-permute-start.15 = (bf16[8,128,256]{2,1,0:T(8,128)(2,1)S(1)}, bf16[8,128,256]{2,1,0:T(8,128)(2,1)S(1)}, u32[]{:S(2)}, u32[]{:S(2)}) collective-permute-start(bf16[8,128,256]{2,1,0:T(8,128)(2,1)S(1)} %pad_maximum_fusion.4), channel_id=1, source_target_pairs={{0,4},{4,0},{8,12},{12,8},{16,20},{20,16},{24,28},{28,24},{1,5},{5... | collective-permute-start | bytes 1572872 | tf_op jit(solution)/shard_map/ppermute | solution.py:386
  91.6 7.4 %operator_2.1 = (f32[8,256,256]{2,1,0:T(8,128)S(1)}, f32[8,256,256]{2,1,0:T(8,128)S(1)}) custom-call(s32[128]{0:T(128)S(1)} %copy-done.15, s32[32]{0:T(128)S(1)} %copy-done.16, s32[32]{0:T(128)S(1)} %copy-done.14, bf16[16,8,256,128]{3,2,1,0:T(8,128)(2,1)S(1)} %bitcast.11, bf16[32,256,128]{2,1,0:T(8,128)(2,1)S(1)} %bitcast.19, ...), custom_call_target="tpu_custom_call" | custom-call | flops 2684354560 | bytes 10485760 | tf_op jit(solution)/shard_map/operator_2/pallas_call | solution.py:200
  100.8 2.6 %rest_2_0.1 = (f32[1024,256]{1,0:T(8,128)S(1)}, bf16[8,128,256]{2,1,0:T(8,128)(2,1)S(1)}, bf16[4,128,256]{2,1,0:T(8,128)(2,1)S(1)}, f32[16,128]{1,0:T(8,128)S(1)}) custom-call(s32[128]{0:T(128)S(1)} %copy-done.7, s32[128]{0:T(128)S(1)} %copy-done.8, s32[128]{0:T(128)S(1)} %copy-done.9, s32[64]{0:T(128)S(1)} %copy-done.10, s32[64]{0:T(128)S(1)} %copy-done.11, ...), custom_call_target="tpu_custom_call" | custom-call | flops 268435456 | bytes 6291456 | tf_op jit(solution)/shard_map/rest_2_0/pallas_call | solution.py:338
  103.4 2.7 %collective-permute-start.17 = (bf16[4,128,256]{2,1,0:T(8,128)(2,1)S(1)}, bf16[4,128,256]{2,1,0:T(8,128)(2,1)S(1)}, u32[]{:S(2)}, u32[]{:S(2)}) collective-permute-start(bf16[4,128,256]{2,1,0:T(8,128)(2,1)S(1)} %get-tuple-element.131), channel_id=1, source_target_pairs={{0,8},{4,28},{8,16},{12,4},{16,24},{20,12},{24,0},{28,20},{1,9},{5... | collective-permute-start | bytes 786440 | tf_op jit(solution)/shard_map/ppermute | solution.py:397
  107.5 2.9 %rest_2_1.1 = (f32[2048,256]{1,0:T(8,128)S(1)}, bf16[8,128,256]{2,1,0:T(8,128)(2,1)S(1)}, f32[16,128]{1,0:T(8,128)S(1)}) custom-call(s32[128]{0:T(128)S(1)} %copy-done.7, s32[128]{0:T(128)S(1)} %copy-done.8, s32[128]{0:T(128)S(1)} %copy-done.9, s32[64]{0:T(128)S(1)} %copy-done.10, s32[64]{0:T(128)S(1)} %copy-done.11, s32[64]{0:T(128)S(1)} %copy-done.12, ...), custom_call_target="tpu_custom_call" | custom-call | flops 268435456 | bytes 6291456 | tf_op jit(solution)/shard_map/rest_2_1/pallas_call | solution.py:338
  110.4 1.7 collective-permute-done.25.refs_6_
  112.1 1.7 collective-permute-done.17.refs_10_
  117.1 1.9 %collective-permute-start.19 = (bf16[8,128,256]{2,1,0:T(8,128)(2,1)S(1)}, bf16[8,128,256]{2,1,0:T(8,128)(2,1)S(1)}, u32[]{:S(2)}, u32[]{:S(2)}) collective-permute-start(bf16[8,128,256]{2,1,0:T(8,128)(2,1)S(1)} %get-tuple-element.133.refs_6_), channel_id=1, source_target_pairs={{0,4},{4,0},{8,12},{12,8},{16,20},{20,16},{24,28},{28,24},{1,5},{5... | collective-permute-start | bytes 1572872 | tf_op jit(solution)/shard_map/ppermute | solution.py:386
  118.9 10.3 %collective-permute-done.19.refs_8_ = bf16[8,128,256]{2,1,0:T(8,128)(2,1)S(1)} collective-permute-done((bf16[8,128,256]{2,1,0:T(8,128)(2,1)S(1)}, bf16[8,128,256]{2,1,0:T(8,128)(2,1)S(1)}, u32[]{:S(2)}, u32[]{:S(2)}) %collective-permute-start.19) | collective-permute-done | bytes 524320 | tf_op jit(solution)/shard_map/ppermute | solution.py:386
  129.6 9.1 %collective-permute-done.20.refs_9_ = bf16[12,128,256]{2,1,0:T(8,128)(2,1)S(1)} collective-permute-done((bf16[12,128,256]{2,1,0:T(8,128)(2,1)S(1)}, bf16[12,128,256]{2,1,0:T(8,128)(2,1)S(1)}, u32[]{:S(2)}, u32[]{:S(2)}) %collective-permute-start.20) | collective-permute-done | bytes 786464 | tf_op jit(solution)/shard_map/ppermute | solution.py:397
  139.0 7.3 %operator_3.1.refs_9_ = f32[16,256,256]{2,1,0:T(8,128)S(1)} custom-call(s32[128]{0:T(128)S(1)} %copy-done.15, s32[32]{0:T(128)S(1)} %copy-done.16, s32[32]{0:T(128)S(1)} %copy-done.14, bf16[16,8,256,128]{3,2,1,0:T(8,128)(2,1)S(1)} %bitcast.14, bf16[32,256,128]{2,1,0:T(8,128)(2,1)S(1)} %bitcast.22, bf16[8,128,256]{2,1,0:T(8,128)(2,1)S(1)} %get-tuple-element.129.refs_5_, ...), custom_call_target="tpu_custom_call" | custom-call | flops 2684354560 | bytes 10485760 | tf_op jit(solution)/shard_map/operator_3/pallas_call | solution.py:200
  148.1 5.3 %rest_3_0.1 = f32[16,128]{1,0:T(8,128)S(1)} custom-call(s32[128]{0:T(128)S(1)} %copy-done.7, s32[128]{0:T(128)S(1)} %copy-done.8, s32[128]{0:T(128)S(1)} %copy-done.9, s32[64]{0:T(128)S(1)} %copy-done.10, s32[64]{0:T(128)S(1)} %copy-done.11, s32[64]{0:T(128)S(1)} %copy-done.12, s32[4]{0:T(128)S(1)} %copy-done.13, bf16[16,8,256,128]{3,2,1,0:T(8,128)(2,1)S(1)} %bitcast.15, ...), custom_call_target="tpu_custom_call" | custom-call | flops 536870912 | bytes 12582912 | tf_op jit(solution)/shard_map/rest_3_0/pallas_call | solution.py:338
  153.5 3.6 %collective-permute-done.23 = f32[16,128]{1,0:T(8,128)S(1)} collective-permute-done((f32[16,128]{1,0:T(8,128)S(1)}, f32[16,128]{1,0:T(8,128)S(1)}, u32[]{:S(2)}, u32[]{:S(2)}) %collective-permute-start.23) | collective-permute-done | bytes 8224 | tf_op jit(solution)/shard_map/ppermute | solution.py:386
  158.5 2.5 %collective-permute-start.29 = (f32[16,128]{1,0:T(8,128)S(1)}, f32[16,128]{1,0:T(8,128)S(1)}, u32[]{:S(2)}, u32[]{:S(2)}) collective-permute-start(f32[16,128]{1,0:T(8,128)S(1)} %add.11.refs_0_), channel_id=1, source_target_pairs={{0,24},{4,28},{8,0},{12,4},{16,8},{20,12},{24,16},{28,20},{1,25},{... | collective-permute-start | bytes 24584 | tf_op jit(solution)/shard_map/ppermute | solution.py:391
  161.1 1.6 collective-permute-done.27.refs_1_
  166.0 2.0 %scattered.1 = f32[2,2048,128]{2,1,0:T(8,128)} custom-call(f32[8,128]{1,0:T(8,128)S(1)} %get-tuple-element.145.coefs, f32[2,2048,128]{2,1,0:T(8,128)S(1)} %bitcast.27, f32[2048,256]{1,0:T(8,128)S(1)} %get-tuple-element.137.refs_12_.first.refs_4_, f32[2048,256]{1,0:T(8,128)S(1)} %get-tuple-element.140.refs_13_.second.refs_8_), custom_call_target="tpu_custom_call" | custom-call | bytes 8392704 | tf_op jit(solution)/shard_map/scattered/pallas_call | solution.py:659
  169.0 2.8 %trace.1 = f32[2048,128]{1,0:T(8,128)} custom-call(s32[4]{0:T(128)S(1)} %iota_xor_fusion.place, f32[2048,128]{1,0:T(8,128)S(1)} %get-tuple-element.146.here, f32[2048,128]{1,0:T(8,128)S(1)} %collective-permute-done.12.away, f32[8,128]{1,0:T(8,128)S(1)} %get-tuple-element.148.refs_0_, f32[8,128]{1,0:T(8,128)S(1)} %collective-permute-done.31.refs_1_, ...), custom_call_target="tpu_custom_call" | custom-call | bytes 19939328 | tf_op jit(solution)/shard_map/trace/pallas_call | solution.py:659
  (108 shorter events, 32.9 us)
Async XLA Ops:
  3.9 17.9 %collective-permute-start = (bf16[8,128,256]{2,1,0:T(8,128)(2,1)S(1)}, bf16[8,128,256]{2,1,0:T(8,128)(2,1)S(1)}, u32[]{:S(2)}, u32[]{:S(2)}) collective-permute-start(bf16[8,128,256]{2,1,0:T(8,128)(2,1)S(1)} %get-tuple-element.78.refs_5_), channel_id=1, source_target_pairs={{0,4},{4,0},{8,12},{12,8},{16,20},{20,16},{24,28},{28,24},{1,5},{5... | collective-permute-start | bytes 1572872 | tf_op jit(solution)/shard_map/ppermute | solution.py:386
  6.9 11.3 %collective-permute-start.1 = (bf16[4,128,256]{2,1,0:T(8,128)(2,1)}, bf16[4,128,256]{2,1,0:T(8,128)(2,1)S(1)}, u32[]{:S(2)}, u32[]{:S(2)}) collective-permute-start(bf16[4,128,256]{2,1,0:T(8,128)(2,1)} %get-tuple-element.79), channel_id=1, source_target_pairs={{0,8},{4,28},{8,16},{12,4},{16,24},{20,12},{24,0},{28,20},{1,9},{5... | collective-permute-start | bytes 786440 | tf_op jit(solution)/shard_map/ppermute | solution.py:397
  8.4 13.4 %collective-permute-start.2 = (bf16[4,128,256]{2,1,0:T(8,128)(2,1)}, bf16[4,128,256]{2,1,0:T(8,128)(2,1)}, u32[]{:S(2)}, u32[]{:S(2)}) collective-permute-start(bf16[4,128,256]{2,1,0:T(8,128)(2,1)} %get-tuple-element.79), channel_id=1, source_target_pairs={{0,24},{4,12},{8,0},{12,20},{16,8},{20,28},{24,16},{28,4},{1,25},{... | collective-permute-start | bytes 786440 | tf_op jit(solution)/shard_map/ppermute | solution.py:397
  21.9 20.7 %collective-permute-start.4 = (bf16[12,128,256]{2,1,0:T(8,128)(2,1)S(1)}, bf16[12,128,256]{2,1,0:T(8,128)(2,1)S(1)}, u32[]{:S(2)}, u32[]{:S(2)}) collective-permute-start(bf16[12,128,256]{2,1,0:T(8,128)(2,1)S(1)} %pad_maximum_fusion), channel_id=1, source_target_pairs={{0,8},{4,28},{8,16},{12,4},{16,24},{20,12},{24,0},{28,20},{1,9},{5... | collective-permute-start | bytes 2359304 | tf_op jit(solution)/shard_map/ppermute | solution.py:397
  24.0 18.8 %collective-permute-start.11 = (f32[2048,128]{1,0:T(8,128)S(1)}, f32[2048,128]{1,0:T(8,128)S(1)}, u32[]{:S(2)}, u32[]{:S(2)}) collective-permute-start(f32[2048,128]{1,0:T(8,128)S(1)} %get-tuple-element.120), channel_id=1, source_target_pairs={{0,1},{1,0},{2,3},{3,2},{4,5},{5,4},{6,7},{7,6},{8,9},{9,8},{10,11... | collective-permute-start | bytes 3145736 | tf_op jit(solution)/shard_map/ppermute | solution.py:386
  24.1 14.5 %collective-permute-start.3 = (bf16[8,128,256]{2,1,0:T(8,128)(2,1)S(1)}, bf16[8,128,256]{2,1,0:T(8,128)(2,1)S(1)}, u32[]{:S(2)}, u32[]{:S(2)}) collective-permute-start(bf16[8,128,256]{2,1,0:T(8,128)(2,1)S(1)} %copy-done.6), channel_id=1, source_target_pairs={{0,4},{4,0},{8,12},{12,8},{16,20},{20,16},{24,28},{28,24},{1,5},{5... | collective-permute-start | bytes 1572872 | tf_op jit(solution)/shard_map/ppermute | solution.py:386
  38.5 15.4 %collective-permute-start.5 = (bf16[8,128,256]{2,1,0:T(8,128)(2,1)S(1)}, bf16[8,128,256]{2,1,0:T(8,128)(2,1)S(1)}, u32[]{:S(2)}, u32[]{:S(2)}) collective-permute-start(bf16[8,128,256]{2,1,0:T(8,128)(2,1)S(1)} %collective-permute-done.3.refs_8_), channel_id=1, source_target_pairs={{0,8},{4,28},{8,16},{12,4},{16,24},{20,12},{24,0},{28,20},{1,9},{5... | collective-permute-start | bytes 1572872 | tf_op jit(solution)/shard_map/ppermute | solution.py:397
  42.7 12.3 %collective-permute-start.6 = (bf16[8,128,256]{2,1,0:T(8,128)(2,1)S(1)}, bf16[8,128,256]{2,1,0:T(8,128)(2,1)S(1)}, u32[]{:S(2)}, u32[]{:S(2)}) collective-permute-start(bf16[8,128,256]{2,1,0:T(8,128)(2,1)S(1)} %pad_maximum_fusion.3), channel_id=1, source_target_pairs={{0,4},{4,0},{8,12},{12,8},{16,20},{20,16},{24,28},{28,24},{1,5},{5... | collective-permute-start | bytes 1572872 | tf_op jit(solution)/shard_map/ppermute | solution.py:386
  43.6 26.5 %collective-permute-start.12 = (f32[2048,128]{1,0:T(8,128)S(1)}, f32[2048,128]{1,0:T(8,128)S(1)}, u32[]{:S(2)}, u32[]{:S(2)}) collective-permute-start(f32[2048,128]{1,0:T(8,128)S(1)} %get-tuple-element.121), channel_id=1, source_target_pairs={{0,2},{1,3},{2,0},{3,1},{4,6},{5,7},{6,4},{7,5},{8,10},{9,11},{10,... | collective-permute-start | bytes 3145736 | tf_op jit(solution)/shard_map/ppermute | solution.py:386
  57.6 12.4 %collective-permute-start.7 = (bf16[8,128,256]{2,1,0:T(8,128)(2,1)S(1)}, bf16[8,128,256]{2,1,0:T(8,128)(2,1)S(1)}, u32[]{:S(2)}, u32[]{:S(2)}) collective-permute-start(bf16[8,128,256]{2,1,0:T(8,128)(2,1)S(1)} %get-tuple-element.111.refs_5_), channel_id=1, source_target_pairs={{0,4},{4,0},{8,12},{12,8},{16,20},{20,16},{24,28},{28,24},{1,5},{5... | collective-permute-start | bytes 1572872 | tf_op jit(solution)/shard_map/ppermute | solution.py:386
  57.6 10.8 %collective-permute-start.8 = (bf16[4,128,256]{2,1,0:T(8,128)(2,1)S(1)}, bf16[4,128,256]{2,1,0:T(8,128)(2,1)S(1)}, u32[]{:S(2)}, u32[]{:S(2)}) collective-permute-start(bf16[4,128,256]{2,1,0:T(8,128)(2,1)S(1)} %get-tuple-element.113), channel_id=1, source_target_pairs={{0,8},{4,28},{8,16},{12,4},{16,24},{20,12},{24,0},{28,20},{1,9},{5... | collective-permute-start | bytes 786440 | tf_op jit(solution)/shard_map/ppermute | solution.py:397
  58.6 11.4 %collective-permute-start.9 = (bf16[4,128,256]{2,1,0:T(8,128)(2,1)S(1)}, bf16[4,128,256]{2,1,0:T(8,128)(2,1)S(1)}, u32[]{:S(2)}, u32[]{:S(2)}) collective-permute-start(bf16[4,128,256]{2,1,0:T(8,128)(2,1)S(1)} %get-tuple-element.113), channel_id=1, source_target_pairs={{0,24},{4,12},{8,0},{12,20},{16,8},{20,28},{24,16},{28,4},{1,25},{... | collective-permute-start | bytes 786440 | tf_op jit(solution)/shard_map/ppermute | solution.py:397
  68.4 43.6 %collective-permute-start.25 = (f32[2048,256]{1,0:T(8,128)S(1)}, f32[2048,256]{1,0:T(8,128)S(1)}, u32[]{:S(2)}, u32[]{:S(2)}) collective-permute-start(f32[2048,256]{1,0:T(8,128)S(1)} %get-tuple-element.137.refs_12_.first.refs_4_), channel_id=1, source_target_pairs={{0,2},{1,3},{2,0},{3,1},{4,6},{5,7},{6,4},{7,5},{8,10},{9,11},{10,... | collective-permute-start | bytes 6291464 | tf_op jit(solution)/shard_map/ppermute | solution.py:386
  70.1 19.5 %collective-permute-start.13 = (bf16[12,128,256]{2,1,0:T(8,128)(2,1)S(1)}, bf16[12,128,256]{2,1,0:T(8,128)(2,1)S(1)}, u32[]{:S(2)}, u32[]{:S(2)}) collective-permute-start(bf16[12,128,256]{2,1,0:T(8,128)(2,1)S(1)} %pad_maximum_fusion.1), channel_id=1, source_target_pairs={{0,8},{4,28},{8,16},{12,4},{16,24},{20,12},{24,0},{28,20},{1,9},{5... | collective-permute-start | bytes 2359304 | tf_op jit(solution)/shard_map/ppermute | solution.py:397
  71.5 13.1 %collective-permute-start.10 = (bf16[8,128,256]{2,1,0:T(8,128)(2,1)S(1)}, bf16[8,128,256]{2,1,0:T(8,128)(2,1)S(1)}, u32[]{:S(2)}, u32[]{:S(2)}) collective-permute-start(bf16[8,128,256]{2,1,0:T(8,128)(2,1)S(1)} %get-tuple-element.117.refs_6_), channel_id=1, source_target_pairs={{0,4},{4,0},{8,12},{12,8},{16,20},{20,16},{24,28},{28,24},{1,5},{5... | collective-permute-start | bytes 1572872 | tf_op jit(solution)/shard_map/ppermute | solution.py:386
  84.7 14.7 %collective-permute-start.14 = (bf16[8,128,256]{2,1,0:T(8,128)(2,1)S(1)}, bf16[8,128,256]{2,1,0:T(8,128)(2,1)S(1)}, u32[]{:S(2)}, u32[]{:S(2)}) collective-permute-start(bf16[8,128,256]{2,1,0:T(8,128)(2,1)S(1)} %collective-permute-done.10.refs_8_), channel_id=1, source_target_pairs={{0,8},{4,28},{8,16},{12,4},{16,24},{20,12},{24,0},{28,20},{1,9},{5... | collective-permute-start | bytes 1572872 | tf_op jit(solution)/shard_map/ppermute | solution.py:397
  89.6 11.2 %collective-permute-start.15 = (bf16[8,128,256]{2,1,0:T(8,128)(2,1)S(1)}, bf16[8,128,256]{2,1,0:T(8,128)(2,1)S(1)}, u32[]{:S(2)}, u32[]{:S(2)}) collective-permute-start(bf16[8,128,256]{2,1,0:T(8,128)(2,1)S(1)} %pad_maximum_fusion.4), channel_id=1, source_target_pairs={{0,4},{4,0},{8,12},{12,8},{16,20},{20,16},{24,28},{28,24},{1,5},{5... | collective-permute-start | bytes 1572872 | tf_op jit(solution)/shard_map/ppermute | solution.py:386
  103.3 13.0 %collective-permute-start.16 = (bf16[8,128,256]{2,1,0:T(8,128)(2,1)S(1)}, bf16[8,128,256]{2,1,0:T(8,128)(2,1)S(1)}, u32[]{:S(2)}, u32[]{:S(2)}) collective-permute-start(bf16[8,128,256]{2,1,0:T(8,128)(2,1)S(1)} %get-tuple-element.129.refs_5_), channel_id=1, source_target_pairs={{0,4},{4,0},{8,12},{12,8},{16,20},{20,16},{24,28},{28,24},{1,5},{5... | collective-permute-start | bytes 1572872 | tf_op jit(solution)/shard_map/ppermute | solution.py:386
  103.4 10.3 %collective-permute-start.17 = (bf16[4,128,256]{2,1,0:T(8,128)(2,1)S(1)}, bf16[4,128,256]{2,1,0:T(8,128)(2,1)S(1)}, u32[]{:S(2)}, u32[]{:S(2)}) collective-permute-start(bf16[4,128,256]{2,1,0:T(8,128)(2,1)S(1)} %get-tuple-element.131), channel_id=1, source_target_pairs={{0,8},{4,28},{8,16},{12,4},{16,24},{20,12},{24,0},{28,20},{1,9},{5... | collective-permute-start | bytes 786440 | tf_op jit(solution)/shard_map/ppermute | solution.py:397
  106.2 10.2 %collective-permute-start.18 = (bf16[4,128,256]{2,1,0:T(8,128)(2,1)S(1)}, bf16[4,128,256]{2,1,0:T(8,128)(2,1)S(1)}, u32[]{:S(2)}, u32[]{:S(2)}) collective-permute-start(bf16[4,128,256]{2,1,0:T(8,128)(2,1)S(1)} %get-tuple-element.131), channel_id=1, source_target_pairs={{0,24},{4,12},{8,0},{12,20},{16,8},{20,28},{24,16},{28,4},{1,25},{... | collective-permute-start | bytes 786440 | tf_op jit(solution)/shard_map/ppermute | solution.py:397
  110.3 46.8 %collective-permute-start.24 = (f32[2048,256]{1,0:T(8,128)S(1)}, f32[2048,256]{1,0:T(8,128)S(1)}, u32[]{:S(2)}, u32[]{:S(2)}) collective-permute-start(f32[2048,256]{1,0:T(8,128)S(1)} %get-tuple-element.140.refs_13_.second.refs_8_), channel_id=1, source_target_pairs={{0,1},{1,0},{2,3},{3,2},{4,5},{5,4},{6,7},{7,6},{8,9},{9,8},{10,11... | collective-permute-start | bytes 6291464 | tf_op jit(solution)/shard_map/ppermute | solution.py:386
  112.1 45.1 %collective-permute-start.26 = (f32[2048,256]{1,0:T(8,128)S(1)}, f32[2048,256]{1,0:T(8,128)S(1)}, u32[]{:S(2)}, u32[]{:S(2)}) collective-permute-start(f32[2048,256]{1,0:T(8,128)S(1)} %collective-permute-done.25.refs_6_), channel_id=1, source_target_pairs={{0,1},{1,0},{2,3},{3,2},{4,5},{5,4},{6,7},{7,6},{8,9},{9,8},{10,11... | collective-permute-start | bytes 6291464 | tf_op jit(solution)/shard_map/ppermute | solution.py:386
  113.8 47.3 %collective-permute-start.30 = (f32[2048,256]{1,0:T(8,128)S(1)}, f32[2048,256]{1,0:T(8,128)S(1)}, u32[]{:S(2)}, u32[]{:S(2)}) collective-permute-start(f32[2048,256]{1,0:T(8,128)S(1)} %get-tuple-element.140.refs_13_.second.refs_8_), channel_id=1, source_target_pairs={{0,2},{1,3},{2,0},{3,1},{4,6},{5,7},{6,4},{7,5},{8,10},{9,11},{10,... | collective-permute-start | bytes 6291464 | tf_op jit(solution)/shard_map/ppermute | solution.py:386
  116.4 22.3 %collective-permute-start.20 = (bf16[12,128,256]{2,1,0:T(8,128)(2,1)S(1)}, bf16[12,128,256]{2,1,0:T(8,128)(2,1)S(1)}, u32[]{:S(2)}, u32[]{:S(2)}) collective-permute-start(bf16[12,128,256]{2,1,0:T(8,128)(2,1)S(1)} %pad_maximum_fusion.2), channel_id=1, source_target_pairs={{0,8},{4,28},{8,16},{12,4},{16,24},{20,12},{24,0},{28,20},{1,9},{5... | collective-permute-start | bytes 2359304 | tf_op jit(solution)/shard_map/ppermute | solution.py:397
  117.1 12.2 %collective-permute-start.19 = (bf16[8,128,256]{2,1,0:T(8,128)(2,1)S(1)}, bf16[8,128,256]{2,1,0:T(8,128)(2,1)S(1)}, u32[]{:S(2)}, u32[]{:S(2)}) collective-permute-start(bf16[8,128,256]{2,1,0:T(8,128)(2,1)S(1)} %get-tuple-element.133.refs_6_), channel_id=1, source_target_pairs={{0,4},{4,0},{8,12},{12,8},{16,20},{20,16},{24,28},{28,24},{1,5},{5... | collective-permute-start | bytes 1572872 | tf_op jit(solution)/shard_map/ppermute | solution.py:386
  129.3 18.3 %collective-permute-start.21 = (bf16[8,128,256]{2,1,0:T(8,128)(2,1)S(1)}, bf16[8,128,256]{2,1,0:T(8,128)(2,1)S(1)}, u32[]{:S(2)}, u32[]{:S(2)}) collective-permute-start(bf16[8,128,256]{2,1,0:T(8,128)(2,1)S(1)} %collective-permute-done.19.refs_8_), channel_id=1, source_target_pairs={{0,8},{4,28},{8,16},{12,4},{16,24},{20,12},{24,0},{28,20},{1,9},{5... | collective-permute-start | bytes 1572872 | tf_op jit(solution)/shard_map/ppermute | solution.py:397
  138.8 9.2 %collective-permute-start.22 = (bf16[8,128,256]{2,1,0:T(8,128)(2,1)S(1)}, bf16[8,128,256]{2,1,0:T(8,128)(2,1)S(1)}, u32[]{:S(2)}, u32[]{:S(2)}) collective-permute-start(bf16[8,128,256]{2,1,0:T(8,128)(2,1)S(1)} %pad_maximum_fusion.5), channel_id=1, source_target_pairs={{0,4},{4,0},{8,12},{12,8},{16,20},{20,16},{24,28},{28,24},{1,5},{5... | collective-permute-start | bytes 1572872 | tf_op jit(solution)/shard_map/ppermute | solution.py:386
  157.2 5.5 %collective-permute-start.27 = (f32[16,128]{1,0:T(8,128)S(1)}, f32[16,128]{1,0:T(8,128)S(1)}, u32[]{:S(2)}, u32[]{:S(2)}) collective-permute-start(f32[16,128]{1,0:T(8,128)S(1)} %add.11.refs_0_), channel_id=1, source_target_pairs={{0,8},{4,12},{8,16},{12,20},{16,24},{20,28},{24,0},{28,4},{1,9},{5... | collective-permute-start | bytes 24584 | tf_op jit(solution)/shard_map/ppermute | solution.py:391
  157.6 5.1 %collective-permute-start.28 = (f32[16,128]{1,0:T(8,128)S(1)}, f32[16,128]{1,0:T(8,128)S(1)}, u32[]{:S(2)}, u32[]{:S(2)}) collective-permute-start(f32[16,128]{1,0:T(8,128)S(1)} %add.11.refs_0_), channel_id=1, source_target_pairs={{0,16},{4,20},{8,24},{12,28},{16,0},{20,4},{24,8},{28,12},{1,17},{... | collective-permute-start | bytes 24584 | tf_op jit(solution)/shard_map/ppermute | solution.py:391
  158.5 4.7 %collective-permute-start.29 = (f32[16,128]{1,0:T(8,128)S(1)}, f32[16,128]{1,0:T(8,128)S(1)}, u32[]{:S(2)}, u32[]{:S(2)}) collective-permute-start(f32[16,128]{1,0:T(8,128)S(1)} %add.11.refs_0_), channel_id=1, source_target_pairs={{0,24},{4,28},{8,0},{12,4},{16,8},{20,12},{24,16},{28,20},{1,25},{... | collective-permute-start | bytes 24584 | tf_op jit(solution)/shard_map/ppermute | solution.py:391
  161.1 6.9 %collective-permute-start.34 = (f32[2048,256]{1,0:T(8,128)S(1)}, f32[2048,256]{1,0:T(8,128)S(1)}, u32[]{:S(2)}, u32[]{:S(2)}) collective-permute-start(f32[2048,256]{1,0:T(8,128)S(1)} %get-tuple-element.137.refs_12_.first.refs_4_), channel_id=1, source_target_pairs={{0,1},{1,0},{2,3},{3,2},{4,5},{5,4},{6,7},{7,6},{8,9},{9,8},{10,11... | collective-permute-start | bytes 6291464 | tf_op jit(solution)/shard_map/ppermute | solution.py:386
  163.2 5.8 %collective-permute-start.35 = (f32[2048,256]{1,0:T(8,128)S(1)}, f32[2048,256]{1,0:T(8,128)S(1)}, u32[]{:S(2)}, u32[]{:S(2)}) collective-permute-start(f32[2048,256]{1,0:T(8,128)S(1)} %collective-permute-done.30.refs_10_), channel_id=1, source_target_pairs={{0,1},{1,0},{2,3},{3,2},{4,5},{5,4},{6,7},{7,6},{8,9},{9,8},{10,11... | collective-permute-start | bytes 6291464 | tf_op jit(solution)/shard_map/ppermute | solution.py:386
  (23 other events, 250.3 us)
